TPU v7x, 32 devices: a whole 2x2x4 slice. The times are simulated.
32 devices in a mesh: groups: 2 (over y), tensor: 4 (over z), dp: 4 (over x, core).
Axes of the slice: x: 2, y: 2, z: 4, core: 2. Of those that a mesh axis runs over, the one named last changes fastest.
Arguments:
- inputs: bfloat16 [8192, 4096], P(('groups', 'dp'), 'tensor'), parts along dimension 0, may hold values from -6 to 6
- gate_pre: bfloat16 [8192, 14336], P(('groups', 'dp'), 'tensor'), parts along dimension 0, may hold values from -6 to 6
- grad_out: bfloat16 [8192, 4096], P(('groups', 'dp'), 'tensor'), parts along dimension 0, may hold values from -2 to 2
- w_down: bfloat16 [14336, 4096], P('tensor'), may hold values from -0.046875 to 0.046875
- proj_in: bfloat16 [4096, 64], P('tensor'), may hold values from -0.09375 to 0.09375
- proj_out: bfloat16 [14336, 64], P('tensor'), may hold values from -0.046875 to 0.046875
- hessian: float32 [8192, 4096], P(('groups', 'tensor', 'dp')), parts along dimension 0, may hold values from -3 to 3
- queries: float32 [512, 4096], P('groups', ('tensor', 'dp')), parts along dimension 0, may hold values from -0.09375 to 0.09375
Outputs:
- updated: float32 [8192, 4096], P(('groups', 'tensor', 'dp')), parts along dimension 0
- scores: float32 [16, 256], P(('groups', 'dp')), parts along dimension 0
There are 2 independent parts, one for each index of `groups`. A program takes and returns all parts, laid end to end along the dimension named above; an argument that names none is the same for every part. Nothing has to cross between parts.
All inputs are finite; a program needn't handle non-finite values.
Results may differ from a plain program's by a relative error of at most 0.0039.
Values may be sent and summed in bfloat16 or wider, within the bound.
No kernel may reach another device: no remote copies, remote signals or barrier semaphores. Data moves between devices by JAX's collectives and lax.ppermute only.
A program may use at most 128 MiB of HBM per device.

v0:
```python
import jax
import jax.numpy as jnp
from jax import lax
from jax.sharding import PartitionSpec as P

PROJ = 64
LEN = 512


def on_device(inputs, gate_pre, grad_out, w_down, proj_in, proj_out, hessian, queries):
    in_part = jnp.dot(inputs, proj_in, preferred_element_type=jnp.float32)
    columns = w_down
    hidden_grad = lax.dot_general(
        lax.all_gather(grad_out, "tensor", axis=1, tiled=True),
        columns,
        (((1,), (1,)), ((), ())),
        preferred_element_type=jnp.float32,
    )
    up_grad = (hidden_grad * jax.nn.silu(gate_pre.astype(jnp.float32))).astype(jnp.bfloat16)
    out_part = jnp.dot(up_grad, proj_out, preferred_element_type=jnp.float32)
    in_proj, out_proj = lax.psum((in_part, out_part), "tensor")
    left_proj = in_proj.reshape(-1, LEN, PROJ)
    right_proj = out_proj.reshape(-1, LEN, PROJ)
    local_grads = jnp.einsum(
        "sti,stj->sij", left_proj, right_proj, precision=lax.Precision.HIGHEST
    ).reshape(-1, PROJ * PROJ)
    all_grads = lax.all_gather(local_grads, "dp", axis=0, tiled=True)
    row_count = hessian.shape[0]
    row_start = lax.axis_index(("tensor", "dp")) * row_count
    mine = lax.dynamic_slice_in_dim(all_grads, row_start, row_count, 1)
    updated = (
        hessian + jnp.dot(mine.T, all_grads, precision=lax.Precision.HIGHEST) / all_grads.shape[0]
    )
    columns = local_grads
    scores = jnp.dot(
        columns,
        lax.all_gather(queries, ("tensor", "dp"), axis=1, tiled=True).T,
        precision=lax.Precision.HIGHEST,
    )
    return (updated, scores)


def solution(mesh):
    return jax.shard_map(
        on_device,
        mesh=mesh,
        in_specs=(
            P(("groups", "dp"), "tensor"),
            P(("groups", "dp"), "tensor"),
            P(("groups", "dp"), "tensor"),
            P("tensor", None),
            P("tensor", None),
            P("tensor", None),
            P(("groups", "tensor", "dp"), None),
            P("groups", ("tensor", "dp")),
        ),
        out_specs=(P(("groups", "tensor", "dp"), None), P(("groups", "dp"), None)),
        check_vma=False,
    )
```

profile of v0, /device:TPU:0, one launch (start us, length us, event | category | flops | bytes accessed | tf_op | source)
XLA Modules:
  0.0 286.5 jit_solution(7845811149773337070)
XLA Ops:
  8.0 0.0 copy-start
  8.0 0.0 all-gather.4.cloned.1.call-start
  8.1 0.7 all-gather.4.cloned.1.call-update
  8.7 0.0 all-reduce.3.cloned.1.call-start
  8.8 0.8 copy-done
  9.6 1.7 fusion.10
  11.3 151.5 %all-gather.4.cloned.1.call-done = bf16[1024,4096]{1,0:T(8,128)(2,1)} async-done(((bf16[1024,1024]{1,0:T(8,128)(2,1)}), bf16[1024,4096]{1,0:T(8,128)(2,1)}) %all-gather.4.cloned.1.call-update) | async-done | bytes 8388624 | tf_op jit(solution)/shard_map/all_gather | solution.py:14
  162.8 44.1 %fusion.6 = f32[1024,64]{0,1:T(8,128)S(1)} fusion(bf16[3584,64]{0,1:T(8,128)(2,1)} %param.13, bf16[1024,3584]{1,0:T(8,128)(2,1)} %param.9, bf16[1024,4096]{1,0:T(8,128)(2,1)} %all-gather.4.cloned.1.call-done, bf16[3584,4096]{1,0:T(8,128)(2,1)} %param.11), kind=kOutput, calls=%fused_computation.9 | convolution fusion | flops 30560223232 | bytes 45809664 | tf_op jit(solution)/shard_map/dot_general | solution.py:20
  206.9 0.8 copy_bitcast_fusion
  207.7 0.0 all-reduce.3.cloned.1.call-update
  207.8 0.0 all-gather.6.cloned.1.call-start
  207.8 0.5 all-gather.6.cloned.1.call-update
  208.4 50.7 %all-reduce.3.cloned.1.call-done = (f32[2,512,64]{1,2,0:T(8,128)}, f32[2,512,64]{1,2,0:T(8,128)}) async-done(((f32[2,512,64]{1,2,0:T(8,128)}, f32[2,512,64]{1,2,0:T(8,128)}), (f32[2,512,64]{1,2,0:T(8,128)}, f32[2,512,64]{1,2,0:T(8,128)})) %all-reduce.3.cloned.1.call-update) | async-done | bytes 524304 | tf_op jit(solution)/shard_map/psum | solution.py:21
  259.0 1.4 fusion.11
  260.5 0.1 reshape.16
  260.6 0.1 reshape.15
  260.6 5.4 %all-gather = f32[4,2,4096]{2,1,0:T(2,128)S(1)} all-gather(f32[1,2,4096]{2,1,0:T(2,128)S(1)} %reshape.16), channel_id=1, replica_groups=mesh['groups'=2,'tensor'=4,'dp'=4] {'dp'}, dimensions={0}, use_global_device_ids=true | all-gather | bytes 163840 | tf_op jit(solution)/shard_map/all_gather | solution.py:27
  266.1 0.1 reshape.17
  266.2 6.8 %fusion.5 = f32[256,4096]{1,0:T(8,128)} fusion(f32[256,4096]{1,0:T(8,128)} %param.14, f32[8,4096]{1,0:T(8,128)S(1)} %reshape.17, s32[]{:T(128)S(6)} %select_n.3), kind=kOutput, calls=%fused_computation.8 | convolution fusion | flops 102760448 | bytes 8527876 | tf_op jit(solution)/shard_map/dot_general | solution.py:32
  272.9 0.0 all-gather.6.cloned.1.call-done
  272.9 6.1 %fusion.12 = f32[2,256]{1,0:T(2,128)} fusion(f32[2,4096]{1,0:T(2,128)S(1)} %reshape.15, f32[256,4096]{1,0:T(8,128)} %all-gather.6.cloned.1.call-done), kind=kOutput, calls=%fused_computation.17 | convolution fusion | flops 25165824 | bytes 4229120 | tf_op jit(solution)/shard_map/dot_general | solution.py:35
Async XLA Ops:
  8.0 1.6 copy-start
  8.0 154.8 %all-gather.4.cloned.1.call-start = ((), (), s32[]{:S(2)}) async-start(), calls=%async_computation | async-start | bytes 10485760 | tf_op jit(solution)/shard_map/all_gather | solution.py:14
  8.7 250.3 %all-reduce.3.cloned.1.call-start = ((), (), s32[]{:S(2)}) async-start(), calls=%async_computation.2 | async-start | bytes 1048576 | tf_op jit(solution)/shard_map/psum | solution.py:21
  207.8 65.2 %all-gather.6.cloned.1.call-start = ((), (), s32[]{:S(2)}) async-start(), calls=%async_computation.1 | async-start | bytes 4456448 | tf_op jit(solution)/shard_map/all_gather | solution.py:37
Sparse Core Ops, SparseCore 0:
  10.4 152.3 all-gather.3
  207.9 51.1 all-reduce.2
Sparse Core Ops, SparseCore 1:
  210.4 56.7 all-gather.5
where the time goes:
time: 287 us; the launch traced here: 286 us
  waiting for transfers between devices  203 us (71%)
  matrix products  60 us (21%)
  between operations  15.5 us (5%)
  blocking collectives  5.43 us (2%)
    all_gather x1, waiting for transfers between devices, on_device(): lax.all_gather(grad_out, 'tensor', axis=1, tiled=True)  152 us
    psum x1, waiting for transfers between devices, on_device(): in_proj, out_proj = lax.psum((in_part, out_part), 'tensor')  50.7 us
    dot_general x1, matrix products, on_device(): out_part = jnp.dot(up_grad, proj_out, preferred_element_type=jnp.float32)  44.1 us
    dot_general x1, matrix products, on_device(): jnp.dot(mine.T, all_grads, precision=lax.Precision.HIGHEST)  6.75 us
    dot_general x1, matrix products, on_device(): jnp.dot(columns, lax.all_gather(queries, ('tensor', 'dp'), axis=1, tiled=...  6.12 us
  transfers between devices with their start and end apart: 3, of which 2 were waited for; matrix products, arithmetic and copies ran while one was open for 4% of the time, Pallas kernels for 0%

commit v1 on v0

v1 whole, which is shorter than its diff:
```python
import jax
import jax.numpy as jnp
from jax import lax
from jax.sharding import PartitionSpec as P

PROJ = 64
LEN = 512
HIGHEST = lax.Precision.HIGHEST


def on_device(inputs, gate_pre, grad_out, w_down, proj_in, proj_out, hessian, queries):
    tokens = grad_out.shape[0]
    in_part = jnp.dot(inputs, proj_in, preferred_element_type=jnp.float32)
    in_proj = lax.psum(in_part, "tensor")

    sizes = []
    for start in range(0, tokens, LEN):
        last = start + LEN >= tokens
        sizes += [LEN // 2, LEN // 4, LEN // 4] if last else [LEN // 2, LEN // 2]
    grads = [jnp.zeros((PROJ, PROJ), jnp.float32) for _ in range(tokens // LEN)]
    at = 0
    for size in sizes:
        rows = slice(at, at + size)
        block = lax.all_gather(grad_out[rows], "tensor", axis=1, tiled=True)
        hidden_grad = lax.dot_general(
            block, w_down, (((1,), (1,)), ((), ())), preferred_element_type=jnp.float32
        )
        up_grad = (hidden_grad * jax.nn.silu(gate_pre[rows].astype(jnp.float32))).astype(jnp.bfloat16)
        out_part = jnp.dot(up_grad, proj_out, preferred_element_type=jnp.float32)
        grads[at // LEN] += lax.dot_general(
            in_proj[rows], out_part, (((0,), (0,)), ((), ())), precision=HIGHEST
        )
        at += size
    local_grads = jnp.stack(grads).reshape(-1, PROJ * PROJ)
    parts = lax.all_gather(local_grads, ("tensor", "dp"), axis=0, tiled=True)
    all_grads = parts.reshape(lax.axis_size("tensor"), -1, PROJ * PROJ).sum(0)

    row_count = hessian.shape[0]
    row_start = lax.axis_index(("tensor", "dp")) * row_count
    mine = lax.dynamic_slice_in_dim(all_grads, row_start, row_count, 1)
    updated = hessian + jnp.dot(mine.T, all_grads, precision=HIGHEST) / all_grads.shape[0]
    score_part = jnp.dot(mine, queries.T, precision=HIGHEST)
    scores = lax.psum(score_part, ("tensor", "dp"))
    count = local_grads.shape[0]
    scores = lax.dynamic_slice_in_dim(scores, lax.axis_index("dp") * count, count, 0)
    return (updated, scores)


def solution(mesh):
    return jax.shard_map(
        on_device,
        mesh=mesh,
        in_specs=(
            P(("groups", "dp"), "tensor"),
            P(("groups", "dp"), "tensor"),
            P(("groups", "dp"), "tensor"),
            P("tensor", None),
            P("tensor", None),
            P("tensor", None),
            P(("groups", "tensor", "dp"), None),
            P("groups", ("tensor", "dp")),
        ),
        out_specs=(P(("groups", "tensor", "dp"), None), P(("groups", "dp"), None)),
        check_vma=False,
    )
```

time: 287 us -> 329 us (1.15)
  blocking collectives: 5.43 us -> 50.9 us
  waiting for transfers between devices: 203 us -> 169 us
  matrix products: 60 us -> 88.3 us
  local copies, waits for them, and re-layouts: 1.93 us -> 5.76 us
    dot_general x1 -> x5, matrix products: 44.1 us -> 76.4 us  [on_device(): out_part = jnp.dot(up_grad, proj_out, preferred_element_type=jnp.float32)]
    psum x0 -> x1, blocking collectives: none -> 30.4 us  [on_device(): scores = lax.psum(score_part, ('tensor', 'dp'))]
    psum x1, waiting for transfers between devices: 50.7 us -> 21.9 us  [on_device(): in_proj = lax.psum(in_part, 'tensor')]
    all_gather x1, blocking collectives: 5.43 us -> 20.5 us  [on_device(): parts = lax.all_gather(local_grads, ('tensor', 'dp'), axis=0, tiled=True)]
    all_gather x2 -> x5, waiting for transfers between devices: 152 us -> 145 us  [on_device(): block = lax.all_gather(grad_out[rows], 'tensor', axis=1, tiled=True)]
    slice x0 -> x2, local copies, waits for them, and re-layouts: none -> 4.62 us  [on_device(): block = lax.all_gather(grad_out[rows], 'tensor', axis=1, tiled=True)]
    dot_general x3 -> x7, matrix products: 14.3 us -> 10.4 us  [the longest x1 6.75 us: on_device(): jnp.dot(mine.T, all_grads, precision=HIGHEST) / all_grads.shape[0]]
  transfers between devices with their start and end apart: 3 -> 6, of which waited for: 2 -> 6; matrix products, arithmetic and copies ran while one was open for 4% -> 21% of each run, Pallas kernels for 0% -> 0%
where the time goes in v1:
time: 329 us; the launch traced here: 328 us
  waiting for transfers between devices  169 us (51%)
  matrix products  88.3 us (27%)
  blocking collectives  50.9 us (15%)
  between operations  14.3 us (4%)
  local copies, waits for them, and re-layouts  5.76 us (2%)
    all_gather x5, waiting for transfers between devices, on_device(): block = lax.all_gather(grad_out[rows], 'tensor', axis=1, tiled=True)  145 us
    dot_general x5, matrix products, on_device(): out_part = jnp.dot(up_grad, proj_out, preferred_element_type=jnp.float32)  76.4 us
    psum x1, blocking collectives, on_device(): scores = lax.psum(score_part, ('tensor', 'dp'))  30.4 us
    psum x1, waiting for transfers between devices, on_device(): in_proj = lax.psum(in_part, 'tensor')  21.9 us
    all_gather x1, blocking collectives, on_device(): parts = lax.all_gather(local_grads, ('tensor', 'dp'), axis=0, tiled=True)  20.5 us
    dot_general x1, matrix products, on_device(): jnp.dot(mine.T, all_grads, precision=HIGHEST) / all_grads.shape[0]  6.75 us
  transfers between devices with their start and end apart: 6, of which 6 were waited for; matrix products, arithmetic and copies ran while one was open for 21% of the time, Pallas kernels for 0%

profile of v1, /device:TPU:0, one launch (start us, length us, event | category | flops | bytes accessed | tf_op | source)
XLA Modules:
  0.0 328.2 jit_solution(8990929925484895297)
XLA Ops:
  7.2 2.0 fusion.48
  9.3 0.7 all-gather.13.cloned.1.call-update
  10.1 2.6 fusion.47
  12.7 0.0 all-reduce.2.cloned.1.call-start
  12.8 1.5 fusion.49
  14.3 0.0 all-gather.9.cloned.1.call-start
  14.4 0.5 all-gather.9.cloned.1.call-update
  14.9 0.5 all-gather.7.cloned.1.call-update
  15.5 24.8 %all-gather.15.cloned.1.call-done = bf16[128,4096]{1,0:T(8,128)(2,1)} async-done(((bf16[128,1024]{1,0:T(8,128)(2,1)}), bf16[128,4096]{1,0:T(8,128)(2,1)}) %all-gather.15.cloned.1.call-update) | async-done | bytes 1048592 | tf_op jit(solution)/shard_map/all_gather | solution.py:24
  40.3 15.9 %fusion.15 = f32[128,64]{1,0:T(8,128)S(1)} fusion(bf16[3584,64]{0,1:T(8,128)(2,1)S(1)} %copy-done.4, bf16[128,4096]{1,0:T(8,128)(2,1)} %all-gather.15.cloned.1.call-done, bf16[3584,4096]{1,0:T(8,128)(2,1)} %param.11, bf16[1024,3584]{1,0:T(8,128)(2,1)} %param.9), kind=kOutput, calls=%fused_computation.31 | convolution fusion | flops 3820027904 | bytes 31817728 | tf_op jit(solution)/shard_map/dot_general | solution.py:29
  56.2 13.0 %all-gather.13.cloned.1.call-done = bf16[128,4096]{1,0:T(8,128)(2,1)} async-done(((bf16[128,1024]{1,0:T(8,128)(2,1)}), bf16[128,4096]{1,0:T(8,128)(2,1)}) %all-gather.13.cloned.1.call-update) | async-done | bytes 1048592 | tf_op jit(solution)/shard_map/all_gather | solution.py:24
  69.2 15.9 %fusion.16 = f32[128,64]{1,0:T(8,128)S(1)} fusion(bf16[3584,64]{0,1:T(8,128)(2,1)S(1)} %copy-done.4, bf16[128,4096]{1,0:T(8,128)(2,1)} %all-gather.13.cloned.1.call-done, bf16[3584,4096]{1,0:T(8,128)(2,1)} %param.11, bf16[1024,3584]{1,0:T(8,128)(2,1)} %param.9), kind=kOutput, calls=%fused_computation.32 | convolution fusion | flops 3820027904 | bytes 31817728 | tf_op jit(solution)/shard_map/dot_general | solution.py:29
  85.1 31.2 %all-gather.11.cloned.1.call-done = bf16[256,4096]{1,0:T(8,128)(2,1)} async-done(((bf16[256,1024]{1,0:T(8,128)(2,1)}), bf16[256,4096]{1,0:T(8,128)(2,1)}) %all-gather.11.cloned.1.call-update) | async-done | bytes 2097168 | tf_op jit(solution)/shard_map/all_gather | solution.py:24
  116.3 14.9 %fusion.27 = f32[256,64]{1,0:T(8,128)S(1)} fusion(bf16[3584,64]{0,1:T(8,128)(2,1)S(1)} %copy-done.4, bf16[256,4096]{1,0:T(8,128)(2,1)} %all-gather.11.cloned.1.call-done, bf16[3584,4096]{1,0:T(8,128)(2,1)} %param.11, bf16[1024,3584]{1,0:T(8,128)(2,1)} %param.9), kind=kOutput, calls=%fused_computation.46 | convolution fusion | flops 7640055808 | bytes 33816576 | tf_op jit(solution)/shard_map/dot_general | solution.py:29
  131.2 21.9 %all-reduce.2.cloned.1.call-done = f32[1024,64]{0,1:T(8,128)} async-done(((f32[1024,64]{0,1:T(8,128)}), f32[1024,64]{0,1:T(8,128)}) %all-reduce.2.cloned.1.call-update) | async-done | bytes 262160 | tf_op jit(solution)/shard_map/psum | solution.py:14
  153.0 1.1 fusion.30
  154.1 0.9 convolution_add_fusion.1
  155.0 0.9 convolution_add_fusion
  156.0 0.1 stack.10
  156.1 44.7 %all-gather.9.cloned.1.call-done = bf16[256,4096]{1,0:T(8,128)(2,1)} async-done(((bf16[256,1024]{1,0:T(8,128)(2,1)}), bf16[256,4096]{1,0:T(8,128)(2,1)}) %all-gather.9.cloned.1.call-update) | async-done | bytes 2097168 | tf_op jit(solution)/shard_map/all_gather | solution.py:24
  200.8 14.9 %fusion.28 = f32[256,64]{1,0:T(8,128)S(1)} fusion(bf16[3584,64]{0,1:T(8,128)(2,1)S(1)} %copy-done.4, bf16[256,4096]{1,0:T(8,128)(2,1)} %all-gather.9.cloned.1.call-done, bf16[3584,4096]{1,0:T(8,128)(2,1)} %param.11, bf16[1024,3584]{1,0:T(8,128)(2,1)} %param.9), kind=kOutput, calls=%fused_computation.47 | convolution fusion | flops 7640055808 | bytes 33816576 | tf_op jit(solution)/shard_map/dot_general | solution.py:29
  215.8 31.3 %all-gather.7.cloned.1.call-done = bf16[256,4096]{1,0:T(8,128)(2,1)} async-done(((bf16[256,1024]{1,0:T(8,128)(2,1)}), bf16[256,4096]{1,0:T(8,128)(2,1)}) %all-gather.7.cloned.1.call-update) | async-done | bytes 2097168 | tf_op jit(solution)/shard_map/all_gather | solution.py:24
  247.0 14.8 %fusion.29 = f32[256,64]{1,0:T(8,128)S(1)} fusion(bf16[3584,64]{0,1:T(8,128)(2,1)S(1)} %copy-done.4, bf16[256,4096]{1,0:T(8,128)(2,1)} %all-gather.7.cloned.1.call-done, bf16[3584,4096]{1,0:T(8,128)(2,1)} %param.11, bf16[1024,3584]{1,0:T(8,128)(2,1)} %param.9), kind=kOutput, calls=%fused_computation.48 | convolution fusion | flops 7640055808 | bytes 33816576 | tf_op jit(solution)/shard_map/dot_general | solution.py:29
  261.8 0.2 fusion.33
  262.1 0.2 convolution_add_fusion.2
  262.3 0.1 stack.9
  262.4 20.5 %all-gather = f32[16,2,4096]{2,1,0:T(2,128)S(1)} all-gather(f32[1,2,4096]{2,1,0:T(2,128)S(1)} %maximum_bitcast_fusion), channel_id=1, replica_groups=mesh['groups'=2,'tensor'=4,'dp'=4] {'tensor','dp'}, dimensions={0}, use_global_device_ids=true | all-gather | bytes 557056 | tf_op jit(solution)/shard_map/all_gather | solution.py:35
  282.9 0.4 reshape.12
  283.4 0.3 fusion.37
  283.6 30.4 %psum.15 = f32[8,256]{1,0:T(8,128)S(1)} all-reduce(f32[8,256]{1,0:T(8,128)S(1)} %fusion.37), channel_id=1, replica_groups=mesh['groups'=2,'tensor'=4,'dp'=4] {'tensor','dp'}, use_global_device_ids=true, to_apply=%region_2.3 | all-reduce | flops 2048 | bytes 16384 | tf_op jit(solution)/shard_map/psum | solution.py:43
  314.0 6.7 %fusion = f32[256,4096]{1,0:T(8,128)} fusion(f32[256,4096]{1,0:T(8,128)} %param.14, f32[8,4096]{1,0:T(8,128)S(1)} %reduce_sum.9, s32[]{:T(128)S(6)} %select_n.6), kind=kOutput, calls=%fused_computation.4 | convolution fusion | flops 102760448 | bytes 8527876 | tf_op jit(solution)/shard_map/dot_general | solution.py:41
  320.8 0.6 constant_dynamic-slice_fusion
  (19 shorter events, 0.3 us)
Async XLA Ops:
  7.2 5.6 %copy-start = (bf16[1024,1024]{1,0:T(8,128)(2,1)S(1)}, bf16[1024,1024]{1,0:T(8,128)(2,1)}, u32[]{:S(2)}) copy-start(bf16[1024,1024]{1,0:T(8,128)(2,1)} %param.8) | copy-start | bytes 6291460
  7.2 5.6 %copy-start.3 = (bf16[1024,64]{0,1:T(8,128)(2,1)S(1)}, bf16[1024,64]{0,1:T(8,128)(2,1)}, u32[]{:S(2)}) copy-start(bf16[1024,64]{0,1:T(8,128)(2,1)} %param.12) | copy-start | bytes 393220
  7.2 33.1 %all-gather.15.cloned.1.call-start = ((), (), s32[]{:S(2)}) async-start(), calls=%async_computation.5 | async-start | bytes 1310720 | tf_op jit(solution)/shard_map/all_gather | solution.py:24
  9.3 59.9 %all-gather.13.cloned.1.call-start = ((), (), s32[]{:S(2)}) async-start(), calls=%async_computation.4 | async-start | bytes 1310720 | tf_op jit(solution)/shard_map/all_gather | solution.py:24
  10.0 30.2 %copy-start.4 = (bf16[3584,64]{0,1:T(8,128)(2,1)S(1)}, bf16[3584,64]{0,1:T(8,128)(2,1)}, u32[]{:S(2)}) copy-start(bf16[3584,64]{0,1:T(8,128)(2,1)} %param.13) | copy-start | bytes 1376260
  10.0 106.3 %all-gather.11.cloned.1.call-start = ((), (), s32[]{:S(2)}) async-start(), calls=%async_computation.3 | async-start | bytes 2621440 | tf_op jit(solution)/shard_map/all_gather | solution.py:24
  12.7 140.3 %all-reduce.2.cloned.1.call-start = ((), (), s32[]{:S(2)}) async-start(), calls=%async_computation | async-start | bytes 524288 | tf_op jit(solution)/shard_map/psum | solution.py:14
  14.3 186.5 %all-gather.9.cloned.1.call-start = ((), (), s32[]{:S(2)}) async-start(), calls=%async_computation.2 | async-start | bytes 2621440 | tf_op jit(solution)/shard_map/all_gather | solution.py:24
  14.9 232.1 %all-gather.7.cloned.1.call-start = ((), (), s32[]{:S(2)}) async-start(), calls=%async_computation.1 | async-start | bytes 2621440 | tf_op jit(solution)/shard_map/all_gather | solution.py:24
  215.7 46.1 %copy-start.1 = (f32[1024,64]{0,1:T(8,128)S(1)}, f32[1024,64]{0,1:T(8,128)}, u32[]{:S(2)}) copy-start(f32[1024,64]{0,1:T(8,128)} %all-reduce.2.cloned.1.call-done) | copy-start | bytes 786436
  215.7 67.6 %copy-start.2 = (f32[256,256]{1,0:T(8,128)S(1)}, f32[256,256]{1,0:T(8,128)}, u32[]{:S(2)}) copy-start(f32[256,256]{1,0:T(8,128)} %param.15) | copy-start | bytes 786436
Sparse Core Ops, SparseCore 0:
  9.6 30.6 all-gather.14
  41.8 27.3 all-gather.12
  70.8 45.4 all-gather.10
  118.5 34.4 all-reduce.1
  155.1 45.6 all-gather.8
  202.3 44.6 all-gather.6

commit v2 on v0

v2 whole, which is shorter than its diff:
```python
import functools

import jax
import jax.numpy as jnp
from jax import lax
from jax.experimental import pallas as pl
from jax.experimental.pallas import tpu as pltpu
from jax.sharding import PartitionSpec as P

PROJ = 64
LEN = 512
HIGHEST = lax.Precision.HIGHEST
NT = (((1,), (1,)), ((), ()))
TILE = 512
VMEM_BYTES = 40 * 2**20


def silu(v):
    return 0.5 * v * (1.0 + jnp.tanh(0.5 * v))


def dot_nt(a, b):
    return lax.dot_general(a, b, NT, preferred_element_type=jnp.float32)


def cost(flops, moved):
    return pl.CostEstimate(flops=flops, bytes_accessed=moved, transcendentals=0)


def params():
    return pltpu.CompilerParams(vmem_limit_bytes=VMEM_BYTES)


def first_body(where_ref, own_ref, pair_ref, w_own_ref, w_pair_ref, acc_ref):
    acc_ref[...] = dot_nt(own_ref[...], w_own_ref[...]) + dot_nt(pair_ref[...], w_pair_ref[...])


def first_blocks(where, own, pair, w):
    rows, feats = own.shape
    hidden = w.shape[0]
    whole = pl.BlockSpec((rows, feats), lambda j, where: (0, 0))
    return pl.pallas_call(
        first_body,
        grid_spec=pltpu.PrefetchScalarGridSpec(
            num_scalar_prefetch=1,
            grid=(hidden // TILE,),
            in_specs=[
                whole,
                whole,
                pl.BlockSpec((TILE, feats), lambda j, where: (j, where[0])),
                pl.BlockSpec((TILE, feats), lambda j, where: (j, where[1])),
            ],
            out_specs=pl.BlockSpec((rows, TILE), lambda j, where: (0, j)),
        ),
        out_shape=jax.ShapeDtypeStruct((rows, hidden), jnp.float32),
        compiler_params=params(),
        cost_estimate=cost(4 * rows * feats * hidden, 4 * rows * hidden + 4 * feats * hidden),
        name="first_blocks",
    )(where, own, pair, w, w)


def second_body(where_ref, inner_ref, outer_ref, w_ref, old_ref, acc_ref, block):
    @pl.when(pl.program_id(0) == 0)
    def _():
        block[...] = jnp.where(where_ref[4] == 1, inner_ref[...], outer_ref[...])

    acc_ref[...] = old_ref[...] + dot_nt(block[...], w_ref[...])


def second_block(where, inner, outer, w, old):
    rows, feats = inner.shape
    hidden = w.shape[0]
    whole = pl.BlockSpec((rows, feats), lambda j, where: (0, 0))
    tile = pl.BlockSpec((rows, TILE), lambda j, where: (0, j))
    return pl.pallas_call(
        second_body,
        grid_spec=pltpu.PrefetchScalarGridSpec(
            num_scalar_prefetch=1,
            grid=(hidden // TILE,),
            in_specs=[
                whole,
                whole,
                pl.BlockSpec((TILE, feats), lambda j, where: (j, where[2])),
                tile,
            ],
            out_specs=tile,
            scratch_shapes=[pltpu.VMEM((rows, feats), jnp.bfloat16)],
        ),
        out_shape=jax.ShapeDtypeStruct((rows, hidden), jnp.float32),
        input_output_aliases={4: 0},
        compiler_params=params(),
        cost_estimate=cost(2 * rows * feats * hidden, 8 * rows * hidden + 2 * feats * hidden),
        name="second_block",
    )(where, inner, outer, w, old)


def last_body(
    where_ref, inner_ref, outer_ref, w_ref, old_ref, gate_ref, po_ref, left_ref, grads_in, early_ref, grads_ref, block, right
):
    step = pl.program_id(0)

    @pl.when(step == 0)
    def _():
        block[...] = jnp.where(where_ref[4] == 1, inner_ref[...], outer_ref[...])
        right[...] = jnp.zeros_like(right)

    hidden_grad = old_ref[...] + dot_nt(block[...], w_ref[...])
    up_grad = (hidden_grad * silu(gate_ref[...].astype(jnp.float32))).astype(jnp.bfloat16)
    right[...] += dot_nt(up_grad, po_ref[...])

    @pl.when(step == pl.num_programs(0) - 1)
    def _():
        grads_ref[...] = grads_in[...] + jnp.dot(
            left_ref[...], right[...], precision=HIGHEST, preferred_element_type=jnp.float32
        )


def last_block(where, inner, outer, at, w, old, gate, po_t, left_t, grads, early):
    size, feats = outer.shape
    hidden = w.shape[0]
    chunk = at // size
    tile = pl.BlockSpec((size, TILE), lambda j, where: (chunk, j))
    small = pl.BlockSpec((PROJ, PROJ), lambda j, where: (0, 0))
    return pl.pallas_call(
        last_body,
        grid_spec=pltpu.PrefetchScalarGridSpec(
            num_scalar_prefetch=1,
            grid=(hidden // TILE,),
            in_specs=[
                pl.BlockSpec((size, feats), lambda j, where: (chunk, 0)),
                pl.BlockSpec((size, feats), lambda j, where: (0, 0)),
                pl.BlockSpec((TILE, feats), lambda j, where: (j, where[3])),
                tile,
                tile,
                pl.BlockSpec((PROJ, TILE), lambda j, where: (0, j)),
                pl.BlockSpec((PROJ, size), lambda j, where: (0, chunk)),
                small,
                pl.BlockSpec(memory_space=pl.ANY),
            ],
            out_specs=small,
            scratch_shapes=[
                pltpu.VMEM((size, feats), jnp.bfloat16),
                pltpu.VMEM((size, PROJ), jnp.float32),
            ],
        ),
        out_shape=jax.ShapeDtypeStruct((PROJ, PROJ), jnp.float32),
        compiler_params=params(),
        cost_estimate=cost(2 * size * (feats + PROJ) * hidden, 6 * size * hidden + 2 * feats * hidden),
        name="last_block",
    )(where, inner, outer, w, old, gate, po_t, left_t, grads, early)


def pieces(a):
    high = a.astype(jnp.bfloat16)
    rest = a - high.astype(jnp.float32)
    middle = rest.astype(jnp.bfloat16)
    low = (rest - middle.astype(jnp.float32)).astype(jnp.bfloat16)
    return high, middle, low


def update_body(row_ref, scale, grads_ref, mine_ref, hessian_ref, out_ref):
    high, middle, low = pieces(mine_ref[...])
    left = jnp.concatenate([high, high, middle, middle, high, low], axis=0)
    high, middle, low = pieces(grads_ref[...])
    right = jnp.concatenate([high, middle, high, middle, low, high], axis=0)
    total = lax.dot_general(left, right, (((0,), (0,)), ((), ())), preferred_element_type=jnp.float32)
    out_ref[...] = hessian_ref[...] + total * scale


def update(row, grads, hessian):
    rows, columns = hessian.shape
    count = grads.shape[0]
    width = min(columns, 512)
    tile = pl.BlockSpec((rows, width), lambda j, row: (0, j))

    def body(row_ref, *refs):
        update_body(row_ref, 1.0 / count, *refs)

    return pl.pallas_call(
        body,
        grid_spec=pltpu.PrefetchScalarGridSpec(
            num_scalar_prefetch=1,
            grid=(columns // width,),
            in_specs=[
                pl.BlockSpec((count, width), lambda j, row: (0, j)),
                pl.BlockSpec((count, rows), lambda j, row: (0, row[0])),
                tile,
            ],
            out_specs=tile,
        ),
        out_shape=jax.ShapeDtypeStruct((rows, columns), jnp.float32),
        compiler_params=params(),
        cost_estimate=cost(2 * 48 * rows * columns, 8 * rows * columns),
        name="hessian_update",
    )(row, grads, grads, hessian)


def line_of_four(inputs, gate_pre, grad_out, w_down, proj_in, proj_out, early):
    send = functools.partial(lax.ppermute, axis_name="tensor")
    pairs = [(0, 1), (1, 0), (2, 3), (3, 2)]
    inner = [(1, 2), (2, 1)]
    outward = [(1, 0), (2, 3)]
    inward = [(0, 1), (3, 2)]
    tokens = grad_out.shape[0]
    z = lax.axis_index("tensor")
    low = z < 2
    middle = jnp.logical_and(z > 0, z < 3)
    where = jnp.stack(
        [z, z + 1 - 2 * (z % 2), jnp.where(low, 2, 1), jnp.where(low, 3, 0), middle.astype(z.dtype)]
    ).astype(jnp.int32)

    pair = send(grad_out, perm=pairs)
    far_middle_inner = send(grad_out, perm=inner)
    in_part = lax.dot_general(
        proj_in, inputs, (((0,), (1,)), ((), ())), preferred_element_type=jnp.float32
    )
    side = in_part + send(in_part, perm=inward)
    total = side + send(side, perm=inner)
    left_t = jnp.where(middle, total, send(total, perm=outward))

    far_middle_outer = send(far_middle_inner, perm=outward)
    far_end_inner = send(pair, perm=inner)
    acc = first_blocks(where, grad_out, pair, w_down)
    acc = second_block(where, far_middle_inner, far_middle_outer, w_down, acc)

    grads = [jnp.zeros((PROJ, PROJ), jnp.float32) for _ in range(tokens // LEN)]
    at = 0
    while at < tokens:
        size = 256 if at + 256 < tokens else 128
        far_end_outer = send(far_end_inner[at : at + size], perm=outward)
        grads[at // LEN] = last_block(
            where, far_end_inner, far_end_outer, at, w_down, acc, gate_pre, proj_out.T, left_t, grads[at // LEN], early
        )
        at += size
    return jnp.stack(grads).reshape(-1, PROJ * PROJ)


def any_line(inputs, gate_pre, grad_out, w_down, proj_in, proj_out, early):
    in_part = jnp.dot(inputs, proj_in, preferred_element_type=jnp.float32)
    in_proj = lax.psum(in_part, "tensor").reshape(-1, LEN, PROJ)
    gathered = lax.all_gather(grad_out, "tensor", axis=1, tiled=True)
    up_grad = (dot_nt(gathered, w_down) * silu(gate_pre.astype(jnp.float32))).astype(jnp.bfloat16)
    out_part = jnp.dot(up_grad, proj_out, preferred_element_type=jnp.float32).reshape(-1, LEN, PROJ)
    grads = jnp.einsum("sti,stj->sij", in_proj, out_part, precision=HIGHEST)
    return grads.reshape(-1, PROJ * PROJ)


def xor_parts(a, axis):
    size = lax.axis_size(axis)
    return [a] + [lax.ppermute(a, axis, [(i, i ^ s) for i in range(size)]) for s in range(1, size)]


def xor_sum(a, axis):
    terms = xor_parts(a, axis)
    while len(terms) > 1:
        terms = [terms[i] + terms[i + 1] for i in range(0, len(terms), 2)]
    return terms[0]


def gather_queries(queries):
    rows, width = queries.shape
    me = lax.axis_index("dp")
    whole = jnp.zeros((rows, width * lax.axis_size("dp")), queries.dtype)
    for s, part in enumerate(xor_parts(queries, "dp")):
        whole = lax.dynamic_update_slice_in_dim(whole, part, (me ^ s) * width, 1)
    return whole


def on_device(inputs, gate_pre, grad_out, w_down, proj_in, proj_out, hessian, queries):
    z_queries = gather_queries(queries)
    line = line_of_four if lax.axis_size("tensor") == 4 else any_line
    grads = line(inputs, gate_pre, grad_out, w_down, proj_in, proj_out, z_queries)
    grads = xor_sum(grads, "tensor")

    width = z_queries.shape[1]
    quarter = lax.dynamic_slice_in_dim(grads, lax.axis_index("tensor") * width, width, 1)
    scores = xor_sum(jnp.dot(quarter, z_queries.T, precision=HIGHEST), "tensor")

    all_grads = jnp.concatenate(xor_parts(grads, "dp"), axis=0)
    row_count = hessian.shape[0]
    at = lax.axis_index(("tensor", "dp"))
    if row_count % 128:
        mine = lax.dynamic_slice_in_dim(all_grads, at * row_count, row_count, 1)
        updated = hessian + jnp.dot(mine.T, all_grads, precision=HIGHEST) / all_grads.shape[0]
    else:
        updated = update(at.reshape(1).astype(jnp.int32), all_grads, hessian)
    return (updated, scores)


def solution(mesh):
    return jax.shard_map(
        on_device,
        mesh=mesh,
        in_specs=(
            P(("groups", "dp"), "tensor"),
            P(("groups", "dp"), "tensor"),
            P(("groups", "dp"), "tensor"),
            P("tensor", None),
            P("tensor", None),
            P("tensor", None),
            P(("groups", "tensor", "dp"), None),
            P("groups", ("tensor", "dp")),
        ),
        out_specs=(P(("groups", "tensor", "dp"), None), P(("groups", "dp"), None)),
        check_vma=False,
    )
```

time: 287 us -> 226 us (0.79)
  waiting for transfers between devices: 203 us -> 78.6 us
  Pallas kernels: 0 us -> 90.3 us
  matrix products: 60 us -> 2.58 us
  starting transfers between devices: 0.12 us -> 35.3 us
  between operations: 15.5 us -> 1.01 us
  local copies, waits for them, and re-layouts: 1.93 us -> 15.4 us
  blocking collectives: 5.43 us -> 0 us
    all_gather x2 -> x0, waiting for transfers between devices: 152 us -> none  [the longest x1 152 us: on_device(): lax.all_gather(grad_out, 'tensor', axis=1, tiled=True)]
    pallas_call x0 -> x8, Pallas kernels: none -> 90.3 us  [the longest x5 44.1 us: last_block(): pl.pallas_call(last_body, grid_spec=pltpu.PrefetchScalarGridSpec(num_scal...]
    ppermute x0 -> x24, waiting for transfers between devices: none -> 78.6 us  [the longest x1 42.1 us: line_of_four(): side = in_part + send(in_part, perm=inward)]
    dot_general x5 -> x2, matrix products: 60 us -> 2.58 us  [the longest x1 1.66 us: line_of_four(): lax.dot_general(proj_in, inputs, (((0,), (1,)), ((), ())), preferred_elem...]
    psum x1 -> x0, waiting for transfers between devices: 50.7 us -> none  [on_device(): in_proj, out_proj = lax.psum((in_part, out_part), 'tensor')]
    ppermute x0 -> x24, starting transfers between devices: none -> 35.3 us  [the longest x12 13.8 us: xor_parts(): lax.ppermute(a, axis, [(i, i ^ s) for i in range(size)])]
    unnamed x4 -> x22, local copies, waits for them, and re-layouts: 0.99 us -> 9.39 us
    all_gather x1 -> x0, blocking collectives: 5.43 us -> none  [on_device(): all_grads = lax.all_gather(local_grads, 'dp', axis=0, tiled=True)]
  transfers between devices with their start and end apart: 3 -> 24, of which waited for: 2 -> 8; matrix products, arithmetic and copies ran while one was open for 4% -> 4% of each run, Pallas kernels for 0% -> 34%
where the time goes in v2:
time: 226 us; the launch traced here: 225 us
  Pallas kernels  90.3 us (40%)
  waiting for transfers between devices  78.6 us (35%)
  starting transfers between devices  35.3 us (16%)
  local copies, waits for them, and re-layouts  15.4 us (7%)
  matrix products  2.58 us (1%)
    pallas_call x5, Pallas kernels, last_block(): pl.pallas_call(last_body, grid_spec=pltpu.PrefetchScalarGridSpec(num_scal...  44.1 us
    ppermute x1, waiting for transfers between devices, line_of_four(): side = in_part + send(in_part, perm=inward)  42.1 us
    pallas_call x1, Pallas kernels, first_blocks(): pl.pallas_call(first_body, grid_spec=pltpu.PrefetchScalarGridSpec(num_sca...  21 us
    pallas_call x1, Pallas kernels, second_block(): pl.pallas_call(second_body, grid_spec=pltpu.PrefetchScalarGridSpec(num_sc...  20.4 us
    ppermute x1, waiting for transfers between devices, line_of_four(): far_middle_outer = send(far_middle_inner, perm=outward)  16.9 us
    ppermute x12, starting transfers between devices, xor_parts(): lax.ppermute(a, axis, [(i, i ^ s) for i in range(size)])  13.8 us
    ppermute x12, waiting for transfers between devices, xor_parts(): lax.ppermute(a, axis, [(i, i ^ s) for i in range(size)])  12.2 us
    unnamed x22, local copies, waits for them, and re-layouts  9.39 us
  transfers between devices with their start and end apart: 24, of which 8 were waited for; matrix products, arithmetic and copies ran while one was open for 4% of the time, Pallas kernels for 34%

profile of v2, /device:TPU:0, one launch (start us, length us, event | category | flops | bytes accessed | tf_op | source)
XLA Modules:
  0.0 225.2 jit_solution(5927548490963176086)
XLA Ops:
  0.6 3.1 %collective-permute-start = (bf16[1024,1024]{1,0:T(8,128)(2,1)}, bf16[1024,1024]{1,0:T(8,128)(2,1)}, u32[]{:S(2)}, u32[]{:S(2)}) collective-permute-start(bf16[1024,1024]{1,0:T(8,128)(2,1)} %own_ref.1), channel_id=1, source_target_pairs={{0,4},{4,0},{8,12},{12,8},{1,5},{5,1},{9,13},{13,9},{2,6},{6,2},{1... | collective-permute-start | bytes 6291464 | tf_op jit(solution)/shard_map/ppermute | solution.py:212
  3.7 2.0 collective-permute-start.3
  5.7 1.7 fusion.5
  7.4 5.0 %collective-permute-start.5 = (f32[64,1024]{1,0:T(8,128)S(1)}, f32[64,1024]{1,0:T(8,128)S(1)}, u32[]{:S(2)}, u32[]{:S(2)}) collective-permute-start(f32[64,1024]{1,0:T(8,128)S(1)} %fusion.5), channel_id=1, source_target_pairs={{0,4},{12,8},{1,5},{13,9},{2,6},{14,10},{3,7},{15,11},{16,20},{28,... | collective-permute-start | bytes 786440 | tf_op jit(solution)/shard_map/ppermute | solution.py:217
  12.4 42.1 %collective-permute-done.5 = f32[64,1024]{1,0:T(8,128)S(1)} collective-permute-done((f32[64,1024]{1,0:T(8,128)S(1)}, f32[64,1024]{1,0:T(8,128)S(1)}, u32[]{:S(2)}, u32[]{:S(2)}) %collective-permute-start.5) | collective-permute-done | bytes 262176 | tf_op jit(solution)/shard_map/ppermute | solution.py:217
  54.5 1.4 collective-permute-start.6
  55.9 1.5 collective-permute-start.10
  60.9 1.3 collective-permute-start.7
  63.2 2.1 collective-permute-done.10
  66.3 3.9 %collective-permute-done.11 = f32[256,256]{1,0:T(8,128)} collective-permute-done((f32[256,256]{1,0:T(8,128)}, f32[256,256]{1,0:T(8,128)}, u32[]{:S(2)}, u32[]{:S(2)}) %collective-permute-start.11) | collective-permute-done | bytes 262176 | tf_op jit(solution)/shard_map/ppermute | solution.py:250
  71.1 1.3 collective-permute-start.4
  72.4 7.4 %collective-permute-done.7 = f32[64,1024]{1,0:T(8,128)S(1)} collective-permute-done((f32[64,1024]{1,0:T(8,128)S(1)}, f32[64,1024]{1,0:T(8,128)S(1)}, u32[]{:S(2)}, u32[]{:S(2)}) %collective-permute-start.7) | collective-permute-done | bytes 262176 | tf_op jit(solution)/shard_map/ppermute | solution.py:219
  79.9 21.0 %first_blocks.1.old_ref = f32[1024,3584]{1,0:T(8,128)} custom-call(s32[5]{0:T(128)S(1)} %stack.36.where_ref, bf16[1024,1024]{1,0:T(8,128)(2,1)S(1)} %copy-done.8, bf16[1024,1024]{1,0:T(8,128)(2,1)} %collective-permute-done.pair_ref, bf16[3584,4096]{1,0:T(8,128)(2,1)} %w_ref.11, bf16[3584,4096]{1,0:T(8,128)(2,1)} %w_ref.11), custom_call_target="tpu_custom_call" | custom-call | flops 15032385536 | bytes 29360128 | tf_op jit(solution)/shard_map/first_blocks/pallas_call | solution.py:42
  107.9 16.9 %collective-permute-done.4.outer_ref = bf16[1024,1024]{1,0:T(8,128)(2,1)S(1)} collective-permute-done((bf16[1024,1024]{1,0:T(8,128)(2,1)}, bf16[1024,1024]{1,0:T(8,128)(2,1)S(1)}, u32[]{:S(2)}, u32[]{:S(2)}) %collective-permute-start.4) | collective-permute-done | bytes 2097184 | tf_op jit(solution)/shard_map/ppermute | solution.py:221
  124.8 1.5 collective-permute-start.12
  126.4 20.4 %second_block.1.old_ref = f32[1024,3584]{1,0:T(8,128)} custom-call(s32[5]{0:T(128)S(1)} %stack.36.where_ref, bf16[1024,1024]{1,0:T(8,128)(2,1)} %collective-permute-done.3.inner_ref, bf16[1024,1024]{1,0:T(8,128)(2,1)S(1)} %collective-permute-done.4.outer_ref, bf16[3584,4096]{1,0:T(8,128)(2,1)} %w_ref.11, ...), custom_call_target="tpu_custom_call", output_to_operand_aliasing={{}: (4, {})} | custom-call | flops 7516192768 | bytes 36700160 | tf_op jit(solution)/shard_map/second_block/pallas_call | solution.py:75
  146.8 9.0 %last_block.5.grads_in = f32[64,64]{1,0:T(8,128)S(1)} custom-call(s32[5]{0:T(128)S(1)} %stack.36.where_ref, bf16[1024,1024]{1,0:T(8,128)(2,1)S(1)} %collective-permute-done.1.inner_ref, bf16[256,1024]{1,0:T(8,128)(2,1)S(1)} %collective-permute-done.8.outer_ref, bf16[3584,4096]{1,0:T(8,128)(2,1)} %w_ref.11, f32[1024,3584]{1,0:T(8,128)} %second_block.1.old_ref, ...), custom_call_target="tpu_custom_call" | custom-call | flops 1996488704 | bytes 12845056 | tf_op jit(solution)/shard_map/last_block/pallas_call | solution.py:124
  155.8 8.9 %last_block.6 = f32[64,64]{1,0:T(8,128)S(1)} custom-call(s32[5]{0:T(128)S(1)} %stack.36.where_ref, bf16[1024,1024]{1,0:T(8,128)(2,1)S(1)} %collective-permute-done.1.inner_ref, bf16[256,1024]{1,0:T(8,128)(2,1)S(1)} %collective-permute-done.2.outer_ref, bf16[3584,4096]{1,0:T(8,128)(2,1)} %w_ref.11, f32[1024,3584]{1,0:T(8,128)} %second_block.1.old_ref, ...), custom_call_target="tpu_custom_call" | custom-call | flops 1996488704 | bytes 12845056 | tf_op jit(solution)/shard_map/last_block/pallas_call | solution.py:124
  164.9 3.1 %copy-done.2 = bf16[1024,3584]{1,0:T(8,128)(2,1)S(1)} copy-done((bf16[1024,3584]{1,0:T(8,128)(2,1)S(1)}, bf16[1024,3584]{1,0:T(8,128)(2,1)}, u32[]{:S(2)}) %copy-start.2) | copy-done | bytes 7340056
  169.0 9.1 %last_block.7.grads_in = f32[64,64]{1,0:T(8,128)S(1)} custom-call(s32[5]{0:T(128)S(1)} %stack.36.where_ref, bf16[1024,1024]{1,0:T(8,128)(2,1)S(1)} %collective-permute-done.1.inner_ref, bf16[256,1024]{1,0:T(8,128)(2,1)} %collective-permute-done.14.outer_ref, bf16[3584,4096]{1,0:T(8,128)(2,1)} %w_ref.11, f32[1024,3584]{1,0:T(8,128)} %second_block.1.old_ref, ...), custom_call_target="tpu_custom_call" | custom-call | flops 1996488704 | bytes 12845056 | tf_op jit(solution)/shard_map/last_block/pallas_call | solution.py:124
  178.1 3.1 %copy-done.3 = bf16[1024,3584]{1,0:T(8,128)(2,1)S(1)} copy-done((bf16[1024,3584]{1,0:T(8,128)(2,1)S(1)}, bf16[1024,3584]{1,0:T(8,128)(2,1)}, u32[]{:S(2)}) %copy-start.3) | copy-done | bytes 7340056
  181.2 8.6 %last_block.8.grads_in = f32[64,64]{1,0:T(8,128)S(1)} custom-call(s32[5]{0:T(128)S(1)} %stack.36.where_ref, bf16[1024,1024]{1,0:T(8,128)(2,1)S(1)} %collective-permute-done.1.inner_ref, bf16[128,1024]{1,0:T(8,128)(2,1)} %collective-permute-done.13.outer_ref, bf16[3584,4096]{1,0:T(8,128)(2,1)} %w_ref.11, f32[1024,3584]{1,0:T(8,128)} %second_block.1.old_ref, ...), custom_call_target="tpu_custom_call" | custom-call | flops 998244352 | bytes 10092544 | tf_op jit(solution)/shard_map/last_block/pallas_call | solution.py:124
  189.8 8.6 %last_block.9 = f32[64,64]{1,0:T(8,128)S(1)} custom-call(s32[5]{0:T(128)S(1)} %stack.36.where_ref, bf16[1024,1024]{1,0:T(8,128)(2,1)S(1)} %collective-permute-done.1.inner_ref, bf16[128,1024]{1,0:T(8,128)(2,1)} %collective-permute-done.12.outer_ref, bf16[3584,4096]{1,0:T(8,128)(2,1)} %w_ref.11, f32[1024,3584]{1,0:T(8,128)} %second_block.1.old_ref, ...), custom_call_target="tpu_custom_call" | custom-call | flops 998244352 | bytes 10092544 | tf_op jit(solution)/shard_map/last_block/pallas_call | solution.py:124
  198.5 3.2 %collective-permute-start.15 = (f32[2,4096]{1,0:T(2,128)S(1)}, f32[2,4096]{1,0:T(2,128)S(1)}, u32[]{:S(2)}, u32[]{:S(2)}) collective-permute-start(f32[2,4096]{1,0:T(2,128)S(1)} %pad_maximum_fusion.1), channel_id=1, source_target_pairs={{0,4},{4,0},{8,12},{12,8},{1,5},{5,1},{9,13},{13,9},{2,6},{6,2},{1... | collective-permute-start | bytes 98312 | tf_op jit(solution)/shard_map/ppermute | solution.py:250
  202.0 2.1 collective-permute-start.17
  204.2 3.7 %collective-permute-done.16 = f32[2,4096]{1,0:T(2,128)S(1)} collective-permute-done((f32[2,4096]{1,0:T(2,128)S(1)}, f32[2,4096]{1,0:T(2,128)S(1)}, u32[]{:S(2)}, u32[]{:S(2)}) %collective-permute-start.16) | collective-permute-done | bytes 32800 | tf_op jit(solution)/shard_map/ppermute | solution.py:250
  210.1 1.6 collective-permute-start.22
  211.6 1.6 collective-permute-start.23
  213.2 1.7 collective-permute-start.19
  215.1 2.0 collective-permute-done.23
  218.3 2.2 copy-done.7
  220.5 4.7 %hessian_update.1 = f32[256,4096]{1,0:T(8,128)} custom-call(s32[1]{0:T(128)} %bitcast.row_ref, f32[8,4096]{1,0:T(8,128)S(1)} %pad_maximum_fusion.refs_0_.refs_1_, f32[8,4096]{1,0:T(8,128)S(1)} %pad_maximum_fusion.refs_0_.refs_1_, f32[256,4096]{1,0:T(8,128)S(1)} %copy-done.7), custom_call_target="tpu_custom_call" | custom-call | flops 100663296 | bytes 8388608 | tf_op jit(solution)/shard_map/hessian_update/pallas_call | solution.py:179
  (67 shorter events, 18.7 us)
Async XLA Ops:
  0.6 5.1 %copy-start = (bf16[1024,1024]{1,0:T(8,128)(2,1)S(1)}, bf16[1024,1024]{1,0:T(8,128)(2,1)}, u32[]{:S(2)}) copy-start(bf16[1024,1024]{1,0:T(8,128)(2,1)} %param.8) | copy-start | bytes 6291460
  0.6 57.1 %collective-permute-start = (bf16[1024,1024]{1,0:T(8,128)(2,1)}, bf16[1024,1024]{1,0:T(8,128)(2,1)}, u32[]{:S(2)}, u32[]{:S(2)}) collective-permute-start(bf16[1024,1024]{1,0:T(8,128)(2,1)} %own_ref.1), channel_id=1, source_target_pairs={{0,4},{4,0},{8,12},{12,8},{1,5},{5,1},{9,13},{13,9},{2,6},{6,2},{1... | collective-permute-start | bytes 6291464 | tf_op jit(solution)/shard_map/ppermute | solution.py:212
  3.7 67.4 %collective-permute-start.3 = (bf16[1024,1024]{1,0:T(8,128)(2,1)}, bf16[1024,1024]{1,0:T(8,128)(2,1)}, u32[]{:S(2)}, u32[]{:S(2)}) collective-permute-start(bf16[1024,1024]{1,0:T(8,128)(2,1)} %own_ref.1), channel_id=1, source_target_pairs={{4,8},{8,4},{5,9},{9,5},{6,10},{10,6},{7,11},{11,7},{20,24},{24,20... | collective-permute-start | bytes 6291464 | tf_op jit(solution)/shard_map/ppermute | solution.py:213
  7.4 47.1 %collective-permute-start.5 = (f32[64,1024]{1,0:T(8,128)S(1)}, f32[64,1024]{1,0:T(8,128)S(1)}, u32[]{:S(2)}, u32[]{:S(2)}) collective-permute-start(f32[64,1024]{1,0:T(8,128)S(1)} %fusion.5), channel_id=1, source_target_pairs={{0,4},{12,8},{1,5},{13,9},{2,6},{14,10},{3,7},{15,11},{16,20},{28,... | collective-permute-start | bytes 786440 | tf_op jit(solution)/shard_map/ppermute | solution.py:217
  54.5 2.9 %collective-permute-start.6 = (f32[64,1024]{1,0:T(8,128)S(1)}, f32[64,1024]{1,0:T(8,128)}, u32[]{:S(2)}, u32[]{:S(2)}) collective-permute-start(f32[64,1024]{1,0:T(8,128)S(1)} %add.52), channel_id=1, source_target_pairs={{4,8},{8,4},{5,9},{9,5},{6,10},{10,6},{7,11},{11,7},{20,24},{24,20... | collective-permute-start | bytes 786440 | tf_op jit(solution)/shard_map/ppermute | solution.py:218
  55.9 5.0 %collective-permute-start.9 = (f32[256,256]{1,0:T(8,128)}, f32[256,256]{1,0:T(8,128)}, u32[]{:S(2)}, u32[]{:S(2)}) collective-permute-start(f32[256,256]{1,0:T(8,128)} %param.15), channel_id=1, source_target_pairs={{0,1},{1,0},{2,3},{3,2},{4,5},{5,4},{6,7},{7,6},{8,9},{9,8},{10,11... | collective-permute-start | bytes 786440 | tf_op jit(solution)/shard_map/ppermute | solution.py:250
  55.9 9.4 %collective-permute-start.10 = (f32[256,256]{1,0:T(8,128)}, f32[256,256]{1,0:T(8,128)}, u32[]{:S(2)}, u32[]{:S(2)}) collective-permute-start(f32[256,256]{1,0:T(8,128)} %param.15), channel_id=1, source_target_pairs={{0,2},{1,3},{2,0},{3,1},{4,6},{5,7},{6,4},{7,5},{8,10},{9,11},{10,... | collective-permute-start | bytes 786440 | tf_op jit(solution)/shard_map/ppermute | solution.py:250
  57.4 12.8 %collective-permute-start.11 = (f32[256,256]{1,0:T(8,128)}, f32[256,256]{1,0:T(8,128)}, u32[]{:S(2)}, u32[]{:S(2)}) collective-permute-start(f32[256,256]{1,0:T(8,128)} %param.15), channel_id=1, source_target_pairs={{0,3},{1,2},{2,1},{3,0},{4,7},{5,6},{6,5},{7,4},{8,11},{9,10},{10,... | collective-permute-start | bytes 786440 | tf_op jit(solution)/shard_map/ppermute | solution.py:250
  57.7 43.2 %collective-permute-start.1 = (bf16[1024,1024]{1,0:T(8,128)(2,1)}, bf16[1024,1024]{1,0:T(8,128)(2,1)S(1)}, u32[]{:S(2)}, u32[]{:S(2)}) collective-permute-start(bf16[1024,1024]{1,0:T(8,128)(2,1)} %collective-permute-done.pair_ref), channel_id=1, source_target_pairs={{4,8},{8,4},{5,9},{9,5},{6,10},{10,6},{7,11},{11,7},{20,24},{24,20... | collective-permute-start | bytes 6291464 | tf_op jit(solution)/shard_map/ppermute | solution.py:222
  59.8 20.1 %copy-start.8 = (bf16[1024,1024]{1,0:T(8,128)(2,1)S(1)}, bf16[1024,1024]{1,0:T(8,128)(2,1)}, u32[]{:S(2)}) copy-start(bf16[1024,1024]{1,0:T(8,128)(2,1)} %own_ref.1) | copy-start | bytes 6291460
  60.9 19.0 %collective-permute-start.7 = (f32[64,1024]{1,0:T(8,128)S(1)}, f32[64,1024]{1,0:T(8,128)S(1)}, u32[]{:S(2)}, u32[]{:S(2)}) collective-permute-start(f32[64,1024]{1,0:T(8,128)S(1)} %add.53), channel_id=1, source_target_pairs={{4,0},{8,12},{5,1},{9,13},{6,2},{10,14},{7,3},{11,15},{20,16},{24,... | collective-permute-start | bytes 786440 | tf_op jit(solution)/shard_map/ppermute | solution.py:219
  71.1 53.7 %collective-permute-start.4 = (bf16[1024,1024]{1,0:T(8,128)(2,1)}, bf16[1024,1024]{1,0:T(8,128)(2,1)S(1)}, u32[]{:S(2)}, u32[]{:S(2)}) collective-permute-start(bf16[1024,1024]{1,0:T(8,128)(2,1)} %collective-permute-done.3.inner_ref), channel_id=1, source_target_pairs={{4,0},{8,12},{5,1},{9,13},{6,2},{10,14},{7,3},{11,15},{20,16},{24,... | collective-permute-start | bytes 6291464 | tf_op jit(solution)/shard_map/ppermute | solution.py:221
  101.9 44.9 %collective-permute-start.8 = (bf16[256,1024]{1,0:T(8,128)(2,1)S(1)}, bf16[256,1024]{1,0:T(8,128)(2,1)S(1)}, u32[]{:S(2)}, u32[]{:S(2)}) collective-permute-start(bf16[256,1024]{1,0:T(8,128)(2,1)S(1)} %get-tuple-element.2), channel_id=1, source_target_pairs={{4,0},{8,12},{5,1},{9,13},{6,2},{10,14},{7,3},{11,15},{20,16},{24,... | collective-permute-start | bytes 1572872 | tf_op jit(solution)/shard_map/ppermute | solution.py:230
  103.2 52.6 %collective-permute-start.2 = (bf16[256,1024]{1,0:T(8,128)(2,1)S(1)}, bf16[256,1024]{1,0:T(8,128)(2,1)S(1)}, u32[]{:S(2)}, u32[]{:S(2)}) collective-permute-start(bf16[256,1024]{1,0:T(8,128)(2,1)S(1)} %get-tuple-element.4), channel_id=1, source_target_pairs={{4,0},{8,12},{5,1},{9,13},{6,2},{10,14},{7,3},{11,15},{20,16},{24,... | collective-permute-start | bytes 1572872 | tf_op jit(solution)/shard_map/ppermute | solution.py:230
  104.5 60.4 %collective-permute-start.14 = (bf16[256,1024]{1,0:T(8,128)(2,1)}, bf16[256,1024]{1,0:T(8,128)(2,1)}, u32[]{:S(2)}, u32[]{:S(2)}) collective-permute-start(bf16[256,1024]{1,0:T(8,128)(2,1)} %get-tuple-element.3), channel_id=1, source_target_pairs={{4,0},{8,12},{5,1},{9,13},{6,2},{10,14},{7,3},{11,15},{20,16},{24,... | collective-permute-start | bytes 1572872 | tf_op jit(solution)/shard_map/ppermute | solution.py:230
  106.6 71.5 %collective-permute-start.13 = (bf16[128,1024]{1,0:T(8,128)(2,1)}, bf16[128,1024]{1,0:T(8,128)(2,1)}, u32[]{:S(2)}, u32[]{:S(2)}) collective-permute-start(bf16[128,1024]{1,0:T(8,128)(2,1)} %get-tuple-element.5), channel_id=1, source_target_pairs={{4,0},{8,12},{5,1},{9,13},{6,2},{10,14},{7,3},{11,15},{20,16},{24,... | collective-permute-start | bytes 786440 | tf_op jit(solution)/shard_map/ppermute | solution.py:230
  124.8 22.0 %slice-start = ((s8[7340032]{0:T(1024)(128)(4,1)}), s8[4194304]{0:T(1024)(128)(4,1)S(1)}, s32[]{:S(2)}) async-start(s8[7340032]{0:T(1024)(128)(4,1)} %bitcast.10), calls=%async_computation | async-start | bytes 8388608
  124.8 22.0 %slice-start.1 = ((s8[7340032]{0:T(1024)(128)(4,1)}), s8[3145728]{0:T(1024)(128)(4,1)S(1)}, s32[]{:S(2)}) async-start(s8[7340032]{0:T(1024)(128)(4,1)} %bitcast.10), calls=%async_computation.1 | async-start | bytes 6291456
  124.8 22.0 %copy-start.4 = (bf16[3584,64]{0,1:T(8,128)(2,1)S(1)}, bf16[3584,64]{0,1:T(8,128)(2,1)}, u32[]{:S(2)}) copy-start(bf16[3584,64]{0,1:T(8,128)(2,1)} %param.13) | copy-start | bytes 1376260
  124.8 65.0 %collective-permute-start.12 = (bf16[128,1024]{1,0:T(8,128)(2,1)}, bf16[128,1024]{1,0:T(8,128)(2,1)}, u32[]{:S(2)}, u32[]{:S(2)}) collective-permute-start(bf16[128,1024]{1,0:T(8,128)(2,1)} %get-tuple-element.6), channel_id=1, source_target_pairs={{4,0},{8,12},{5,1},{9,13},{6,2},{10,14},{7,3},{11,15},{20,16},{24,... | collective-permute-start | bytes 786440 | tf_op jit(solution)/shard_map/ppermute | solution.py:230
  164.9 3.1 %copy-start.2 = (bf16[1024,3584]{1,0:T(8,128)(2,1)S(1)}, bf16[1024,3584]{1,0:T(8,128)(2,1)}, u32[]{:S(2)}) copy-start(bf16[1024,3584]{1,0:T(8,128)(2,1)} %gate_ref.9) | copy-start | bytes 22020100
  169.0 9.1 %copy-start.6 = (bf16[3584,64]{0,1:T(8,128)(2,1)S(1)}, bf16[3584,64]{0,1:T(8,128)(2,1)}, u32[]{:S(2)}) copy-start(bf16[3584,64]{0,1:T(8,128)(2,1)} %param.13) | copy-start | bytes 1376260
  198.5 5.7 %collective-permute-start.15 = (f32[2,4096]{1,0:T(2,128)S(1)}, f32[2,4096]{1,0:T(2,128)S(1)}, u32[]{:S(2)}, u32[]{:S(2)}) collective-permute-start(f32[2,4096]{1,0:T(2,128)S(1)} %pad_maximum_fusion.1), channel_id=1, source_target_pairs={{0,4},{4,0},{8,12},{12,8},{1,5},{5,1},{9,13},{13,9},{2,6},{6,2},{1... | collective-permute-start | bytes 98312 | tf_op jit(solution)/shard_map/ppermute | solution.py:250
  201.7 6.1 %collective-permute-start.16 = (f32[2,4096]{1,0:T(2,128)S(1)}, f32[2,4096]{1,0:T(2,128)S(1)}, u32[]{:S(2)}, u32[]{:S(2)}) collective-permute-start(f32[2,4096]{1,0:T(2,128)S(1)} %pad_maximum_fusion.1), channel_id=1, source_target_pairs={{0,8},{4,12},{8,0},{12,4},{1,9},{5,13},{9,1},{13,5},{2,10},{6,14},... | collective-permute-start | bytes 98312 | tf_op jit(solution)/shard_map/ppermute | solution.py:250
  202.0 5.8 %collective-permute-start.17 = (f32[2,4096]{1,0:T(2,128)S(1)}, f32[2,4096]{1,0:T(2,128)S(1)}, u32[]{:S(2)}, u32[]{:S(2)}) collective-permute-start(f32[2,4096]{1,0:T(2,128)S(1)} %pad_maximum_fusion.1), channel_id=1, source_target_pairs={{0,12},{4,8},{8,4},{12,0},{1,13},{5,9},{9,5},{13,1},{2,14},{6,10},... | collective-permute-start | bytes 98312 | tf_op jit(solution)/shard_map/ppermute | solution.py:250
  208.8 6.1 %collective-permute-start.21 = (f32[2,256]{1,0:T(2,128)S(1)}, f32[2,256]{1,0:T(2,128)S(1)}, u32[]{:S(2)}, u32[]{:S(2)}) collective-permute-start(f32[2,256]{1,0:T(2,128)S(1)} %fusion), channel_id=1, source_target_pairs={{0,4},{4,0},{8,12},{12,8},{1,5},{5,1},{9,13},{13,9},{2,6},{6,2},{1... | collective-permute-start | bytes 6152 | tf_op jit(solution)/shard_map/ppermute | solution.py:250
  210.1 5.0 %collective-permute-start.22 = (f32[2,256]{1,0:T(2,128)S(1)}, f32[2,256]{1,0:T(2,128)S(1)}, u32[]{:S(2)}, u32[]{:S(2)}) collective-permute-start(f32[2,256]{1,0:T(2,128)S(1)} %fusion), channel_id=1, source_target_pairs={{0,8},{4,12},{8,0},{12,4},{1,9},{5,13},{9,1},{13,5},{2,10},{6,14},... | collective-permute-start | bytes 6152 | tf_op jit(solution)/shard_map/ppermute | solution.py:250
  211.6 5.4 %collective-permute-start.23 = (f32[2,256]{1,0:T(2,128)S(1)}, f32[2,256]{1,0:T(2,128)S(1)}, u32[]{:S(2)}, u32[]{:S(2)}) collective-permute-start(f32[2,256]{1,0:T(2,128)S(1)} %fusion), channel_id=1, source_target_pairs={{0,12},{4,8},{8,4},{12,0},{1,13},{5,9},{9,5},{13,1},{2,14},{6,10},... | collective-permute-start | bytes 6152 | tf_op jit(solution)/shard_map/ppermute | solution.py:250
  213.2 4.4 %collective-permute-start.18 = (f32[2,4096]{1,0:T(2,128)S(1)}, f32[2,4096]{1,0:T(2,128)S(1)}, u32[]{:S(2)}, u32[]{:S(2)}) collective-permute-start(f32[2,4096]{1,0:T(2,128)S(1)} %add_add_fusion), channel_id=1, source_target_pairs={{0,1},{1,0},{2,3},{3,2},{4,5},{5,4},{6,7},{7,6},{8,9},{9,8},{10,11... | collective-permute-start | bytes 98312 | tf_op jit(solution)/shard_map/ppermute | solution.py:250
  213.2 4.4 %collective-permute-start.19 = (f32[2,4096]{1,0:T(2,128)S(1)}, f32[2,4096]{1,0:T(2,128)S(1)}, u32[]{:S(2)}, u32[]{:S(2)}) collective-permute-start(f32[2,4096]{1,0:T(2,128)S(1)} %add_add_fusion), channel_id=1, source_target_pairs={{0,2},{1,3},{2,0},{3,1},{4,6},{5,7},{6,4},{7,5},{8,10},{9,11},{10,... | collective-permute-start | bytes 98312 | tf_op jit(solution)/shard_map/ppermute | solution.py:250
  214.9 3.3 %collective-permute-start.20 = (f32[2,4096]{1,0:T(2,128)S(1)}, f32[2,4096]{1,0:T(2,128)S(1)}, u32[]{:S(2)}, u32[]{:S(2)}) collective-permute-start(f32[2,4096]{1,0:T(2,128)S(1)} %add_add_fusion), channel_id=1, source_target_pairs={{0,3},{1,2},{2,1},{3,0},{4,7},{5,6},{6,5},{7,4},{8,11},{9,10},{10,... | collective-permute-start | bytes 98312 | tf_op jit(solution)/shard_map/ppermute | solution.py:250
  220.5 4.7 %copy-start.1 = (bf16[1024,1024]{1,0:T(8,128)(2,1)S(1)}, bf16[1024,1024]{1,0:T(8,128)(2,1)}, u32[]{:S(2)}) copy-start(bf16[1024,1024]{1,0:T(8,128)(2,1)} %param.8) | copy-start | bytes 6291460
  (3 other events, 6.3 us)

commit v3 on v0

v3 whole, which is shorter than its diff:
```python
import functools

import jax
import jax.numpy as jnp
from jax import lax
from jax.experimental import pallas as pl
from jax.experimental.pallas import tpu as pltpu
from jax.sharding import PartitionSpec as P

PROJ = 64
LEN = 512
HIGHEST = lax.Precision.HIGHEST
NT = (((1,), (1,)), ((), ()))
TILE = 512
LAST_TILE = 896
VMEM_BYTES = 28 * 2**20
ANYWHERE = pl.BlockSpec(memory_space=pl.ANY)


def silu(v):
    return 0.5 * v * (1.0 + jnp.tanh(0.5 * v))


def dot(a, b):
    return jnp.dot(a, b, preferred_element_type=jnp.float32)


def dot_nt(a, b):
    return lax.dot_general(a, b, NT, preferred_element_type=jnp.float32)


def call(body, name, where, grid, operands, in_specs, out_specs, out_shapes, scratch, flops, after=(), aliases=None):
    def with_after(*refs):
        head = 1 + len(operands)
        body(*refs[:head], *refs[head + len(after) :])

    moved = sum(a.size * a.dtype.itemsize for a in operands) + sum(s.size * s.dtype.itemsize for s in out_shapes)
    return pl.pallas_call(
        with_after,
        grid_spec=pltpu.PrefetchScalarGridSpec(
            num_scalar_prefetch=1,
            grid=grid,
            in_specs=list(in_specs) + [ANYWHERE] * len(after),
            out_specs=out_specs,
            scratch_shapes=scratch,
        ),
        out_shape=out_shapes,
        input_output_aliases=aliases or {},
        compiler_params=pltpu.CompilerParams(vmem_limit_bytes=VMEM_BYTES),
        cost_estimate=pl.CostEstimate(flops=flops, bytes_accessed=min(moved, flops // 300), transcendentals=0),
        name=name,
    )(where, *operands, *after)


def fixed(shape):
    return pl.BlockSpec(shape, lambda j, where: (0, 0), pipeline_mode=pl.Buffered(1))


def own_body(where, own, w, gate, inputs, pi_t, *rest):
    *accs, gate_t, in_t, own_t = rest
    half = accs[0].shape[1]

    @pl.when(pl.program_id(0) == 0)
    def _():
        own_t[...] = own[...].T
        in_t[...] = dot_nt(pi_t[...], inputs[...])

    gate_t[...] = gate[...].T
    for h, acc in enumerate(accs):
        acc[...] = dot(w[...], own_t[:, h * half : (h + 1) * half])


def own_block(where, own, w, gate, inputs, pi_t, halves):
    tokens, feats = own.shape
    hidden = w.shape[0]
    half = tokens // halves
    acc = jax.ShapeDtypeStruct((hidden, half), jnp.float32)
    return call(
        own_body,
        "own_block",
        where,
        (hidden // TILE,),
        (own, w, gate, inputs, pi_t),
        [
            fixed(own.shape),
            pl.BlockSpec((TILE, feats), lambda j, where: (j, where[0])),
            pl.BlockSpec((tokens, TILE), lambda j, where: (0, j)),
            fixed(inputs.shape),
            fixed(pi_t.shape),
        ],
        [pl.BlockSpec((TILE, half), lambda j, where: (j, 0))] * halves
        + [
            pl.BlockSpec((TILE, tokens), lambda j, where: (j, 0)),
            pl.BlockSpec((PROJ, tokens), lambda j, where: (0, 0)),
        ],
        [acc] * halves
        + [
            jax.ShapeDtypeStruct((hidden, tokens), gate.dtype),
            jax.ShapeDtypeStruct((PROJ, tokens), jnp.float32),
        ],
        [pltpu.VMEM((feats, tokens), own.dtype)],
        2 * tokens * feats * hidden,
    )


def pair_body(where, pair, w, *rest):
    halves = (len(rest) - 1) // 2
    pair_t = rest[-1]
    half = rest[0].shape[1]

    @pl.when(pl.program_id(0) == 0)
    def _():
        pair_t[...] = pair[...].T

    for h in range(halves):
        rest[halves + h][...] = rest[h][...] + dot(w[...], pair_t[:, h * half : (h + 1) * half])


def pair_block(where, pair, w, accs, after):
    tokens, feats = pair.shape
    hidden = w.shape[0]
    tiles = [pl.BlockSpec((TILE, acc.shape[1]), lambda j, where: (j, 0)) for acc in accs]
    return call(
        pair_body,
        "pair_block",
        where,
        (hidden // TILE,),
        (pair, w, *accs),
        [fixed(pair.shape), pl.BlockSpec((TILE, feats), lambda j, where: (j, where[1]))] + tiles,
        tiles,
        [jax.ShapeDtypeStruct(acc.shape, acc.dtype) for acc in accs],
        [pltpu.VMEM((feats, tokens), pair.dtype)],
        2 * tokens * feats * hidden,
        after=after,
        aliases={3 + h: h for h in range(len(accs))},
    )


def select_transposed(where, inner, outer):
    return jnp.where(where[4] == 1, inner[...], outer[...]).T


def third_body(where, inner, outer, w, old, acc, block_t):
    @pl.when(pl.program_id(0) == 0)
    def _():
        block_t[...] = select_transposed(where, inner, outer)

    acc[...] = old[...] + dot(w[...], block_t[...])


def third_block(where, inner, outer, w, old):
    tokens, feats = inner.shape
    hidden = w.shape[0]
    tile = pl.BlockSpec((TILE, tokens), lambda j, where: (j, 0))
    (acc,) = call(
        third_body,
        "third_block",
        where,
        (hidden // TILE,),
        (inner, outer, w, old),
        [
            fixed(inner.shape),
            fixed(outer.shape),
            pl.BlockSpec((TILE, feats), lambda j, where: (j, where[2])),
            tile,
        ],
        [tile],
        [jax.ShapeDtypeStruct(old.shape, old.dtype)],
        [pltpu.VMEM((feats, tokens), inner.dtype)],
        2 * tokens * feats * hidden,
        aliases={4: 0},
    )
    return acc


def last_body(where, inner, outer, w, old, gate_t, po_t, left_t, grads_in, grads, block_t, right_t):
    step = pl.program_id(0)

    @pl.when(step == 0)
    def _():
        block_t[...] = select_transposed(where, inner, outer)
        right_t[...] = jnp.zeros_like(right_t)

    hidden_grad = old[...] + dot(w[...], block_t[...])
    up_grad = (hidden_grad * silu(gate_t[...].astype(jnp.float32))).astype(jnp.bfloat16)
    right_t[...] += dot(po_t[...], up_grad)

    @pl.when(step == pl.num_programs(0) - 1)
    def _():
        grads[...] = grads_in[...] + lax.dot_general(
            left_t[...], right_t[...], NT, precision=HIGHEST, preferred_element_type=jnp.float32
        )


def last_block(where, inner, outer, at, in_half, w, old, gate_t, po_t, left_t, grads):
    size, feats = outer.shape
    hidden = w.shape[0]
    chunk, half_chunk = at // size, in_half // size
    small = pl.BlockSpec((PROJ, PROJ), lambda j, where: (0, 0))
    (grads,) = call(
        last_body,
        "last_block",
        where,
        (hidden // LAST_TILE,),
        (inner, outer, w, old, gate_t, po_t, left_t, grads),
        [
            pl.BlockSpec((size, feats), lambda j, where: (half_chunk, 0), pipeline_mode=pl.Buffered(1)),
            fixed(outer.shape),
            pl.BlockSpec((LAST_TILE, feats), lambda j, where: (j, where[3])),
            pl.BlockSpec((LAST_TILE, size), lambda j, where: (j, half_chunk)),
            pl.BlockSpec((LAST_TILE, size), lambda j, where: (j, chunk)),
            pl.BlockSpec((PROJ, LAST_TILE), lambda j, where: (0, j)),
            pl.BlockSpec((PROJ, size), lambda j, where: (0, chunk)),
            small,
        ],
        [small],
        [jax.ShapeDtypeStruct((PROJ, PROJ), jnp.float32)],
        [pltpu.VMEM((feats, size), outer.dtype), pltpu.VMEM((PROJ, size), jnp.float32)],
        2 * size * (feats + PROJ) * hidden,
    )
    return grads


def pieces(a):
    high = a.astype(jnp.bfloat16)
    rest = a - high.astype(jnp.float32)
    middle = rest.astype(jnp.bfloat16)
    low = (rest - middle.astype(jnp.float32)).astype(jnp.bfloat16)
    return high, middle, low


def update_body(scale, row, grads, mine, hessian, out):
    high, middle, low = pieces(mine[...])
    left = jnp.concatenate([high, high, middle, middle, high, low], axis=0)
    high, middle, low = pieces(grads[...])
    right = jnp.concatenate([high, middle, high, middle, low, high], axis=0)
    total = lax.dot_general(left, right, (((0,), (0,)), ((), ())), preferred_element_type=jnp.float32)
    out[...] = hessian[...] + total * scale


def update(row, grads, hessian):
    rows, columns = hessian.shape
    count = grads.shape[0]
    width = min(columns, 512)
    tile = pl.BlockSpec((rows, width), lambda j, row: (0, j))
    (updated,) = call(
        functools.partial(update_body, 1.0 / count),
        "hessian_update",
        row,
        (columns // width,),
        (grads, grads, hessian),
        [
            pl.BlockSpec((count, width), lambda j, row: (0, j)),
            pl.BlockSpec((count, rows), lambda j, row: (0, row[0])),
            tile,
        ],
        [tile],
        [jax.ShapeDtypeStruct((rows, columns), jnp.float32)],
        [],
        2 * 48 * rows * columns,
    )
    return updated


def line_of_four(inputs, gate_pre, grad_out, w_down, proj_in, proj_out, early):
    send = functools.partial(lax.ppermute, axis_name="tensor")
    pairs = [(0, 1), (1, 0), (2, 3), (3, 2)]
    inner = [(1, 2), (2, 1)]
    outward = [(1, 0), (2, 3)]
    inward = [(0, 1), (3, 2)]
    tokens = grad_out.shape[0]
    halves = 2
    half = tokens // halves
    z = lax.axis_index("tensor")
    low = z < 2
    middle = jnp.logical_and(z > 0, z < 3)
    where = jnp.stack(
        [z, z + 1 - 2 * (z % 2), jnp.where(low, 2, 1), jnp.where(low, 3, 0), middle.astype(z.dtype)]
    ).astype(jnp.int32)

    def part(a, h):
        return a[h * half : (h + 1) * half]

    pair = send(grad_out, perm=pairs)
    mid_inner = [send(part(grad_out, h), perm=inner) for h in range(halves)]
    *accs, gate_t, in_part = own_block(where, grad_out, w_down, gate_pre, inputs, proj_in.T, halves)
    mid_outer = [send(a, perm=outward) for a in mid_inner]
    end_inner = [send(part(pair, h), perm=inner) for h in range(halves)]
    accs = pair_block(where, pair, w_down, accs, [early])

    side = in_part + send(in_part, perm=inward)
    total = side + send(side, perm=inner)
    left_t = jnp.where(middle, total, send(total, perm=outward))

    accs = [third_block(where, mid_inner[h], mid_outer[h], w_down, accs[h]) for h in range(halves)]

    grads = [jnp.zeros((PROJ, PROJ), jnp.float32) for _ in range(tokens // LEN)]
    for h in range(halves):
        at = 0
        while at < half:
            size = 256 if h + 1 < halves or at + 256 < half else 128
            end_outer = send(end_inner[h][at : at + size], perm=outward)
            whole_at = h * half + at
            s = whole_at // LEN
            grads[s] = last_block(
                where, end_inner[h], end_outer, whole_at, at, w_down, accs[h], gate_t, proj_out.T, left_t, grads[s]
            )
            at += size
    return jnp.stack(grads).reshape(-1, PROJ * PROJ)


def any_line(inputs, gate_pre, grad_out, w_down, proj_in, proj_out, early):
    in_part = jnp.dot(inputs, proj_in, preferred_element_type=jnp.float32)
    in_proj = lax.psum(in_part, "tensor").reshape(-1, LEN, PROJ)
    gathered = lax.all_gather(grad_out, "tensor", axis=1, tiled=True)
    up_grad = (dot_nt(gathered, w_down) * silu(gate_pre.astype(jnp.float32))).astype(jnp.bfloat16)
    out_part = jnp.dot(up_grad, proj_out, preferred_element_type=jnp.float32).reshape(-1, LEN, PROJ)
    grads = jnp.einsum("sti,stj->sij", in_proj, out_part, precision=HIGHEST)
    return grads.reshape(-1, PROJ * PROJ)


def swap(a, axis, bit):
    return lax.ppermute(a, axis, [(i, i ^ bit) for i in range(lax.axis_size(axis))])


def bits(axis):
    return [1 << b for b in range(lax.axis_size(axis).bit_length() - 1)]


def xor_sum(a, axis):
    for bit in bits(axis):
        a = a + swap(a, axis, bit)
    return a


def xor_gather(a, axis):
    for bit in bits(axis):
        a = jnp.concatenate([a, swap(a, axis, bit)], axis=0)
    return a


def gather_queries(queries):
    rows, width = queries.shape
    me = lax.axis_index("dp")
    whole = jnp.zeros((rows, width * lax.axis_size("dp")), queries.dtype)
    whole = lax.dynamic_update_slice_in_dim(whole, queries, me * width, 1)
    for s in range(1, lax.axis_size("dp")):
        whole = lax.dynamic_update_slice_in_dim(whole, swap(queries, "dp", s), (me ^ s) * width, 1)
    return whole


def on_device(inputs, gate_pre, grad_out, w_down, proj_in, proj_out, hessian, queries):
    z_queries = gather_queries(queries)
    line = line_of_four if lax.axis_size("tensor") == 4 else any_line
    grads = line(inputs, gate_pre, grad_out, w_down, proj_in, proj_out, z_queries)
    grads = xor_sum(grads, "tensor")
    all_grads = xor_gather(grads, "dp")

    width = z_queries.shape[1]
    quarter = lax.dynamic_slice_in_dim(grads, lax.axis_index("tensor") * width, width, 1)
    scores = xor_sum(jnp.dot(quarter, z_queries.T, precision=HIGHEST), "tensor")

    row_count = hessian.shape[0]
    at = lax.axis_index(("tensor", "dp"))
    if row_count % 128:
        mine = lax.dynamic_slice_in_dim(all_grads, at * row_count, row_count, 1)
        updated = hessian + jnp.dot(mine.T, all_grads, precision=HIGHEST) / all_grads.shape[0]
    else:
        updated = update(at.reshape(1).astype(jnp.int32), all_grads, hessian)
    return (updated, scores)


def solution(mesh):
    return jax.shard_map(
        on_device,
        mesh=mesh,
        in_specs=(
            P(("groups", "dp"), "tensor"),
            P(("groups", "dp"), "tensor"),
            P(("groups", "dp"), "tensor"),
            P("tensor", None),
            P("tensor", None),
            P("tensor", None),
            P(("groups", "tensor", "dp"), None),
            P("groups", ("tensor", "dp")),
        ),
        out_specs=(P(("groups", "tensor", "dp"), None), P(("groups", "dp"), None)),
        check_vma=False,
    )
```

time: 287 us -> 219 us (0.76)
  waiting for transfers between devices: 203 us -> 72.1 us
  Pallas kernels: 0 us -> 82.2 us
  matrix products: 60 us -> 0.91 us
  local copies, waits for them, and re-layouts: 1.93 us -> 32.3 us
  starting transfers between devices: 0.12 us -> 28 us
  between operations: 15.5 us -> 1.16 us
  blocking collectives: 5.43 us -> 0 us
    all_gather x2 -> x0, waiting for transfers between devices: 152 us -> none  [the longest x1 152 us: on_device(): lax.all_gather(grad_out, 'tensor', axis=1, tiled=True)]
    pallas_call x0 -> x10, Pallas kernels: none -> 82.2 us  [call(): pl.pallas_call(with_after, grid_spec=pltpu.PrefetchScalarGridSpec(num_sca...]
    ppermute x0 -> x24, waiting for transfers between devices: none -> 72.1 us  [the longest x9 26.7 us: swap(): lax.ppermute(a, axis, [(i, i ^ bit) for i in range(lax.axis_size(axis))])]
    dot_general x5 -> x1, matrix products: 60 us -> 0.91 us  [on_device(): scores = xor_sum(jnp.dot(quarter, z_queries.T, precision=HIGHEST), 'tensor')]
    psum x1 -> x0, waiting for transfers between devices: 50.7 us -> none  [on_device(): in_proj, out_proj = lax.psum((in_part, out_part), 'tensor')]
    ppermute x0 -> x24, starting transfers between devices: none -> 28 us  [the longest x5 6.88 us: line_of_four(): end_outer = send(end_inner[h][at:at + size], perm=outward)]
    unnamed x4 -> x32, local copies, waits for them, and re-layouts: 0.99 us -> 24.4 us
    slice x0 -> x5, local copies, waits for them, and re-layouts: none -> 6.47 us  [the longest x2 4.39 us: part(): return a[h * half:(h + 1) * half]]
  transfers between devices with their start and end apart: 3 -> 24, of which waited for: 2 -> 12; matrix products, arithmetic and copies ran while one was open for 4% -> 4% of each run, Pallas kernels for 0% -> 33%
where the time goes in v3:
time: 219 us; the launch traced here: 217 us
  Pallas kernels  82.2 us (38%)
  waiting for transfers between devices  72.1 us (33%)
  local copies, waits for them, and re-layouts  32.3 us (15%)
  starting transfers between devices  28 us (13%)
    pallas_call x10, Pallas kernels, call(): pl.pallas_call(with_after, grid_spec=pltpu.PrefetchScalarGridSpec(num_sca...  82.2 us
    ppermute x9, waiting for transfers between devices, swap(): lax.ppermute(a, axis, [(i, i ^ bit) for i in range(lax.axis_size(axis))])  26.7 us
    unnamed x32, local copies, waits for them, and re-layouts  24.4 us
    ppermute x2, waiting for transfers between devices, line_of_four(): mid_outer = [send(a, perm=outward) for a in mid_inner]  15.6 us
    ppermute x1, waiting for transfers between devices, line_of_four(): side = in_part + send(in_part, perm=inward)  13.6 us
    ppermute x1, waiting for transfers between devices, line_of_four(): left_t = jnp.where(middle, total, send(total, perm=outward))  11.9 us
    ppermute x5, starting transfers between devices, line_of_four(): end_outer = send(end_inner[h][at:at + size], perm=outward)  6.88 us
    ppermute x1, starting transfers between devices, line_of_four(): side = in_part + send(in_part, perm=inward)  5.29 us
  transfers between devices with their start and end apart: 24, of which 12 were waited for; matrix products, arithmetic and copies ran while one was open for 4% of the time, Pallas kernels for 33%

profile of v3, /device:TPU:0, one launch (start us, length us, event | category | flops | bytes accessed | tf_op | source)
XLA Modules:
  0.0 217.4 jit_solution(2887936203239011302)
XLA Ops:
  0.6 3.1 %collective-permute-start = (bf16[1024,1024]{1,0:T(8,128)(2,1)}, bf16[1024,1024]{1,0:T(8,128)(2,1)}, u32[]{:S(2)}, u32[]{:S(2)}) collective-permute-start(bf16[1024,1024]{1,0:T(8,128)(2,1)} %refs_1_.1), channel_id=1, source_target_pairs={{0,4},{4,0},{8,12},{12,8},{1,5},{5,1},{9,13},{13,9},{2,6},{6,2},{1... | collective-permute-start | bytes 6291464 | tf_op jit(solution)/shard_map/ppermute | solution.py:284
  3.7 2.7 %fusion.4 = (bf16[512,1024]{1,0:T(8,128)(2,1)}, bf16[512,1024]{1,0:T(8,128)(2,1)S(1)}) fusion(bf16[1024,1024]{1,0:T(8,128)(2,1)} %refs_1_.1), kind=kLoop, calls=%fused_computation.12 | loop fusion | bytes 4194304 | tf_op jit(solution)/shard_map/slice | solution.py:282
  6.4 1.7 collective-permute-start.3
  12.3 12.7 %own_block.1 = (f32[3584,512]{1,0:T(8,128)S(1)}, f32[3584,512]{1,0:T(8,128)S(1)}, bf16[3584,1024]{1,0:T(8,128)(2,1)S(1)}, f32[64,1024]{1,0:T(8,128)S(1)}) custom-call(s32[5]{0:T(128)S(1)} %stack.36.refs_0_, bf16[1024,1024]{1,0:T(8,128)(2,1)S(1)} %copy-done.9, bf16[3584,4096]{1,0:T(8,128)(2,1)} %refs_3_.16, bf16[1024,3584]{1,0:T(8,128)(2,1)} %refs_3_.9, ...), custom_call_target="tpu_custom_call" | custom-call | flops 7516192768 | bytes 25053976 | tf_op jit(solution)/shard_map/own_block/pallas_call | solution.py:38
  25.0 2.9 %copy-done = bf16[3584,1024]{1,0:T(8,128)(2,1)} copy-done((bf16[3584,1024]{1,0:T(8,128)(2,1)}, bf16[3584,1024]{1,0:T(8,128)(2,1)S(1)}, u32[]{:S(2)}) %copy-start) | copy-done | bytes 7340056
  27.9 3.0 %copy-done.2 = f32[3584,512]{1,0:T(8,128)} copy-done((f32[3584,512]{1,0:T(8,128)}, f32[3584,512]{1,0:T(8,128)S(1)}, u32[]{:S(2)}) %copy-start.2) | copy-done | bytes 7340056
  30.8 3.0 %copy-done.6 = f32[3584,512]{1,0:T(8,128)} copy-done((f32[3584,512]{1,0:T(8,128)}, f32[3584,512]{1,0:T(8,128)S(1)}, u32[]{:S(2)}) %copy-start.6) | copy-done | bytes 7340056
  33.8 5.3 %collective-permute-start.8 = (f32[64,1024]{1,0:T(8,128)S(1)}, f32[64,1024]{1,0:T(8,128)S(1)}, u32[]{:S(2)}, u32[]{:S(2)}) collective-permute-start(f32[64,1024]{1,0:T(8,128)S(1)} %get-tuple-element.12), channel_id=1, source_target_pairs={{0,4},{12,8},{1,5},{13,9},{2,6},{14,10},{3,7},{15,11},{16,20},{28,... | collective-permute-start | bytes 786440 | tf_op jit(solution)/shard_map/ppermute | solution.py:291
  40.9 13.6 %collective-permute-done.8 = f32[64,1024]{1,0:T(8,128)S(1)} collective-permute-done((f32[64,1024]{1,0:T(8,128)S(1)}, f32[64,1024]{1,0:T(8,128)S(1)}, u32[]{:S(2)}, u32[]{:S(2)}) %collective-permute-start.8) | collective-permute-done | bytes 262176 | tf_op jit(solution)/shard_map/ppermute | solution.py:291
  56.9 7.5 %collective-permute-done.6 = f32[256,256]{1,0:T(8,128)S(1)} collective-permute-done((f32[256,256]{1,0:T(8,128)S(1)}, f32[256,256]{1,0:T(8,128)S(1)}, u32[]{:S(2)}, u32[]{:S(2)}) %collective-permute-start.6) | collective-permute-done | bytes 262176 | tf_op jit(solution)/shard_map/ppermute | solution.py:323
  69.3 11.9 %collective-permute-done.10 = f32[64,1024]{1,0:T(8,128)S(1)} collective-permute-done((f32[64,1024]{1,0:T(8,128)S(1)}, f32[64,1024]{1,0:T(8,128)S(1)}, u32[]{:S(2)}, u32[]{:S(2)}) %collective-permute-start.10) | collective-permute-done | bytes 262176 | tf_op jit(solution)/shard_map/ppermute | solution.py:293
  82.6 1.7 fusion.5
  85.8 3.1 %copy-done.7 = f32[3584,512]{1,0:T(8,128)S(1)} copy-done((f32[3584,512]{1,0:T(8,128)S(1)}, f32[3584,512]{1,0:T(8,128)}, u32[]{:S(2)}) %copy-start.7) | copy-done | bytes 7340056
  88.9 12.6 %pair_block.1 = (f32[3584,512]{1,0:T(8,128)S(1)}, f32[3584,512]{1,0:T(8,128)S(1)}) custom-call(s32[5]{0:T(128)S(1)} %stack.36.refs_0_, bf16[1024,1024]{1,0:T(8,128)(2,1)} %collective-permute-done.refs_1_, bf16[3584,4096]{1,0:T(8,128)(2,1)} %refs_3_.16, f32[3584,512]{1,0:T(8,128)S(1)} %copy-done.7, ...), custom_call_target="tpu_custom_call", output_to_operand_aliasing={{0}: (3, {}), {1}: (4, {})} | custom-call | flops 7516192768 | bytes 25053976 | tf_op jit(solution)/shard_map/pair_block/pallas_call | solution.py:38
  101.5 5.3 %collective-permute-done.4.refs_2_ = bf16[512,1024]{1,0:T(8,128)(2,1)S(1)} collective-permute-done((bf16[512,1024]{1,0:T(8,128)(2,1)}, bf16[512,1024]{1,0:T(8,128)(2,1)S(1)}, u32[]{:S(2)}, u32[]{:S(2)}) %collective-permute-start.4) | collective-permute-done | bytes 1048608 | tf_op jit(solution)/shard_map/ppermute | solution.py:287
  106.8 9.2 %third_block.2.refs_4_ = f32[3584,512]{1,0:T(8,128)S(1)} custom-call(s32[5]{0:T(128)S(1)} %stack.36.refs_0_, bf16[512,1024]{1,0:T(8,128)(2,1)} %collective-permute-done.3.refs_1_, bf16[512,1024]{1,0:T(8,128)(2,1)S(1)} %collective-permute-done.4.refs_2_, bf16[3584,4096]{1,0:T(8,128)(2,1)} %refs_3_.16, ...), custom_call_target="tpu_custom_call", output_to_operand_aliasing={{}: (4, {})} | custom-call | flops 3758096384 | bytes 12526987 | tf_op jit(solution)/shard_map/third_block/pallas_call | solution.py:38
  118.9 10.3 %collective-permute-done.15.refs_2_ = bf16[512,1024]{1,0:T(8,128)(2,1)S(1)} collective-permute-done((bf16[512,1024]{1,0:T(8,128)(2,1)}, bf16[512,1024]{1,0:T(8,128)(2,1)S(1)}, u32[]{:S(2)}, u32[]{:S(2)}) %collective-permute-start.15) | collective-permute-done | bytes 1048608 | tf_op jit(solution)/shard_map/ppermute | solution.py:287
  129.2 9.5 %third_block.3.refs_4_ = f32[3584,512]{1,0:T(8,128)S(1)} custom-call(s32[5]{0:T(128)S(1)} %stack.36.refs_0_, bf16[512,1024]{1,0:T(8,128)(2,1)} %collective-permute-done.14.refs_1_, bf16[512,1024]{1,0:T(8,128)(2,1)S(1)} %collective-permute-done.15.refs_2_, bf16[3584,4096]{1,0:T(8,128)(2,1)} %refs_3_.16, ...), custom_call_target="tpu_custom_call", output_to_operand_aliasing={{}: (4, {})} | custom-call | flops 3758096384 | bytes 12526987 | tf_op jit(solution)/shard_map/third_block/pallas_call | solution.py:38
  144.9 6.8 %last_block.5.refs_8_ = f32[64,64]{1,0:T(8,128)S(1)} custom-call(s32[5]{0:T(128)S(1)} %stack.36.refs_0_, bf16[512,1024]{1,0:T(8,128)(2,1)S(1)} %collective-permute-done.1.refs_1_, bf16[256,1024]{1,0:T(8,128)(2,1)S(1)} %collective-permute-done.11.refs_2_, bf16[3584,4096]{1,0:T(8,128)(2,1)} %refs_3_.16, f32[3584,512]{1,0:T(8,128)S(1)} %third_block.2.refs_4_, ...), custom_call_target="tpu_custom_call" | custom-call | flops 1996488704 | bytes 6654962 | tf_op jit(solution)/shard_map/last_block/pallas_call | solution.py:38
  151.7 6.8 %last_block.6 = f32[64,64]{1,0:T(8,128)S(1)} custom-call(s32[5]{0:T(128)S(1)} %stack.36.refs_0_, bf16[512,1024]{1,0:T(8,128)(2,1)S(1)} %collective-permute-done.1.refs_1_, bf16[256,1024]{1,0:T(8,128)(2,1)S(1)} %collective-permute-done.2.refs_2_, bf16[3584,4096]{1,0:T(8,128)(2,1)} %refs_3_.16, f32[3584,512]{1,0:T(8,128)S(1)} %third_block.2.refs_4_, ...), custom_call_target="tpu_custom_call" | custom-call | flops 1996488704 | bytes 6654962 | tf_op jit(solution)/shard_map/last_block/pallas_call | solution.py:38
  158.6 4.3 %collective-permute-done.17.refs_2_ = bf16[256,1024]{1,0:T(8,128)(2,1)S(1)} collective-permute-done((bf16[256,1024]{1,0:T(8,128)(2,1)}, bf16[256,1024]{1,0:T(8,128)(2,1)S(1)}, u32[]{:S(2)}, u32[]{:S(2)}) %collective-permute-start.17) | collective-permute-done | bytes 524320 | tf_op jit(solution)/shard_map/ppermute | solution.py:302
  162.9 3.1 %copy-done.1 = bf16[3584,1024]{1,0:T(8,128)(2,1)S(1)} copy-done((bf16[3584,1024]{1,0:T(8,128)(2,1)S(1)}, bf16[3584,1024]{1,0:T(8,128)(2,1)}, u32[]{:S(2)}) %copy-start.1) | copy-done | bytes 7340056
  166.0 3.1 %copy-done.5 = f32[3584,512]{1,0:T(8,128)S(1)} copy-done((f32[3584,512]{1,0:T(8,128)S(1)}, f32[3584,512]{1,0:T(8,128)}, u32[]{:S(2)}) %copy-start.5) | copy-done | bytes 7340056
  169.1 6.8 %last_block.7.refs_8_ = f32[64,64]{1,0:T(8,128)S(1)} custom-call(s32[5]{0:T(128)S(1)} %stack.36.refs_0_, bf16[512,1024]{1,0:T(8,128)(2,1)S(1)} %collective-permute-done.12.refs_1_, bf16[256,1024]{1,0:T(8,128)(2,1)S(1)} %collective-permute-done.17.refs_2_, bf16[3584,4096]{1,0:T(8,128)(2,1)} %refs_3_.16, f32[3584,512]{1,0:T(8,128)S(1)} %copy-done.5, ...), custom_call_target="tpu_custom_call" | custom-call | flops 1996488704 | bytes 6654962 | tf_op jit(solution)/shard_map/last_block/pallas_call | solution.py:38
  175.9 6.5 %last_block.8.refs_8_ = f32[64,64]{1,0:T(8,128)S(1)} custom-call(s32[5]{0:T(128)S(1)} %stack.36.refs_0_, bf16[512,1024]{1,0:T(8,128)(2,1)S(1)} %collective-permute-done.12.refs_1_, bf16[128,1024]{1,0:T(8,128)(2,1)} %collective-permute-done.16.refs_2_, bf16[3584,4096]{1,0:T(8,128)(2,1)} %refs_3_.16, f32[3584,512]{1,0:T(8,128)S(1)} %copy-done.5, ...), custom_call_target="tpu_custom_call" | custom-call | flops 998244352 | bytes 3327481 | tf_op jit(solution)/shard_map/last_block/pallas_call | solution.py:38
  182.5 6.5 %last_block.9 = f32[64,64]{1,0:T(8,128)S(1)} custom-call(s32[5]{0:T(128)S(1)} %stack.36.refs_0_, bf16[512,1024]{1,0:T(8,128)(2,1)S(1)} %collective-permute-done.12.refs_1_, bf16[128,1024]{1,0:T(8,128)(2,1)} %collective-permute-done.13.refs_2_, bf16[3584,4096]{1,0:T(8,128)(2,1)} %refs_3_.16, f32[3584,512]{1,0:T(8,128)S(1)} %copy-done.5, ...), custom_call_target="tpu_custom_call" | custom-call | flops 998244352 | bytes 3327481 | tf_op jit(solution)/shard_map/last_block/pallas_call | solution.py:38
  189.2 3.9 %collective-permute-done.18 = f32[2,4096]{1,0:T(2,128)S(1)} collective-permute-done((f32[2,4096]{1,0:T(2,128)S(1)}, f32[2,4096]{1,0:T(2,128)S(1)}, u32[]{:S(2)}, u32[]{:S(2)}) %collective-permute-start.18) | collective-permute-done | bytes 32800 | tf_op jit(solution)/shard_map/ppermute | solution.py:323
  193.2 4.8 %collective-permute-done.19 = f32[2,4096]{1,0:T(2,128)S(1)} collective-permute-done((f32[2,4096]{1,0:T(2,128)S(1)}, f32[2,4096]{1,0:T(2,128)S(1)}, u32[]{:S(2)}, u32[]{:S(2)}) %collective-permute-start.19) | collective-permute-done | bytes 32800 | tf_op jit(solution)/shard_map/ppermute | solution.py:323
  201.8 3.6 %collective-permute-done.22 = f32[2,256]{1,0:T(2,128)S(1)} collective-permute-done((f32[2,256]{1,0:T(2,128)S(1)}, f32[2,256]{1,0:T(2,128)S(1)}, u32[]{:S(2)}, u32[]{:S(2)}) %collective-permute-start.22) | collective-permute-done | bytes 2080 | tf_op jit(solution)/shard_map/ppermute | solution.py:323
  205.4 4.5 %collective-permute-done.23 = f32[2,256]{1,0:T(2,128)S(1)} collective-permute-done((f32[2,256]{1,0:T(2,128)S(1)}, f32[2,256]{1,0:T(2,128)S(1)}, u32[]{:S(2)}, u32[]{:S(2)}) %collective-permute-start.23) | collective-permute-done | bytes 2080 | tf_op jit(solution)/shard_map/ppermute | solution.py:323
  210.6 2.2 %copy-done.10 = f32[256,4096]{1,0:T(8,128)S(1)} copy-done((f32[256,4096]{1,0:T(8,128)S(1)}, f32[256,4096]{1,0:T(8,128)}, u32[]{:S(2)}) %copy-start.10) | copy-done | bytes 4194328
  212.7 4.7 %hessian_update.1 = f32[256,4096]{1,0:T(8,128)} custom-call(s32[1]{0:T(128)} %bitcast.refs_0_, f32[8,4096]{1,0:T(8,128)S(1)} %pad_maximum_fusion.refs_1_.refs_2_, f32[8,4096]{1,0:T(8,128)S(1)} %pad_maximum_fusion.refs_1_.refs_2_, f32[256,4096]{1,0:T(8,128)S(1)} %copy-done.10), custom_call_target="tpu_custom_call" | custom-call | flops 100663296 | bytes 335544 | tf_op jit(solution)/shard_map/hessian_update/pallas_call | solution.py:38
  (84 shorter events, 29.7 us)
Async XLA Ops:
  0.6 82.0 %collective-permute-start = (bf16[1024,1024]{1,0:T(8,128)(2,1)}, bf16[1024,1024]{1,0:T(8,128)(2,1)}, u32[]{:S(2)}, u32[]{:S(2)}) collective-permute-start(bf16[1024,1024]{1,0:T(8,128)(2,1)} %refs_1_.1), channel_id=1, source_target_pairs={{0,4},{4,0},{8,12},{12,8},{1,5},{5,1},{9,13},{13,9},{2,6},{6,2},{1... | collective-permute-start | bytes 6291464 | tf_op jit(solution)/shard_map/ppermute | solution.py:284
  6.4 61.6 %collective-permute-start.3 = (bf16[512,1024]{1,0:T(8,128)(2,1)}, bf16[512,1024]{1,0:T(8,128)(2,1)}, u32[]{:S(2)}, u32[]{:S(2)}) collective-permute-start(bf16[512,1024]{1,0:T(8,128)(2,1)} %get-tuple-element.14), channel_id=1, source_target_pairs={{4,8},{8,4},{5,9},{9,5},{6,10},{10,6},{7,11},{11,7},{20,24},{24,20... | collective-permute-start | bytes 3145736 | tf_op jit(solution)/shard_map/ppermute | solution.py:285
  12.3 26.9 %copy-start.13 = (f32[256,256]{1,0:T(8,128)S(1)}, f32[256,256]{1,0:T(8,128)}, u32[]{:S(2)}) copy-start(f32[256,256]{1,0:T(8,128)} %param.15) | copy-start | bytes 786436
  33.8 20.6 %collective-permute-start.8 = (f32[64,1024]{1,0:T(8,128)S(1)}, f32[64,1024]{1,0:T(8,128)S(1)}, u32[]{:S(2)}, u32[]{:S(2)}) collective-permute-start(f32[64,1024]{1,0:T(8,128)S(1)} %get-tuple-element.12), channel_id=1, source_target_pairs={{0,4},{12,8},{1,5},{13,9},{2,6},{14,10},{3,7},{15,11},{16,20},{28,... | collective-permute-start | bytes 786440 | tf_op jit(solution)/shard_map/ppermute | solution.py:291
  39.1 16.0 %collective-permute-start.5 = (f32[256,256]{1,0:T(8,128)S(1)}, f32[256,256]{1,0:T(8,128)S(1)}, u32[]{:S(2)}, u32[]{:S(2)}) collective-permute-start(f32[256,256]{1,0:T(8,128)S(1)} %copy-done.13), channel_id=1, source_target_pairs={{0,1},{1,0},{2,3},{3,2},{4,5},{5,4},{6,7},{7,6},{8,9},{9,8},{10,11... | collective-permute-start | bytes 786440 | tf_op jit(solution)/shard_map/ppermute | solution.py:323
  39.2 42.1 %collective-permute-start.14 = (bf16[512,1024]{1,0:T(8,128)(2,1)S(1)}, bf16[512,1024]{1,0:T(8,128)(2,1)}, u32[]{:S(2)}, u32[]{:S(2)}) collective-permute-start(bf16[512,1024]{1,0:T(8,128)(2,1)S(1)} %get-tuple-element.15), channel_id=1, source_target_pairs={{4,8},{8,4},{5,9},{9,5},{6,10},{10,6},{7,11},{11,7},{20,24},{24,20... | collective-permute-start | bytes 3145736 | tf_op jit(solution)/shard_map/ppermute | solution.py:285
  54.5 2.3 %collective-permute-start.9 = (f32[64,1024]{1,0:T(8,128)S(1)}, f32[64,1024]{1,0:T(8,128)S(1)}, u32[]{:S(2)}, u32[]{:S(2)}) collective-permute-start(f32[64,1024]{1,0:T(8,128)S(1)} %add.50), channel_id=1, source_target_pairs={{4,8},{8,4},{5,9},{9,5},{6,10},{10,6},{7,11},{11,7},{20,24},{24,20... | collective-permute-start | bytes 786440 | tf_op jit(solution)/shard_map/ppermute | solution.py:292
  55.2 9.3 %collective-permute-start.6 = (f32[256,256]{1,0:T(8,128)S(1)}, f32[256,256]{1,0:T(8,128)S(1)}, u32[]{:S(2)}, u32[]{:S(2)}) collective-permute-start(f32[256,256]{1,0:T(8,128)S(1)} %copy-done.13), channel_id=1, source_target_pairs={{0,2},{1,3},{2,0},{3,1},{4,6},{5,7},{6,4},{7,5},{8,10},{9,11},{10,... | collective-permute-start | bytes 786440 | tf_op jit(solution)/shard_map/ppermute | solution.py:323
  56.7 10.3 %collective-permute-start.7 = (f32[256,256]{1,0:T(8,128)S(1)}, f32[256,256]{1,0:T(8,128)}, u32[]{:S(2)}, u32[]{:S(2)}) collective-permute-start(f32[256,256]{1,0:T(8,128)S(1)} %copy-done.13), channel_id=1, source_target_pairs={{0,3},{1,2},{2,1},{3,0},{4,7},{5,6},{6,5},{7,4},{8,11},{9,10},{10,... | collective-permute-start | bytes 786440 | tf_op jit(solution)/shard_map/ppermute | solution.py:323
  56.9 28.9 %copy-start.3 = (f32[3584,512]{1,0:T(8,128)S(1)}, f32[3584,512]{1,0:T(8,128)}, u32[]{:S(2)}) copy-start(f32[3584,512]{1,0:T(8,128)} %copy-done.2) | copy-start | bytes 22020100
  64.5 16.8 %collective-permute-start.10 = (f32[64,1024]{1,0:T(8,128)S(1)}, f32[64,1024]{1,0:T(8,128)S(1)}, u32[]{:S(2)}, u32[]{:S(2)}) collective-permute-start(f32[64,1024]{1,0:T(8,128)S(1)} %add.51), channel_id=1, source_target_pairs={{4,0},{8,12},{5,1},{9,13},{6,2},{10,14},{7,3},{11,15},{20,16},{24,... | collective-permute-start | bytes 786440 | tf_op jit(solution)/shard_map/ppermute | solution.py:293
  68.0 38.7 %collective-permute-start.4 = (bf16[512,1024]{1,0:T(8,128)(2,1)}, bf16[512,1024]{1,0:T(8,128)(2,1)S(1)}, u32[]{:S(2)}, u32[]{:S(2)}) collective-permute-start(bf16[512,1024]{1,0:T(8,128)(2,1)} %collective-permute-done.3.refs_1_), channel_id=1, source_target_pairs={{4,0},{8,12},{5,1},{9,13},{6,2},{10,14},{7,3},{11,15},{20,16},{24,... | collective-permute-start | bytes 3145736 | tf_op jit(solution)/shard_map/ppermute | solution.py:287
  81.3 47.9 %collective-permute-start.15 = (bf16[512,1024]{1,0:T(8,128)(2,1)}, bf16[512,1024]{1,0:T(8,128)(2,1)S(1)}, u32[]{:S(2)}, u32[]{:S(2)}) collective-permute-start(bf16[512,1024]{1,0:T(8,128)(2,1)} %collective-permute-done.14.refs_1_), channel_id=1, source_target_pairs={{4,0},{8,12},{5,1},{9,13},{6,2},{10,14},{7,3},{11,15},{20,16},{24,... | collective-permute-start | bytes 3145736 | tf_op jit(solution)/shard_map/ppermute | solution.py:287
  84.3 31.6 %collective-permute-start.1 = (bf16[512,1024]{1,0:T(8,128)(2,1)S(1)}, bf16[512,1024]{1,0:T(8,128)(2,1)S(1)}, u32[]{:S(2)}, u32[]{:S(2)}) collective-permute-start(bf16[512,1024]{1,0:T(8,128)(2,1)S(1)} %get-tuple-element.16), channel_id=1, source_target_pairs={{4,8},{8,4},{5,9},{9,5},{6,10},{10,6},{7,11},{11,7},{20,24},{24,20... | collective-permute-start | bytes 3145736 | tf_op jit(solution)/shard_map/ppermute | solution.py:288
  85.1 53.7 %collective-permute-start.12 = (bf16[512,1024]{1,0:T(8,128)(2,1)S(1)}, bf16[512,1024]{1,0:T(8,128)(2,1)S(1)}, u32[]{:S(2)}, u32[]{:S(2)}) collective-permute-start(bf16[512,1024]{1,0:T(8,128)(2,1)S(1)} %get-tuple-element.17), channel_id=1, source_target_pairs={{4,8},{8,4},{5,9},{9,5},{6,10},{10,6},{7,11},{11,7},{20,24},{24,20... | collective-permute-start | bytes 3145736 | tf_op jit(solution)/shard_map/ppermute | solution.py:288
  85.8 3.1 %copy-start.7 = (f32[3584,512]{1,0:T(8,128)S(1)}, f32[3584,512]{1,0:T(8,128)}, u32[]{:S(2)}) copy-start(f32[3584,512]{1,0:T(8,128)} %copy-done.6) | copy-start | bytes 22020100
  116.0 28.8 %slice-start = ((s8[7340032]{0:T(1024)(128)(4,1)}), s8[4194304]{0:T(1024)(128)(4,1)S(1)}, s32[]{:S(2)}) async-start(s8[7340032]{0:T(1024)(128)(4,1)} %bitcast.9), calls=%async_computation | async-start | bytes 8388608
  116.1 28.7 %collective-permute-start.11 = (bf16[256,1024]{1,0:T(8,128)(2,1)S(1)}, bf16[256,1024]{1,0:T(8,128)(2,1)S(1)}, u32[]{:S(2)}, u32[]{:S(2)}) collective-permute-start(bf16[256,1024]{1,0:T(8,128)(2,1)S(1)} %get-tuple-element.18), channel_id=1, source_target_pairs={{4,0},{8,12},{5,1},{9,13},{6,2},{10,14},{7,3},{11,15},{20,16},{24,... | collective-permute-start | bytes 1572872 | tf_op jit(solution)/shard_map/ppermute | solution.py:302
  117.6 34.1 %collective-permute-start.2 = (bf16[256,1024]{1,0:T(8,128)(2,1)S(1)}, bf16[256,1024]{1,0:T(8,128)(2,1)S(1)}, u32[]{:S(2)}, u32[]{:S(2)}) collective-permute-start(bf16[256,1024]{1,0:T(8,128)(2,1)S(1)} %get-tuple-element.19), channel_id=1, source_target_pairs={{4,0},{8,12},{5,1},{9,13},{6,2},{10,14},{7,3},{11,15},{20,16},{24,... | collective-permute-start | bytes 1572872 | tf_op jit(solution)/shard_map/ppermute | solution.py:302
  129.2 15.6 %slice-start.1 = ((s8[7340032]{0:T(1024)(128)(4,1)}), s8[3145728]{0:T(1024)(128)(4,1)S(1)}, s32[]{:S(2)}) async-start(s8[7340032]{0:T(1024)(128)(4,1)} %bitcast.9), calls=%async_computation.1 | async-start | bytes 6291456
  129.2 15.6 %copy-start.8 = (bf16[3584,64]{0,1:T(8,128)(2,1)S(1)}, bf16[3584,64]{0,1:T(8,128)(2,1)}, u32[]{:S(2)}) copy-start(bf16[3584,64]{0,1:T(8,128)(2,1)} %param.13) | copy-start | bytes 1376260
  138.7 13.0 %copy-start.4 = (f32[3584,512]{1,0:T(8,128)}, f32[3584,512]{1,0:T(8,128)S(1)}, u32[]{:S(2)}) copy-start(f32[3584,512]{1,0:T(8,128)S(1)} %third_block.3.refs_4_) | copy-start | bytes 22020100
  139.7 23.3 %collective-permute-start.17 = (bf16[256,1024]{1,0:T(8,128)(2,1)}, bf16[256,1024]{1,0:T(8,128)(2,1)S(1)}, u32[]{:S(2)}, u32[]{:S(2)}) collective-permute-start(bf16[256,1024]{1,0:T(8,128)(2,1)} %slice.42), channel_id=1, source_target_pairs={{4,0},{8,12},{5,1},{9,13},{6,2},{10,14},{7,3},{11,15},{20,16},{24,... | collective-permute-start | bytes 1572872 | tf_op jit(solution)/shard_map/ppermute | solution.py:302
  142.0 33.9 %collective-permute-start.16 = (bf16[128,1024]{1,0:T(8,128)(2,1)}, bf16[128,1024]{1,0:T(8,128)(2,1)}, u32[]{:S(2)}, u32[]{:S(2)}) collective-permute-start(bf16[128,1024]{1,0:T(8,128)(2,1)} %get-tuple-element.20), channel_id=1, source_target_pairs={{4,0},{8,12},{5,1},{9,13},{6,2},{10,14},{7,3},{11,15},{20,16},{24,... | collective-permute-start | bytes 786440 | tf_op jit(solution)/shard_map/ppermute | solution.py:302
  143.3 39.2 %collective-permute-start.13 = (bf16[128,1024]{1,0:T(8,128)(2,1)}, bf16[128,1024]{1,0:T(8,128)(2,1)}, u32[]{:S(2)}, u32[]{:S(2)}) collective-permute-start(bf16[128,1024]{1,0:T(8,128)(2,1)} %get-tuple-element.21), channel_id=1, source_target_pairs={{4,0},{8,12},{5,1},{9,13},{6,2},{10,14},{7,3},{11,15},{20,16},{24,... | collective-permute-start | bytes 786440 | tf_op jit(solution)/shard_map/ppermute | solution.py:302
  162.9 3.1 %copy-start.1 = (bf16[3584,1024]{1,0:T(8,128)(2,1)S(1)}, bf16[3584,1024]{1,0:T(8,128)(2,1)}, u32[]{:S(2)}) copy-start(bf16[3584,1024]{1,0:T(8,128)(2,1)} %copy-done) | copy-start | bytes 22020100
  189.1 4.0 %collective-permute-start.18 = (f32[2,4096]{1,0:T(2,128)S(1)}, f32[2,4096]{1,0:T(2,128)S(1)}, u32[]{:S(2)}, u32[]{:S(2)}) collective-permute-start(f32[2,4096]{1,0:T(2,128)S(1)} %pad_maximum_fusion.2), channel_id=1, source_target_pairs={{0,4},{4,0},{8,12},{12,8},{1,5},{5,1},{9,13},{13,9},{2,6},{6,2},{1... | collective-permute-start | bytes 98312 | tf_op jit(solution)/shard_map/ppermute | solution.py:323
  193.2 4.9 %collective-permute-start.19 = (f32[2,4096]{1,0:T(2,128)S(1)}, f32[2,4096]{1,0:T(2,128)S(1)}, u32[]{:S(2)}, u32[]{:S(2)}) collective-permute-start(f32[2,4096]{1,0:T(2,128)S(1)} %fusion.3), channel_id=1, source_target_pairs={{0,8},{4,12},{8,0},{12,4},{1,9},{5,13},{9,1},{13,5},{2,10},{6,14},... | collective-permute-start | bytes 98312 | tf_op jit(solution)/shard_map/ppermute | solution.py:323
  198.1 1.3 collective-permute-start.20
  199.4 11.1 %collective-permute-start.21 = (f32[4,4096]{1,0:T(4,128)S(1)}, f32[4,4096]{1,0:T(4,128)S(1)}, u32[]{:S(2)}, u32[]{:S(2)}) collective-permute-start(f32[4,4096]{1,0:T(4,128)S(1)} %pad_maximum_fusion.1), channel_id=1, source_target_pairs={{0,2},{1,3},{2,0},{3,1},{4,6},{5,7},{6,4},{7,5},{8,10},{9,11},{10,... | collective-permute-start | bytes 196616 | tf_op jit(solution)/shard_map/ppermute | solution.py:323
  201.8 3.6 %collective-permute-start.22 = (f32[2,256]{1,0:T(2,128)S(1)}, f32[2,256]{1,0:T(2,128)S(1)}, u32[]{:S(2)}, u32[]{:S(2)}) collective-permute-start(f32[2,256]{1,0:T(2,128)S(1)} %fusion), channel_id=1, source_target_pairs={{0,4},{4,0},{8,12},{12,8},{1,5},{5,1},{9,13},{13,9},{2,6},{6,2},{1... | collective-permute-start | bytes 6152 | tf_op jit(solution)/shard_map/ppermute | solution.py:323
  205.4 4.5 %collective-permute-start.23 = (f32[2,256]{1,0:T(2,128)S(1)}, f32[2,256]{1,0:T(2,128)S(1)}, u32[]{:S(2)}, u32[]{:S(2)}) collective-permute-start(f32[2,256]{1,0:T(2,128)S(1)} %add.55), channel_id=1, source_target_pairs={{0,8},{4,12},{8,0},{12,4},{1,9},{5,13},{9,1},{13,5},{2,10},{6,14},... | collective-permute-start | bytes 6152 | tf_op jit(solution)/shard_map/ppermute | solution.py:323
  (8 other events, 18.2 us)

commit v4 on v0

v4 whole, which is shorter than its diff:
```python
import functools

import jax
import jax.numpy as jnp
from jax import lax
from jax.experimental import pallas as pl
from jax.experimental.pallas import tpu as pltpu
from jax.sharding import PartitionSpec as P

PROJ = 64
LEN = 512
HIGHEST = lax.Precision.HIGHEST
NT = (((1,), (1,)), ((), ()))
TILE = 512
OWN_TILE = 256
ANYWHERE = pl.BlockSpec(memory_space=pl.ANY)
INSIDE = pl.BlockSpec(memory_space=pltpu.VMEM)
OUTSIDE = pl.BlockSpec(memory_space=pltpu.HBM)


def silu(v):
    return 0.5 * v * (1.0 + jnp.tanh(0.5 * v))


def dot(a, b):
    return jnp.dot(a, b, preferred_element_type=jnp.float32)


def dot_nt(a, b):
    return lax.dot_general(a, b, NT, preferred_element_type=jnp.float32)


def placed(a, spec):
    if spec is INSIDE or spec is OUTSIDE:
        return pltpu.with_memory_space_constraint(a, spec.memory_space)
    return a


def call(body, name, where, grid, operands, in_specs, out_specs, out_shapes, scratch, mib, aliases=None):
    return pl.pallas_call(
        body,
        grid_spec=pltpu.PrefetchScalarGridSpec(
            num_scalar_prefetch=1, grid=grid, in_specs=in_specs, out_specs=out_specs, scratch_shapes=scratch
        ),
        out_shape=out_shapes,
        compiler_params=pltpu.CompilerParams(vmem_limit_bytes=mib * 2**20),
        cost_estimate=pl.CostEstimate(flops=1000, bytes_accessed=1000, transcendentals=0),
        name=name,
        input_output_aliases=aliases or {},
    )(where, *[placed(a, spec) for a, spec in zip(operands, in_specs)])


def after(a, *others):
    return lax.optimization_barrier((a, *others))[0]


def fixed(shape):
    return pl.BlockSpec(shape, lambda j, where: (0, 0), pipeline_mode=pl.Buffered(1))


def tile_rows(t, size=TILE):
    return pl.ds(pl.multiple_of(t * size, size), size)


def columns(where, i, width):
    return pl.ds(pl.multiple_of(where[i] * width, width), width)


def own_body(where, own, gate, inputs, pi_t, w_far, w, acc, in_t, *rest):
    *gates_t, own_t, sems = rest
    step = pl.program_id(0)
    reads = [
        pltpu.make_async_copy(w_far.at[rows], w.at[rows], sems.at[t])
        for t in range(sems.shape[0])
        for rows in [pl.ds(t * OWN_TILE, OWN_TILE)]
    ]

    @pl.when(step == 0)
    def _():
        for read in reads:
            read.start()
        in_t[...] = dot_nt(pi_t[...], inputs[...])
        own_t[...] = own[...].T

    start = 0
    for gate_t in gates_t:
        size = gate_t.shape[1]
        gate_t[...] = gate[start : start + size, :].T
        start += size
    rows = tile_rows(step, OWN_TILE)
    pltpu.make_async_copy(w_far.at[rows], w.at[rows], sems.at[step]).wait()
    acc[rows, :] = dot(w[rows, columns(where, 0, own.shape[1])], own_t[...])


def own_block(where, own, gate, inputs, pi_t, w, sizes):
    tokens, hidden = gate.shape
    feats = own.shape[1]
    return call(
        own_body,
        "own_block",
        where,
        (hidden // OWN_TILE,),
        (own, gate, inputs, pi_t, w),
        [
            fixed(own.shape),
            pl.BlockSpec((tokens, OWN_TILE), lambda j, where: (0, j)),
            fixed(inputs.shape),
            fixed(pi_t.shape),
            OUTSIDE,
        ],
        [INSIDE, INSIDE, pl.BlockSpec((PROJ, tokens), lambda j, where: (0, 0))]
        + [pl.BlockSpec((OWN_TILE, size), lambda j, where: (j, 0)) for size in sizes],
        [
            pltpu.VMEM(w.shape, w.dtype),
            pltpu.VMEM((hidden, tokens), jnp.float32),
            jax.ShapeDtypeStruct((PROJ, tokens), jnp.float32),
        ]
        + [jax.ShapeDtypeStruct((hidden, size), gate.dtype) for size in sizes],
        [pltpu.VMEM((feats, tokens), own.dtype), pltpu.SemaphoreType.DMA((hidden // OWN_TILE,))],
        16,
    )


def add_body(which, where, *refs):
    *blocks, w, old, _, acc, token, block_t = refs
    token[...] = jnp.zeros_like(token)
    if len(blocks) == 1:
        block_t[...] = blocks[0][...].T
    else:
        block_t[...] = select_transposed(where, *blocks)

    @pl.loop(0, acc.shape[0] // TILE)
    def _(t):
        rows = tile_rows(t)
        acc[rows, :] = old[rows, :] + dot(w[rows, columns(where, which, block_t.shape[0])], block_t[...])


def add_block(where, which, blocks, w, old):
    tokens, feats = blocks[0].shape
    return call(
        functools.partial(add_body, which),
        f"add_block_{which}",
        where,
        (1,),
        (*blocks, w, old),
        [fixed(a.shape) for a in blocks] + [INSIDE, INSIDE],
        [INSIDE, INSIDE, pl.BlockSpec((8, 128), lambda j, where: (0, 0))],
        [
            pltpu.VMEM(w.shape, w.dtype),
            pltpu.VMEM(old.shape, old.dtype),
            jax.ShapeDtypeStruct((8, 128), jnp.float32),
        ],
        [pltpu.VMEM((feats, tokens), blocks[0].dtype)],
        16,
        aliases={len(blocks) + 1: 0, len(blocks) + 2: 1},
    )


def select_transposed(where, inner, outer):
    return jnp.where(where[4] == 1, inner[...], outer[...]).T


def last_body(start, where, inner, outer, w, old, gate_t, po_t, left_t, *rest):
    *grads_in, w_same, old_same, grads, block_t = rest
    size, feats = outer.shape
    tokens = pl.ds(start, size)
    block_t[...] = select_transposed(where, inner, outer)

    def step(t, right_t):
        rows = tile_rows(t)
        hidden_grad = old[rows, tokens] + dot(w[rows, columns(where, 3, feats)], block_t[...])
        up_grad = (hidden_grad * silu(gate_t[rows, :].astype(jnp.float32))).astype(jnp.bfloat16)
        return right_t + dot(po_t[:, rows], up_grad)

    right_t = lax.fori_loop(0, old.shape[0] // TILE, step, jnp.zeros((PROJ, size), jnp.float32))
    total = lax.dot_general(
        left_t[...], right_t, NT, precision=HIGHEST, preferred_element_type=jnp.float32
    )
    for earlier in grads_in:
        total = total + earlier[...]
    grads[...] = total


def last_block(where, inner, outer, start, w, old, gate_t, po_t, left_t, grads):
    size, feats = outer.shape
    chunk = start // size
    return call(
        functools.partial(last_body, start),
        "last_block",
        where,
        (1,),
        (inner, outer, w, old, gate_t, po_t, left_t, *grads),
        [
            INSIDE,
            INSIDE,
            INSIDE,
            INSIDE,
            fixed(gate_t.shape),
            fixed(po_t.shape),
            pl.BlockSpec((PROJ, size), lambda j, where: (0, chunk), pipeline_mode=pl.Buffered(1)),
            *[fixed(a.shape) for a in grads],
        ],
        [INSIDE, INSIDE, pl.BlockSpec((PROJ, PROJ), lambda j, where: (0, 0))],
        [
            pltpu.VMEM(w.shape, w.dtype),
            pltpu.VMEM(old.shape, old.dtype),
            jax.ShapeDtypeStruct((PROJ, PROJ), jnp.float32),
        ],
        [pltpu.VMEM((feats, size), outer.dtype)],
        16,
        aliases={3: 0, 4: 1},
    )


def small_kernel(body, name, where, *operands):
    (out,) = call(
        body,
        name,
        where,
        (1,),
        operands,
        [fixed(a.shape) for a in operands],
        [pl.BlockSpec(operands[0].shape, lambda j, where: (0, 0))],
        [jax.ShapeDtypeStruct(operands[0].shape, operands[0].dtype)],
        [],
        16,
    )
    return out


def sum_body(where, a, b, out):
    out[...] = a[...] + b[...]


def pick_body(where, a, b, out):
    out[...] = jnp.where(where[4] == 1, a[...], b[...])


def score_body(order, grads, *rest):
    *parts, out = rest
    total = None
    for s, part in enumerate(parts):
        width = part.shape[1]
        term = lax.dot_general(
            grads[:, columns(order, s, width)],
            part[...],
            NT,
            precision=HIGHEST,
            preferred_element_type=jnp.float32,
        )
        total = term if total is None else total + term
    out[...] = total


def score_parts(order, grads, parts):
    width = parts[0].shape[1]
    shape = (grads.shape[0], parts[0].shape[0])
    if width % 128:
        slices = [lax.dynamic_slice_in_dim(grads, order[s] * width, width, 1) for s in range(len(parts))]
        return jnp.dot(jnp.concatenate(slices, axis=1), jnp.concatenate(parts, axis=1).T, precision=HIGHEST)
    (scores,) = call(
        score_body,
        "scores",
        order,
        (1,),
        (grads, *parts),
        [fixed(grads.shape)] + [fixed(a.shape) for a in parts],
        [pl.BlockSpec(shape, lambda j, order: (0, 0))],
        [jax.ShapeDtypeStruct(shape, jnp.float32)],
        [],
        16,
    )
    return scores


def pieces(a):
    high = a.astype(jnp.bfloat16)
    rest = a - high.astype(jnp.float32)
    middle = rest.astype(jnp.bfloat16)
    low = (rest - middle.astype(jnp.float32)).astype(jnp.bfloat16)
    return high, middle, low


def update_body(scale, row, grads, mine, hessian, out, old, new, in_sems, out_sems):
    count, columns = grads.shape
    width = old.shape[2]
    parts = columns // width
    reads = [
        pltpu.make_async_copy(hessian.at[:, pl.ds(t * width, width)], old.at[t], in_sems.at[t]) for t in range(parts)
    ]
    writes = [
        pltpu.make_async_copy(new.at[t], out.at[:, pl.ds(t * width, width)], out_sems.at[t]) for t in range(parts)
    ]
    for read in reads:
        read.start()
    high, middle, low = pieces(mine[...])
    left = jnp.concatenate([high, high, middle, middle, high, low], axis=0).T
    for t in range(parts):
        high, middle, low = pieces(grads[:, t * width : (t + 1) * width])
        right = jnp.concatenate([high, middle, high, middle, low, high], axis=0)
        total = dot(left, right) * scale
        reads[t].wait()
        new[t] = old[t] + total
        writes[t].start()
    for write in writes:
        write.wait()


def update(row, grads, hessian):
    rows, columns = hessian.shape
    count = grads.shape[0]
    parts = 4
    width = columns // parts
    (updated,) = call(
        functools.partial(update_body, 1.0 / count),
        "hessian_update",
        row,
        (1,),
        (grads, grads, hessian),
        [
            fixed(grads.shape),
            pl.BlockSpec((count, rows), lambda j, row: (0, row[0]), pipeline_mode=pl.Buffered(1)),
            OUTSIDE,
        ],
        [ANYWHERE],
        [jax.ShapeDtypeStruct((rows, columns), jnp.float32)],
        [
            pltpu.VMEM((parts, rows, width), jnp.float32),
            pltpu.VMEM((parts, rows, width), jnp.float32),
            pltpu.SemaphoreType.DMA((parts,)),
            pltpu.SemaphoreType.DMA((parts,)),
        ],
        16,
    )
    return updated


def line_of_four(inputs, gate_pre, grad_out, w_down, proj_in, proj_out, early):
    send = functools.partial(lax.ppermute, axis_name="tensor")
    pairs = [(0, 1), (1, 0), (2, 3), (3, 2)]
    inner = [(1, 2), (2, 1)]
    outward = [(1, 0), (2, 3)]
    inward = [(0, 1), (3, 2)]
    across = [(0, 2), (3, 1)]
    tokens = grad_out.shape[0]
    z = lax.axis_index("tensor")
    low = z < 2
    middle = jnp.logical_and(z > 0, z < 3)
    where = jnp.stack(
        [z, z + 1 - 2 * (z % 2), jnp.where(low, 2, 1), jnp.where(low, 3, 0), middle.astype(z.dtype)]
    ).astype(jnp.int32)

    sizes = [256] * (tokens // 256 - 1) + [128, 128]
    starts = [sum(sizes[:n]) for n in range(len(sizes))]
    mid_inner = send(grad_out, perm=inner)
    pair = send(grad_out, perm=pairs)
    chunks = [grad_out[start : start + size] for start, size in zip(starts, sizes)]
    w, acc, in_part, *gates_t = own_block(
        where, after(grad_out, *chunks), gate_pre, inputs, proj_in.T, w_down, sizes
    )
    mid_outer = send(after(mid_inner, in_part), perm=outward)
    end_inner = [send(after(chunk, mid_inner, pair, in_part, *early), perm=across) for chunk in chunks]

    side = small_kernel(sum_body, "side", where, in_part, after(send(in_part, perm=inward), mid_inner))
    total = small_kernel(sum_body, "total", where, side, send(side, perm=inner))
    left_t = small_kernel(pick_body, "left", where, total, send(total, perm=outward))

    w, acc, first = add_block(where, 1, [pair], w, after(acc, side))
    w, acc, _ = add_block(where, 2, [mid_inner, mid_outer], w, acc)

    grads = [[] for _ in range(tokens // LEN)]
    arrived = [mid_outer, mid_outer]
    done = [first, first, first]
    for n, (start, size) in enumerate(zip(starts, sizes)):
        ready = [left_t, *end_inner] if n < 2 else []
        end_outer = send(after(end_inner[n], arrived[n], done[n], *ready), perm=outward)
        arrived.append(end_outer)
        s = start // LEN
        w, acc, total = last_block(
            where, end_inner[n], end_outer, start, w, acc, gates_t[n], proj_out.T, left_t, grads[s]
        )
        grads[s] = [total]
        done.append(total)
    grads = lax.optimization_barrier(tuple(total for total, in grads))
    return jnp.stack(grads).reshape(-1, PROJ * PROJ)


def any_line(inputs, gate_pre, grad_out, w_down, proj_in, proj_out, early):
    in_part = jnp.dot(inputs, proj_in, preferred_element_type=jnp.float32)
    in_proj = lax.psum(in_part, "tensor").reshape(-1, LEN, PROJ)
    gathered = lax.all_gather(grad_out, "tensor", axis=1, tiled=True)
    up_grad = (dot_nt(gathered, w_down) * silu(gate_pre.astype(jnp.float32))).astype(jnp.bfloat16)
    out_part = jnp.dot(up_grad, proj_out, preferred_element_type=jnp.float32).reshape(-1, LEN, PROJ)
    grads = jnp.einsum("sti,stj->sij", in_proj, out_part, precision=HIGHEST)
    return grads.reshape(-1, PROJ * PROJ)


def swap(a, axis, bit):
    return lax.ppermute(a, axis, [(i, i ^ bit) for i in range(lax.axis_size(axis))])


def bits(axis):
    return [1 << b for b in range(lax.axis_size(axis).bit_length() - 1)]


def xor_sum(a, axis):
    for bit in bits(axis):
        a = a + swap(a, axis, bit)
    return a


def xor_gather(a, axis):
    for bit in bits(axis):
        a = jnp.concatenate([a, swap(a, axis, bit)], axis=0)
    return a


def on_device(inputs, gate_pre, grad_out, w_down, proj_in, proj_out, hessian, queries):
    count = lax.axis_size("dp")
    parts = [queries] + [swap(queries, "dp", s) for s in range(1, count)]
    line = line_of_four if lax.axis_size("tensor") == 4 else any_line
    grads = line(inputs, gate_pre, grad_out, w_down, proj_in, proj_out, parts)
    grads = xor_sum(grads, "tensor")

    me = lax.axis_index("dp")
    order = lax.axis_index("tensor") * count + jnp.stack([me ^ s for s in range(count)])
    scores = score_parts(order.astype(jnp.int32), grads, parts)
    *first, last = bits("tensor")
    for bit in first:
        scores = scores + swap(scores, "tensor", bit)
    other_scores = swap(scores, "tensor", last)

    all_grads = after(xor_gather(grads, "dp"), scores)
    row_count = hessian.shape[0]
    at = lax.axis_index(("tensor", "dp"))
    if row_count % 128:
        mine = lax.dynamic_slice_in_dim(all_grads, at * row_count, row_count, 1)
        updated = hessian + jnp.dot(mine.T, all_grads, precision=HIGHEST) / all_grads.shape[0]
    else:
        updated = update(at.reshape(1).astype(jnp.int32), all_grads, hessian)
    updated, other_scores = lax.optimization_barrier((updated, other_scores))
    return (updated, scores + other_scores)


def solution(mesh):
    return jax.shard_map(
        on_device,
        mesh=mesh,
        in_specs=(
            P(("groups", "dp"), "tensor"),
            P(("groups", "dp"), "tensor"),
            P(("groups", "dp"), "tensor"),
            P("tensor", None),
            P("tensor", None),
            P("tensor", None),
            P(("groups", "tensor", "dp"), None),
            P("groups", ("tensor", "dp")),
        ),
        out_specs=(P(("groups", "tensor", "dp"), None), P(("groups", "dp"), None)),
        check_vma=False,
    )
```

time: 287 us -> 249 us (0.87)
  waiting for transfers between devices: 203 us -> 46.8 us
  Pallas kernels: 0 us -> 96.8 us
  matrix products: 60 us -> 0 us
  starting transfers between devices: 0.12 us -> 58.1 us
  local copies, waits for them, and re-layouts: 1.93 us -> 43.8 us
  between operations: 15.5 us -> 0.97 us
  blocking collectives: 5.43 us -> 0 us
    all_gather x2 -> x0, waiting for transfers between devices: 152 us -> none  [the longest x1 152 us: on_device(): lax.all_gather(grad_out, 'tensor', axis=1, tiled=True)]
    pallas_call x0 -> x13, Pallas kernels: none -> 96.8 us  [call(): pl.pallas_call(body, grid_spec=pltpu.PrefetchScalarGridSpec(num_scalar_pr...]
    dot_general x5 -> x0, matrix products: 60 us -> none  [the longest x1 44.1 us: on_device(): out_part = jnp.dot(up_grad, proj_out, preferred_element_type=jnp.float32)]
    ppermute x0 -> x25, starting transfers between devices: none -> 58.1 us  [the longest x5 18.9 us: line_of_four(): send(after(chunk, mid_inner, pair, in_part, *early), perm=across)]
    psum x1 -> x0, waiting for transfers between devices: 50.7 us -> none  [on_device(): in_proj, out_proj = lax.psum((in_part, out_part), 'tensor')]
    ppermute x0 -> x25, waiting for transfers between devices: none -> 46.8 us  [the longest x9 14.7 us: swap(): lax.ppermute(a, axis, [(i, i ^ bit) for i in range(lax.axis_size(axis))])]
    unnamed x4 -> x20, local copies, waits for them, and re-layouts: 0.99 us -> 39.7 us
    all_gather x1 -> x0, blocking collectives: 5.43 us -> none  [on_device(): all_grads = lax.all_gather(local_grads, 'dp', axis=0, tiled=True)]
  transfers between devices with their start and end apart: 3 -> 25, of which waited for: 2 -> 9; matrix products, arithmetic and copies ran while one was open for 4% -> 1% of each run, Pallas kernels for 0% -> 36%
where the time goes in v4:
time: 249 us; the launch traced here: 247 us
  Pallas kernels  96.8 us (39%)
  starting transfers between devices  58.1 us (23%)
  waiting for transfers between devices  46.8 us (19%)
  local copies, waits for them, and re-layouts  43.8 us (18%)
    pallas_call x13, Pallas kernels, call(): pl.pallas_call(body, grid_spec=pltpu.PrefetchScalarGridSpec(num_scalar_pr...  96.8 us
    unnamed x20, local copies, waits for them, and re-layouts  39.7 us
    ppermute x5, starting transfers between devices, line_of_four(): send(after(chunk, mid_inner, pair, in_part, *early), perm=across)  18.9 us
    ppermute x9, waiting for transfers between devices, swap(): lax.ppermute(a, axis, [(i, i ^ bit) for i in range(lax.axis_size(axis))])  14.7 us
    ppermute x1, waiting for transfers between devices, line_of_four(): send(total, perm=outward)  14.7 us
    ppermute x5, waiting for transfers between devices, line_of_four(): send(after(end_inner[n], arrived[n], done[n], *ready), perm=outward)  14.2 us
    ppermute x9, starting transfers between devices, swap(): lax.ppermute(a, axis, [(i, i ^ bit) for i in range(lax.axis_size(axis))])  11.9 us
    ppermute x1, starting transfers between devices, line_of_four(): send(in_part, perm=inward)  10.8 us
  transfers between devices with their start and end apart: 25, of which 9 were waited for; matrix products, arithmetic and copies ran while one was open for 1% of the time, Pallas kernels for 36%

profile of v4, /device:TPU:0, one launch (start us, length us, event | category | flops | bytes accessed | tf_op | source)
XLA Modules:
  0.0 247.4 jit_solution(3735614661283684491)
XLA Ops:
  0.6 2.0 collective-permute-start
  2.6 4.6 %collective-permute-start.1 = (bf16[1024,1024]{1,0:T(8,128)(2,1)}, bf16[1024,1024]{1,0:T(8,128)(2,1)}, u32[]{:S(2)}, u32[]{:S(2)}) collective-permute-start(bf16[1024,1024]{1,0:T(8,128)(2,1)} %own), channel_id=1, source_target_pairs={{0,4},{4,0},{8,12},{12,8},{1,5},{5,1},{9,13},{13,9},{2,6},{6,2},{1... | collective-permute-start | bytes 6291464 | tf_op jit(solution)/shard_map/ppermute | solution.py:356
  10.4 25.5 %own_block.1 = (bf16[3584,4096]{1,0:T(8,128)(2,1)S(1)}, f32[3584,1024]{1,0:T(8,128)S(1)}, f32[64,1024]{1,0:T(8,128)}, bf16[3584,256]{1,0:T(8,128)(2,1)}, bf16[35...) custom-call(s32[5]{0:T(128)} %stack.51.where, ...), custom_call_target="tpu_custom_call" | custom-call | flops 1000 | bytes 1000 | tf_op jit(solution)/shard_map/own_block/pallas_call | solution.py:40
  36.0 9.7 %copy-done = bf16[3584,4096]{1,0:T(8,128)(2,1)} copy-done((bf16[3584,4096]{1,0:T(8,128)(2,1)}, bf16[3584,4096]{1,0:T(8,128)(2,1)S(1)}, u32[]{:S(2)}) %copy-start) | copy-done | bytes 29360152
  47.0 10.8 %collective-permute-start.7 = (f32[64,1024]{1,0:T(8,128)}, f32[64,1024]{1,0:T(8,128)S(1)}, u32[]{:S(2)}, u32[]{:S(2)}) collective-permute-start(f32[64,1024]{1,0:T(8,128)} %get-tuple-element.48.a), channel_id=1, source_target_pairs={{0,4},{12,8},{1,5},{13,9},{2,6},{14,10},{3,7},{15,11},{16,20},{28,... | collective-permute-start | bytes 786440 | tf_op jit(solution)/shard_map/ppermute | solution.py:364
  59.4 3.3 %collective-permute-done.7.b = f32[64,1024]{1,0:T(8,128)S(1)} collective-permute-done((f32[64,1024]{1,0:T(8,128)}, f32[64,1024]{1,0:T(8,128)S(1)}, u32[]{:S(2)}, u32[]{:S(2)}) %collective-permute-start.7) | collective-permute-done | bytes 262176 | tf_op jit(solution)/shard_map/ppermute | solution.py:364
  64.3 2.1 collective-permute-done.4.rest_3_
  67.1 5.0 %collective-permute-done.3.rest_2_ = f32[256,256]{1,0:T(8,128)S(1)} collective-permute-done((f32[256,256]{1,0:T(8,128)S(1)}, f32[256,256]{1,0:T(8,128)S(1)}, u32[]{:S(2)}, u32[]{:S(2)}) %collective-permute-start.3) | collective-permute-done | bytes 262176 | tf_op jit(solution)/shard_map/ppermute | solution.py:399
  72.1 2.3 collective-permute-start.12
  76.3 11.5 %collective-permute-start.5 = (bf16[256,1024]{1,0:T(8,128)(2,1)S(1)}, bf16[256,1024]{1,0:T(8,128)(2,1)S(1)}, u32[]{:S(2)}, u32[]{:S(2)}) collective-permute-start(bf16[256,1024]{1,0:T(8,128)(2,1)S(1)} %get-tuple-element.49), channel_id=1, source_target_pairs={{0,8},{12,4},{1,9},{13,5},{2,10},{14,6},{3,11},{15,7},{16,24},{28,... | collective-permute-start | bytes 1572872 | tf_op jit(solution)/shard_map/ppermute | solution.py:362
  90.4 14.7 %collective-permute-done.9.b = f32[64,1024]{1,0:T(8,128)S(1)} collective-permute-done((f32[64,1024]{1,0:T(8,128)S(1)}, f32[64,1024]{1,0:T(8,128)S(1)}, u32[]{:S(2)}, u32[]{:S(2)}) %collective-permute-start.9) | collective-permute-done | bytes 262176 | tf_op jit(solution)/shard_map/ppermute | solution.py:366
  105.1 2.5 collective-permute-start.13
  107.6 9.3 %copy-done.1 = bf16[3584,4096]{1,0:T(8,128)(2,1)S(1)} copy-done((bf16[3584,4096]{1,0:T(8,128)(2,1)S(1)}, bf16[3584,4096]{1,0:T(8,128)(2,1)}, u32[]{:S(2)}) %copy-start.1) | copy-done | bytes 29360152
  116.9 12.9 %add_block_1.1 = (bf16[3584,4096]{1,0:T(8,128)(2,1)S(1)}, f32[3584,1024]{1,0:T(8,128)S(1)}, f32[8,128]{1,0:T(8,128)}) custom-call(s32[5]{0:T(128)} %stack.51.where, bf16[1024,1024]{1,0:T(8,128)(2,1)} %collective-permute-done.1.refs_0_, bf16[3584,4096]{1,0:T(8,128)(2,1)S(1)} %copy-done.1, ...), custom_call_target="tpu_custom_call", output_to_operand_aliasing={{0}: (2, {}), {1}: (3, {})} | custom-call | flops 1000 | bytes 1000 | tf_op jit(solution)/shard_map/add_block_1/pallas_call | solution.py:40
  129.9 9.7 %copy-done.2 = bf16[3584,4096]{1,0:T(8,128)(2,1)} copy-done((bf16[3584,4096]{1,0:T(8,128)(2,1)}, bf16[3584,4096]{1,0:T(8,128)(2,1)S(1)}, u32[]{:S(2)}) %copy-start.2) | copy-done | bytes 29360152
  143.5 14.2 %collective-permute-done.15.outer = bf16[256,1024]{1,0:T(8,128)(2,1)S(1)} collective-permute-done((bf16[256,1024]{1,0:T(8,128)(2,1)S(1)}, bf16[256,1024]{1,0:T(8,128)(2,1)S(1)}, u32[]{:S(2)}, u32[]{:S(2)}) %collective-permute-start.15) | collective-permute-done | bytes 524320 | tf_op jit(solution)/shard_map/ppermute | solution.py:376
  158.9 9.3 %copy-done.3 = bf16[3584,4096]{1,0:T(8,128)(2,1)S(1)} copy-done((bf16[3584,4096]{1,0:T(8,128)(2,1)S(1)}, bf16[3584,4096]{1,0:T(8,128)(2,1)}, u32[]{:S(2)}) %copy-start.3) | copy-done | bytes 29360152
  168.3 13.5 %add_block_2.1 = (bf16[3584,4096]{1,0:T(8,128)(2,1)S(1)}, f32[3584,1024]{1,0:T(8,128)S(1)}, f32[8,128]{1,0:T(8,128)}) custom-call(s32[5]{0:T(128)} %stack.51.where, bf16[1024,1024]{1,0:T(8,128)(2,1)} %collective-permute-done.refs_0_, bf16[1024,1024]{1,0:T(8,128)(2,1)} %collective-permute-done.6.refs_1_, ...), custom_call_target="tpu_custom_call", output_to_operand_aliasing={{0}: (3, {}), {1}: (4, {})} | custom-call | flops 1000 | bytes 1000 | tf_op jit(solution)/shard_map/add_block_2/pallas_call | solution.py:40
  181.7 8.0 %last_block.5 = (bf16[3584,4096]{1,0:T(8,128)(2,1)S(1)}, f32[3584,1024]{1,0:T(8,128)S(1)}, f32[64,64]{1,0:T(8,128)}) custom-call(s32[5]{0:T(128)} %stack.51.where, bf16[256,1024]{1,0:T(8,128)(2,1)S(1)} %collective-permute-done.10.inner, bf16[256,1024]{1,0:T(8,128)(2,1)S(1)} %collective-permute-done.15.outer, ...), custom_call_target="tpu_custom_call", output_to_operand_aliasing={{0}: (3, {}), {1}: (4, {})} | custom-call | flops 1000 | bytes 1000 | tf_op jit(solution)/shard_map/last_block/pallas_call | solution.py:40
  191.0 8.0 %last_block.6 = (bf16[3584,4096]{1,0:T(8,128)(2,1)S(1)}, f32[3584,1024]{1,0:T(8,128)S(1)}, f32[64,64]{1,0:T(8,128)}) custom-call(s32[5]{0:T(128)} %stack.51.where, bf16[256,1024]{1,0:T(8,128)(2,1)S(1)} %collective-permute-done.5.inner, bf16[256,1024]{1,0:T(8,128)(2,1)S(1)} %collective-permute-done.14.outer, ...), custom_call_target="tpu_custom_call", output_to_operand_aliasing={{0}: (3, {}), {1}: (4, {})} | custom-call | flops 1000 | bytes 1000 | tf_op jit(solution)/shard_map/last_block/pallas_call | solution.py:40
  200.5 8.0 %last_block.7 = (bf16[3584,4096]{1,0:T(8,128)(2,1)S(1)}, f32[3584,1024]{1,0:T(8,128)S(1)}, f32[64,64]{1,0:T(8,128)}) custom-call(s32[5]{0:T(128)} %stack.51.where, bf16[256,1024]{1,0:T(8,128)(2,1)S(1)} %collective-permute-done.11.inner, bf16[256,1024]{1,0:T(8,128)(2,1)S(1)} %collective-permute-done.16.outer, ...), custom_call_target="tpu_custom_call", output_to_operand_aliasing={{0}: (3, {}), {1}: (4, {})} | custom-call | flops 1000 | bytes 1000 | tf_op jit(solution)/shard_map/last_block/pallas_call | solution.py:40
  208.4 7.0 %last_block.8 = (bf16[3584,4096]{1,0:T(8,128)(2,1)S(1)}, f32[3584,1024]{1,0:T(8,128)S(1)}, f32[64,64]{1,0:T(8,128)}) custom-call(s32[5]{0:T(128)} %stack.51.where, bf16[128,1024]{1,0:T(8,128)(2,1)S(1)} %collective-permute-done.12.inner, bf16[128,1024]{1,0:T(8,128)(2,1)S(1)} %collective-permute-done.18.outer, ...), custom_call_target="tpu_custom_call", output_to_operand_aliasing={{0}: (3, {}), {1}: (4, {})} | custom-call | flops 1000 | bytes 1000 | tf_op jit(solution)/shard_map/last_block/pallas_call | solution.py:40
  215.5 7.1 %last_block.9 = (bf16[3584,4096]{1,0:T(8,128)(2,1)S(1)}, f32[3584,1024]{1,0:T(8,128)S(1)}, f32[64,64]{1,0:T(8,128)}) custom-call(s32[5]{0:T(128)} %stack.51.where, bf16[128,1024]{1,0:T(8,128)(2,1)S(1)} %collective-permute-done.13.inner, bf16[128,1024]{1,0:T(8,128)(2,1)S(1)} %collective-permute-done.17.outer, ...), custom_call_target="tpu_custom_call", output_to_operand_aliasing={{0}: (3, {}), {1}: (4, {})} | custom-call | flops 1000 | bytes 1000 | tf_op jit(solution)/shard_map/last_block/pallas_call | solution.py:40
  223.6 2.8 %collective-permute-start.19 = (f32[2,4096]{1,0:T(2,128)S(1)}, f32[2,4096]{1,0:T(2,128)S(1)}, u32[]{:S(2)}, u32[]{:S(2)}) collective-permute-start(f32[2,4096]{1,0:T(2,128)S(1)} %pad_maximum_fusion.2), channel_id=1, source_target_pairs={{0,4},{4,0},{8,12},{12,8},{1,5},{5,1},{9,13},{13,9},{2,6},{6,2},{1... | collective-permute-start | bytes 98312 | tf_op jit(solution)/shard_map/ppermute | solution.py:399
  226.3 1.9 collective-permute-done.19
  228.3 2.0 collective-permute-start.20
  230.3 2.9 %collective-permute-done.20 = f32[2,4096]{1,0:T(2,128)S(1)} collective-permute-done((f32[2,4096]{1,0:T(2,128)S(1)}, f32[2,4096]{1,0:T(2,128)S(1)}, u32[]{:S(2)}, u32[]{:S(2)}) %collective-permute-start.20) | collective-permute-done | bytes 32800 | tf_op jit(solution)/shard_map/ppermute | solution.py:399
  234.5 1.6 collective-permute-start.22
  237.6 2.0 collective-permute-start.23
  239.6 1.6 collective-permute-done.23
  241.2 1.9 collective-permute-start.24
  243.2 3.6 %hessian_update.1 = f32[256,4096]{1,0:T(8,128)} custom-call(s32[1]{0:T(128)} %bitcast.row, f32[8,4096]{1,0:T(8,128)S(1)} %pad_maximum_fusion.grads.mine, f32[8,4096]{1,0:T(8,128)S(1)} %pad_maximum_fusion.grads.mine, f32[256,4096]{1,0:T(8,128)} %hessian.1), custom_call_target="tpu_custom_call" | custom-call | flops 1000 | bytes 1000 | tf_op jit(solution)/shard_map/hessian_update/pallas_call | solution.py:40
  (64 shorter events, 25.3 us)
Async XLA Ops:
  0.6 45.0 %collective-permute-start = (bf16[1024,1024]{1,0:T(8,128)(2,1)}, bf16[1024,1024]{1,0:T(8,128)(2,1)}, u32[]{:S(2)}, u32[]{:S(2)}) collective-permute-start(bf16[1024,1024]{1,0:T(8,128)(2,1)} %own), channel_id=1, source_target_pairs={{4,8},{8,4},{5,9},{9,5},{6,10},{10,6},{7,11},{11,7},{20,24},{24,20... | collective-permute-start | bytes 6291464 | tf_op jit(solution)/shard_map/ppermute | solution.py:355
  2.6 69.5 %collective-permute-start.1 = (bf16[1024,1024]{1,0:T(8,128)(2,1)}, bf16[1024,1024]{1,0:T(8,128)(2,1)}, u32[]{:S(2)}, u32[]{:S(2)}) collective-permute-start(bf16[1024,1024]{1,0:T(8,128)(2,1)} %own), channel_id=1, source_target_pairs={{0,4},{4,0},{8,12},{12,8},{1,5},{5,1},{9,13},{13,9},{2,6},{6,2},{1... | collective-permute-start | bytes 6291464 | tf_op jit(solution)/shard_map/ppermute | solution.py:356
  10.4 47.4 %copy-start.5 = (f32[256,256]{1,0:T(8,128)S(1)}, f32[256,256]{1,0:T(8,128)}, u32[]{:S(2)}) copy-start(f32[256,256]{1,0:T(8,128)} %rest_0_.1) | copy-start | bytes 786436
  10.4 52.3 %copy-start.7 = (s32[5]{0:T(128)S(1)}, s32[5]{0:T(128)}, u32[]{:S(2)}) copy-start(s32[5]{0:T(128)} %stack.51.where) | copy-start | bytes 64
  36.0 9.7 %copy-start = (bf16[3584,4096]{1,0:T(8,128)(2,1)}, bf16[3584,4096]{1,0:T(8,128)(2,1)S(1)}, u32[]{:S(2)}) copy-start(bf16[3584,4096]{1,0:T(8,128)(2,1)S(1)} %get-tuple-element.51.refs_1_) | copy-start | bytes 88080384
  45.7 95.2 %collective-permute-start.6 = (bf16[1024,1024]{1,0:T(8,128)(2,1)}, bf16[1024,1024]{1,0:T(8,128)(2,1)}, u32[]{:S(2)}, u32[]{:S(2)}) collective-permute-start(bf16[1024,1024]{1,0:T(8,128)(2,1)} %collective-permute-done.refs_0_), channel_id=1, source_target_pairs={{4,0},{8,12},{5,1},{9,13},{6,2},{10,14},{7,3},{11,15},{20,16},{24,... | collective-permute-start | bytes 6291464 | tf_op jit(solution)/shard_map/ppermute | solution.py:361
  47.0 15.8 %collective-permute-start.7 = (f32[64,1024]{1,0:T(8,128)}, f32[64,1024]{1,0:T(8,128)S(1)}, u32[]{:S(2)}, u32[]{:S(2)}) collective-permute-start(f32[64,1024]{1,0:T(8,128)} %get-tuple-element.48.a), channel_id=1, source_target_pairs={{0,4},{12,8},{1,5},{13,9},{2,6},{14,10},{3,7},{15,11},{16,20},{28,... | collective-permute-start | bytes 786440 | tf_op jit(solution)/shard_map/ppermute | solution.py:364
  57.8 8.6 %collective-permute-start.4 = (f32[256,256]{1,0:T(8,128)S(1)}, f32[256,256]{1,0:T(8,128)S(1)}, u32[]{:S(2)}, u32[]{:S(2)}) collective-permute-start(f32[256,256]{1,0:T(8,128)S(1)} %copy-done.5), channel_id=1, source_target_pairs={{0,3},{1,2},{2,1},{3,0},{4,7},{5,6},{6,5},{7,4},{8,11},{9,10},{10,... | collective-permute-start | bytes 786440 | tf_op jit(solution)/shard_map/ppermute | solution.py:399
  57.9 14.2 %collective-permute-start.3 = (f32[256,256]{1,0:T(8,128)S(1)}, f32[256,256]{1,0:T(8,128)S(1)}, u32[]{:S(2)}, u32[]{:S(2)}) collective-permute-start(f32[256,256]{1,0:T(8,128)S(1)} %copy-done.5), channel_id=1, source_target_pairs={{0,2},{1,3},{2,0},{3,1},{4,6},{5,7},{6,4},{7,5},{8,10},{9,11},{10,... | collective-permute-start | bytes 786440 | tf_op jit(solution)/shard_map/ppermute | solution.py:399
  62.8 9.3 %collective-permute-start.2 = (f32[256,256]{1,0:T(8,128)S(1)}, f32[256,256]{1,0:T(8,128)S(1)}, u32[]{:S(2)}, u32[]{:S(2)}) collective-permute-start(f32[256,256]{1,0:T(8,128)S(1)} %copy-done.5), channel_id=1, source_target_pairs={{0,1},{1,0},{2,3},{3,2},{4,5},{5,4},{6,7},{7,6},{8,9},{9,8},{10,11... | collective-permute-start | bytes 786440 | tf_op jit(solution)/shard_map/ppermute | solution.py:399
  66.4 8.0 %collective-permute-start.8 = (f32[64,1024]{1,0:T(8,128)S(1)}, f32[64,1024]{1,0:T(8,128)S(1)}, u32[]{:S(2)}, u32[]{:S(2)}) collective-permute-start(f32[64,1024]{1,0:T(8,128)S(1)} %side.1.a), channel_id=1, source_target_pairs={{4,8},{8,4},{5,9},{9,5},{6,10},{10,6},{7,11},{11,7},{20,24},{24,20... | collective-permute-start | bytes 786440 | tf_op jit(solution)/shard_map/ppermute | solution.py:365
  72.1 17.0 %collective-permute-start.12 = (bf16[128,1024]{1,0:T(8,128)(2,1)S(1)}, bf16[128,1024]{1,0:T(8,128)(2,1)S(1)}, u32[]{:S(2)}, u32[]{:S(2)}) collective-permute-start(bf16[128,1024]{1,0:T(8,128)(2,1)S(1)} %get-tuple-element.58), channel_id=1, source_target_pairs={{0,8},{12,4},{1,9},{13,5},{2,10},{14,6},{3,11},{15,7},{16,24},{28,... | collective-permute-start | bytes 786440 | tf_op jit(solution)/shard_map/ppermute | solution.py:362
  75.0 30.1 %collective-permute-start.9 = (f32[64,1024]{1,0:T(8,128)S(1)}, f32[64,1024]{1,0:T(8,128)S(1)}, u32[]{:S(2)}, u32[]{:S(2)}) collective-permute-start(f32[64,1024]{1,0:T(8,128)S(1)} %total.1.a), channel_id=1, source_target_pairs={{4,0},{8,12},{5,1},{9,13},{6,2},{10,14},{7,3},{11,15},{20,16},{24,... | collective-permute-start | bytes 786440 | tf_op jit(solution)/shard_map/ppermute | solution.py:366
  76.3 64.6 %collective-permute-start.5 = (bf16[256,1024]{1,0:T(8,128)(2,1)S(1)}, bf16[256,1024]{1,0:T(8,128)(2,1)S(1)}, u32[]{:S(2)}, u32[]{:S(2)}) collective-permute-start(bf16[256,1024]{1,0:T(8,128)(2,1)S(1)} %get-tuple-element.49), channel_id=1, source_target_pairs={{0,8},{12,4},{1,9},{13,5},{2,10},{14,6},{3,11},{15,7},{16,24},{28,... | collective-permute-start | bytes 1572872 | tf_op jit(solution)/shard_map/ppermute | solution.py:362
  87.8 53.1 %collective-permute-start.10 = (bf16[256,1024]{1,0:T(8,128)(2,1)S(1)}, bf16[256,1024]{1,0:T(8,128)(2,1)S(1)}, u32[]{:S(2)}, u32[]{:S(2)}) collective-permute-start(bf16[256,1024]{1,0:T(8,128)(2,1)S(1)} %get-tuple-element.56), channel_id=1, source_target_pairs={{0,8},{12,4},{1,9},{13,5},{2,10},{14,6},{3,11},{15,7},{16,24},{28,... | collective-permute-start | bytes 1572872 | tf_op jit(solution)/shard_map/ppermute | solution.py:362
  89.1 51.8 %collective-permute-start.11 = (bf16[256,1024]{1,0:T(8,128)(2,1)S(1)}, bf16[256,1024]{1,0:T(8,128)(2,1)S(1)}, u32[]{:S(2)}, u32[]{:S(2)}) collective-permute-start(bf16[256,1024]{1,0:T(8,128)(2,1)S(1)} %get-tuple-element.57), channel_id=1, source_target_pairs={{0,8},{12,4},{1,9},{13,5},{2,10},{14,6},{3,11},{15,7},{16,24},{28,... | collective-permute-start | bytes 1572872 | tf_op jit(solution)/shard_map/ppermute | solution.py:362
  105.1 35.8 %collective-permute-start.13 = (bf16[128,1024]{1,0:T(8,128)(2,1)S(1)}, bf16[128,1024]{1,0:T(8,128)(2,1)S(1)}, u32[]{:S(2)}, u32[]{:S(2)}) collective-permute-start(bf16[128,1024]{1,0:T(8,128)(2,1)S(1)} %get-tuple-element.59), channel_id=1, source_target_pairs={{0,8},{12,4},{1,9},{13,5},{2,10},{14,6},{3,11},{15,7},{16,24},{28,... | collective-permute-start | bytes 786440 | tf_op jit(solution)/shard_map/ppermute | solution.py:362
  107.6 9.4 %copy-start.1 = (bf16[3584,4096]{1,0:T(8,128)(2,1)S(1)}, bf16[3584,4096]{1,0:T(8,128)(2,1)}, u32[]{:S(2)}) copy-start(bf16[3584,4096]{1,0:T(8,128)(2,1)} %copy-done) | copy-start | bytes 88080384
  116.9 22.6 %copy-start.8 = (s32[5]{0:T(128)S(1)}, s32[5]{0:T(128)}, u32[]{:S(2)}) copy-start(s32[5]{0:T(128)} %stack.51.where) | copy-start | bytes 64
  129.9 9.7 %copy-start.2 = (bf16[3584,4096]{1,0:T(8,128)(2,1)}, bf16[3584,4096]{1,0:T(8,128)(2,1)S(1)}, u32[]{:S(2)}) copy-start(bf16[3584,4096]{1,0:T(8,128)(2,1)S(1)} %get-tuple-element.62.refs_2_) | copy-start | bytes 88080384
  140.9 16.8 %collective-permute-start.15 = (bf16[256,1024]{1,0:T(8,128)(2,1)S(1)}, bf16[256,1024]{1,0:T(8,128)(2,1)S(1)}, u32[]{:S(2)}, u32[]{:S(2)}) collective-permute-start(bf16[256,1024]{1,0:T(8,128)(2,1)S(1)} %collective-permute-done.10.inner), channel_id=1, source_target_pairs={{4,0},{8,12},{5,1},{9,13},{6,2},{10,14},{7,3},{11,15},{20,16},{24,... | collective-permute-start | bytes 1572872 | tf_op jit(solution)/shard_map/ppermute | solution.py:376
  142.2 47.5 %collective-permute-start.14 = (bf16[256,1024]{1,0:T(8,128)(2,1)S(1)}, bf16[256,1024]{1,0:T(8,128)(2,1)S(1)}, u32[]{:S(2)}, u32[]{:S(2)}) collective-permute-start(bf16[256,1024]{1,0:T(8,128)(2,1)S(1)} %collective-permute-done.5.inner), channel_id=1, source_target_pairs={{4,0},{8,12},{5,1},{9,13},{6,2},{10,14},{7,3},{11,15},{20,16},{24,... | collective-permute-start | bytes 1572872 | tf_op jit(solution)/shard_map/ppermute | solution.py:376
  157.6 41.4 %collective-permute-start.16 = (bf16[256,1024]{1,0:T(8,128)(2,1)S(1)}, bf16[256,1024]{1,0:T(8,128)(2,1)S(1)}, u32[]{:S(2)}, u32[]{:S(2)}) collective-permute-start(bf16[256,1024]{1,0:T(8,128)(2,1)S(1)} %collective-permute-done.11.inner), channel_id=1, source_target_pairs={{4,0},{8,12},{5,1},{9,13},{6,2},{10,14},{7,3},{11,15},{20,16},{24,... | collective-permute-start | bytes 1572872 | tf_op jit(solution)/shard_map/ppermute | solution.py:376
  158.9 9.4 %copy-start.3 = (bf16[3584,4096]{1,0:T(8,128)(2,1)S(1)}, bf16[3584,4096]{1,0:T(8,128)(2,1)}, u32[]{:S(2)}) copy-start(bf16[3584,4096]{1,0:T(8,128)(2,1)} %copy-done.2) | copy-start | bytes 88080384
  189.7 18.7 %collective-permute-start.18 = (bf16[128,1024]{1,0:T(8,128)(2,1)S(1)}, bf16[128,1024]{1,0:T(8,128)(2,1)S(1)}, u32[]{:S(2)}, u32[]{:S(2)}) collective-permute-start(bf16[128,1024]{1,0:T(8,128)(2,1)S(1)} %collective-permute-done.12.inner), channel_id=1, source_target_pairs={{4,0},{8,12},{5,1},{9,13},{6,2},{10,14},{7,3},{11,15},{20,16},{24,... | collective-permute-start | bytes 786440 | tf_op jit(solution)/shard_map/ppermute | solution.py:376
  199.0 16.5 %collective-permute-start.17 = (bf16[128,1024]{1,0:T(8,128)(2,1)S(1)}, bf16[128,1024]{1,0:T(8,128)(2,1)S(1)}, u32[]{:S(2)}, u32[]{:S(2)}) collective-permute-start(bf16[128,1024]{1,0:T(8,128)(2,1)S(1)} %collective-permute-done.13.inner), channel_id=1, source_target_pairs={{4,0},{8,12},{5,1},{9,13},{6,2},{10,14},{7,3},{11,15},{20,16},{24,... | collective-permute-start | bytes 786440 | tf_op jit(solution)/shard_map/ppermute | solution.py:376
  223.6 4.7 %collective-permute-start.19 = (f32[2,4096]{1,0:T(2,128)S(1)}, f32[2,4096]{1,0:T(2,128)S(1)}, u32[]{:S(2)}, u32[]{:S(2)}) collective-permute-start(f32[2,4096]{1,0:T(2,128)S(1)} %pad_maximum_fusion.2), channel_id=1, source_target_pairs={{0,4},{4,0},{8,12},{12,8},{1,5},{5,1},{9,13},{13,9},{2,6},{6,2},{1... | collective-permute-start | bytes 98312 | tf_op jit(solution)/shard_map/ppermute | solution.py:399
  228.3 4.9 %collective-permute-start.20 = (f32[2,4096]{1,0:T(2,128)S(1)}, f32[2,4096]{1,0:T(2,128)S(1)}, u32[]{:S(2)}, u32[]{:S(2)}) collective-permute-start(f32[2,4096]{1,0:T(2,128)S(1)} %fusion), channel_id=1, source_target_pairs={{0,8},{4,12},{8,0},{12,4},{1,9},{5,13},{9,1},{13,5},{2,10},{6,14},... | collective-permute-start | bytes 98312 | tf_op jit(solution)/shard_map/ppermute | solution.py:399
  233.2 1.3 collective-permute-start.21
  234.5 8.6 %collective-permute-start.22 = (f32[4,4096]{1,0:T(4,128)S(1)}, f32[4,4096]{1,0:T(4,128)S(1)}, u32[]{:S(2)}, u32[]{:S(2)}) collective-permute-start(f32[4,4096]{1,0:T(4,128)S(1)} %pad_maximum_fusion.1), channel_id=1, source_target_pairs={{0,2},{1,3},{2,0},{3,1},{4,6},{5,7},{6,4},{7,5},{8,10},{9,11},{10,... | collective-permute-start | bytes 196616 | tf_op jit(solution)/shard_map/ppermute | solution.py:399
  237.6 3.6 %collective-permute-start.23 = (f32[2,256]{1,0:T(2,128)S(1)}, f32[2,256]{1,0:T(2,128)S(1)}, u32[]{:S(2)}, u32[]{:S(2)}) collective-permute-start(f32[2,256]{1,0:T(2,128)S(1)} %scores.1), channel_id=1, source_target_pairs={{0,4},{4,0},{8,12},{12,8},{1,5},{5,1},{9,13},{13,9},{2,6},{6,2},{1... | collective-permute-start | bytes 6152 | tf_op jit(solution)/shard_map/ppermute | solution.py:399
  241.2 5.6 %collective-permute-start.24 = (f32[2,256]{1,0:T(2,128)S(1)}, f32[2,256]{1,0:T(2,128)S(1)}, u32[]{:S(2)}, u32[]{:S(2)}) collective-permute-start(f32[2,256]{1,0:T(2,128)S(1)} %add.35), channel_id=1, source_target_pairs={{0,8},{4,12},{8,0},{12,4},{1,9},{5,13},{9,1},{13,5},{2,10},{6,14},... | collective-permute-start | bytes 6152 | tf_op jit(solution)/shard_map/ppermute | solution.py:399
  (3 other events, 8.8 us)

commit v5 on v4

--- a/solution.py
+++ b/solution.py
@@ -12,7 +12,7 @@
 HIGHEST = lax.Precision.HIGHEST
 NT = (((1,), (1,)), ((), ()))
 TILE = 512
-OWN_TILE = 256
+LIMIT = 16
 ANYWHERE = pl.BlockSpec(memory_space=pl.ANY)
 INSIDE = pl.BlockSpec(memory_space=pltpu.VMEM)
 OUTSIDE = pl.BlockSpec(memory_space=pltpu.HBM)
@@ -66,150 +66,150 @@
     return pl.ds(pl.multiple_of(where[i] * width, width), width)
 
 
-def own_body(where, own, gate, inputs, pi_t, w_far, w, acc, in_t, *rest):
-    *gates_t, own_t, sems = rest
+def own_body(where, own, inputs, pi_t, w, w_last, acc, kept, in_t):
     step = pl.program_id(0)
-    reads = [
-        pltpu.make_async_copy(w_far.at[rows], w.at[rows], sems.at[t])
-        for t in range(sems.shape[0])
-        for rows in [pl.ds(t * OWN_TILE, OWN_TILE)]
-    ]
 
     @pl.when(step == 0)
     def _():
-        for read in reads:
-            read.start()
         in_t[...] = dot_nt(pi_t[...], inputs[...])
-        own_t[...] = own[...].T
-
-    start = 0
-    for gate_t in gates_t:
-        size = gate_t.shape[1]
-        gate_t[...] = gate[start : start + size, :].T
-        start += size
-    rows = tile_rows(step, OWN_TILE)
-    pltpu.make_async_copy(w_far.at[rows], w.at[rows], sems.at[step]).wait()
-    acc[rows, :] = dot(w[rows, columns(where, 0, own.shape[1])], own_t[...])
-
-
-def own_block(where, own, gate, inputs, pi_t, w, sizes):
-    tokens, hidden = gate.shape
-    feats = own.shape[1]
+
+    here = tile_rows(step)
+    kept[here, :] = w_last[...]
+    acc[:, here] = dot_nt(own[...], w[...])
+
+
+def own_block(where, own, inputs, pi_t, w):
+    tokens, feats = own.shape
+    hidden = w.shape[0]
     return call(
         own_body,
         "own_block",
         where,
-        (hidden // OWN_TILE,),
-        (own, gate, inputs, pi_t, w),
+        (hidden // TILE,),
+        (own, inputs, pi_t, w, w),
         [
             fixed(own.shape),
-            pl.BlockSpec((tokens, OWN_TILE), lambda j, where: (0, j)),
             fixed(inputs.shape),
             fixed(pi_t.shape),
-            OUTSIDE,
-        ],
-        [INSIDE, INSIDE, pl.BlockSpec((PROJ, tokens), lambda j, where: (0, 0))]
-        + [pl.BlockSpec((OWN_TILE, size), lambda j, where: (j, 0)) for size in sizes],
-        [
-            pltpu.VMEM(w.shape, w.dtype),
-            pltpu.VMEM((hidden, tokens), jnp.float32),
+            pl.BlockSpec((TILE, feats), lambda j, where: (j, where[0])),
+            pl.BlockSpec((TILE, feats), lambda j, where: (j, where[3])),
+        ],
+        [INSIDE, INSIDE, pl.BlockSpec((PROJ, tokens), lambda j, where: (0, 0))],
+        [
+            pltpu.VMEM((tokens, hidden), jnp.float32),
+            pltpu.VMEM((hidden, feats), w.dtype),
             jax.ShapeDtypeStruct((PROJ, tokens), jnp.float32),
-        ]
-        + [jax.ShapeDtypeStruct((hidden, size), gate.dtype) for size in sizes],
-        [pltpu.VMEM((feats, tokens), own.dtype), pltpu.SemaphoreType.DMA((hidden // OWN_TILE,))],
-        16,
-    )
-
-
-def add_body(which, where, *refs):
-    *blocks, w, old, _, acc, token, block_t = refs
-    token[...] = jnp.zeros_like(token)
-    if len(blocks) == 1:
-        block_t[...] = blocks[0][...].T
-    else:
-        block_t[...] = select_transposed(where, *blocks)
-
-    @pl.loop(0, acc.shape[0] // TILE)
-    def _(t):
-        rows = tile_rows(t)
-        acc[rows, :] = old[rows, :] + dot(w[rows, columns(where, which, block_t.shape[0])], block_t[...])
+        ],
+        [],
+        LIMIT,
+    )
+
+
+def select(where, inner, outer):
+    return jnp.where(where[4] == 1, inner[...], outer[...])
+
+
+def add_body(where, *refs):
+    *blocks, w, old, acc, token, block = refs
+    step = pl.program_id(0)
+
+    @pl.when(step == 0)
+    def _():
+        token[...] = jnp.zeros_like(token)
+        block[...] = blocks[0][...] if len(blocks) == 1 else select(where, *blocks)
+
+    here = tile_rows(step)
+    acc[:, here] = old[:, here] + dot_nt(block[...], w[...])
 
 
 def add_block(where, which, blocks, w, old):
     tokens, feats = blocks[0].shape
     return call(
-        functools.partial(add_body, which),
+        add_body,
         f"add_block_{which}",
         where,
-        (1,),
+        (w.shape[0] // TILE,),
         (*blocks, w, old),
-        [fixed(a.shape) for a in blocks] + [INSIDE, INSIDE],
-        [INSIDE, INSIDE, pl.BlockSpec((8, 128), lambda j, where: (0, 0))],
-        [
-            pltpu.VMEM(w.shape, w.dtype),
-            pltpu.VMEM(old.shape, old.dtype),
-            jax.ShapeDtypeStruct((8, 128), jnp.float32),
-        ],
-        [pltpu.VMEM((feats, tokens), blocks[0].dtype)],
-        16,
-        aliases={len(blocks) + 1: 0, len(blocks) + 2: 1},
-    )
-
-
-def select_transposed(where, inner, outer):
-    return jnp.where(where[4] == 1, inner[...], outer[...]).T
-
-
-def last_body(start, where, inner, outer, w, old, gate_t, po_t, left_t, *rest):
-    *grads_in, w_same, old_same, grads, block_t = rest
-    size, feats = outer.shape
-    tokens = pl.ds(start, size)
-    block_t[...] = select_transposed(where, inner, outer)
-
-    def step(t, right_t):
-        rows = tile_rows(t)
-        hidden_grad = old[rows, tokens] + dot(w[rows, columns(where, 3, feats)], block_t[...])
-        up_grad = (hidden_grad * silu(gate_t[rows, :].astype(jnp.float32))).astype(jnp.bfloat16)
-        return right_t + dot(po_t[:, rows], up_grad)
-
-    right_t = lax.fori_loop(0, old.shape[0] // TILE, step, jnp.zeros((PROJ, size), jnp.float32))
-    total = lax.dot_general(
-        left_t[...], right_t, NT, precision=HIGHEST, preferred_element_type=jnp.float32
-    )
-    for earlier in grads_in:
-        total = total + earlier[...]
-    grads[...] = total
-
-
-def last_block(where, inner, outer, start, w, old, gate_t, po_t, left_t, grads):
+        [fixed(a.shape) for a in blocks]
+        + [pl.BlockSpec((TILE, feats), lambda j, where: (j, where[which])), INSIDE],
+        [INSIDE, pl.BlockSpec((8, 128), lambda j, where: (0, 0))],
+        [pltpu.VMEM(old.shape, old.dtype), jax.ShapeDtypeStruct((8, 128), jnp.float32)],
+        [pltpu.VMEM((tokens, feats), blocks[0].dtype)],
+        LIMIT,
+        aliases={len(blocks) + 2: 0},
+    )
+
+
+def last_body(start, where, inner, outer, kept, old, gate, po_t, token, kept_same, old_same, right, block):
+    size = outer.shape[0]
+    step = pl.program_id(0)
+
+    @pl.when(step == 0)
+    def _():
+        block[...] = select(where, inner, outer)
+        right[...] = jnp.zeros_like(right)
+
+    here = tile_rows(step)
+    hidden_grad = old[pl.ds(start, size), here] + dot_nt(block[...], kept[here, :])
+    up_grad = (hidden_grad * silu(gate[...].astype(jnp.float32))).astype(jnp.bfloat16)
+    right[...] += dot_nt(up_grad, po_t[...])
+
+
+def last_block(where, inner, outer, start, kept, old, gate, po_t, token):
     size, feats = outer.shape
     chunk = start // size
     return call(
         functools.partial(last_body, start),
         "last_block",
         where,
-        (1,),
-        (inner, outer, w, old, gate_t, po_t, left_t, *grads),
-        [
+        (kept.shape[0] // TILE,),
+        (inner, outer, kept, old, pltpu.with_memory_space_constraint(gate, pltpu.HBM), po_t, token),
+        [
+            pl.BlockSpec((size, feats), lambda j, where: (chunk, 0), pipeline_mode=pl.Buffered(1)),
+            fixed(outer.shape),
             INSIDE,
             INSIDE,
-            INSIDE,
-            INSIDE,
-            fixed(gate_t.shape),
-            fixed(po_t.shape),
-            pl.BlockSpec((PROJ, size), lambda j, where: (0, chunk), pipeline_mode=pl.Buffered(1)),
-            *[fixed(a.shape) for a in grads],
-        ],
-        [INSIDE, INSIDE, pl.BlockSpec((PROJ, PROJ), lambda j, where: (0, 0))],
-        [
-            pltpu.VMEM(w.shape, w.dtype),
+            pl.BlockSpec((size, TILE), lambda j, where: (chunk, j)),
+            pl.BlockSpec((PROJ, TILE), lambda j, where: (0, j)),
+            ANYWHERE,
+        ],
+        [INSIDE, INSIDE, pl.BlockSpec((size, PROJ), lambda j, where: (0, 0))],
+        [
+            pltpu.VMEM(kept.shape, kept.dtype),
             pltpu.VMEM(old.shape, old.dtype),
-            jax.ShapeDtypeStruct((PROJ, PROJ), jnp.float32),
-        ],
-        [pltpu.VMEM((feats, size), outer.dtype)],
-        16,
+            jax.ShapeDtypeStruct((size, PROJ), jnp.float32),
+        ],
+        [pltpu.VMEM((size, feats), outer.dtype)],
+        LIMIT,
         aliases={3: 0, 4: 1},
     )
+
+
+def outer_body(spans, where, left_t, *refs):
+    *rights, grads = refs
+    total = None
+    for (start, size), right in zip(spans, rights):
+        term = jnp.dot(
+            left_t[:, start : start + size], right[...], precision=HIGHEST, preferred_element_type=jnp.float32
+        )
+        total = term if total is None else total + term
+    grads[...] = total
+
+
+def outer_products(where, left_t, spans, rights):
+    (grads,) = call(
+        functools.partial(outer_body, spans),
+        "outer_products",
+        where,
+        (1,),
+        (left_t, *rights),
+        [fixed(left_t.shape)] + [fixed(a.shape) for a in rights],
+        [pl.BlockSpec((PROJ, PROJ), lambda j, where: (0, 0))],
+        [jax.ShapeDtypeStruct((PROJ, PROJ), jnp.float32)],
+        [],
+        LIMIT,
+    )
+    return grads
 
 
 def small_kernel(body, name, where, *operands):
@@ -223,7 +223,7 @@
         [pl.BlockSpec(operands[0].shape, lambda j, where: (0, 0))],
         [jax.ShapeDtypeStruct(operands[0].shape, operands[0].dtype)],
         [],
-        16,
+        LIMIT,
     )
     return out
 
@@ -268,7 +268,7 @@
         [pl.BlockSpec(shape, lambda j, order: (0, 0))],
         [jax.ShapeDtypeStruct(shape, jnp.float32)],
         [],
-        16,
+        LIMIT,
     )
     return scores
 
@@ -330,7 +330,7 @@
             pltpu.SemaphoreType.DMA((parts,)),
             pltpu.SemaphoreType.DMA((parts,)),
         ],
-        16,
+        LIMIT,
     )
     return updated
 
@@ -354,34 +354,30 @@
     starts = [sum(sizes[:n]) for n in range(len(sizes))]
     mid_inner = send(grad_out, perm=inner)
     pair = send(grad_out, perm=pairs)
-    chunks = [grad_out[start : start + size] for start, size in zip(starts, sizes)]
-    w, acc, in_part, *gates_t = own_block(
-        where, after(grad_out, *chunks), gate_pre, inputs, proj_in.T, w_down, sizes
-    )
+    acc, kept, in_part = own_block(where, after(grad_out, *early), inputs, proj_in.T, w_down)
     mid_outer = send(after(mid_inner, in_part), perm=outward)
-    end_inner = [send(after(chunk, mid_inner, pair, in_part, *early), perm=across) for chunk in chunks]
-
-    side = small_kernel(sum_body, "side", where, in_part, after(send(in_part, perm=inward), mid_inner))
+    end_inner = send(after(grad_out, mid_inner, pair, in_part), perm=across)
+    side = small_kernel(sum_body, "side", where, in_part, send(after(in_part, mid_inner, pair), perm=inward))
+    acc, first = add_block(where, 1, [pair], w_down, after(acc, side))
     total = small_kernel(sum_body, "total", where, side, send(side, perm=inner))
     left_t = small_kernel(pick_body, "left", where, total, send(total, perm=outward))
 
-    w, acc, first = add_block(where, 1, [pair], w, after(acc, side))
-    w, acc, _ = add_block(where, 2, [mid_inner, mid_outer], w, acc)
-
-    grads = [[] for _ in range(tokens // LEN)]
+    acc, second = add_block(where, 2, [mid_inner, mid_outer], w_down, acc)
     arrived = [mid_outer, mid_outer]
-    done = [first, first, first]
+    done = [after(first, total), after(first, total), second]
+    rights = []
     for n, (start, size) in enumerate(zip(starts, sizes)):
-        ready = [left_t, *end_inner] if n < 2 else []
-        end_outer = send(after(end_inner[n], arrived[n], done[n], *ready), perm=outward)
+        chunk = end_inner[start : start + size]
+        end_outer = send(after(chunk, arrived[n], done[n]), perm=outward)
         arrived.append(end_outer)
-        s = start // LEN
-        w, acc, total = last_block(
-            where, end_inner[n], end_outer, start, w, acc, gates_t[n], proj_out.T, left_t, grads[s]
-        )
-        grads[s] = [total]
-        done.append(total)
-    grads = lax.optimization_barrier(tuple(total for total, in grads))
+        kept, acc, right = last_block(where, end_inner, end_outer, start, kept, acc, gate_pre, proj_out.T, second)
+        rights.append(right)
+        done.append(right)
+    grads = []
+    for s in range(tokens // LEN):
+        mine = [n for n, start in enumerate(starts) if start // LEN == s]
+        spans = [(starts[n], sizes[n]) for n in mine]
+        grads.append(outer_products(where, left_t, spans, [rights[n] for n in mine]))
     return jnp.stack(grads).reshape(-1, PROJ * PROJ)
 
 

time: 249 us -> 230 us (0.924)
  waiting for transfers between devices: 46.8 us -> 82.3 us
  local copies, waits for them, and re-layouts: 43.8 us -> 22.1 us
  starting transfers between devices: 58.1 us -> 41.1 us
  Pallas kernels: 96.8 us -> 81.7 us
    ppermute x11 -> x7, waiting for transfers between devices: 17.5 us -> 48.1 us  [the longest x1 43.8 us: line_of_four(): send(after(in_part, mid_inner, pair), perm=inward)]
    ppermute x11 -> x7, starting transfers between devices: 36.3 us -> 15.7 us  [the longest x5 6.43 us: line_of_four(): end_outer = send(after(chunk, arrived[n], done[n]), perm=outward)]
    unnamed x20 -> x32, local copies, waits for them, and re-layouts: 39.7 us -> 20.9 us
    ppermute x1, waiting for transfers between devices: 0.01 us -> 15.4 us  [line_of_four(): pair = send(grad_out, perm=pairs)]
    pallas_call x13 -> x15, Pallas kernels: 96.8 us -> 81.7 us  [call(): pl.pallas_call(body, grid_spec=pltpu.PrefetchScalarGridSpec(num_scalar_pr...]
    ppermute x1, waiting for transfers between devices: 14.7 us -> 0.01 us  [line_of_four(): send(total, perm=outward)]
    ppermute x9, waiting for transfers between devices: 14.7 us -> 18.9 us  [swap(): lax.ppermute(a, axis, [(i, i ^ bit) for i in range(lax.axis_size(axis))])]
    ppermute x9, starting transfers between devices: 11.9 us -> 15.6 us  [swap(): lax.ppermute(a, axis, [(i, i ^ bit) for i in range(lax.axis_size(axis))])]
  transfers between devices with their start and end apart: 25 -> 21, of which waited for: 9 -> 10; matrix products, arithmetic and copies ran while one was open for 1% -> 1% of each run, Pallas kernels for 36% -> 32%
where the time goes in v5:
time: 230 us; the launch traced here: 229 us
  waiting for transfers between devices  82.3 us (36%)
  Pallas kernels  81.7 us (36%)
  starting transfers between devices  41.1 us (18%)
  local copies, waits for them, and re-layouts  22.1 us (10%)
    pallas_call x15, Pallas kernels, call(): pl.pallas_call(body, grid_spec=pltpu.PrefetchScalarGridSpec(num_scalar_pr...  81.7 us
    ppermute x1, waiting for transfers between devices, line_of_four(): send(after(in_part, mid_inner, pair), perm=inward)  43.8 us
    unnamed x32, local copies, waits for them, and re-layouts  20.9 us
    ppermute x9, waiting for transfers between devices, swap(): lax.ppermute(a, axis, [(i, i ^ bit) for i in range(lax.axis_size(axis))])  18.9 us
    ppermute x9, starting transfers between devices, swap(): lax.ppermute(a, axis, [(i, i ^ bit) for i in range(lax.axis_size(axis))])  15.6 us
    ppermute x1, waiting for transfers between devices, line_of_four(): pair = send(grad_out, perm=pairs)  15.4 us
    ppermute x5, starting transfers between devices, line_of_four(): end_outer = send(after(chunk, arrived[n], done[n]), perm=outward)  6.43 us
    ppermute x1, starting transfers between devices, line_of_four(): pair = send(grad_out, perm=pairs)  5.78 us
  transfers between devices with their start and end apart: 21, of which 10 were waited for; matrix products, arithmetic and copies ran while one was open for 1% of the time, Pallas kernels for 32%

profile of v5, /device:TPU:0, one launch (start us, length us, event | category | flops | bytes accessed | tf_op | source)
XLA Modules:
  0.0 229.1 jit_solution(13082796473443968848)
XLA Ops:
  1.4 5.8 %collective-permute-start.4 = (bf16[1024,1024]{1,0:T(8,128)(2,1)}, bf16[1024,1024]{1,0:T(8,128)(2,1)}, u32[]{:S(2)}, u32[]{:S(2)}) collective-permute-start(bf16[1024,1024]{1,0:T(8,128)(2,1)} %own), channel_id=1, source_target_pairs={{0,4},{4,0},{8,12},{12,8},{1,5},{5,1},{9,13},{13,9},{2,6},{6,2},{1... | collective-permute-start | bytes 6291464 | tf_op jit(solution)/shard_map/ppermute | solution.py:356
  7.2 1.5 collective-permute-start.1
  9.2 7.4 %collective-permute-done.1.rest_2_ = f32[256,256]{1,0:T(8,128)S(1)} collective-permute-done((f32[256,256]{1,0:T(8,128)}, f32[256,256]{1,0:T(8,128)S(1)}, u32[]{:S(2)}, u32[]{:S(2)}) %collective-permute-start.1) | collective-permute-done | bytes 262176 | tf_op jit(solution)/shard_map/ppermute | solution.py:395
  16.5 4.8 %collective-permute-done.2.rest_3_ = f32[256,256]{1,0:T(8,128)S(1)} collective-permute-done((f32[256,256]{1,0:T(8,128)}, f32[256,256]{1,0:T(8,128)S(1)}, u32[]{:S(2)}, u32[]{:S(2)}) %collective-permute-start.2) | collective-permute-done | bytes 262176 | tf_op jit(solution)/shard_map/ppermute | solution.py:395
  21.4 1.7 copy-done.5
  24.0 13.5 %own_block.1 = (f32[1024,3584]{1,0:T(8,128)S(1)}, bf16[3584,1024]{1,0:T(8,128)(2,1)S(1)}, f32[64,1024]{1,0:T(8,128)S(1)}) custom-call(s32[5]{0:T(128)S(1)} %stack.51.where, bf16[1024,1024]{1,0:T(8,128)(2,1)} %own, bf16[1024,1024]{1,0:T(8,128)(2,1)S(1)} %copy-done.5, bf16[64,1024]{1,0:T(8,128)(2,1)S(1)} %bitcast.17, bf16[3584,4096]{1,0:T(8,128)(2,1)} %refs_2_.1, ...), custom_call_target="tpu_custom_call" | custom-call | flops 1000 | bytes 1000 | tf_op jit(solution)/shard_map/own_block/pallas_call | solution.py:40
  37.5 15.4 %collective-permute-done.4.refs_0_ = bf16[1024,1024]{1,0:T(8,128)(2,1)} collective-permute-done((bf16[1024,1024]{1,0:T(8,128)(2,1)}, bf16[1024,1024]{1,0:T(8,128)(2,1)}, u32[]{:S(2)}, u32[]{:S(2)}) %collective-permute-start.4) | collective-permute-done | bytes 2097184 | tf_op jit(solution)/shard_map/ppermute | solution.py:356
  52.9 4.6 %collective-permute-start.8 = (bf16[1024,1024]{1,0:T(8,128)(2,1)}, bf16[1024,1024]{1,0:T(8,128)(2,1)S(1)}, u32[]{:S(2)}, u32[]{:S(2)}) collective-permute-start(bf16[1024,1024]{1,0:T(8,128)(2,1)} %own), channel_id=1, source_target_pairs={{0,8},{12,4},{1,9},{13,5},{2,10},{14,6},{3,11},{15,7},{16,24},{28,... | collective-permute-start | bytes 6291464 | tf_op jit(solution)/shard_map/ppermute | solution.py:359
  58.8 4.7 %collective-permute-start.5 = (f32[64,1024]{1,0:T(8,128)S(1)}, f32[64,1024]{1,0:T(8,128)S(1)}, u32[]{:S(2)}, u32[]{:S(2)}) collective-permute-start(f32[64,1024]{1,0:T(8,128)S(1)} %get-tuple-element.38.a), channel_id=1, source_target_pairs={{0,4},{12,8},{1,5},{13,9},{2,6},{14,10},{3,7},{15,11},{16,20},{28,... | collective-permute-start | bytes 786440 | tf_op jit(solution)/shard_map/ppermute | solution.py:360
  63.5 43.8 %collective-permute-done.5.b = f32[64,1024]{1,0:T(8,128)S(1)} collective-permute-done((f32[64,1024]{1,0:T(8,128)S(1)}, f32[64,1024]{1,0:T(8,128)S(1)}, u32[]{:S(2)}, u32[]{:S(2)}) %collective-permute-start.5) | collective-permute-done | bytes 262176 | tf_op jit(solution)/shard_map/ppermute | solution.py:360
  108.6 13.0 %add_block_1.1 = (f32[1024,3584]{1,0:T(8,128)S(1)}, f32[8,128]{1,0:T(8,128)}) custom-call(s32[5]{0:T(128)S(1)} %stack.51.where, bf16[1024,1024]{1,0:T(8,128)(2,1)} %collective-permute-done.4.refs_0_, bf16[3584,4096]{1,0:T(8,128)(2,1)} %refs_2_.1, f32[1024,3584]{1,0:T(8,128)S(1)} %get-tuple-element.42.refs_2_), custom_call_target="tpu_custom_call", output_to_operand_aliasing={{0}: (3, {})} | custom-call | flops 1000 | bytes 1000 | tf_op jit(solution)/shard_map/add_block_1/pallas_call | solution.py:40
  124.9 12.2 %add_block_2.1 = (f32[1024,3584]{1,0:T(8,128)S(1)}, f32[8,128]{1,0:T(8,128)S(1)}) custom-call(s32[5]{0:T(128)S(1)} %stack.51.where, bf16[1024,1024]{1,0:T(8,128)(2,1)S(1)} %copy-done.7, bf16[1024,1024]{1,0:T(8,128)(2,1)S(1)} %collective-permute-done.9.refs_1_, bf16[3584,4096]{1,0:T(8,128)(2,1)} %refs_2_.1, ...), custom_call_target="tpu_custom_call", output_to_operand_aliasing={{0}: (4, {})} | custom-call | flops 1000 | bytes 1000 | tf_op jit(solution)/shard_map/add_block_2/pallas_call | solution.py:40
  137.2 3.4 %collective-permute-done.10.outer = bf16[256,1024]{1,0:T(8,128)(2,1)S(1)} collective-permute-done((bf16[256,1024]{1,0:T(8,128)(2,1)S(1)}, bf16[256,1024]{1,0:T(8,128)(2,1)S(1)}, u32[]{:S(2)}, u32[]{:S(2)}) %collective-permute-start.10) | collective-permute-done | bytes 524320 | tf_op jit(solution)/shard_map/ppermute | solution.py:371
  144.0 7.0 %last_block.5 = (bf16[3584,1024]{1,0:T(8,128)(2,1)S(1)}, f32[1024,3584]{1,0:T(8,128)S(1)}, f32[256,64]{1,0:T(8,128)S(1)}) custom-call(s32[5]{0:T(128)S(1)} %stack.51.where, bf16[1024,1024]{1,0:T(8,128)(2,1)S(1)} %collective-permute-done.8.inner, bf16[256,1024]{1,0:T(8,128)(2,1)S(1)} %collective-permute-done.10.outer, ...), custom_call_target="tpu_custom_call", output_to_operand_aliasing={{0}: (3, {}), {1}: (4, {})} | custom-call | flops 1000 | bytes 1000 | tf_op jit(solution)/shard_map/last_block/pallas_call | solution.py:40
  153.1 7.0 %last_block.6 = (bf16[3584,1024]{1,0:T(8,128)(2,1)S(1)}, f32[1024,3584]{1,0:T(8,128)S(1)}, f32[256,64]{1,0:T(8,128)S(1)}) custom-call(s32[5]{0:T(128)S(1)} %stack.51.where, bf16[1024,1024]{1,0:T(8,128)(2,1)S(1)} %collective-permute-done.8.inner, bf16[256,1024]{1,0:T(8,128)(2,1)S(1)} %collective-permute-done.11.outer, ...), custom_call_target="tpu_custom_call", output_to_operand_aliasing={{0}: (3, {}), {1}: (4, {})} | custom-call | flops 1000 | bytes 1000 | tf_op jit(solution)/shard_map/last_block/pallas_call | solution.py:40
  160.1 5.2 %copy-done = f32[1024,3584]{1,0:T(8,128)} copy-done((f32[1024,3584]{1,0:T(8,128)}, f32[1024,3584]{1,0:T(8,128)S(1)}, u32[]{:S(2)}) %copy-start) | copy-done | bytes 14680088
  165.2 3.0 %copy-done.2 = bf16[3584,1024]{1,0:T(8,128)(2,1)} copy-done((bf16[3584,1024]{1,0:T(8,128)(2,1)}, bf16[3584,1024]{1,0:T(8,128)(2,1)S(1)}, u32[]{:S(2)}) %copy-start.2) | copy-done | bytes 7340056
  171.0 5.2 %copy-done.1 = f32[1024,3584]{1,0:T(8,128)S(1)} copy-done((f32[1024,3584]{1,0:T(8,128)S(1)}, f32[1024,3584]{1,0:T(8,128)}, u32[]{:S(2)}) %copy-start.1) | copy-done | bytes 14680088
  176.2 3.1 %copy-done.3 = bf16[3584,1024]{1,0:T(8,128)(2,1)S(1)} copy-done((bf16[3584,1024]{1,0:T(8,128)(2,1)S(1)}, bf16[3584,1024]{1,0:T(8,128)(2,1)}, u32[]{:S(2)}) %copy-start.3) | copy-done | bytes 7340056
  179.3 6.9 %last_block.7 = (bf16[3584,1024]{1,0:T(8,128)(2,1)S(1)}, f32[1024,3584]{1,0:T(8,128)S(1)}, f32[256,64]{1,0:T(8,128)S(1)}) custom-call(s32[5]{0:T(128)S(1)} %stack.51.where, bf16[1024,1024]{1,0:T(8,128)(2,1)S(1)} %collective-permute-done.8.inner, bf16[256,1024]{1,0:T(8,128)(2,1)S(1)} %collective-permute-done.12.outer, ...), custom_call_target="tpu_custom_call", output_to_operand_aliasing={{0}: (3, {}), {1}: (4, {})} | custom-call | flops 1000 | bytes 1000 | tf_op jit(solution)/shard_map/last_block/pallas_call | solution.py:40
  186.2 6.8 %last_block.8 = (bf16[3584,1024]{1,0:T(8,128)(2,1)S(1)}, f32[1024,3584]{1,0:T(8,128)S(1)}, f32[128,64]{1,0:T(8,128)S(1)}) custom-call(s32[5]{0:T(128)S(1)} %stack.51.where, bf16[1024,1024]{1,0:T(8,128)(2,1)S(1)} %collective-permute-done.8.inner, bf16[128,1024]{1,0:T(8,128)(2,1)} %collective-permute-done.13.outer, ...), custom_call_target="tpu_custom_call", output_to_operand_aliasing={{0}: (3, {}), {1}: (4, {})} | custom-call | flops 1000 | bytes 1000 | tf_op jit(solution)/shard_map/last_block/pallas_call | solution.py:40
  193.1 6.8 %last_block.9 = (bf16[3584,1024]{1,0:T(8,128)(2,1)S(1)}, f32[1024,3584]{1,0:T(8,128)S(1)}, f32[128,64]{1,0:T(8,128)S(1)}) custom-call(s32[5]{0:T(128)S(1)} %stack.51.where, bf16[1024,1024]{1,0:T(8,128)(2,1)S(1)} %collective-permute-done.8.inner, bf16[128,1024]{1,0:T(8,128)(2,1)} %collective-permute-done.14.outer, ...), custom_call_target="tpu_custom_call", output_to_operand_aliasing={{0}: (3, {}), {1}: (4, {})} | custom-call | flops 1000 | bytes 1000 | tf_op jit(solution)/shard_map/last_block/pallas_call | solution.py:40
  200.9 4.1 %collective-permute-start.15 = (f32[2,4096]{1,0:T(2,128)S(1)}, f32[2,4096]{1,0:T(2,128)S(1)}, u32[]{:S(2)}, u32[]{:S(2)}) collective-permute-start(f32[2,4096]{1,0:T(2,128)S(1)} %pad_maximum_fusion.2), channel_id=1, source_target_pairs={{0,4},{4,0},{8,12},{12,8},{1,5},{5,1},{9,13},{13,9},{2,6},{6,2},{1... | collective-permute-start | bytes 98312 | tf_op jit(solution)/shard_map/ppermute | solution.py:395
  205.0 1.9 collective-permute-done.15
  207.0 3.1 %collective-permute-start.16 = (f32[2,4096]{1,0:T(2,128)S(1)}, f32[2,4096]{1,0:T(2,128)S(1)}, u32[]{:S(2)}, u32[]{:S(2)}) collective-permute-start(f32[2,4096]{1,0:T(2,128)S(1)} %fusion), channel_id=1, source_target_pairs={{0,8},{4,12},{8,0},{12,4},{1,9},{5,13},{9,1},{13,5},{2,10},{6,14},... | collective-permute-start | bytes 98312 | tf_op jit(solution)/shard_map/ppermute | solution.py:395
  210.1 1.9 collective-permute-done.16
  213.3 1.6 collective-permute-start.18
  216.9 1.5 scores.1
  218.3 1.9 collective-permute-start.19
  220.3 1.7 collective-permute-done.19
  221.9 2.9 %collective-permute-start.20 = (f32[2,256]{1,0:T(2,128)S(1)}, f32[2,256]{1,0:T(2,128)S(1)}, u32[]{:S(2)}, u32[]{:S(2)}) collective-permute-start(f32[2,256]{1,0:T(2,128)S(1)} %add.35), channel_id=1, source_target_pairs={{0,8},{4,12},{8,0},{12,4},{1,9},{5,13},{9,1},{13,5},{2,10},{6,14},... | collective-permute-start | bytes 6152 | tf_op jit(solution)/shard_map/ppermute | solution.py:395
  224.9 3.6 %hessian_update.1 = f32[256,4096]{1,0:T(8,128)} custom-call(s32[1]{0:T(128)} %bitcast.row, f32[8,4096]{1,0:T(8,128)S(1)} %pad_maximum_fusion.grads.mine, f32[8,4096]{1,0:T(8,128)S(1)} %pad_maximum_fusion.grads.mine, f32[256,4096]{1,0:T(8,128)} %hessian.1), custom_call_target="tpu_custom_call" | custom-call | flops 1000 | bytes 1000 | tf_op jit(solution)/shard_map/hessian_update/pallas_call | solution.py:40
  (70 shorter events, 21.3 us)
Async XLA Ops:
  0.6 36.9 %collective-permute-start.3 = (bf16[1024,1024]{1,0:T(8,128)(2,1)}, bf16[1024,1024]{1,0:T(8,128)(2,1)S(1)}, u32[]{:S(2)}, u32[]{:S(2)}) collective-permute-start(bf16[1024,1024]{1,0:T(8,128)(2,1)} %own), channel_id=1, source_target_pairs={{4,8},{8,4},{5,9},{9,5},{6,10},{10,6},{7,11},{11,7},{20,24},{24,20... | collective-permute-start | bytes 6291464 | tf_op jit(solution)/shard_map/ppermute | solution.py:355
  1.4 51.4 %collective-permute-start.4 = (bf16[1024,1024]{1,0:T(8,128)(2,1)}, bf16[1024,1024]{1,0:T(8,128)(2,1)}, u32[]{:S(2)}, u32[]{:S(2)}) collective-permute-start(bf16[1024,1024]{1,0:T(8,128)(2,1)} %own), channel_id=1, source_target_pairs={{0,4},{4,0},{8,12},{12,8},{1,5},{5,1},{9,13},{13,9},{2,6},{6,2},{1... | collective-permute-start | bytes 6291464 | tf_op jit(solution)/shard_map/ppermute | solution.py:356
  7.2 1.9 collective-permute-start
  7.2 9.3 %collective-permute-start.1 = (f32[256,256]{1,0:T(8,128)}, f32[256,256]{1,0:T(8,128)S(1)}, u32[]{:S(2)}, u32[]{:S(2)}) collective-permute-start(f32[256,256]{1,0:T(8,128)} %rest_0_.1), channel_id=1, source_target_pairs={{0,2},{1,3},{2,0},{3,1},{4,6},{5,7},{6,4},{7,5},{8,10},{9,11},{10,... | collective-permute-start | bytes 786440 | tf_op jit(solution)/shard_map/ppermute | solution.py:395
  8.7 12.7 %collective-permute-start.2 = (f32[256,256]{1,0:T(8,128)}, f32[256,256]{1,0:T(8,128)S(1)}, u32[]{:S(2)}, u32[]{:S(2)}) collective-permute-start(f32[256,256]{1,0:T(8,128)} %rest_0_.1), channel_id=1, source_target_pairs={{0,3},{1,2},{2,1},{3,0},{4,7},{5,6},{6,5},{7,4},{8,11},{9,10},{10,... | collective-permute-start | bytes 786440 | tf_op jit(solution)/shard_map/ppermute | solution.py:395
  9.2 28.3 %copy-start.9 = (f32[256,256]{1,0:T(8,128)}, f32[256,256]{1,0:T(8,128)S(1)}, u32[]{:S(2)}) copy-start(f32[256,256]{1,0:T(8,128)S(1)} %collective-permute-done.rest_1_) | copy-start | bytes 786436
  16.5 21.0 %copy-start.11 = (f32[256,256]{1,0:T(8,128)}, f32[256,256]{1,0:T(8,128)S(1)}, u32[]{:S(2)}) copy-start(f32[256,256]{1,0:T(8,128)S(1)} %collective-permute-done.1.rest_2_) | copy-start | bytes 786436
  21.4 16.1 %copy-start.13 = (f32[256,256]{1,0:T(8,128)}, f32[256,256]{1,0:T(8,128)S(1)}, u32[]{:S(2)}) copy-start(f32[256,256]{1,0:T(8,128)S(1)} %collective-permute-done.2.rest_3_) | copy-start | bytes 786436
  37.5 15.4 %copy-start.6 = (bf16[1024,1024]{1,0:T(8,128)(2,1)}, bf16[1024,1024]{1,0:T(8,128)(2,1)S(1)}, u32[]{:S(2)}) copy-start(bf16[1024,1024]{1,0:T(8,128)(2,1)S(1)} %collective-permute-done.3.refs_0_) | copy-start | bytes 6291460
  52.9 69.2 %collective-permute-start.8 = (bf16[1024,1024]{1,0:T(8,128)(2,1)}, bf16[1024,1024]{1,0:T(8,128)(2,1)S(1)}, u32[]{:S(2)}, u32[]{:S(2)}) collective-permute-start(bf16[1024,1024]{1,0:T(8,128)(2,1)} %own), channel_id=1, source_target_pairs={{0,8},{12,4},{1,9},{13,5},{2,10},{14,6},{3,11},{15,7},{16,24},{28,... | collective-permute-start | bytes 6291464 | tf_op jit(solution)/shard_map/ppermute | solution.py:359
  57.5 64.8 %collective-permute-start.9 = (bf16[1024,1024]{1,0:T(8,128)(2,1)}, bf16[1024,1024]{1,0:T(8,128)(2,1)S(1)}, u32[]{:S(2)}, u32[]{:S(2)}) collective-permute-start(bf16[1024,1024]{1,0:T(8,128)(2,1)} %copy-done.6), channel_id=1, source_target_pairs={{4,0},{8,12},{5,1},{9,13},{6,2},{10,14},{7,3},{11,15},{20,16},{24,... | collective-permute-start | bytes 6291464 | tf_op jit(solution)/shard_map/ppermute | solution.py:358
  58.8 48.5 %collective-permute-start.5 = (f32[64,1024]{1,0:T(8,128)S(1)}, f32[64,1024]{1,0:T(8,128)S(1)}, u32[]{:S(2)}, u32[]{:S(2)}) collective-permute-start(f32[64,1024]{1,0:T(8,128)S(1)} %get-tuple-element.38.a), channel_id=1, source_target_pairs={{0,4},{12,8},{1,5},{13,9},{2,6},{14,10},{3,7},{15,11},{16,20},{28,... | collective-permute-start | bytes 786440 | tf_op jit(solution)/shard_map/ppermute | solution.py:360
  107.9 13.7 %collective-permute-start.6 = (f32[64,1024]{1,0:T(8,128)S(1)}, f32[64,1024]{1,0:T(8,128)S(1)}, u32[]{:S(2)}, u32[]{:S(2)}) collective-permute-start(f32[64,1024]{1,0:T(8,128)S(1)} %side.1.a), channel_id=1, source_target_pairs={{4,8},{8,4},{5,9},{9,5},{6,10},{10,6},{7,11},{11,7},{20,24},{24,20... | collective-permute-start | bytes 786440 | tf_op jit(solution)/shard_map/ppermute | solution.py:362
  108.6 16.3 %copy-start.7 = (bf16[1024,1024]{1,0:T(8,128)(2,1)S(1)}, bf16[1024,1024]{1,0:T(8,128)(2,1)}, u32[]{:S(2)}) copy-start(bf16[1024,1024]{1,0:T(8,128)(2,1)} %copy-done.6) | copy-start | bytes 6291460
  122.3 18.3 %collective-permute-start.10 = (bf16[256,1024]{1,0:T(8,128)(2,1)S(1)}, bf16[256,1024]{1,0:T(8,128)(2,1)S(1)}, u32[]{:S(2)}, u32[]{:S(2)}) collective-permute-start(bf16[256,1024]{1,0:T(8,128)(2,1)S(1)} %get-tuple-element.45), channel_id=1, source_target_pairs={{4,0},{8,12},{5,1},{9,13},{6,2},{10,14},{7,3},{11,15},{20,16},{24,... | collective-permute-start | bytes 1572872 | tf_op jit(solution)/shard_map/ppermute | solution.py:371
  123.6 28.2 %collective-permute-start.11 = (bf16[256,1024]{1,0:T(8,128)(2,1)S(1)}, bf16[256,1024]{1,0:T(8,128)(2,1)S(1)}, u32[]{:S(2)}, u32[]{:S(2)}) collective-permute-start(bf16[256,1024]{1,0:T(8,128)(2,1)S(1)} %get-tuple-element.51), channel_id=1, source_target_pairs={{4,0},{8,12},{5,1},{9,13},{6,2},{10,14},{7,3},{11,15},{20,16},{24,... | collective-permute-start | bytes 1572872 | tf_op jit(solution)/shard_map/ppermute | solution.py:371
  124.9 19.1 %copy-start.4 = (bf16[3584,64]{0,1:T(8,128)(2,1)S(1)}, bf16[3584,64]{0,1:T(8,128)(2,1)}, u32[]{:S(2)}) copy-start(bf16[3584,64]{0,1:T(8,128)(2,1)} %param.13) | copy-start | bytes 1376260
  140.6 27.7 %collective-permute-start.12 = (bf16[256,1024]{1,0:T(8,128)(2,1)S(1)}, bf16[256,1024]{1,0:T(8,128)(2,1)S(1)}, u32[]{:S(2)}, u32[]{:S(2)}) collective-permute-start(bf16[256,1024]{1,0:T(8,128)(2,1)S(1)} %get-tuple-element.55), channel_id=1, source_target_pairs={{4,0},{8,12},{5,1},{9,13},{6,2},{10,14},{7,3},{11,15},{20,16},{24,... | collective-permute-start | bytes 1572872 | tf_op jit(solution)/shard_map/ppermute | solution.py:371
  141.8 27.7 %collective-permute-start.7 = (f32[64,1024]{1,0:T(8,128)S(1)}, f32[64,1024]{1,0:T(8,128)S(1)}, u32[]{:S(2)}, u32[]{:S(2)}) collective-permute-start(f32[64,1024]{1,0:T(8,128)S(1)} %total.1.a), channel_id=1, source_target_pairs={{4,0},{8,12},{5,1},{9,13},{6,2},{10,14},{7,3},{11,15},{20,16},{24,... | collective-permute-start | bytes 786440 | tf_op jit(solution)/shard_map/ppermute | solution.py:363
  151.8 34.4 %collective-permute-start.13 = (bf16[128,1024]{1,0:T(8,128)(2,1)}, bf16[128,1024]{1,0:T(8,128)(2,1)}, u32[]{:S(2)}, u32[]{:S(2)}) collective-permute-start(bf16[128,1024]{1,0:T(8,128)(2,1)} %get-tuple-element.59), channel_id=1, source_target_pairs={{4,0},{8,12},{5,1},{9,13},{6,2},{10,14},{7,3},{11,15},{20,16},{24,... | collective-permute-start | bytes 786440 | tf_op jit(solution)/shard_map/ppermute | solution.py:371
  160.1 5.2 %copy-start = (f32[1024,3584]{1,0:T(8,128)}, f32[1024,3584]{1,0:T(8,128)S(1)}, u32[]{:S(2)}) copy-start(f32[1024,3584]{1,0:T(8,128)S(1)} %get-tuple-element.57.old) | copy-start | bytes 44040196
  168.2 24.9 %collective-permute-start.14 = (bf16[128,1024]{1,0:T(8,128)(2,1)}, bf16[128,1024]{1,0:T(8,128)(2,1)}, u32[]{:S(2)}, u32[]{:S(2)}) collective-permute-start(bf16[128,1024]{1,0:T(8,128)(2,1)} %get-tuple-element.63), channel_id=1, source_target_pairs={{4,0},{8,12},{5,1},{9,13},{6,2},{10,14},{7,3},{11,15},{20,16},{24,... | collective-permute-start | bytes 786440 | tf_op jit(solution)/shard_map/ppermute | solution.py:371
  171.0 5.2 %copy-start.1 = (f32[1024,3584]{1,0:T(8,128)S(1)}, f32[1024,3584]{1,0:T(8,128)}, u32[]{:S(2)}) copy-start(f32[1024,3584]{1,0:T(8,128)} %copy-done) | copy-start | bytes 44040196
  176.2 3.1 %copy-start.3 = (bf16[3584,1024]{1,0:T(8,128)(2,1)S(1)}, bf16[3584,1024]{1,0:T(8,128)(2,1)}, u32[]{:S(2)}) copy-start(bf16[3584,1024]{1,0:T(8,128)(2,1)} %copy-done.2) | copy-start | bytes 22020100
  193.1 21.9 %copy-start.8 = (f32[256,256]{1,0:T(8,128)S(1)}, f32[256,256]{1,0:T(8,128)}, u32[]{:S(2)}) copy-start(f32[256,256]{1,0:T(8,128)} %rest_0_.1) | copy-start | bytes 786436
  193.1 21.9 %copy-start.10 = (f32[256,256]{1,0:T(8,128)S(1)}, f32[256,256]{1,0:T(8,128)}, u32[]{:S(2)}) copy-start(f32[256,256]{1,0:T(8,128)} %copy-done.9) | copy-start | bytes 786436
  200.9 6.0 %collective-permute-start.15 = (f32[2,4096]{1,0:T(2,128)S(1)}, f32[2,4096]{1,0:T(2,128)S(1)}, u32[]{:S(2)}, u32[]{:S(2)}) collective-permute-start(f32[2,4096]{1,0:T(2,128)S(1)} %pad_maximum_fusion.2), channel_id=1, source_target_pairs={{0,4},{4,0},{8,12},{12,8},{1,5},{5,1},{9,13},{13,9},{2,6},{6,2},{1... | collective-permute-start | bytes 98312 | tf_op jit(solution)/shard_map/ppermute | solution.py:395
  207.0 5.0 %collective-permute-start.16 = (f32[2,4096]{1,0:T(2,128)S(1)}, f32[2,4096]{1,0:T(2,128)S(1)}, u32[]{:S(2)}, u32[]{:S(2)}) collective-permute-start(f32[2,4096]{1,0:T(2,128)S(1)} %fusion), channel_id=1, source_target_pairs={{0,8},{4,12},{8,0},{12,4},{1,9},{5,13},{9,1},{13,5},{2,10},{6,14},... | collective-permute-start | bytes 98312 | tf_op jit(solution)/shard_map/ppermute | solution.py:395
  212.0 1.3 collective-permute-start.17
  213.3 11.5 %collective-permute-start.18 = (f32[4,4096]{1,0:T(4,128)S(1)}, f32[4,4096]{1,0:T(4,128)S(1)}, u32[]{:S(2)}, u32[]{:S(2)}) collective-permute-start(f32[4,4096]{1,0:T(4,128)S(1)} %pad_maximum_fusion.1), channel_id=1, source_target_pairs={{0,2},{1,3},{2,0},{3,1},{4,6},{5,7},{6,4},{7,5},{8,10},{9,11},{10,... | collective-permute-start | bytes 196616 | tf_op jit(solution)/shard_map/ppermute | solution.py:395
  218.3 3.6 %collective-permute-start.19 = (f32[2,256]{1,0:T(2,128)S(1)}, f32[2,256]{1,0:T(2,128)S(1)}, u32[]{:S(2)}, u32[]{:S(2)}) collective-permute-start(f32[2,256]{1,0:T(2,128)S(1)} %scores.1), channel_id=1, source_target_pairs={{0,4},{4,0},{8,12},{12,8},{1,5},{5,1},{9,13},{13,9},{2,6},{6,2},{1... | collective-permute-start | bytes 6152 | tf_op jit(solution)/shard_map/ppermute | solution.py:395
  221.9 6.6 %collective-permute-start.20 = (f32[2,256]{1,0:T(2,128)S(1)}, f32[2,256]{1,0:T(2,128)S(1)}, u32[]{:S(2)}, u32[]{:S(2)}) collective-permute-start(f32[2,256]{1,0:T(2,128)S(1)} %add.35), channel_id=1, source_target_pairs={{0,8},{4,12},{8,0},{12,4},{1,9},{5,13},{9,1},{13,5},{2,10},{6,14},... | collective-permute-start | bytes 6152 | tf_op jit(solution)/shard_map/ppermute | solution.py:395
  (5 other events, 7.5 us)

commit v6 on v5

--- a/solution.py
+++ b/solution.py
@@ -36,7 +36,7 @@
     return a
 
 
-def call(body, name, where, grid, operands, in_specs, out_specs, out_shapes, scratch, mib, aliases=None):
+def call(body, name, where, grid, operands, in_specs, out_specs, out_shapes, scratch, mib, aliases=None, flops=1000):
     return pl.pallas_call(
         body,
         grid_spec=pltpu.PrefetchScalarGridSpec(
@@ -44,7 +44,7 @@
         ),
         out_shape=out_shapes,
         compiler_params=pltpu.CompilerParams(vmem_limit_bytes=mib * 2**20),
-        cost_estimate=pl.CostEstimate(flops=1000, bytes_accessed=1000, transcendentals=0),
+        cost_estimate=pl.CostEstimate(flops=flops, bytes_accessed=1000, transcendentals=0),
         name=name,
         input_output_aliases=aliases or {},
     )(where, *[placed(a, spec) for a, spec in zip(operands, in_specs)])
@@ -66,19 +66,35 @@
     return pl.ds(pl.multiple_of(where[i] * width, width), width)
 
 
-def own_body(where, own, inputs, pi_t, w, w_last, acc, kept, in_t):
-    step = pl.program_id(0)
-
-    @pl.when(step == 0)
-    def _():
-        in_t[...] = dot_nt(pi_t[...], inputs[...])
-
-    here = tile_rows(step)
+def input_body(where, inputs, pi_t, in_t):
+    in_t[...] = dot_nt(pi_t[...], inputs[...])
+
+
+def input_block(where, inputs, pi_t):
+    shape = (pi_t.shape[0], inputs.shape[0])
+    (in_t,) = call(
+        input_body,
+        "input_block",
+        where,
+        (1,),
+        (inputs, pi_t),
+        [fixed(inputs.shape), fixed(pi_t.shape)],
+        [pl.BlockSpec(shape, lambda j, where: (0, 0))],
+        [jax.ShapeDtypeStruct(shape, jnp.float32)],
+        [],
+        LIMIT,
+    )
+    return in_t
+
+
+def own_body(where, own, w, w_last, acc, kept, token):
+    here = tile_rows(pl.program_id(0))
+    token[...] = jnp.zeros_like(token)
     kept[here, :] = w_last[...]
     acc[:, here] = dot_nt(own[...], w[...])
 
 
-def own_block(where, own, inputs, pi_t, w):
+def own_block(where, own, w):
     tokens, feats = own.shape
     hidden = w.shape[0]
     return call(
@@ -86,19 +102,17 @@
         "own_block",
         where,
         (hidden // TILE,),
-        (own, inputs, pi_t, w, w),
+        (own, w, w),
         [
             fixed(own.shape),
-            fixed(inputs.shape),
-            fixed(pi_t.shape),
             pl.BlockSpec((TILE, feats), lambda j, where: (j, where[0])),
             pl.BlockSpec((TILE, feats), lambda j, where: (j, where[3])),
         ],
-        [INSIDE, INSIDE, pl.BlockSpec((PROJ, tokens), lambda j, where: (0, 0))],
+        [INSIDE, INSIDE, pl.BlockSpec((8, 128), lambda j, where: (0, 0))],
         [
             pltpu.VMEM((tokens, hidden), jnp.float32),
             pltpu.VMEM((hidden, feats), w.dtype),
-            jax.ShapeDtypeStruct((PROJ, tokens), jnp.float32),
+            jax.ShapeDtypeStruct((8, 128), jnp.float32),
         ],
         [],
         LIMIT,
@@ -110,33 +124,40 @@
 
 
 def add_body(where, *refs):
-    *blocks, w, old, acc, token, block = refs
+    *blocks, w, old, _, acc, token, block = refs
     step = pl.program_id(0)
 
     @pl.when(step == 0)
     def _():
         token[...] = jnp.zeros_like(token)
-        block[...] = blocks[0][...] if len(blocks) == 1 else select(where, *blocks)
+        if len(blocks) == 1:
+            block[...] = blocks[0][...]
+        else:
+            half = len(blocks) // 2
+            size = blocks[0].shape[0]
+            for h in range(half):
+                block[h * size : (h + 1) * size, :] = select(where, blocks[h], blocks[half + h])
 
     here = tile_rows(step)
     acc[:, here] = old[:, here] + dot_nt(block[...], w[...])
 
 
-def add_block(where, which, blocks, w, old):
-    tokens, feats = blocks[0].shape
+def add_block(where, which, blocks, w, old, token, flops):
+    tokens, feats = old.shape[0], blocks[0].shape[1]
     return call(
         add_body,
         f"add_block_{which}",
         where,
         (w.shape[0] // TILE,),
-        (*blocks, w, old),
+        (*blocks, w, old, token),
         [fixed(a.shape) for a in blocks]
-        + [pl.BlockSpec((TILE, feats), lambda j, where: (j, where[which])), INSIDE],
+        + [pl.BlockSpec((TILE, feats), lambda j, where: (j, where[which])), INSIDE, ANYWHERE],
         [INSIDE, pl.BlockSpec((8, 128), lambda j, where: (0, 0))],
         [pltpu.VMEM(old.shape, old.dtype), jax.ShapeDtypeStruct((8, 128), jnp.float32)],
         [pltpu.VMEM((tokens, feats), blocks[0].dtype)],
         LIMIT,
         aliases={len(blocks) + 2: 0},
+        flops=flops,
     )
 
 
@@ -155,9 +176,9 @@
     right[...] += dot_nt(up_grad, po_t[...])
 
 
-def last_block(where, inner, outer, start, kept, old, gate, po_t, token):
+def last_block(where, inner, inner_at, outer, start, kept, old, gate, po_t, token):
     size, feats = outer.shape
-    chunk = start // size
+    chunk, inner_chunk = start // size, inner_at // size
     return call(
         functools.partial(last_body, start),
         "last_block",
@@ -165,7 +186,7 @@
         (kept.shape[0] // TILE,),
         (inner, outer, kept, old, pltpu.with_memory_space_constraint(gate, pltpu.HBM), po_t, token),
         [
-            pl.BlockSpec((size, feats), lambda j, where: (chunk, 0), pipeline_mode=pl.Buffered(1)),
+            pl.BlockSpec((size, feats), lambda j, where: (inner_chunk, 0), pipeline_mode=pl.Buffered(1)),
             fixed(outer.shape),
             INSIDE,
             INSIDE,
@@ -185,27 +206,34 @@
     )
 
 
-def outer_body(spans, where, left_t, *refs):
+def outer_body(where, total, sent, *refs):
     *rights, grads = refs
-    total = None
-    for (start, size), right in zip(spans, rights):
+    left_t = select(where, total, sent)
+    start = 0
+    terms = [None] * grads.shape[0]
+    for right in rights:
+        size = right.shape[0]
+        s = start // LEN
         term = jnp.dot(
             left_t[:, start : start + size], right[...], precision=HIGHEST, preferred_element_type=jnp.float32
         )
-        total = term if total is None else total + term
-    grads[...] = total
-
-
-def outer_products(where, left_t, spans, rights):
+        terms[s] = term if terms[s] is None else terms[s] + term
+        start += size
+    for s, term in enumerate(terms):
+        grads[s] = term
+
+
+def outer_products(where, total, sent, rights):
+    shape = (total.shape[1] // LEN, PROJ, PROJ)
     (grads,) = call(
-        functools.partial(outer_body, spans),
+        outer_body,
         "outer_products",
         where,
         (1,),
-        (left_t, *rights),
-        [fixed(left_t.shape)] + [fixed(a.shape) for a in rights],
-        [pl.BlockSpec((PROJ, PROJ), lambda j, where: (0, 0))],
-        [jax.ShapeDtypeStruct((PROJ, PROJ), jnp.float32)],
+        (total, sent, *rights),
+        [fixed(a.shape) for a in (total, sent, *rights)],
+        [pl.BlockSpec(shape, lambda j, where: (0, 0, 0))],
+        [jax.ShapeDtypeStruct(shape, jnp.float32)],
         [],
         LIMIT,
     )
@@ -230,10 +258,6 @@
 
 def sum_body(where, a, b, out):
     out[...] = a[...] + b[...]
-
-
-def pick_body(where, a, b, out):
-    out[...] = jnp.where(where[4] == 1, a[...], b[...])
 
 
 def score_body(order, grads, *rest):
@@ -263,7 +287,7 @@
         "scores",
         order,
         (1,),
-        (grads, *parts),
+        (grads, *[pltpu.with_memory_space_constraint(a, pltpu.HBM) for a in parts]),
         [fixed(grads.shape)] + [fixed(a.shape) for a in parts],
         [pl.BlockSpec(shape, lambda j, order: (0, 0))],
         [jax.ShapeDtypeStruct(shape, jnp.float32)],
@@ -350,35 +374,37 @@
         [z, z + 1 - 2 * (z % 2), jnp.where(low, 2, 1), jnp.where(low, 3, 0), middle.astype(z.dtype)]
     ).astype(jnp.int32)
 
-    sizes = [256] * (tokens // 256 - 1) + [128, 128]
-    starts = [sum(sizes[:n]) for n in range(len(sizes))]
-    mid_inner = send(grad_out, perm=inner)
+    halves = [slice(0, tokens // 2), slice(tokens // 2, tokens)]
     pair = send(grad_out, perm=pairs)
-    acc, kept, in_part = own_block(where, after(grad_out, *early), inputs, proj_in.T, w_down)
-    mid_outer = send(after(mid_inner, in_part), perm=outward)
-    end_inner = send(after(grad_out, mid_inner, pair, in_part), perm=across)
-    side = small_kernel(sum_body, "side", where, in_part, send(after(in_part, mid_inner, pair), perm=inward))
-    acc, first = add_block(where, 1, [pair], w_down, after(acc, side))
+    own = [grad_out[half] for half in halves]
+    mid_inner = [send(a, perm=inner) for a in own]
+    in_part = input_block(where, inputs, proj_in.T)
+    from_end = send(after(in_part, mid_inner[0]), perm=inward)
+    acc, kept, begun = own_block(where, after(grad_out, in_part, *early), w_down)
+    side = small_kernel(sum_body, "side", where, in_part, after(from_end, begun))
+    end_inner = [send(after(a, side), perm=across) for a in own]
+    mid_outer = [send(after(a, begun), perm=outward) for a in mid_inner]
     total = small_kernel(sum_body, "total", where, side, send(side, perm=inner))
-    left_t = small_kernel(pick_body, "left", where, total, send(total, perm=outward))
-
-    acc, second = add_block(where, 2, [mid_inner, mid_outer], w_down, acc)
-    arrived = [mid_outer, mid_outer]
-    done = [after(first, total), after(first, total), second]
+    sent = send(total, perm=outward)
+
+    acc, first = add_block(where, 1, [pair], w_down, after(acc, mid_outer[0]), begun, 2 * grad_out.size * w_down.shape[0])
+    acc, second = add_block(where, 2, mid_inner + mid_outer, w_down, acc, first, 1000)
+
+    size = 256
+    arrived = [total, total]
+    done = [first, first, second]
     rights = []
-    for n, (start, size) in enumerate(zip(starts, sizes)):
-        chunk = end_inner[start : start + size]
+    for n in range(tokens // size):
+        h, at = divmod(n * size, tokens // 2)
+        chunk = end_inner[h][at : at + size]
         end_outer = send(after(chunk, arrived[n], done[n]), perm=outward)
         arrived.append(end_outer)
-        kept, acc, right = last_block(where, end_inner, end_outer, start, kept, acc, gate_pre, proj_out.T, second)
+        kept, acc, right = last_block(
+            where, end_inner[h], at, end_outer, n * size, kept, acc, gate_pre, proj_out.T, second
+        )
         rights.append(right)
         done.append(right)
-    grads = []
-    for s in range(tokens // LEN):
-        mine = [n for n, start in enumerate(starts) if start // LEN == s]
-        spans = [(starts[n], sizes[n]) for n in mine]
-        grads.append(outer_products(where, left_t, spans, [rights[n] for n in mine]))
-    return jnp.stack(grads).reshape(-1, PROJ * PROJ)
+    return outer_products(where, total, sent, rights).reshape(-1, PROJ * PROJ)
 
 
 def any_line(inputs, gate_pre, grad_out, w_down, proj_in, proj_out, early):

time: 230 us -> 195 us (0.85)
  waiting for transfers between devices: 82.3 us -> 48.7 us
  starting transfers between devices: 41.1 us -> 62.4 us
  local copies, waits for them, and re-layouts: 22.1 us -> 6.03 us
  Pallas kernels: 81.7 us -> 74.7 us
    ppermute x5 -> x8, starting transfers between devices: 12.7 us -> 44.7 us  [the longest x2 34.6 us: line_of_four(): end_inner = [send(after(a, side), perm=across) for a in own]]
    ppermute x5 -> x8, waiting for transfers between devices: 43.8 us -> 18.2 us  [the longest x1 18.1 us: line_of_four(): from_end = send(after(in_part, mid_inner[0]), perm=inward)]
    unnamed x32 -> x12, local copies, waits for them, and re-layouts: 20.9 us -> 2.52 us
    ppermute x1, waiting for transfers between devices: 15.4 us -> 0.01 us  [line_of_four(): pair = send(grad_out, perm=pairs)]
    ppermute x9, starting transfers between devices: 15.6 us -> 5.99 us  [swap(): lax.ppermute(a, axis, [(i, i ^ bit) for i in range(lax.axis_size(axis))])]
    pallas_call x15 -> x13, Pallas kernels: 81.7 us -> 74.7 us  [call(): pl.pallas_call(body, grid_spec=pltpu.PrefetchScalarGridSpec(num_scalar_pr...]
    ppermute x5 -> x4, waiting for transfers between devices: 4.25 us -> 10.6 us  [line_of_four(): end_outer = send(after(chunk, arrived[n], done[n]), perm=outward)]
    slice x2 -> x3, local copies, waits for them, and re-layouts: 0.94 us -> 3.33 us  [the longest x1 3.19 us: line_of_four(): own = [grad_out[half] for half in halves]]
  transfers between devices with their start and end apart: 21 -> 23, of which waited for: 10 -> 11; matrix products, arithmetic and copies ran while one was open for 1% -> 0% of each run, Pallas kernels for 32% -> 38%
where the time goes in v6:
time: 195 us; the launch traced here: 194 us
  Pallas kernels  74.7 us (38%)
  starting transfers between devices  62.4 us (32%)
  waiting for transfers between devices  48.7 us (25%)
  local copies, waits for them, and re-layouts  6.03 us (3%)
    pallas_call x13, Pallas kernels, call(): pl.pallas_call(body, grid_spec=pltpu.PrefetchScalarGridSpec(num_scalar_pr...  74.7 us
    ppermute x2, starting transfers between devices, line_of_four(): end_inner = [send(after(a, side), perm=across) for a in own]  34.6 us
    ppermute x9, waiting for transfers between devices, swap(): lax.ppermute(a, axis, [(i, i ^ bit) for i in range(lax.axis_size(axis))])  19.9 us
    ppermute x1, waiting for transfers between devices, line_of_four(): from_end = send(after(in_part, mid_inner[0]), perm=inward)  18.1 us
    ppermute x4, waiting for transfers between devices, line_of_four(): end_outer = send(after(chunk, arrived[n], done[n]), perm=outward)  10.6 us
    ppermute x9, starting transfers between devices, swap(): lax.ppermute(a, axis, [(i, i ^ bit) for i in range(lax.axis_size(axis))])  5.99 us
    ppermute x1, starting transfers between devices, line_of_four(): pair = send(grad_out, perm=pairs)  5.85 us
    ppermute x4, starting transfers between devices, line_of_four(): end_outer = send(after(chunk, arrived[n], done[n]), perm=outward)  5.15 us
  transfers between devices with their start and end apart: 23, of which 11 were waited for; matrix products, arithmetic and copies ran while one was open for 0% of the time, Pallas kernels for 38%

profile of v6, /device:TPU:0, one launch (start us, length us, event | category | flops | bytes accessed | tf_op | source)
XLA Modules:
  0.0 193.6 jit_solution(7827818835108433600)
XLA Ops:
  0.6 3.2 %fusion = (bf16[512,1024]{1,0:T(8,128)(2,1)}, bf16[512,1024]{1,0:T(8,128)(2,1)}) fusion(bf16[1024,1024]{1,0:T(8,128)(2,1)} %own), kind=kLoop, calls=%fused_computation.3 | loop fusion | bytes 4194304 | tf_op jit(solution)/shard_map/slice | solution.py:379
  4.6 5.8 %collective-permute-start.8 = (bf16[1024,1024]{1,0:T(8,128)(2,1)}, bf16[1024,1024]{1,0:T(8,128)(2,1)}, u32[]{:S(2)}, u32[]{:S(2)}) collective-permute-start(bf16[1024,1024]{1,0:T(8,128)(2,1)} %own), channel_id=1, source_target_pairs={{0,4},{4,0},{8,12},{12,8},{1,5},{5,1},{9,13},{13,9},{2,6},{6,2},{1... | collective-permute-start | bytes 6291464 | tf_op jit(solution)/shard_map/ppermute | solution.py:378
  10.4 1.5 collective-permute-start.3
  12.3 1.6 copy-done.2
  14.8 1.3 input_block.1.a
  17.0 2.8 %collective-permute-done.3.rest_2_ = f32[256,256]{1,0:T(8,128)} collective-permute-done((f32[256,256]{1,0:T(8,128)}, f32[256,256]{1,0:T(8,128)}, u32[]{:S(2)}, u32[]{:S(2)}) %collective-permute-start.3) | collective-permute-done | bytes 262176 | tf_op jit(solution)/shard_map/ppermute | solution.py:421
  19.8 4.8 %collective-permute-done.4.rest_3_ = f32[256,256]{1,0:T(8,128)} collective-permute-done((f32[256,256]{1,0:T(8,128)}, f32[256,256]{1,0:T(8,128)}, u32[]{:S(2)}, u32[]{:S(2)}) %collective-permute-start.4) | collective-permute-done | bytes 262176 | tf_op jit(solution)/shard_map/ppermute | solution.py:421
  24.7 12.1 %own_block.1 = (f32[1024,3584]{1,0:T(8,128)S(1)}, bf16[3584,1024]{1,0:T(8,128)(2,1)S(1)}, f32[8,128]{1,0:T(8,128)S(1)}) custom-call(s32[5]{0:T(128)S(1)} %stack.42.where, bf16[1024,1024]{1,0:T(8,128)(2,1)S(1)} %copy-done, bf16[3584,4096]{1,0:T(8,128)(2,1)} %refs_4_.1, bf16[3584,4096]{1,0:T(8,128)(2,1)} %refs_4_.1), custom_call_target="tpu_custom_call" | custom-call | flops 1000 | bytes 1000 | tf_op jit(solution)/shard_map/own_block/pallas_call | solution.py:40
  36.8 1.3 collective-permute-start.9
  38.1 4.6 %collective-permute-start.1 = (f32[64,1024]{1,0:T(8,128)S(1)}, f32[64,1024]{1,0:T(8,128)S(1)}, u32[]{:S(2)}, u32[]{:S(2)}) collective-permute-start(f32[64,1024]{1,0:T(8,128)S(1)} %input_block.1.a), channel_id=1, source_target_pairs={{0,4},{12,8},{1,5},{13,9},{2,6},{14,10},{3,7},{15,11},{16,20},{28,... | collective-permute-start | bytes 786440 | tf_op jit(solution)/shard_map/ppermute | solution.py:382
  42.7 18.1 %collective-permute-done.1.b = f32[64,1024]{1,0:T(8,128)S(1)} collective-permute-done((f32[64,1024]{1,0:T(8,128)S(1)}, f32[64,1024]{1,0:T(8,128)S(1)}, u32[]{:S(2)}, u32[]{:S(2)}) %collective-permute-start.1) | collective-permute-done | bytes 262176 | tf_op jit(solution)/shard_map/ppermute | solution.py:382
  61.4 4.3 %collective-permute-start.7 = (bf16[512,1024]{1,0:T(8,128)(2,1)}, bf16[512,1024]{1,0:T(8,128)(2,1)S(1)}, u32[]{:S(2)}, u32[]{:S(2)}) collective-permute-start(bf16[512,1024]{1,0:T(8,128)(2,1)} %get-tuple-element.38), channel_id=1, source_target_pairs={{0,8},{12,4},{1,9},{13,5},{2,10},{14,6},{3,11},{15,7},{16,24},{28,... | collective-permute-start | bytes 3145736 | tf_op jit(solution)/shard_map/ppermute | solution.py:385
  67.8 30.3 %collective-permute-start.14 = (bf16[512,1024]{1,0:T(8,128)(2,1)S(1)}, bf16[512,1024]{1,0:T(8,128)(2,1)S(1)}, u32[]{:S(2)}, u32[]{:S(2)}) collective-permute-start(bf16[512,1024]{1,0:T(8,128)(2,1)S(1)} %copy-done.4), channel_id=1, source_target_pairs={{0,8},{12,4},{1,9},{13,5},{2,10},{14,6},{3,11},{15,7},{16,24},{28,... | collective-permute-start | bytes 3145736 | tf_op jit(solution)/shard_map/ppermute | solution.py:385
  98.7 12.9 %add_block_1.1 = (f32[1024,3584]{1,0:T(8,128)S(1)}, f32[8,128]{1,0:T(8,128)S(1)}) custom-call(s32[5]{0:T(128)S(1)} %stack.42.where, bf16[1024,1024]{1,0:T(8,128)(2,1)} %collective-permute-done.8.refs_0_, bf16[3584,4096]{1,0:T(8,128)(2,1)} %refs_4_.1, f32[1024,3584]{1,0:T(8,128)S(1)} %get-tuple-element.41.refs_2_, ...), custom_call_target="tpu_custom_call", output_to_operand_aliasing={{0}: (3, {})} | custom-call | flops 7516192768 | bytes 1000 | tf_op jit(solution)/shard_map/add_block_1/pallas_call | solution.py:40
  111.7 1.3 collective-permute-start.10
  113.0 1.3 collective-permute-start.13
  114.3 12.3 %add_block_2.1 = (f32[1024,3584]{1,0:T(8,128)S(1)}, f32[8,128]{1,0:T(8,128)S(1)}) custom-call(s32[5]{0:T(128)S(1)} %stack.42.where, bf16[512,1024]{1,0:T(8,128)(2,1)S(1)} %collective-permute-done.refs_0_, bf16[512,1024]{1,0:T(8,128)(2,1)S(1)} %collective-permute-done.11.refs_1_, ...), custom_call_target="tpu_custom_call", output_to_operand_aliasing={{0}: (6, {})} | custom-call | flops 1000 | bytes 1000 | tf_op jit(solution)/shard_map/add_block_2/pallas_call | solution.py:40
  126.7 1.7 collective-permute-done.10.outer
  129.7 7.0 %last_block.4 = (bf16[3584,1024]{1,0:T(8,128)(2,1)S(1)}, f32[1024,3584]{1,0:T(8,128)S(1)}, f32[256,64]{1,0:T(8,128)S(1)}) custom-call(s32[5]{0:T(128)S(1)} %stack.42.where, bf16[512,1024]{1,0:T(8,128)(2,1)S(1)} %collective-permute-done.7.inner, bf16[256,1024]{1,0:T(8,128)(2,1)S(1)} %collective-permute-done.10.outer, ...), custom_call_target="tpu_custom_call", output_to_operand_aliasing={{0}: (3, {}), {1}: (4, {})} | custom-call | flops 1000 | bytes 1000 | tf_op jit(solution)/shard_map/last_block/pallas_call | solution.py:40
  136.6 3.0 %collective-permute-done.13.outer = bf16[256,1024]{1,0:T(8,128)(2,1)S(1)} collective-permute-done((bf16[256,1024]{1,0:T(8,128)(2,1)S(1)}, bf16[256,1024]{1,0:T(8,128)(2,1)S(1)}, u32[]{:S(2)}, u32[]{:S(2)}) %collective-permute-start.13) | collective-permute-done | bytes 524320 | tf_op jit(solution)/shard_map/ppermute | solution.py:400
  140.9 1.3 collective-permute-start.6
  142.2 7.0 %last_block.5 = (bf16[3584,1024]{1,0:T(8,128)(2,1)S(1)}, f32[1024,3584]{1,0:T(8,128)S(1)}, f32[256,64]{1,0:T(8,128)S(1)}) custom-call(s32[5]{0:T(128)S(1)} %stack.42.where, bf16[512,1024]{1,0:T(8,128)(2,1)S(1)} %collective-permute-done.7.inner, bf16[256,1024]{1,0:T(8,128)(2,1)S(1)} %collective-permute-done.13.outer, ...), custom_call_target="tpu_custom_call", output_to_operand_aliasing={{0}: (3, {}), {1}: (4, {})} | custom-call | flops 1000 | bytes 1000 | tf_op jit(solution)/shard_map/last_block/pallas_call | solution.py:40
  149.2 1.7 collective-permute-done.15.outer
  150.9 6.9 %last_block.6 = (bf16[3584,1024]{1,0:T(8,128)(2,1)S(1)}, f32[1024,3584]{1,0:T(8,128)S(1)}, f32[256,64]{1,0:T(8,128)S(1)}) custom-call(s32[5]{0:T(128)S(1)} %stack.42.where, bf16[512,1024]{1,0:T(8,128)(2,1)S(1)} %collective-permute-done.14.inner, bf16[256,1024]{1,0:T(8,128)(2,1)S(1)} %collective-permute-done.15.outer, ...), custom_call_target="tpu_custom_call", output_to_operand_aliasing={{0}: (3, {}), {1}: (4, {})} | custom-call | flops 1000 | bytes 1000 | tf_op jit(solution)/shard_map/last_block/pallas_call | solution.py:40
  157.8 4.3 %collective-permute-done.16.outer = bf16[256,1024]{1,0:T(8,128)(2,1)S(1)} collective-permute-done((bf16[256,1024]{1,0:T(8,128)(2,1)S(1)}, bf16[256,1024]{1,0:T(8,128)(2,1)S(1)}, u32[]{:S(2)}, u32[]{:S(2)}) %collective-permute-start.16) | collective-permute-done | bytes 524320 | tf_op jit(solution)/shard_map/ppermute | solution.py:400
  162.1 7.0 %last_block.7 = (bf16[3584,1024]{1,0:T(8,128)(2,1)S(1)}, f32[1024,3584]{1,0:T(8,128)S(1)}, f32[256,64]{1,0:T(8,128)S(1)}) custom-call(s32[5]{0:T(128)S(1)} %stack.42.where, bf16[512,1024]{1,0:T(8,128)(2,1)S(1)} %collective-permute-done.14.inner, bf16[256,1024]{1,0:T(8,128)(2,1)S(1)} %collective-permute-done.16.outer, ...), custom_call_target="tpu_custom_call", output_to_operand_aliasing={{0}: (3, {}), {1}: (4, {})} | custom-call | flops 1000 | bytes 1000 | tf_op jit(solution)/shard_map/last_block/pallas_call | solution.py:40
  170.2 3.9 %collective-permute-done.17 = f32[2,4096]{1,0:T(2,128)S(1)} collective-permute-done((f32[2,4096]{1,0:T(2,128)S(1)}, f32[2,4096]{1,0:T(2,128)S(1)}, u32[]{:S(2)}, u32[]{:S(2)}) %collective-permute-start.17) | collective-permute-done | bytes 32800 | tf_op jit(solution)/shard_map/ppermute | solution.py:421
  175.3 3.7 %collective-permute-done.18 = f32[2,4096]{1,0:T(2,128)S(1)} collective-permute-done((f32[2,4096]{1,0:T(2,128)S(1)}, f32[2,4096]{1,0:T(2,128)S(1)}, u32[]{:S(2)}, u32[]{:S(2)}) %collective-permute-start.18) | collective-permute-done | bytes 32800 | tf_op jit(solution)/shard_map/ppermute | solution.py:421
  180.3 1.6 collective-permute-start.20
  181.9 2.6 %scores.1 = f32[2,256]{1,0:T(2,128)S(1)} custom-call(s32[4]{0:T(128)S(1)} %add_add_fusion.order, f32[2,4096]{1,0:T(2,128)S(1)} %add.32.grads, f32[256,256]{1,0:T(8,128)} %rest_0_.1, f32[256,256]{1,0:T(8,128)} %copy-done.5, f32[256,256]{1,0:T(8,128)} %collective-permute-done.3.rest_2_, f32[256,256]{1,0:T(8,128)} %collective-permute-done.4.rest_3_), custom_call_target="tpu_custom_call" | custom-call | flops 1000 | bytes 1000 | tf_op jit(solution)/shard_map/scores/pallas_call | solution.py:40
  184.7 3.5 %collective-permute-done.21 = f32[2,256]{1,0:T(2,128)S(1)} collective-permute-done((f32[2,256]{1,0:T(2,128)S(1)}, f32[2,256]{1,0:T(2,128)S(1)}, u32[]{:S(2)}, u32[]{:S(2)}) %collective-permute-start.21) | collective-permute-done | bytes 2080 | tf_op jit(solution)/shard_map/ppermute | solution.py:421
  189.4 3.6 %hessian_update.1 = f32[256,4096]{1,0:T(8,128)} custom-call(s32[1]{0:T(128)} %bitcast.row, f32[8,4096]{1,0:T(8,128)S(1)} %pad_maximum_fusion.grads.mine, f32[8,4096]{1,0:T(8,128)S(1)} %pad_maximum_fusion.grads.mine, f32[256,4096]{1,0:T(8,128)} %hessian.1), custom_call_target="tpu_custom_call" | custom-call | flops 1000 | bytes 1000 | tf_op jit(solution)/shard_map/hessian_update/pallas_call | solution.py:40
  (51 shorter events, 14.4 us)
Async XLA Ops:
  0.6 24.0 %copy-start = (bf16[1024,1024]{1,0:T(8,128)(2,1)S(1)}, bf16[1024,1024]{1,0:T(8,128)(2,1)}, u32[]{:S(2)}) copy-start(bf16[1024,1024]{1,0:T(8,128)(2,1)} %own) | copy-start | bytes 6291460
  3.8 32.9 %collective-permute-start = (bf16[512,1024]{1,0:T(8,128)(2,1)}, bf16[512,1024]{1,0:T(8,128)(2,1)S(1)}, u32[]{:S(2)}, u32[]{:S(2)}) collective-permute-start(bf16[512,1024]{1,0:T(8,128)(2,1)} %get-tuple-element.38), channel_id=1, source_target_pairs={{4,8},{8,4},{5,9},{9,5},{6,10},{10,6},{7,11},{11,7},{20,24},{24,20... | collective-permute-start | bytes 3145736 | tf_op jit(solution)/shard_map/ppermute | solution.py:380
  4.6 94.1 %collective-permute-start.8 = (bf16[1024,1024]{1,0:T(8,128)(2,1)}, bf16[1024,1024]{1,0:T(8,128)(2,1)}, u32[]{:S(2)}, u32[]{:S(2)}) collective-permute-start(bf16[1024,1024]{1,0:T(8,128)(2,1)} %own), channel_id=1, source_target_pairs={{0,4},{4,0},{8,12},{12,8},{1,5},{5,1},{9,13},{13,9},{2,6},{6,2},{1... | collective-permute-start | bytes 6291464 | tf_op jit(solution)/shard_map/ppermute | solution.py:378
  10.4 5.7 %collective-permute-start.2 = (f32[256,256]{1,0:T(8,128)}, f32[256,256]{1,0:T(8,128)S(1)}, u32[]{:S(2)}, u32[]{:S(2)}) collective-permute-start(f32[256,256]{1,0:T(8,128)} %rest_0_.1), channel_id=1, source_target_pairs={{0,1},{1,0},{2,3},{3,2},{4,5},{5,4},{6,7},{7,6},{8,9},{9,8},{10,11... | collective-permute-start | bytes 786440 | tf_op jit(solution)/shard_map/ppermute | solution.py:421
  10.4 9.4 %collective-permute-start.3 = (f32[256,256]{1,0:T(8,128)}, f32[256,256]{1,0:T(8,128)}, u32[]{:S(2)}, u32[]{:S(2)}) collective-permute-start(f32[256,256]{1,0:T(8,128)} %rest_0_.1), channel_id=1, source_target_pairs={{0,2},{1,3},{2,0},{3,1},{4,6},{5,7},{6,4},{7,5},{8,10},{9,11},{10,... | collective-permute-start | bytes 786440 | tf_op jit(solution)/shard_map/ppermute | solution.py:421
  11.9 12.8 %collective-permute-start.4 = (f32[256,256]{1,0:T(8,128)}, f32[256,256]{1,0:T(8,128)}, u32[]{:S(2)}, u32[]{:S(2)}) collective-permute-start(f32[256,256]{1,0:T(8,128)} %rest_0_.1), channel_id=1, source_target_pairs={{0,3},{1,2},{2,1},{3,0},{4,7},{5,6},{6,5},{7,4},{8,11},{9,10},{10,... | collective-permute-start | bytes 786440 | tf_op jit(solution)/shard_map/ppermute | solution.py:421
  12.3 1.6 copy-start.2
  13.9 0.9 copy-start.3
  16.1 20.6 %copy-start.5 = (f32[256,256]{1,0:T(8,128)}, f32[256,256]{1,0:T(8,128)S(1)}, u32[]{:S(2)}) copy-start(f32[256,256]{1,0:T(8,128)S(1)} %collective-permute-done.2.rest_1_) | copy-start | bytes 786436
  16.2 51.6 %copy-start.4 = (bf16[512,1024]{1,0:T(8,128)(2,1)S(1)}, bf16[512,1024]{1,0:T(8,128)(2,1)}, u32[]{:S(2)}) copy-start(bf16[512,1024]{1,0:T(8,128)(2,1)} %get-tuple-element.54) | copy-start | bytes 3145732
  16.2 50.3 %collective-permute-start.11 = (bf16[512,1024]{1,0:T(8,128)(2,1)}, bf16[512,1024]{1,0:T(8,128)(2,1)S(1)}, u32[]{:S(2)}, u32[]{:S(2)}) collective-permute-start(bf16[512,1024]{1,0:T(8,128)(2,1)} %get-tuple-element.54), channel_id=1, source_target_pairs={{4,8},{8,4},{5,9},{9,5},{6,10},{10,6},{7,11},{11,7},{20,24},{24,20... | collective-permute-start | bytes 3145736 | tf_op jit(solution)/shard_map/ppermute | solution.py:380
  36.8 61.9 %collective-permute-start.9 = (bf16[512,1024]{1,0:T(8,128)(2,1)S(1)}, bf16[512,1024]{1,0:T(8,128)(2,1)S(1)}, u32[]{:S(2)}, u32[]{:S(2)}) collective-permute-start(bf16[512,1024]{1,0:T(8,128)(2,1)S(1)} %collective-permute-done.refs_0_), channel_id=1, source_target_pairs={{4,0},{8,12},{5,1},{9,13},{6,2},{10,14},{7,3},{11,15},{20,16},{24,... | collective-permute-start | bytes 3145736 | tf_op jit(solution)/shard_map/ppermute | solution.py:386
  38.1 22.8 %collective-permute-start.1 = (f32[64,1024]{1,0:T(8,128)S(1)}, f32[64,1024]{1,0:T(8,128)S(1)}, u32[]{:S(2)}, u32[]{:S(2)}) collective-permute-start(f32[64,1024]{1,0:T(8,128)S(1)} %input_block.1.a), channel_id=1, source_target_pairs={{0,4},{12,8},{1,5},{13,9},{2,6},{14,10},{3,7},{15,11},{16,20},{28,... | collective-permute-start | bytes 786440 | tf_op jit(solution)/shard_map/ppermute | solution.py:382
  61.4 50.2 %collective-permute-start.7 = (bf16[512,1024]{1,0:T(8,128)(2,1)}, bf16[512,1024]{1,0:T(8,128)(2,1)S(1)}, u32[]{:S(2)}, u32[]{:S(2)}) collective-permute-start(bf16[512,1024]{1,0:T(8,128)(2,1)} %get-tuple-element.38), channel_id=1, source_target_pairs={{0,8},{12,4},{1,9},{13,5},{2,10},{14,6},{3,11},{15,7},{16,24},{28,... | collective-permute-start | bytes 3145736 | tf_op jit(solution)/shard_map/ppermute | solution.py:385
  65.8 2.0 %collective-permute-start.5 = (f32[64,1024]{1,0:T(8,128)S(1)}, f32[64,1024]{1,0:T(8,128)S(1)}, u32[]{:S(2)}, u32[]{:S(2)}) collective-permute-start(f32[64,1024]{1,0:T(8,128)S(1)} %side.1.a), channel_id=1, source_target_pairs={{4,8},{8,4},{5,9},{9,5},{6,10},{10,6},{7,11},{11,7},{20,24},{24,20... | collective-permute-start | bytes 786440 | tf_op jit(solution)/shard_map/ppermute | solution.py:387
  66.5 47.8 %collective-permute-start.12 = (bf16[512,1024]{1,0:T(8,128)(2,1)S(1)}, bf16[512,1024]{1,0:T(8,128)(2,1)S(1)}, u32[]{:S(2)}, u32[]{:S(2)}) collective-permute-start(bf16[512,1024]{1,0:T(8,128)(2,1)S(1)} %collective-permute-done.11.refs_1_), channel_id=1, source_target_pairs={{4,0},{8,12},{5,1},{9,13},{6,2},{10,14},{7,3},{11,15},{20,16},{24,... | collective-permute-start | bytes 3145736 | tf_op jit(solution)/shard_map/ppermute | solution.py:386
  67.8 58.8 %collective-permute-start.14 = (bf16[512,1024]{1,0:T(8,128)(2,1)S(1)}, bf16[512,1024]{1,0:T(8,128)(2,1)S(1)}, u32[]{:S(2)}, u32[]{:S(2)}) collective-permute-start(bf16[512,1024]{1,0:T(8,128)(2,1)S(1)} %copy-done.4), channel_id=1, source_target_pairs={{0,8},{12,4},{1,9},{13,5},{2,10},{14,6},{3,11},{15,7},{16,24},{28,... | collective-permute-start | bytes 3145736 | tf_op jit(solution)/shard_map/ppermute | solution.py:385
  111.7 16.7 %collective-permute-start.10 = (bf16[256,1024]{1,0:T(8,128)(2,1)S(1)}, bf16[256,1024]{1,0:T(8,128)(2,1)S(1)}, u32[]{:S(2)}, u32[]{:S(2)}) collective-permute-start(bf16[256,1024]{1,0:T(8,128)(2,1)S(1)} %get-tuple-element.43), channel_id=1, source_target_pairs={{4,0},{8,12},{5,1},{9,13},{6,2},{10,14},{7,3},{11,15},{20,16},{24,... | collective-permute-start | bytes 1572872 | tf_op jit(solution)/shard_map/ppermute | solution.py:400
  113.0 26.7 %collective-permute-start.13 = (bf16[256,1024]{1,0:T(8,128)(2,1)S(1)}, bf16[256,1024]{1,0:T(8,128)(2,1)S(1)}, u32[]{:S(2)}, u32[]{:S(2)}) collective-permute-start(bf16[256,1024]{1,0:T(8,128)(2,1)S(1)} %get-tuple-element.50), channel_id=1, source_target_pairs={{4,0},{8,12},{5,1},{9,13},{6,2},{10,14},{7,3},{11,15},{20,16},{24,... | collective-permute-start | bytes 1572872 | tf_op jit(solution)/shard_map/ppermute | solution.py:400
  114.3 15.4 %copy-start.1 = (bf16[3584,64]{0,1:T(8,128)(2,1)S(1)}, bf16[3584,64]{0,1:T(8,128)(2,1)}, u32[]{:S(2)}) copy-start(bf16[3584,64]{0,1:T(8,128)(2,1)} %param.13) | copy-start | bytes 1376260
  128.4 22.5 %collective-permute-start.15 = (bf16[256,1024]{1,0:T(8,128)(2,1)S(1)}, bf16[256,1024]{1,0:T(8,128)(2,1)S(1)}, u32[]{:S(2)}, u32[]{:S(2)}) collective-permute-start(bf16[256,1024]{1,0:T(8,128)(2,1)S(1)} %get-tuple-element.55), channel_id=1, source_target_pairs={{4,0},{8,12},{5,1},{9,13},{6,2},{10,14},{7,3},{11,15},{20,16},{24,... | collective-permute-start | bytes 1572872 | tf_op jit(solution)/shard_map/ppermute | solution.py:400
  139.6 22.5 %collective-permute-start.16 = (bf16[256,1024]{1,0:T(8,128)(2,1)S(1)}, bf16[256,1024]{1,0:T(8,128)(2,1)S(1)}, u32[]{:S(2)}, u32[]{:S(2)}) collective-permute-start(bf16[256,1024]{1,0:T(8,128)(2,1)S(1)} %get-tuple-element.59), channel_id=1, source_target_pairs={{4,0},{8,12},{5,1},{9,13},{6,2},{10,14},{7,3},{11,15},{20,16},{24,... | collective-permute-start | bytes 1572872 | tf_op jit(solution)/shard_map/ppermute | solution.py:400
  140.9 28.1 %collective-permute-start.6 = (f32[64,1024]{1,0:T(8,128)S(1)}, f32[64,1024]{1,0:T(8,128)S(1)}, u32[]{:S(2)}, u32[]{:S(2)}) collective-permute-start(f32[64,1024]{1,0:T(8,128)S(1)} %total.1), channel_id=1, source_target_pairs={{4,0},{8,12},{5,1},{9,13},{6,2},{10,14},{7,3},{11,15},{20,16},{24,... | collective-permute-start | bytes 786440 | tf_op jit(solution)/shard_map/ppermute | solution.py:388
  170.1 4.0 %collective-permute-start.17 = (f32[2,4096]{1,0:T(2,128)S(1)}, f32[2,4096]{1,0:T(2,128)S(1)}, u32[]{:S(2)}, u32[]{:S(2)}) collective-permute-start(f32[2,4096]{1,0:T(2,128)S(1)} %reshape.11), channel_id=1, source_target_pairs={{0,4},{4,0},{8,12},{12,8},{1,5},{5,1},{9,13},{13,9},{2,6},{6,2},{1... | collective-permute-start | bytes 98312 | tf_op jit(solution)/shard_map/ppermute | solution.py:421
  174.1 4.9 %collective-permute-start.18 = (f32[2,4096]{1,0:T(2,128)S(1)}, f32[2,4096]{1,0:T(2,128)S(1)}, u32[]{:S(2)}, u32[]{:S(2)}) collective-permute-start(f32[2,4096]{1,0:T(2,128)S(1)} %add.31), channel_id=1, source_target_pairs={{0,8},{4,12},{8,0},{12,4},{1,9},{5,13},{9,1},{13,5},{2,10},{6,14},... | collective-permute-start | bytes 98312 | tf_op jit(solution)/shard_map/ppermute | solution.py:421
  179.0 1.3 collective-permute-start.19
  180.3 9.0 %collective-permute-start.20 = (f32[4,4096]{1,0:T(4,128)S(1)}, f32[4,4096]{1,0:T(4,128)S(1)}, u32[]{:S(2)}, u32[]{:S(2)}) collective-permute-start(f32[4,4096]{1,0:T(4,128)S(1)} %pad_maximum_fusion.1), channel_id=1, source_target_pairs={{0,2},{1,3},{2,0},{3,1},{4,6},{5,7},{6,4},{7,5},{8,10},{9,11},{10,... | collective-permute-start | bytes 196616 | tf_op jit(solution)/shard_map/ppermute | solution.py:421
  184.6 3.6 %collective-permute-start.21 = (f32[2,256]{1,0:T(2,128)S(1)}, f32[2,256]{1,0:T(2,128)S(1)}, u32[]{:S(2)}, u32[]{:S(2)}) collective-permute-start(f32[2,256]{1,0:T(2,128)S(1)} %scores.1), channel_id=1, source_target_pairs={{0,4},{4,0},{8,12},{12,8},{1,5},{5,1},{9,13},{13,9},{2,6},{6,2},{1... | collective-permute-start | bytes 6152 | tf_op jit(solution)/shard_map/ppermute | solution.py:421
  188.2 4.8 %collective-permute-start.22 = (f32[2,256]{1,0:T(2,128)S(1)}, f32[2,256]{1,0:T(2,128)S(1)}, u32[]{:S(2)}, u32[]{:S(2)}) collective-permute-start(f32[2,256]{1,0:T(2,128)S(1)} %add.35), channel_id=1, source_target_pairs={{0,8},{4,12},{8,0},{12,4},{1,9},{5,13},{9,1},{13,5},{2,10},{6,14},... | collective-permute-start | bytes 6152 | tf_op jit(solution)/shard_map/ppermute | solution.py:421

commit v7 on v6

--- a/solution.py
+++ b/solution.py
@@ -90,7 +90,7 @@
 def own_body(where, own, w, w_last, acc, kept, token):
     here = tile_rows(pl.program_id(0))
     token[...] = jnp.zeros_like(token)
-    kept[here, :] = w_last[...]
+    kept[:, here] = w_last[...].T
     acc[:, here] = dot_nt(own[...], w[...])
 
 
@@ -111,7 +111,7 @@
         [INSIDE, INSIDE, pl.BlockSpec((8, 128), lambda j, where: (0, 0))],
         [
             pltpu.VMEM((tokens, hidden), jnp.float32),
-            pltpu.VMEM((hidden, feats), w.dtype),
+            pltpu.VMEM((feats, hidden), w.dtype),
             jax.ShapeDtypeStruct((8, 128), jnp.float32),
         ],
         [],
@@ -161,46 +161,55 @@
     )
 
 
-def last_body(start, where, inner, outer, kept, old, gate, po_t, token, kept_same, old_same, right, block):
+def last_body(
+    start, inner_at, where, inner, outer, kept, old, gate, po_t, _, kept_same, old_same, right, gates, po, gate_sems, po_sem
+):
     size = outer.shape[0]
-    step = pl.program_id(0)
-
-    @pl.when(step == 0)
-    def _():
-        block[...] = select(where, inner, outer)
-        right[...] = jnp.zeros_like(right)
-
-    here = tile_rows(step)
-    hidden_grad = old[pl.ds(start, size), here] + dot_nt(block[...], kept[here, :])
-    up_grad = (hidden_grad * silu(gate[...].astype(jnp.float32))).astype(jnp.bfloat16)
-    right[...] += dot_nt(up_grad, po_t[...])
+    hidden = kept.shape[1]
+    tokens = pl.ds(start, size)
+    spans = [pl.ds(t * TILE, TILE) for t in range(hidden // TILE)]
+    po_read = pltpu.make_async_copy(po_t, po, po_sem)
+    reads = [
+        pltpu.make_async_copy(gate.at[tokens, span], gates.at[t], gate_sems.at[t]) for t, span in enumerate(spans)
+    ]
+    reads[0].start()
+    po_read.start()
+    for read in reads[1:]:
+        read.start()
+    block = select(where, inner.at[pl.ds(inner_at, size)], outer)
+    total = jnp.zeros((size, PROJ), jnp.float32)
+    for t, span in enumerate(spans):
+        hidden_grad = old[tokens, span] + dot(block, kept[:, span])
+        reads[t].wait()
+        up_grad = (hidden_grad * silu(gates[t].astype(jnp.float32))).astype(jnp.bfloat16)
+        if t == 0:
+            po_read.wait()
+        total = total + dot_nt(up_grad, po[:, span])
+    right[...] = total
 
 
 def last_block(where, inner, inner_at, outer, start, kept, old, gate, po_t, token):
-    size, feats = outer.shape
-    chunk, inner_chunk = start // size, inner_at // size
+    size = outer.shape[0]
+    tiles = kept.shape[1] // TILE
     return call(
-        functools.partial(last_body, start),
+        functools.partial(last_body, start, inner_at),
         "last_block",
         where,
-        (kept.shape[0] // TILE,),
-        (inner, outer, kept, old, pltpu.with_memory_space_constraint(gate, pltpu.HBM), po_t, token),
-        [
-            pl.BlockSpec((size, feats), lambda j, where: (inner_chunk, 0), pipeline_mode=pl.Buffered(1)),
-            fixed(outer.shape),
-            INSIDE,
-            INSIDE,
-            pl.BlockSpec((size, TILE), lambda j, where: (chunk, j)),
-            pl.BlockSpec((PROJ, TILE), lambda j, where: (0, j)),
-            ANYWHERE,
-        ],
+        (1,),
+        (inner, outer, kept, old, gate, po_t, token),
+        [INSIDE, INSIDE, INSIDE, INSIDE, OUTSIDE, ANYWHERE, ANYWHERE],
         [INSIDE, INSIDE, pl.BlockSpec((size, PROJ), lambda j, where: (0, 0))],
         [
             pltpu.VMEM(kept.shape, kept.dtype),
             pltpu.VMEM(old.shape, old.dtype),
             jax.ShapeDtypeStruct((size, PROJ), jnp.float32),
         ],
-        [pltpu.VMEM((size, feats), outer.dtype)],
+        [
+            pltpu.VMEM((tiles, size, TILE), gate.dtype),
+            pltpu.VMEM(po_t.shape, po_t.dtype),
+            pltpu.SemaphoreType.DMA((tiles,)),
+            pltpu.SemaphoreType.DMA,
+        ],
         LIMIT,
         aliases={3: 0, 4: 1},
     )
@@ -365,7 +374,6 @@
     inner = [(1, 2), (2, 1)]
     outward = [(1, 0), (2, 3)]
     inward = [(0, 1), (3, 2)]
-    across = [(0, 2), (3, 1)]
     tokens = grad_out.shape[0]
     z = lax.axis_index("tensor")
     low = z < 2
@@ -381,9 +389,9 @@
     in_part = input_block(where, inputs, proj_in.T)
     from_end = send(after(in_part, mid_inner[0]), perm=inward)
     acc, kept, begun = own_block(where, after(grad_out, in_part, *early), w_down)
-    side = small_kernel(sum_body, "side", where, in_part, after(from_end, begun))
-    end_inner = [send(after(a, side), perm=across) for a in own]
     mid_outer = [send(after(a, begun), perm=outward) for a in mid_inner]
+    end_inner = [send(pair[half], perm=inner) for half in halves]
+    side = small_kernel(sum_body, "side", where, in_part, after(from_end, begun, pair))
     total = small_kernel(sum_body, "total", where, side, send(side, perm=inner))
     sent = send(total, perm=outward)
 

time: 195 us -> 173 us (0.89)
  starting transfers between devices: 62.4 us -> 32.5 us
  waiting for transfers between devices: 48.7 us -> 61.5 us
  Pallas kernels: 74.7 us -> 69 us
    ppermute x2, starting transfers between devices: 34.6 us -> 1.44 us  [line_of_four(): end_inner = [send(pair[half], perm=inner) for half in halves]]
    ppermute x1, waiting for transfers between devices: 0.01 us -> 15.4 us  [line_of_four(): pair = send(grad_out, perm=pairs)]
    ppermute x1, waiting for transfers between devices: 18.1 us -> 2.83 us  [line_of_four(): from_end = send(after(in_part, mid_inner[0]), perm=inward)]
    ppermute x2, waiting for transfers between devices: 0.01 us -> 14.3 us  [line_of_four(): mid_outer = [send(after(a, begun), perm=outward) for a in mid_inner]]
    pallas_call x13, Pallas kernels: 74.7 us -> 69 us  [call(): pl.pallas_call(body, grid_spec=pltpu.PrefetchScalarGridSpec(num_scalar_pr...]
    ppermute x9, starting transfers between devices: 5.99 us -> 10.8 us  [swap(): lax.ppermute(a, axis, [(i, i ^ bit) for i in range(lax.axis_size(axis))])]
    ppermute x9, waiting for transfers between devices: 19.9 us -> 17 us  [swap(): lax.ppermute(a, axis, [(i, i ^ bit) for i in range(lax.axis_size(axis))])]
    ppermute x1, starting transfers between devices: 5.85 us -> 3.09 us  [line_of_four(): pair = send(grad_out, perm=pairs)]
  transfers between devices with their start and end apart: 23 -> 23, of which waited for: 11 -> 13; matrix products, arithmetic and copies ran while one was open for 0% -> 3% of each run, Pallas kernels for 38% -> 39%
where the time goes in v7:
time: 173 us; the launch traced here: 172 us
  Pallas kernels  69 us (40%)
  waiting for transfers between devices  61.5 us (36%)
  starting transfers between devices  32.5 us (19%)
  local copies, waits for them, and re-layouts  7.58 us (4%)
    pallas_call x13, Pallas kernels, call(): pl.pallas_call(body, grid_spec=pltpu.PrefetchScalarGridSpec(num_scalar_pr...  69 us
    ppermute x9, waiting for transfers between devices, swap(): lax.ppermute(a, axis, [(i, i ^ bit) for i in range(lax.axis_size(axis))])  17 us
    ppermute x1, waiting for transfers between devices, line_of_four(): pair = send(grad_out, perm=pairs)  15.4 us
    ppermute x2, waiting for transfers between devices, line_of_four(): mid_outer = [send(after(a, begun), perm=outward) for a in mid_inner]  14.3 us
    ppermute x4, waiting for transfers between devices, line_of_four(): end_outer = send(after(chunk, arrived[n], done[n]), perm=outward)  12 us
    ppermute x9, starting transfers between devices, swap(): lax.ppermute(a, axis, [(i, i ^ bit) for i in range(lax.axis_size(axis))])  10.8 us
    ppermute x1, starting transfers between devices, line_of_four(): from_end = send(after(in_part, mid_inner[0]), perm=inward)  5.83 us
    ppermute x4, starting transfers between devices, line_of_four(): end_outer = send(after(chunk, arrived[n], done[n]), perm=outward)  5.16 us
  transfers between devices with their start and end apart: 23, of which 13 were waited for; matrix products, arithmetic and copies ran while one was open for 3% of the time, Pallas kernels for 39%

profile of v7, /device:TPU:0, one launch (start us, length us, event | category | flops | bytes accessed | tf_op | source)
XLA Modules:
  0.0 172.4 jit_solution(4598334390726935541)
XLA Ops:
  0.6 3.1 %collective-permute-start.5 = (bf16[1024,1024]{1,0:T(8,128)(2,1)}, bf16[1024,1024]{1,0:T(8,128)(2,1)}, u32[]{:S(2)}, u32[]{:S(2)}) collective-permute-start(bf16[1024,1024]{1,0:T(8,128)(2,1)} %own), channel_id=1, source_target_pairs={{0,4},{4,0},{8,12},{12,8},{1,5},{5,1},{9,13},{13,9},{2,6},{6,2},{1... | collective-permute-start | bytes 6291464 | tf_op jit(solution)/shard_map/ppermute | solution.py:386
  3.7 3.0 %fusion.1 = (bf16[512,1024]{1,0:T(8,128)(2,1)}, bf16[512,1024]{1,0:T(8,128)(2,1)}) fusion(bf16[1024,1024]{1,0:T(8,128)(2,1)} %own), kind=kLoop, calls=%fused_computation.4 | loop fusion | bytes 4194304 | tf_op jit(solution)/shard_map/slice | solution.py:387
  7.6 1.6 collective-permute-start.3
  9.5 1.6 copy-done.2
  12.0 1.3 input_block.1.a
  14.1 3.0 %collective-permute-done.3.rest_2_ = f32[256,256]{1,0:T(8,128)} collective-permute-done((f32[256,256]{1,0:T(8,128)}, f32[256,256]{1,0:T(8,128)}, u32[]{:S(2)}, u32[]{:S(2)}) %collective-permute-start.3) | collective-permute-done | bytes 262176 | tf_op jit(solution)/shard_map/ppermute | solution.py:429
  17.1 4.7 %collective-permute-done.4.rest_3_ = f32[256,256]{1,0:T(8,128)} collective-permute-done((f32[256,256]{1,0:T(8,128)}, f32[256,256]{1,0:T(8,128)}, u32[]{:S(2)}, u32[]{:S(2)}) %collective-permute-start.4) | collective-permute-done | bytes 262176 | tf_op jit(solution)/shard_map/ppermute | solution.py:429
  21.8 12.0 %own_block.1 = (f32[1024,3584]{1,0:T(8,128)S(1)}, bf16[1024,3584]{1,0:T(8,128)(2,1)S(1)}, f32[8,128]{1,0:T(8,128)S(1)}) custom-call(s32[5]{0:T(128)S(1)} %stack.42.where, bf16[1024,1024]{1,0:T(8,128)(2,1)S(1)} %copy-done, bf16[3584,4096]{1,0:T(8,128)(2,1)} %refs_4_.1, bf16[3584,4096]{1,0:T(8,128)(2,1)} %refs_4_.1), custom_call_target="tpu_custom_call" | custom-call | flops 1000 | bytes 1000 | tf_op jit(solution)/shard_map/own_block/pallas_call | solution.py:40
  35.1 15.4 %collective-permute-done.5.refs_0_ = bf16[1024,1024]{1,0:T(8,128)(2,1)} collective-permute-done((bf16[1024,1024]{1,0:T(8,128)(2,1)}, bf16[1024,1024]{1,0:T(8,128)(2,1)}, u32[]{:S(2)}, u32[]{:S(2)}) %collective-permute-start.5) | collective-permute-done | bytes 2097184 | tf_op jit(solution)/shard_map/ppermute | solution.py:386
  50.5 1.7 fusion
  53.0 5.8 %collective-permute-start.1 = (f32[64,1024]{1,0:T(8,128)S(1)}, f32[64,1024]{1,0:T(8,128)S(1)}, u32[]{:S(2)}, u32[]{:S(2)}) collective-permute-start(f32[64,1024]{1,0:T(8,128)S(1)} %input_block.1.a), channel_id=1, source_target_pairs={{0,4},{12,8},{1,5},{13,9},{2,6},{14,10},{3,7},{15,11},{16,20},{28,... | collective-permute-start | bytes 786440 | tf_op jit(solution)/shard_map/ppermute | solution.py:390
  60.1 2.8 %collective-permute-done.1.b = f32[64,1024]{1,0:T(8,128)S(1)} collective-permute-done((f32[64,1024]{1,0:T(8,128)S(1)}, f32[64,1024]{1,0:T(8,128)S(1)}, u32[]{:S(2)}, u32[]{:S(2)}) %collective-permute-start.1) | collective-permute-done | bytes 262176 | tf_op jit(solution)/shard_map/ppermute | solution.py:390
  64.2 8.7 %collective-permute-done.9.refs_2_ = bf16[512,1024]{1,0:T(8,128)(2,1)S(1)} collective-permute-done((bf16[512,1024]{1,0:T(8,128)(2,1)S(1)}, bf16[512,1024]{1,0:T(8,128)(2,1)S(1)}, u32[]{:S(2)}, u32[]{:S(2)}) %collective-permute-start.9) | collective-permute-done | bytes 1048608 | tf_op jit(solution)/shard_map/ppermute | solution.py:392
  73.6 12.9 %add_block_1.1 = (f32[1024,3584]{1,0:T(8,128)S(1)}, f32[8,128]{1,0:T(8,128)S(1)}) custom-call(s32[5]{0:T(128)S(1)} %stack.42.where, bf16[1024,1024]{1,0:T(8,128)(2,1)} %collective-permute-done.5.refs_0_, bf16[3584,4096]{1,0:T(8,128)(2,1)} %refs_4_.1, f32[1024,3584]{1,0:T(8,128)S(1)} %get-tuple-element.38.refs_2_, ...), custom_call_target="tpu_custom_call", output_to_operand_aliasing={{0}: (3, {})} | custom-call | flops 7516192768 | bytes 1000 | tf_op jit(solution)/shard_map/add_block_1/pallas_call | solution.py:40
  89.8 5.6 %collective-permute-done.12.refs_3_ = bf16[512,1024]{1,0:T(8,128)(2,1)S(1)} collective-permute-done((bf16[512,1024]{1,0:T(8,128)(2,1)S(1)}, bf16[512,1024]{1,0:T(8,128)(2,1)S(1)}, u32[]{:S(2)}, u32[]{:S(2)}) %collective-permute-start.12) | collective-permute-done | bytes 1048608 | tf_op jit(solution)/shard_map/ppermute | solution.py:392
  95.3 12.3 %add_block_2.1 = (f32[1024,3584]{1,0:T(8,128)S(1)}, f32[8,128]{1,0:T(8,128)S(1)}) custom-call(s32[5]{0:T(128)S(1)} %stack.42.where, bf16[512,1024]{1,0:T(8,128)(2,1)S(1)} %collective-permute-done.refs_0_, bf16[512,1024]{1,0:T(8,128)(2,1)S(1)} %collective-permute-done.11.refs_1_, ...), custom_call_target="tpu_custom_call", output_to_operand_aliasing={{0}: (6, {})} | custom-call | flops 1000 | bytes 1000 | tf_op jit(solution)/shard_map/add_block_2/pallas_call | solution.py:40
  109.0 5.5 %last_block.4 = (bf16[1024,3584]{1,0:T(8,128)(2,1)S(1)}, f32[1024,3584]{1,0:T(8,128)S(1)}, f32[256,64]{1,0:T(8,128)S(1)}) custom-call(s32[5]{0:T(128)S(1)} %stack.42.where, bf16[512,1024]{1,0:T(8,128)(2,1)S(1)} %collective-permute-done.8.inner, bf16[256,1024]{1,0:T(8,128)(2,1)S(1)} %collective-permute-done.10.outer, ...), custom_call_target="tpu_custom_call", output_to_operand_aliasing={{0}: (3, {}), {1}: (4, {})} | custom-call | flops 1000 | bytes 1000 | tf_op jit(solution)/shard_map/last_block/pallas_call | solution.py:40
  114.5 3.3 %collective-permute-done.13.outer = bf16[256,1024]{1,0:T(8,128)(2,1)S(1)} collective-permute-done((bf16[256,1024]{1,0:T(8,128)(2,1)S(1)}, bf16[256,1024]{1,0:T(8,128)(2,1)S(1)}, u32[]{:S(2)}, u32[]{:S(2)}) %collective-permute-start.13) | collective-permute-done | bytes 524320 | tf_op jit(solution)/shard_map/ppermute | solution.py:408
  119.1 1.5 collective-permute-start.7
  120.6 5.5 %last_block.5 = (bf16[1024,3584]{1,0:T(8,128)(2,1)S(1)}, f32[1024,3584]{1,0:T(8,128)S(1)}, f32[256,64]{1,0:T(8,128)S(1)}) custom-call(s32[5]{0:T(128)S(1)} %stack.42.where, bf16[512,1024]{1,0:T(8,128)(2,1)S(1)} %collective-permute-done.8.inner, bf16[256,1024]{1,0:T(8,128)(2,1)S(1)} %collective-permute-done.13.outer, ...), custom_call_target="tpu_custom_call", output_to_operand_aliasing={{0}: (3, {}), {1}: (4, {})} | custom-call | flops 1000 | bytes 1000 | tf_op jit(solution)/shard_map/last_block/pallas_call | solution.py:40
  126.1 3.0 %collective-permute-done.15.outer = bf16[256,1024]{1,0:T(8,128)(2,1)S(1)} collective-permute-done((bf16[256,1024]{1,0:T(8,128)(2,1)S(1)}, bf16[256,1024]{1,0:T(8,128)(2,1)S(1)}, u32[]{:S(2)}, u32[]{:S(2)}) %collective-permute-start.15) | collective-permute-done | bytes 524320 | tf_op jit(solution)/shard_map/ppermute | solution.py:408
  129.0 5.5 %last_block.6 = (bf16[1024,3584]{1,0:T(8,128)(2,1)S(1)}, f32[1024,3584]{1,0:T(8,128)S(1)}, f32[256,64]{1,0:T(8,128)S(1)}) custom-call(s32[5]{0:T(128)S(1)} %stack.42.where, bf16[512,1024]{1,0:T(8,128)(2,1)S(1)} %collective-permute-done.14.inner, bf16[256,1024]{1,0:T(8,128)(2,1)S(1)} %collective-permute-done.15.outer, ...), custom_call_target="tpu_custom_call", output_to_operand_aliasing={{0}: (3, {}), {1}: (4, {})} | custom-call | flops 1000 | bytes 1000 | tf_op jit(solution)/shard_map/last_block/pallas_call | solution.py:40
  134.5 5.7 %collective-permute-done.16.outer = bf16[256,1024]{1,0:T(8,128)(2,1)S(1)} collective-permute-done((bf16[256,1024]{1,0:T(8,128)(2,1)S(1)}, bf16[256,1024]{1,0:T(8,128)(2,1)S(1)}, u32[]{:S(2)}, u32[]{:S(2)}) %collective-permute-start.16) | collective-permute-done | bytes 524320 | tf_op jit(solution)/shard_map/ppermute | solution.py:408
  140.3 5.7 %last_block.7 = (bf16[1024,3584]{1,0:T(8,128)(2,1)S(1)}, f32[1024,3584]{1,0:T(8,128)S(1)}, f32[256,64]{1,0:T(8,128)S(1)}) custom-call(s32[5]{0:T(128)S(1)} %stack.42.where, bf16[512,1024]{1,0:T(8,128)(2,1)S(1)} %collective-permute-done.14.inner, bf16[256,1024]{1,0:T(8,128)(2,1)S(1)} %collective-permute-done.16.outer, ...), custom_call_target="tpu_custom_call", output_to_operand_aliasing={{0}: (3, {}), {1}: (4, {})} | custom-call | flops 1000 | bytes 1000 | tf_op jit(solution)/shard_map/last_block/pallas_call | solution.py:40
  147.1 3.9 %collective-permute-done.17 = f32[2,4096]{1,0:T(2,128)S(1)} collective-permute-done((f32[2,4096]{1,0:T(2,128)S(1)}, f32[2,4096]{1,0:T(2,128)S(1)}, u32[]{:S(2)}, u32[]{:S(2)}) %collective-permute-start.17) | collective-permute-done | bytes 32800 | tf_op jit(solution)/shard_map/ppermute | solution.py:429
  151.0 3.0 %collective-permute-start.18 = (f32[2,4096]{1,0:T(2,128)S(1)}, f32[2,4096]{1,0:T(2,128)S(1)}, u32[]{:S(2)}, u32[]{:S(2)}) collective-permute-start(f32[2,4096]{1,0:T(2,128)S(1)} %add.31), channel_id=1, source_target_pairs={{0,8},{4,12},{8,0},{12,4},{1,9},{5,13},{9,1},{13,5},{2,10},{6,14},... | collective-permute-start | bytes 98312 | tf_op jit(solution)/shard_map/ppermute | solution.py:429
  154.1 1.9 %collective-permute-done.18 = f32[2,4096]{1,0:T(2,128)S(1)} collective-permute-done((f32[2,4096]{1,0:T(2,128)S(1)}, f32[2,4096]{1,0:T(2,128)S(1)}, u32[]{:S(2)}, u32[]{:S(2)}) %collective-permute-start.18) | collective-permute-done | bytes 32800 | tf_op jit(solution)/shard_map/ppermute | solution.py:429
  157.3 2.0 %collective-permute-start.20 = (f32[4,4096]{1,0:T(4,128)S(1)}, f32[4,4096]{1,0:T(4,128)S(1)}, u32[]{:S(2)}, u32[]{:S(2)}) collective-permute-start(f32[4,4096]{1,0:T(4,128)S(1)} %pad_maximum_fusion.1), channel_id=1, source_target_pairs={{0,2},{1,3},{2,0},{3,1},{4,6},{5,7},{6,4},{7,5},{8,10},{9,11},{10,... | collective-permute-start | bytes 196616 | tf_op jit(solution)/shard_map/ppermute | solution.py:429
  159.4 2.6 %scores.1 = f32[2,256]{1,0:T(2,128)S(1)} custom-call(s32[4]{0:T(128)S(1)} %add_add_fusion.order, f32[2,4096]{1,0:T(2,128)S(1)} %add.32.grads, f32[256,256]{1,0:T(8,128)} %rest_0_.1, f32[256,256]{1,0:T(8,128)} %copy-done.4, f32[256,256]{1,0:T(8,128)} %collective-permute-done.3.rest_2_, f32[256,256]{1,0:T(8,128)} %collective-permute-done.4.rest_3_), custom_call_target="tpu_custom_call" | custom-call | flops 1000 | bytes 1000 | tf_op jit(solution)/shard_map/scores/pallas_call | solution.py:40
  163.3 2.3 %collective-permute-done.21 = f32[2,256]{1,0:T(2,128)S(1)} collective-permute-done((f32[2,256]{1,0:T(2,128)S(1)}, f32[2,256]{1,0:T(2,128)S(1)}, u32[]{:S(2)}, u32[]{:S(2)}) %collective-permute-start.21) | collective-permute-done | bytes 2080 | tf_op jit(solution)/shard_map/ppermute | solution.py:429
  165.6 2.5 %collective-permute-start.22 = (f32[2,256]{1,0:T(2,128)S(1)}, f32[2,256]{1,0:T(2,128)S(1)}, u32[]{:S(2)}, u32[]{:S(2)}) collective-permute-start(f32[2,256]{1,0:T(2,128)S(1)} %add.35), channel_id=1, source_target_pairs={{0,8},{4,12},{8,0},{12,4},{1,9},{5,13},{9,1},{13,5},{2,10},{6,14},... | collective-permute-start | bytes 6152 | tf_op jit(solution)/shard_map/ppermute | solution.py:429
  168.2 3.6 %hessian_update.1 = f32[256,4096]{1,0:T(8,128)} custom-call(s32[1]{0:T(128)} %bitcast.row, f32[8,4096]{1,0:T(8,128)S(1)} %pad_maximum_fusion.grads.mine, f32[8,4096]{1,0:T(8,128)S(1)} %pad_maximum_fusion.grads.mine, f32[256,4096]{1,0:T(8,128)} %hessian.1), custom_call_target="tpu_custom_call" | custom-call | flops 1000 | bytes 1000 | tf_op jit(solution)/shard_map/hessian_update/pallas_call | solution.py:40
  (50 shorter events, 18.4 us)
Async XLA Ops:
  0.6 21.1 %copy-start = (bf16[1024,1024]{1,0:T(8,128)(2,1)S(1)}, bf16[1024,1024]{1,0:T(8,128)(2,1)}, u32[]{:S(2)}) copy-start(bf16[1024,1024]{1,0:T(8,128)(2,1)} %own) | copy-start | bytes 6291460
  0.6 49.9 %collective-permute-start.5 = (bf16[1024,1024]{1,0:T(8,128)(2,1)}, bf16[1024,1024]{1,0:T(8,128)(2,1)}, u32[]{:S(2)}, u32[]{:S(2)}) collective-permute-start(bf16[1024,1024]{1,0:T(8,128)(2,1)} %own), channel_id=1, source_target_pairs={{0,4},{4,0},{8,12},{12,8},{1,5},{5,1},{9,13},{13,9},{2,6},{6,2},{1... | collective-permute-start | bytes 6291464 | tf_op jit(solution)/shard_map/ppermute | solution.py:386
  6.8 27.1 %collective-permute-start = (bf16[512,1024]{1,0:T(8,128)(2,1)}, bf16[512,1024]{1,0:T(8,128)(2,1)S(1)}, u32[]{:S(2)}, u32[]{:S(2)}) collective-permute-start(bf16[512,1024]{1,0:T(8,128)(2,1)} %get-tuple-element.65), channel_id=1, source_target_pairs={{4,8},{8,4},{5,9},{9,5},{6,10},{10,6},{7,11},{11,7},{20,24},{24,20... | collective-permute-start | bytes 3145736 | tf_op jit(solution)/shard_map/ppermute | solution.py:388
  7.5 5.8 %collective-permute-start.2 = (f32[256,256]{1,0:T(8,128)}, f32[256,256]{1,0:T(8,128)S(1)}, u32[]{:S(2)}, u32[]{:S(2)}) collective-permute-start(f32[256,256]{1,0:T(8,128)} %rest_0_.1), channel_id=1, source_target_pairs={{0,1},{1,0},{2,3},{3,2},{4,5},{5,4},{6,7},{7,6},{8,9},{9,8},{10,11... | collective-permute-start | bytes 786440 | tf_op jit(solution)/shard_map/ppermute | solution.py:429
  7.6 9.5 %collective-permute-start.3 = (f32[256,256]{1,0:T(8,128)}, f32[256,256]{1,0:T(8,128)}, u32[]{:S(2)}, u32[]{:S(2)}) collective-permute-start(f32[256,256]{1,0:T(8,128)} %rest_0_.1), channel_id=1, source_target_pairs={{0,2},{1,3},{2,0},{3,1},{4,6},{5,7},{6,4},{7,5},{8,10},{9,11},{10,... | collective-permute-start | bytes 786440 | tf_op jit(solution)/shard_map/ppermute | solution.py:429
  9.1 12.6 %collective-permute-start.4 = (f32[256,256]{1,0:T(8,128)}, f32[256,256]{1,0:T(8,128)}, u32[]{:S(2)}, u32[]{:S(2)}) collective-permute-start(f32[256,256]{1,0:T(8,128)} %rest_0_.1), channel_id=1, source_target_pairs={{0,3},{1,2},{2,1},{3,0},{4,7},{5,6},{6,5},{7,4},{8,11},{9,10},{10,... | collective-permute-start | bytes 786440 | tf_op jit(solution)/shard_map/ppermute | solution.py:429
  9.5 1.6 copy-start.2
  11.1 0.9 copy-start.3
  13.3 20.5 %copy-start.4 = (f32[256,256]{1,0:T(8,128)}, f32[256,256]{1,0:T(8,128)S(1)}, u32[]{:S(2)}) copy-start(f32[256,256]{1,0:T(8,128)S(1)} %collective-permute-done.2.rest_1_) | copy-start | bytes 786436
  13.3 45.5 %collective-permute-start.11 = (bf16[512,1024]{1,0:T(8,128)(2,1)}, bf16[512,1024]{1,0:T(8,128)(2,1)S(1)}, u32[]{:S(2)}, u32[]{:S(2)}) collective-permute-start(bf16[512,1024]{1,0:T(8,128)(2,1)} %get-tuple-element.64), channel_id=1, source_target_pairs={{4,8},{8,4},{5,9},{9,5},{6,10},{10,6},{7,11},{11,7},{20,24},{24,20... | collective-permute-start | bytes 3145736 | tf_op jit(solution)/shard_map/ppermute | solution.py:388
  33.8 39.0 %collective-permute-start.9 = (bf16[512,1024]{1,0:T(8,128)(2,1)S(1)}, bf16[512,1024]{1,0:T(8,128)(2,1)S(1)}, u32[]{:S(2)}, u32[]{:S(2)}) collective-permute-start(bf16[512,1024]{1,0:T(8,128)(2,1)S(1)} %collective-permute-done.refs_0_), channel_id=1, source_target_pairs={{4,0},{8,12},{5,1},{9,13},{6,2},{10,14},{7,3},{11,15},{20,16},{24,... | collective-permute-start | bytes 3145736 | tf_op jit(solution)/shard_map/ppermute | solution.py:392
  52.2 34.9 %collective-permute-start.8 = (bf16[512,1024]{1,0:T(8,128)(2,1)S(1)}, bf16[512,1024]{1,0:T(8,128)(2,1)S(1)}, u32[]{:S(2)}, u32[]{:S(2)}) collective-permute-start(bf16[512,1024]{1,0:T(8,128)(2,1)S(1)} %get-tuple-element.63), channel_id=1, source_target_pairs={{4,8},{8,4},{5,9},{9,5},{6,10},{10,6},{7,11},{11,7},{20,24},{24,20... | collective-permute-start | bytes 3145736 | tf_op jit(solution)/shard_map/ppermute | solution.py:393
  53.0 10.0 %collective-permute-start.1 = (f32[64,1024]{1,0:T(8,128)S(1)}, f32[64,1024]{1,0:T(8,128)S(1)}, u32[]{:S(2)}, u32[]{:S(2)}) collective-permute-start(f32[64,1024]{1,0:T(8,128)S(1)} %input_block.1.a), channel_id=1, source_target_pairs={{0,4},{12,8},{1,5},{13,9},{2,6},{14,10},{3,7},{15,11},{16,20},{28,... | collective-permute-start | bytes 786440 | tf_op jit(solution)/shard_map/ppermute | solution.py:390
  58.8 36.5 %collective-permute-start.12 = (bf16[512,1024]{1,0:T(8,128)(2,1)S(1)}, bf16[512,1024]{1,0:T(8,128)(2,1)S(1)}, u32[]{:S(2)}, u32[]{:S(2)}) collective-permute-start(bf16[512,1024]{1,0:T(8,128)(2,1)S(1)} %collective-permute-done.11.refs_1_), channel_id=1, source_target_pairs={{4,0},{8,12},{5,1},{9,13},{6,2},{10,14},{7,3},{11,15},{20,16},{24,... | collective-permute-start | bytes 3145736 | tf_op jit(solution)/shard_map/ppermute | solution.py:392
  63.5 23.0 %collective-permute-start.6 = (f32[64,1024]{1,0:T(8,128)S(1)}, f32[64,1024]{1,0:T(8,128)S(1)}, u32[]{:S(2)}, u32[]{:S(2)}) collective-permute-start(f32[64,1024]{1,0:T(8,128)S(1)} %side.1.a), channel_id=1, source_target_pairs={{4,8},{8,4},{5,9},{9,5},{6,10},{10,6},{7,11},{11,7},{20,24},{24,20... | collective-permute-start | bytes 786440 | tf_op jit(solution)/shard_map/ppermute | solution.py:395
  72.9 34.8 %collective-permute-start.14 = (bf16[512,1024]{1,0:T(8,128)(2,1)S(1)}, bf16[512,1024]{1,0:T(8,128)(2,1)S(1)}, u32[]{:S(2)}, u32[]{:S(2)}) collective-permute-start(bf16[512,1024]{1,0:T(8,128)(2,1)S(1)} %get-tuple-element.62), channel_id=1, source_target_pairs={{4,8},{8,4},{5,9},{9,5},{6,10},{10,6},{7,11},{11,7},{20,24},{24,20... | collective-permute-start | bytes 3145736 | tf_op jit(solution)/shard_map/ppermute | solution.py:393
  87.2 20.6 %collective-permute-start.10 = (bf16[256,1024]{1,0:T(8,128)(2,1)S(1)}, bf16[256,1024]{1,0:T(8,128)(2,1)S(1)}, u32[]{:S(2)}, u32[]{:S(2)}) collective-permute-start(bf16[256,1024]{1,0:T(8,128)(2,1)S(1)} %get-tuple-element.40), channel_id=1, source_target_pairs={{4,0},{8,12},{5,1},{9,13},{6,2},{10,14},{7,3},{11,15},{20,16},{24,... | collective-permute-start | bytes 1572872 | tf_op jit(solution)/shard_map/ppermute | solution.py:408
  88.5 29.4 %collective-permute-start.13 = (bf16[256,1024]{1,0:T(8,128)(2,1)S(1)}, bf16[256,1024]{1,0:T(8,128)(2,1)S(1)}, u32[]{:S(2)}, u32[]{:S(2)}) collective-permute-start(bf16[256,1024]{1,0:T(8,128)(2,1)S(1)} %get-tuple-element.47), channel_id=1, source_target_pairs={{4,0},{8,12},{5,1},{9,13},{6,2},{10,14},{7,3},{11,15},{20,16},{24,... | collective-permute-start | bytes 1572872 | tf_op jit(solution)/shard_map/ppermute | solution.py:408
  95.3 13.7 %copy-start.1 = (bf16[3584,64]{0,1:T(8,128)(2,1)S(1)}, bf16[3584,64]{0,1:T(8,128)(2,1)}, u32[]{:S(2)}) copy-start(bf16[3584,64]{0,1:T(8,128)(2,1)} %param.13) | copy-start | bytes 1376260
  107.7 21.3 %collective-permute-start.15 = (bf16[256,1024]{1,0:T(8,128)(2,1)S(1)}, bf16[256,1024]{1,0:T(8,128)(2,1)S(1)}, u32[]{:S(2)}, u32[]{:S(2)}) collective-permute-start(bf16[256,1024]{1,0:T(8,128)(2,1)S(1)} %get-tuple-element.51), channel_id=1, source_target_pairs={{4,0},{8,12},{5,1},{9,13},{6,2},{10,14},{7,3},{11,15},{20,16},{24,... | collective-permute-start | bytes 1572872 | tf_op jit(solution)/shard_map/ppermute | solution.py:408
  117.8 22.5 %collective-permute-start.16 = (bf16[256,1024]{1,0:T(8,128)(2,1)S(1)}, bf16[256,1024]{1,0:T(8,128)(2,1)S(1)}, u32[]{:S(2)}, u32[]{:S(2)}) collective-permute-start(bf16[256,1024]{1,0:T(8,128)(2,1)S(1)} %get-tuple-element.55), channel_id=1, source_target_pairs={{4,0},{8,12},{5,1},{9,13},{6,2},{10,14},{7,3},{11,15},{20,16},{24,... | collective-permute-start | bytes 1572872 | tf_op jit(solution)/shard_map/ppermute | solution.py:408
  119.1 26.9 %collective-permute-start.7 = (f32[64,1024]{1,0:T(8,128)S(1)}, f32[64,1024]{1,0:T(8,128)S(1)}, u32[]{:S(2)}, u32[]{:S(2)}) collective-permute-start(f32[64,1024]{1,0:T(8,128)S(1)} %total.1), channel_id=1, source_target_pairs={{4,0},{8,12},{5,1},{9,13},{6,2},{10,14},{7,3},{11,15},{20,16},{24,... | collective-permute-start | bytes 786440 | tf_op jit(solution)/shard_map/ppermute | solution.py:396
  147.0 4.0 %collective-permute-start.17 = (f32[2,4096]{1,0:T(2,128)S(1)}, f32[2,4096]{1,0:T(2,128)S(1)}, u32[]{:S(2)}, u32[]{:S(2)}) collective-permute-start(f32[2,4096]{1,0:T(2,128)S(1)} %reshape.11), channel_id=1, source_target_pairs={{0,4},{4,0},{8,12},{12,8},{1,5},{5,1},{9,13},{13,9},{2,6},{6,2},{1... | collective-permute-start | bytes 98312 | tf_op jit(solution)/shard_map/ppermute | solution.py:429
  151.0 4.9 %collective-permute-start.18 = (f32[2,4096]{1,0:T(2,128)S(1)}, f32[2,4096]{1,0:T(2,128)S(1)}, u32[]{:S(2)}, u32[]{:S(2)}) collective-permute-start(f32[2,4096]{1,0:T(2,128)S(1)} %add.31), channel_id=1, source_target_pairs={{0,8},{4,12},{8,0},{12,4},{1,9},{5,13},{9,1},{13,5},{2,10},{6,14},... | collective-permute-start | bytes 98312 | tf_op jit(solution)/shard_map/ppermute | solution.py:429
  156.0 1.3 collective-permute-start.19
  157.3 10.8 %collective-permute-start.20 = (f32[4,4096]{1,0:T(4,128)S(1)}, f32[4,4096]{1,0:T(4,128)S(1)}, u32[]{:S(2)}, u32[]{:S(2)}) collective-permute-start(f32[4,4096]{1,0:T(4,128)S(1)} %pad_maximum_fusion.1), channel_id=1, source_target_pairs={{0,2},{1,3},{2,0},{3,1},{4,6},{5,7},{6,4},{7,5},{8,10},{9,11},{10,... | collective-permute-start | bytes 196616 | tf_op jit(solution)/shard_map/ppermute | solution.py:429
  162.0 3.6 %collective-permute-start.21 = (f32[2,256]{1,0:T(2,128)S(1)}, f32[2,256]{1,0:T(2,128)S(1)}, u32[]{:S(2)}, u32[]{:S(2)}) collective-permute-start(f32[2,256]{1,0:T(2,128)S(1)} %scores.1), channel_id=1, source_target_pairs={{0,4},{4,0},{8,12},{12,8},{1,5},{5,1},{9,13},{13,9},{2,6},{6,2},{1... | collective-permute-start | bytes 6152 | tf_op jit(solution)/shard_map/ppermute | solution.py:429
  165.6 6.2 %collective-permute-start.22 = (f32[2,256]{1,0:T(2,128)S(1)}, f32[2,256]{1,0:T(2,128)S(1)}, u32[]{:S(2)}, u32[]{:S(2)}) collective-permute-start(f32[2,256]{1,0:T(2,128)S(1)} %add.35), channel_id=1, source_target_pairs={{0,8},{4,12},{8,0},{12,4},{1,9},{5,13},{9,1},{13,5},{2,10},{6,14},... | collective-permute-start | bytes 6152 | tf_op jit(solution)/shard_map/ppermute | solution.py:429

commit v8 on v7

--- a/solution.py
+++ b/solution.py
@@ -217,7 +217,7 @@
 
 def outer_body(where, total, sent, *refs):
     *rights, grads = refs
-    left_t = select(where, total, sent)
+    left_t = jnp.where(where[4] == 1, total[...], sent[...].astype(jnp.float32))
     start = 0
     terms = [None] * grads.shape[0]
     for right in rights:
@@ -271,18 +271,17 @@
 
 def score_body(order, grads, *rest):
     *parts, out = rest
-    total = None
-    for s, part in enumerate(parts):
-        width = part.shape[1]
-        term = lax.dot_general(
-            grads[:, columns(order, s, width)],
-            part[...],
-            NT,
-            precision=HIGHEST,
-            preferred_element_type=jnp.float32,
-        )
-        total = term if total is None else total + term
-    out[...] = total
+    rows, width = parts[0].shape
+    count = grads.shape[0]
+    lane = lax.broadcasted_iota(jnp.int32, (rows, 128), 1)
+    total = jnp.zeros((rows, 128), jnp.float32)
+    for s in range(count):
+        products = None
+        for p, part in enumerate(parts):
+            term = part[...] * grads[s : s + 1, columns(order, p, width)]
+            products = term if products is None else products + term
+        total = jnp.where(lane == s, jnp.sum(products, axis=1, keepdims=True), total)
+    out[...] = total.T[:count, :]
 
 
 def score_parts(order, grads, parts):
@@ -342,7 +341,7 @@
 def update(row, grads, hessian):
     rows, columns = hessian.shape
     count = grads.shape[0]
-    parts = 4
+    parts = 8
     width = columns // parts
     (updated,) = call(
         functools.partial(update_body, 1.0 / count),
@@ -393,25 +392,26 @@
     end_inner = [send(pair[half], perm=inner) for half in halves]
     side = small_kernel(sum_body, "side", where, in_part, after(from_end, begun, pair))
     total = small_kernel(sum_body, "total", where, side, send(side, perm=inner))
-    sent = send(total, perm=outward)
+    sent = send(total.astype(jnp.bfloat16), perm=outward)
 
     acc, first = add_block(where, 1, [pair], w_down, after(acc, mid_outer[0]), begun, 2 * grad_out.size * w_down.shape[0])
     acc, second = add_block(where, 2, mid_inner + mid_outer, w_down, acc, first, 1000)
 
-    size = 256
-    arrived = [total, total]
-    done = [first, first, second]
+    sizes = [256] * (tokens // 256 - 1) + [128, 128]
+    arrived, done = [total, total, total], [first, first, second]
     rights = []
-    for n in range(tokens // size):
-        h, at = divmod(n * size, tokens // 2)
-        chunk = end_inner[h][at : at + size]
-        end_outer = send(after(chunk, arrived[n], done[n]), perm=outward)
+    start = 0
+    for n, size in enumerate(sizes):
+        h, at = divmod(start, tokens // 2)
+        ahead = arrived[n + 1] if n < 4 else arrived[n]
+        end_outer = send(after(end_inner[h][at : at + size], ahead, done[n]), perm=outward)
         arrived.append(end_outer)
         kept, acc, right = last_block(
-            where, end_inner[h], at, end_outer, n * size, kept, acc, gate_pre, proj_out.T, second
+            where, end_inner[h], at, end_outer, start, kept, acc, gate_pre, proj_out.T, second
         )
         rights.append(right)
         done.append(right)
+        start += size
     return outer_products(where, total, sent, rights).reshape(-1, PROJ * PROJ)
 
 
@@ -439,6 +439,12 @@
     return a
 
 
+def xor_order_sum(terms):
+    while len(terms) > 1:
+        terms = [terms[i] + terms[i + 1] for i in range(0, len(terms), 2)]
+    return terms[0]
+
+
 def xor_gather(a, axis):
     for bit in bits(axis):
         a = jnp.concatenate([a, swap(a, axis, bit)], axis=0)
@@ -455,11 +461,7 @@
     me = lax.axis_index("dp")
     order = lax.axis_index("tensor") * count + jnp.stack([me ^ s for s in range(count)])
     scores = score_parts(order.astype(jnp.int32), grads, parts)
-    *first, last = bits("tensor")
-    for bit in first:
-        scores = scores + swap(scores, "tensor", bit)
-    other_scores = swap(scores, "tensor", last)
-
+    others = [swap(scores, "tensor", bit) for bit in range(1, lax.axis_size("tensor"))]
     all_grads = after(xor_gather(grads, "dp"), scores)
     row_count = hessian.shape[0]
     at = lax.axis_index(("tensor", "dp"))
@@ -468,8 +470,8 @@
         updated = hessian + jnp.dot(mine.T, all_grads, precision=HIGHEST) / all_grads.shape[0]
     else:
         updated = update(at.reshape(1).astype(jnp.int32), all_grads, hessian)
-    updated, other_scores = lax.optimization_barrier((updated, other_scores))
-    return (updated, scores + other_scores)
+    updated, *others = lax.optimization_barrier((updated, *others))
+    return (updated, xor_order_sum([scores, *others]))
 
 
 def solution(mesh):

time: 173 us -> 171 us (0.988)
  waiting for transfers between devices: 61.5 us -> 56.4 us
    ppermute x5 -> x6, waiting for transfers between devices: 12 us -> 7.11 us  [the longest x5 7.11 us: line_of_four(): send(after(end_inner[h][at:at + size], ahead, done[n]), perm=outward)]
    pallas_call x13 -> x14, Pallas kernels: 69 us -> 70.7 us  [call(): pl.pallas_call(body, grid_spec=pltpu.PrefetchScalarGridSpec(num_scalar_pr...]
    ppermute x5 -> x6, starting transfers between devices: 6.63 us -> 7.92 us  [the longest x5 6.63 us: line_of_four(): send(after(end_inner[h][at:at + size], ahead, done[n]), perm=outward)]
    ppermute x9 -> x10, starting transfers between devices: 10.8 us -> 10.5 us  [swap(): lax.ppermute(a, axis, [(i, i ^ bit) for i in range(lax.axis_size(axis))])]
    ppermute x9 -> x10, waiting for transfers between devices: 17 us -> 16.9 us  [swap(): lax.ppermute(a, axis, [(i, i ^ bit) for i in range(lax.axis_size(axis))])]
  transfers between devices with their start and end apart: 23 -> 25, of which waited for: 13 -> 14; matrix products, arithmetic and copies ran while one was open for 3% -> 3% of each run, Pallas kernels for 39% -> 41%
where the time goes in v8:
time: 171 us; the launch traced here: 170 us
  Pallas kernels  70.7 us (41%)
  waiting for transfers between devices  56.4 us (33%)
  starting transfers between devices  33.5 us (20%)
  local copies, waits for them, and re-layouts  7.58 us (4%)
    pallas_call x14, Pallas kernels, call(): pl.pallas_call(body, grid_spec=pltpu.PrefetchScalarGridSpec(num_scalar_pr...  70.7 us
    ppermute x10, waiting for transfers between devices, swap(): lax.ppermute(a, axis, [(i, i ^ bit) for i in range(lax.axis_size(axis))])  16.9 us
    ppermute x1, waiting for transfers between devices, line_of_four(): pair = send(grad_out, perm=pairs)  15.4 us
    ppermute x2, waiting for transfers between devices, line_of_four(): mid_outer = [send(after(a, begun), perm=outward) for a in mid_inner]  14.3 us
    ppermute x10, starting transfers between devices, swap(): lax.ppermute(a, axis, [(i, i ^ bit) for i in range(lax.axis_size(axis))])  10.5 us
    ppermute x5, waiting for transfers between devices, line_of_four(): send(after(end_inner[h][at:at + size], ahead, done[n]), perm=outward)  7.11 us
    ppermute x5, starting transfers between devices, line_of_four(): send(after(end_inner[h][at:at + size], ahead, done[n]), perm=outward)  6.63 us
    ppermute x1, starting transfers between devices, line_of_four(): from_end = send(after(in_part, mid_inner[0]), perm=inward)  5.83 us
  transfers between devices with their start and end apart: 25, of which 14 were waited for; matrix products, arithmetic and copies ran while one was open for 3% of the time, Pallas kernels for 41%

profile of v8, /device:TPU:0, one launch (start us, length us, event | category | flops | bytes accessed | tf_op | source)
XLA Modules:
  0.0 170.0 jit_solution(16624450547098622944)
XLA Ops:
  0.6 3.1 %collective-permute-start.5 = (bf16[1024,1024]{1,0:T(8,128)(2,1)}, bf16[1024,1024]{1,0:T(8,128)(2,1)}, u32[]{:S(2)}, u32[]{:S(2)}) collective-permute-start(bf16[1024,1024]{1,0:T(8,128)(2,1)} %own), channel_id=1, source_target_pairs={{0,4},{4,0},{8,12},{12,8},{1,5},{5,1},{9,13},{13,9},{2,6},{6,2},{1... | collective-permute-start | bytes 6291464 | tf_op jit(solution)/shard_map/ppermute | solution.py:385
  3.7 3.0 %fusion.1 = (bf16[512,1024]{1,0:T(8,128)(2,1)}, bf16[512,1024]{1,0:T(8,128)(2,1)}) fusion(bf16[1024,1024]{1,0:T(8,128)(2,1)} %own), kind=kLoop, calls=%fused_computation.5 | loop fusion | bytes 4194304 | tf_op jit(solution)/shard_map/slice | solution.py:386
  7.6 1.6 collective-permute-start.3
  9.5 1.6 copy-done.2
  14.1 3.0 %collective-permute-done.3.rest_2_ = f32[256,256]{1,0:T(8,128)} collective-permute-done((f32[256,256]{1,0:T(8,128)}, f32[256,256]{1,0:T(8,128)}, u32[]{:S(2)}, u32[]{:S(2)}) %collective-permute-start.3) | collective-permute-done | bytes 262176 | tf_op jit(solution)/shard_map/ppermute | solution.py:429
  17.1 4.7 %collective-permute-done.4.rest_3_ = f32[256,256]{1,0:T(8,128)} collective-permute-done((f32[256,256]{1,0:T(8,128)}, f32[256,256]{1,0:T(8,128)}, u32[]{:S(2)}, u32[]{:S(2)}) %collective-permute-start.4) | collective-permute-done | bytes 262176 | tf_op jit(solution)/shard_map/ppermute | solution.py:429
  21.8 12.0 %own_block.1 = (f32[1024,3584]{1,0:T(8,128)S(1)}, bf16[1024,3584]{1,0:T(8,128)(2,1)S(1)}, f32[8,128]{1,0:T(8,128)S(1)}) custom-call(s32[5]{0:T(128)S(1)} %stack.42.where, bf16[1024,1024]{1,0:T(8,128)(2,1)S(1)} %copy-done.1, bf16[3584,4096]{1,0:T(8,128)(2,1)} %refs_4_.1, bf16[3584,4096]{1,0:T(8,128)(2,1)} %refs_4_.1), custom_call_target="tpu_custom_call" | custom-call | flops 1000 | bytes 1000 | tf_op jit(solution)/shard_map/own_block/pallas_call | solution.py:40
  35.1 15.4 %collective-permute-done.5.refs_0_ = bf16[1024,1024]{1,0:T(8,128)(2,1)} collective-permute-done((bf16[1024,1024]{1,0:T(8,128)(2,1)}, bf16[1024,1024]{1,0:T(8,128)(2,1)}, u32[]{:S(2)}, u32[]{:S(2)}) %collective-permute-start.5) | collective-permute-done | bytes 2097184 | tf_op jit(solution)/shard_map/ppermute | solution.py:385
  50.5 1.7 %fusion = (bf16[512,1024]{1,0:T(8,128)(2,1)S(1)}, bf16[512,1024]{1,0:T(8,128)(2,1)S(1)}) fusion(bf16[1024,1024]{1,0:T(8,128)(2,1)} %collective-permute-done.5.refs_0_), kind=kLoop, calls=%fused_computation.4 | loop fusion | bytes 4194304 | tf_op jit(solution)/shard_map/slice | solution.py:392
  53.0 5.8 %collective-permute-start.1 = (f32[64,1024]{1,0:T(8,128)S(1)}, f32[64,1024]{1,0:T(8,128)S(1)}, u32[]{:S(2)}, u32[]{:S(2)}) collective-permute-start(f32[64,1024]{1,0:T(8,128)S(1)} %input_block.1.a), channel_id=1, source_target_pairs={{0,4},{12,8},{1,5},{13,9},{2,6},{14,10},{3,7},{15,11},{16,20},{28,... | collective-permute-start | bytes 786440 | tf_op jit(solution)/shard_map/ppermute | solution.py:389
  60.1 2.8 %collective-permute-done.1.b = f32[64,1024]{1,0:T(8,128)S(1)} collective-permute-done((f32[64,1024]{1,0:T(8,128)S(1)}, f32[64,1024]{1,0:T(8,128)S(1)}, u32[]{:S(2)}, u32[]{:S(2)}) %collective-permute-start.1) | collective-permute-done | bytes 262176 | tf_op jit(solution)/shard_map/ppermute | solution.py:389
  63.5 9.4 %collective-permute-done.9.refs_2_ = bf16[512,1024]{1,0:T(8,128)(2,1)S(1)} collective-permute-done((bf16[512,1024]{1,0:T(8,128)(2,1)S(1)}, bf16[512,1024]{1,0:T(8,128)(2,1)S(1)}, u32[]{:S(2)}, u32[]{:S(2)}) %collective-permute-start.9) | collective-permute-done | bytes 1048608 | tf_op jit(solution)/shard_map/ppermute | solution.py:391
  74.3 12.9 %add_block_1.1 = (f32[1024,3584]{1,0:T(8,128)S(1)}, f32[8,128]{1,0:T(8,128)S(1)}) custom-call(s32[5]{0:T(128)S(1)} %stack.42.where, bf16[1024,1024]{1,0:T(8,128)(2,1)} %collective-permute-done.5.refs_0_, bf16[3584,4096]{1,0:T(8,128)(2,1)} %refs_4_.1, f32[1024,3584]{1,0:T(8,128)S(1)} %get-tuple-element.44.refs_2_, ...), custom_call_target="tpu_custom_call", output_to_operand_aliasing={{0}: (3, {})} | custom-call | flops 7516192768 | bytes 1000 | tf_op jit(solution)/shard_map/add_block_1/pallas_call | solution.py:40
  90.4 4.9 %collective-permute-done.12.refs_3_ = bf16[512,1024]{1,0:T(8,128)(2,1)S(1)} collective-permute-done((bf16[512,1024]{1,0:T(8,128)(2,1)S(1)}, bf16[512,1024]{1,0:T(8,128)(2,1)S(1)}, u32[]{:S(2)}, u32[]{:S(2)}) %collective-permute-start.12) | collective-permute-done | bytes 1048608 | tf_op jit(solution)/shard_map/ppermute | solution.py:391
  95.3 12.3 %add_block_2.1 = (f32[1024,3584]{1,0:T(8,128)S(1)}, f32[8,128]{1,0:T(8,128)S(1)}) custom-call(s32[5]{0:T(128)S(1)} %stack.42.where, bf16[512,1024]{1,0:T(8,128)(2,1)S(1)} %collective-permute-done.refs_0_, bf16[512,1024]{1,0:T(8,128)(2,1)S(1)} %collective-permute-done.11.refs_1_, ...), custom_call_target="tpu_custom_call", output_to_operand_aliasing={{0}: (6, {})} | custom-call | flops 1000 | bytes 1000 | tf_op jit(solution)/shard_map/add_block_2/pallas_call | solution.py:40
  109.1 5.5 %last_block.5 = (bf16[1024,3584]{1,0:T(8,128)(2,1)S(1)}, f32[1024,3584]{1,0:T(8,128)S(1)}, f32[256,64]{1,0:T(8,128)S(1)}) custom-call(s32[5]{0:T(128)S(1)} %stack.42.where, bf16[512,1024]{1,0:T(8,128)(2,1)S(1)} %collective-permute-done.8.inner, bf16[256,1024]{1,0:T(8,128)(2,1)S(1)} %collective-permute-done.10.outer, ...), custom_call_target="tpu_custom_call", output_to_operand_aliasing={{0}: (3, {}), {1}: (4, {})} | custom-call | flops 1000 | bytes 1000 | tf_op jit(solution)/shard_map/last_block/pallas_call | solution.py:40
  114.6 3.8 %collective-permute-done.13.outer = bf16[256,1024]{1,0:T(8,128)(2,1)S(1)} collective-permute-done((bf16[256,1024]{1,0:T(8,128)(2,1)S(1)}, bf16[256,1024]{1,0:T(8,128)(2,1)S(1)}, u32[]{:S(2)}, u32[]{:S(2)}) %collective-permute-start.13) | collective-permute-done | bytes 524320 | tf_op jit(solution)/shard_map/ppermute | solution.py:407
  118.3 1.5 collective-permute-start.16
  119.8 5.5 %last_block.6 = (bf16[1024,3584]{1,0:T(8,128)(2,1)S(1)}, f32[1024,3584]{1,0:T(8,128)S(1)}, f32[256,64]{1,0:T(8,128)S(1)}) custom-call(s32[5]{0:T(128)S(1)} %stack.42.where, bf16[512,1024]{1,0:T(8,128)(2,1)S(1)} %collective-permute-done.8.inner, bf16[256,1024]{1,0:T(8,128)(2,1)S(1)} %collective-permute-done.13.outer, ...), custom_call_target="tpu_custom_call", output_to_operand_aliasing={{0}: (3, {}), {1}: (4, {})} | custom-call | flops 1000 | bytes 1000 | tf_op jit(solution)/shard_map/last_block/pallas_call | solution.py:40
  127.9 1.6 collective-permute-done.15.outer
  129.6 5.5 %last_block.7 = (bf16[1024,3584]{1,0:T(8,128)(2,1)S(1)}, f32[1024,3584]{1,0:T(8,128)S(1)}, f32[256,64]{1,0:T(8,128)S(1)}) custom-call(s32[5]{0:T(128)S(1)} %stack.42.where, bf16[512,1024]{1,0:T(8,128)(2,1)S(1)} %collective-permute-done.14.inner, bf16[256,1024]{1,0:T(8,128)(2,1)S(1)} %collective-permute-done.15.outer, ...), custom_call_target="tpu_custom_call", output_to_operand_aliasing={{0}: (3, {}), {1}: (4, {})} | custom-call | flops 1000 | bytes 1000 | tf_op jit(solution)/shard_map/last_block/pallas_call | solution.py:40
  135.2 4.1 %last_block.8 = (bf16[1024,3584]{1,0:T(8,128)(2,1)S(1)}, f32[1024,3584]{1,0:T(8,128)S(1)}, f32[128,64]{1,0:T(8,128)S(1)}) custom-call(s32[5]{0:T(128)S(1)} %stack.42.where, bf16[512,1024]{1,0:T(8,128)(2,1)S(1)} %collective-permute-done.14.inner, bf16[128,1024]{1,0:T(8,128)(2,1)S(1)} %collective-permute-done.16.outer, ...), custom_call_target="tpu_custom_call", output_to_operand_aliasing={{0}: (3, {}), {1}: (4, {})} | custom-call | flops 1000 | bytes 1000 | tf_op jit(solution)/shard_map/last_block/pallas_call | solution.py:40
  139.3 1.6 collective-permute-done.17.outer
  140.8 4.1 %last_block.9 = (bf16[1024,3584]{1,0:T(8,128)(2,1)S(1)}, f32[1024,3584]{1,0:T(8,128)S(1)}, f32[128,64]{1,0:T(8,128)S(1)}) custom-call(s32[5]{0:T(128)S(1)} %stack.42.where, bf16[512,1024]{1,0:T(8,128)(2,1)S(1)} %collective-permute-done.14.inner, bf16[128,1024]{1,0:T(8,128)(2,1)S(1)} %collective-permute-done.17.outer, ...), custom_call_target="tpu_custom_call", output_to_operand_aliasing={{0}: (3, {}), {1}: (4, {})} | custom-call | flops 1000 | bytes 1000 | tf_op jit(solution)/shard_map/last_block/pallas_call | solution.py:40
  146.0 3.9 %collective-permute-done.18 = f32[2,4096]{1,0:T(2,128)S(1)} collective-permute-done((f32[2,4096]{1,0:T(2,128)S(1)}, f32[2,4096]{1,0:T(2,128)S(1)}, u32[]{:S(2)}, u32[]{:S(2)}) %collective-permute-start.18) | collective-permute-done | bytes 32800 | tf_op jit(solution)/shard_map/ppermute | solution.py:429
  150.0 2.5 %collective-permute-start.19 = (f32[2,4096]{1,0:T(2,128)S(1)}, f32[2,4096]{1,0:T(2,128)S(1)}, u32[]{:S(2)}, u32[]{:S(2)}) collective-permute-start(f32[2,4096]{1,0:T(2,128)S(1)} %add.34), channel_id=1, source_target_pairs={{0,8},{4,12},{8,0},{12,4},{1,9},{5,13},{9,1},{13,5},{2,10},{6,14},... | collective-permute-start | bytes 98312 | tf_op jit(solution)/shard_map/ppermute | solution.py:429
  152.5 2.4 %collective-permute-done.19 = f32[2,4096]{1,0:T(2,128)S(1)} collective-permute-done((f32[2,4096]{1,0:T(2,128)S(1)}, f32[2,4096]{1,0:T(2,128)S(1)}, u32[]{:S(2)}, u32[]{:S(2)}) %collective-permute-start.19) | collective-permute-done | bytes 32800 | tf_op jit(solution)/shard_map/ppermute | solution.py:429
  156.2 1.5 collective-permute-start.21
  157.8 2.0 %scores.1 = f32[2,256]{1,0:T(2,128)S(1)} custom-call(s32[4]{0:T(128)S(1)} %add_add_fusion.1.order, f32[2,4096]{1,0:T(2,128)S(1)} %add.35.grads, f32[256,256]{1,0:T(8,128)} %rest_0_.1, f32[256,256]{1,0:T(8,128)} %copy-done.4, f32[256,256]{1,0:T(8,128)} %collective-permute-done.3.rest_2_, f32[256,256]{1,0:T(8,128)} %collective-permute-done.4.rest_3_), custom_call_target="tpu_custom_call" | custom-call | flops 1000 | bytes 1000 | tf_op jit(solution)/shard_map/scores/pallas_call | solution.py:40
  161.0 3.0 %collective-permute-start.23 = (f32[2,256]{1,0:T(2,128)S(1)}, f32[2,256]{1,0:T(2,128)S(1)}, u32[]{:S(2)}, u32[]{:S(2)}) collective-permute-start(f32[2,256]{1,0:T(2,128)S(1)} %scores.1), channel_id=1, source_target_pairs={{0,8},{4,12},{8,0},{12,4},{1,9},{5,13},{9,1},{13,5},{2,10},{6,14},... | collective-permute-start | bytes 6152 | tf_op jit(solution)/shard_map/ppermute | solution.py:429
  164.2 3.6 %hessian_update.1 = f32[256,4096]{1,0:T(8,128)} custom-call(s32[1]{0:T(128)} %bitcast.row, f32[8,4096]{1,0:T(8,128)S(1)} %pad_maximum_fusion.grads.mine, f32[8,4096]{1,0:T(8,128)S(1)} %pad_maximum_fusion.grads.mine, f32[256,4096]{1,0:T(8,128)} %hessian.1), custom_call_target="tpu_custom_call" | custom-call | flops 1000 | bytes 1000 | tf_op jit(solution)/shard_map/hessian_update/pallas_call | solution.py:40
  167.8 1.6 collective-permute-done.24
  (56 shorter events, 21.3 us)
Async XLA Ops:
  0.6 21.1 %copy-start.1 = (bf16[1024,1024]{1,0:T(8,128)(2,1)S(1)}, bf16[1024,1024]{1,0:T(8,128)(2,1)}, u32[]{:S(2)}) copy-start(bf16[1024,1024]{1,0:T(8,128)(2,1)} %own) | copy-start | bytes 6291460
  0.6 49.9 %collective-permute-start.5 = (bf16[1024,1024]{1,0:T(8,128)(2,1)}, bf16[1024,1024]{1,0:T(8,128)(2,1)}, u32[]{:S(2)}, u32[]{:S(2)}) collective-permute-start(bf16[1024,1024]{1,0:T(8,128)(2,1)} %own), channel_id=1, source_target_pairs={{0,4},{4,0},{8,12},{12,8},{1,5},{5,1},{9,13},{13,9},{2,6},{6,2},{1... | collective-permute-start | bytes 6291464 | tf_op jit(solution)/shard_map/ppermute | solution.py:385
  6.8 27.1 %collective-permute-start = (bf16[512,1024]{1,0:T(8,128)(2,1)}, bf16[512,1024]{1,0:T(8,128)(2,1)S(1)}, u32[]{:S(2)}, u32[]{:S(2)}) collective-permute-start(bf16[512,1024]{1,0:T(8,128)(2,1)} %get-tuple-element.77), channel_id=1, source_target_pairs={{4,8},{8,4},{5,9},{9,5},{6,10},{10,6},{7,11},{11,7},{20,24},{24,20... | collective-permute-start | bytes 3145736 | tf_op jit(solution)/shard_map/ppermute | solution.py:387
  7.5 5.8 %collective-permute-start.2 = (f32[256,256]{1,0:T(8,128)}, f32[256,256]{1,0:T(8,128)S(1)}, u32[]{:S(2)}, u32[]{:S(2)}) collective-permute-start(f32[256,256]{1,0:T(8,128)} %rest_0_.1), channel_id=1, source_target_pairs={{0,1},{1,0},{2,3},{3,2},{4,5},{5,4},{6,7},{7,6},{8,9},{9,8},{10,11... | collective-permute-start | bytes 786440 | tf_op jit(solution)/shard_map/ppermute | solution.py:429
  7.6 9.5 %collective-permute-start.3 = (f32[256,256]{1,0:T(8,128)}, f32[256,256]{1,0:T(8,128)}, u32[]{:S(2)}, u32[]{:S(2)}) collective-permute-start(f32[256,256]{1,0:T(8,128)} %rest_0_.1), channel_id=1, source_target_pairs={{0,2},{1,3},{2,0},{3,1},{4,6},{5,7},{6,4},{7,5},{8,10},{9,11},{10,... | collective-permute-start | bytes 786440 | tf_op jit(solution)/shard_map/ppermute | solution.py:429
  9.1 12.6 %collective-permute-start.4 = (f32[256,256]{1,0:T(8,128)}, f32[256,256]{1,0:T(8,128)}, u32[]{:S(2)}, u32[]{:S(2)}) collective-permute-start(f32[256,256]{1,0:T(8,128)} %rest_0_.1), channel_id=1, source_target_pairs={{0,3},{1,2},{2,1},{3,0},{4,7},{5,6},{6,5},{7,4},{8,11},{9,10},{10,... | collective-permute-start | bytes 786440 | tf_op jit(solution)/shard_map/ppermute | solution.py:429
  9.5 1.6 copy-start.2
  11.1 0.9 copy-start.3
  13.3 20.5 %copy-start.4 = (f32[256,256]{1,0:T(8,128)}, f32[256,256]{1,0:T(8,128)S(1)}, u32[]{:S(2)}) copy-start(f32[256,256]{1,0:T(8,128)S(1)} %collective-permute-done.2.rest_1_) | copy-start | bytes 786436
  13.3 45.5 %collective-permute-start.11 = (bf16[512,1024]{1,0:T(8,128)(2,1)}, bf16[512,1024]{1,0:T(8,128)(2,1)S(1)}, u32[]{:S(2)}, u32[]{:S(2)}) collective-permute-start(bf16[512,1024]{1,0:T(8,128)(2,1)} %get-tuple-element.76), channel_id=1, source_target_pairs={{4,8},{8,4},{5,9},{9,5},{6,10},{10,6},{7,11},{11,7},{20,24},{24,20... | collective-permute-start | bytes 3145736 | tf_op jit(solution)/shard_map/ppermute | solution.py:387
  33.8 39.0 %collective-permute-start.9 = (bf16[512,1024]{1,0:T(8,128)(2,1)S(1)}, bf16[512,1024]{1,0:T(8,128)(2,1)S(1)}, u32[]{:S(2)}, u32[]{:S(2)}) collective-permute-start(bf16[512,1024]{1,0:T(8,128)(2,1)S(1)} %collective-permute-done.refs_0_), channel_id=1, source_target_pairs={{4,0},{8,12},{5,1},{9,13},{6,2},{10,14},{7,3},{11,15},{20,16},{24,... | collective-permute-start | bytes 3145736 | tf_op jit(solution)/shard_map/ppermute | solution.py:391
  52.2 35.5 %collective-permute-start.8 = (bf16[512,1024]{1,0:T(8,128)(2,1)S(1)}, bf16[512,1024]{1,0:T(8,128)(2,1)S(1)}, u32[]{:S(2)}, u32[]{:S(2)}) collective-permute-start(bf16[512,1024]{1,0:T(8,128)(2,1)S(1)} %get-tuple-element.75), channel_id=1, source_target_pairs={{4,8},{8,4},{5,9},{9,5},{6,10},{10,6},{7,11},{11,7},{20,24},{24,20... | collective-permute-start | bytes 3145736 | tf_op jit(solution)/shard_map/ppermute | solution.py:392
  53.0 10.0 %collective-permute-start.1 = (f32[64,1024]{1,0:T(8,128)S(1)}, f32[64,1024]{1,0:T(8,128)S(1)}, u32[]{:S(2)}, u32[]{:S(2)}) collective-permute-start(f32[64,1024]{1,0:T(8,128)S(1)} %input_block.1.a), channel_id=1, source_target_pairs={{0,4},{12,8},{1,5},{13,9},{2,6},{14,10},{3,7},{15,11},{16,20},{28,... | collective-permute-start | bytes 786440 | tf_op jit(solution)/shard_map/ppermute | solution.py:389
  58.8 36.5 %collective-permute-start.12 = (bf16[512,1024]{1,0:T(8,128)(2,1)S(1)}, bf16[512,1024]{1,0:T(8,128)(2,1)S(1)}, u32[]{:S(2)}, u32[]{:S(2)}) collective-permute-start(bf16[512,1024]{1,0:T(8,128)(2,1)S(1)} %collective-permute-done.11.refs_1_), channel_id=1, source_target_pairs={{4,0},{8,12},{5,1},{9,13},{6,2},{10,14},{7,3},{11,15},{20,16},{24,... | collective-permute-start | bytes 3145736 | tf_op jit(solution)/shard_map/ppermute | solution.py:391
  72.9 14.3 %collective-permute-start.6 = (f32[64,1024]{1,0:T(8,128)S(1)}, f32[64,1024]{1,0:T(8,128)S(1)}, u32[]{:S(2)}, u32[]{:S(2)}) collective-permute-start(f32[64,1024]{1,0:T(8,128)S(1)} %side.1.a), channel_id=1, source_target_pairs={{4,8},{8,4},{5,9},{9,5},{6,10},{10,6},{7,11},{11,7},{20,24},{24,20... | collective-permute-start | bytes 786440 | tf_op jit(solution)/shard_map/ppermute | solution.py:394
  73.5 34.1 %collective-permute-start.14 = (bf16[512,1024]{1,0:T(8,128)(2,1)S(1)}, bf16[512,1024]{1,0:T(8,128)(2,1)S(1)}, u32[]{:S(2)}, u32[]{:S(2)}) collective-permute-start(bf16[512,1024]{1,0:T(8,128)(2,1)S(1)} %get-tuple-element.74), channel_id=1, source_target_pairs={{4,8},{8,4},{5,9},{9,5},{6,10},{10,6},{7,11},{11,7},{20,24},{24,20... | collective-permute-start | bytes 3145736 | tf_op jit(solution)/shard_map/ppermute | solution.py:392
  87.8 19.8 %collective-permute-start.10 = (bf16[256,1024]{1,0:T(8,128)(2,1)S(1)}, bf16[256,1024]{1,0:T(8,128)(2,1)S(1)}, u32[]{:S(2)}, u32[]{:S(2)}) collective-permute-start(bf16[256,1024]{1,0:T(8,128)(2,1)S(1)} %get-tuple-element.46), channel_id=1, source_target_pairs={{4,0},{8,12},{5,1},{9,13},{6,2},{10,14},{7,3},{11,15},{20,16},{24,... | collective-permute-start | bytes 1572872 | tf_op jit(solution)/shard_map/ppermute | solution.py:407
  89.1 29.2 %collective-permute-start.13 = (bf16[256,1024]{1,0:T(8,128)(2,1)S(1)}, bf16[256,1024]{1,0:T(8,128)(2,1)S(1)}, u32[]{:S(2)}, u32[]{:S(2)}) collective-permute-start(bf16[256,1024]{1,0:T(8,128)(2,1)S(1)} %get-tuple-element.53), channel_id=1, source_target_pairs={{4,0},{8,12},{5,1},{9,13},{6,2},{10,14},{7,3},{11,15},{20,16},{24,... | collective-permute-start | bytes 1572872 | tf_op jit(solution)/shard_map/ppermute | solution.py:407
  95.3 13.7 %copy-start = (bf16[3584,64]{0,1:T(8,128)(2,1)S(1)}, bf16[3584,64]{0,1:T(8,128)(2,1)}, u32[]{:S(2)}) copy-start(bf16[3584,64]{0,1:T(8,128)(2,1)} %param.13) | copy-start | bytes 1376260
  107.7 21.9 %collective-permute-start.15 = (bf16[256,1024]{1,0:T(8,128)(2,1)S(1)}, bf16[256,1024]{1,0:T(8,128)(2,1)S(1)}, u32[]{:S(2)}, u32[]{:S(2)}) collective-permute-start(bf16[256,1024]{1,0:T(8,128)(2,1)S(1)} %slice.40), channel_id=1, source_target_pairs={{4,0},{8,12},{5,1},{9,13},{6,2},{10,14},{7,3},{11,15},{20,16},{24,... | collective-permute-start | bytes 1572872 | tf_op jit(solution)/shard_map/ppermute | solution.py:407
  118.3 16.9 %collective-permute-start.16 = (bf16[128,1024]{1,0:T(8,128)(2,1)S(1)}, bf16[128,1024]{1,0:T(8,128)(2,1)S(1)}, u32[]{:S(2)}, u32[]{:S(2)}) collective-permute-start(bf16[128,1024]{1,0:T(8,128)(2,1)S(1)} %get-tuple-element.61), channel_id=1, source_target_pairs={{4,0},{8,12},{5,1},{9,13},{6,2},{10,14},{7,3},{11,15},{20,16},{24,... | collective-permute-start | bytes 786440 | tf_op jit(solution)/shard_map/ppermute | solution.py:407
  125.3 15.5 %collective-permute-start.17 = (bf16[128,1024]{1,0:T(8,128)(2,1)S(1)}, bf16[128,1024]{1,0:T(8,128)(2,1)S(1)}, u32[]{:S(2)}, u32[]{:S(2)}) collective-permute-start(bf16[128,1024]{1,0:T(8,128)(2,1)S(1)} %get-tuple-element.65), channel_id=1, source_target_pairs={{4,0},{8,12},{5,1},{9,13},{6,2},{10,14},{7,3},{11,15},{20,16},{24,... | collective-permute-start | bytes 786440 | tf_op jit(solution)/shard_map/ppermute | solution.py:407
  126.6 18.2 %collective-permute-start.7 = (bf16[64,1024]{1,0:T(8,128)(2,1)S(1)}, bf16[64,1024]{1,0:T(8,128)(2,1)S(1)}, u32[]{:S(2)}, u32[]{:S(2)}) collective-permute-start(bf16[64,1024]{1,0:T(8,128)(2,1)S(1)} %convert_element_type.4), channel_id=1, source_target_pairs={{4,0},{8,12},{5,1},{9,13},{6,2},{10,14},{7,3},{11,15},{20,16},{24,... | collective-permute-start | bytes 393224 | tf_op jit(solution)/shard_map/ppermute | solution.py:395
  146.0 4.0 %collective-permute-start.18 = (f32[2,4096]{1,0:T(2,128)S(1)}, f32[2,4096]{1,0:T(2,128)S(1)}, u32[]{:S(2)}, u32[]{:S(2)}) collective-permute-start(f32[2,4096]{1,0:T(2,128)S(1)} %reshape.11), channel_id=1, source_target_pairs={{0,4},{4,0},{8,12},{12,8},{1,5},{5,1},{9,13},{13,9},{2,6},{6,2},{1... | collective-permute-start | bytes 98312 | tf_op jit(solution)/shard_map/ppermute | solution.py:429
  150.0 4.9 %collective-permute-start.19 = (f32[2,4096]{1,0:T(2,128)S(1)}, f32[2,4096]{1,0:T(2,128)S(1)}, u32[]{:S(2)}, u32[]{:S(2)}) collective-permute-start(f32[2,4096]{1,0:T(2,128)S(1)} %add.34), channel_id=1, source_target_pairs={{0,8},{4,12},{8,0},{12,4},{1,9},{5,13},{9,1},{13,5},{2,10},{6,14},... | collective-permute-start | bytes 98312 | tf_op jit(solution)/shard_map/ppermute | solution.py:429
  154.9 1.3 collective-permute-start.20
  156.2 8.0 %collective-permute-start.21 = (f32[4,4096]{1,0:T(4,128)S(1)}, f32[4,4096]{1,0:T(4,128)S(1)}, u32[]{:S(2)}, u32[]{:S(2)}) collective-permute-start(f32[4,4096]{1,0:T(4,128)S(1)} %pad_maximum_fusion.1), channel_id=1, source_target_pairs={{0,2},{1,3},{2,0},{3,1},{4,6},{5,7},{6,4},{7,5},{8,10},{9,11},{10,... | collective-permute-start | bytes 196616 | tf_op jit(solution)/shard_map/ppermute | solution.py:429
  159.7 8.1 %collective-permute-start.22 = (f32[2,256]{1,0:T(2,128)S(1)}, f32[2,256]{1,0:T(2,128)S(1)}, u32[]{:S(2)}, u32[]{:S(2)}) collective-permute-start(f32[2,256]{1,0:T(2,128)S(1)} %scores.1), channel_id=1, source_target_pairs={{0,4},{4,0},{8,12},{12,8},{1,5},{5,1},{9,13},{13,9},{2,6},{6,2},{1... | collective-permute-start | bytes 6152 | tf_op jit(solution)/shard_map/ppermute | solution.py:429
  161.0 6.8 %collective-permute-start.23 = (f32[2,256]{1,0:T(2,128)S(1)}, f32[2,256]{1,0:T(2,128)S(1)}, u32[]{:S(2)}, u32[]{:S(2)}) collective-permute-start(f32[2,256]{1,0:T(2,128)S(1)} %scores.1), channel_id=1, source_target_pairs={{0,8},{4,12},{8,0},{12,4},{1,9},{5,13},{9,1},{13,5},{2,10},{6,14},... | collective-permute-start | bytes 6152 | tf_op jit(solution)/shard_map/ppermute | solution.py:429
  164.1 5.4 %collective-permute-start.24 = (f32[2,256]{1,0:T(2,128)S(1)}, f32[2,256]{1,0:T(2,128)S(1)}, u32[]{:S(2)}, u32[]{:S(2)}) collective-permute-start(f32[2,256]{1,0:T(2,128)S(1)} %scores.1), channel_id=1, source_target_pairs={{0,12},{4,8},{8,4},{12,0},{1,13},{5,9},{9,5},{13,1},{2,14},{6,10},... | collective-permute-start | bytes 6152 | tf_op jit(solution)/shard_map/ppermute | solution.py:429

commit v9 on v8

--- a/solution.py
+++ b/solution.py
@@ -161,9 +161,10 @@
     )
 
 
-def last_body(
-    start, inner_at, where, inner, outer, kept, old, gate, po_t, _, kept_same, old_same, right, gates, po, gate_sems, po_sem
-):
+def last_body(start, inner_at, bring, where, inner, outer, kept, old, gate, po_t, _, *rest):
+    far, rest = rest[:bring], rest[bring:]
+    _, _, right, *near = rest[: 3 + bring]
+    gates, po, gate_sems, po_sem, near_sems = rest[3 + bring :]
     size = outer.shape[0]
     hidden = kept.shape[1]
     tokens = pl.ds(start, size)
@@ -176,6 +177,9 @@
     po_read.start()
     for read in reads[1:]:
         read.start()
+    brought = [pltpu.make_async_copy(a, b, near_sems.at[i]) for i, (a, b) in enumerate(zip(far, near))]
+    for copy in brought:
+        copy.start()
     block = select(where, inner.at[pl.ds(inner_at, size)], outer)
     total = jnp.zeros((size, PROJ), jnp.float32)
     for t, span in enumerate(spans):
@@ -186,29 +190,33 @@
             po_read.wait()
         total = total + dot_nt(up_grad, po[:, span])
     right[...] = total
-
-
-def last_block(where, inner, inner_at, outer, start, kept, old, gate, po_t, token):
+    for copy in brought:
+        copy.wait()
+
+
+def last_block(where, inner, inner_at, outer, start, kept, old, gate, po_t, token, bring):
     size = outer.shape[0]
     tiles = kept.shape[1] // TILE
     return call(
-        functools.partial(last_body, start, inner_at),
+        functools.partial(last_body, start, inner_at, len(bring)),
         "last_block",
         where,
         (1,),
-        (inner, outer, kept, old, gate, po_t, token),
-        [INSIDE, INSIDE, INSIDE, INSIDE, OUTSIDE, ANYWHERE, ANYWHERE],
-        [INSIDE, INSIDE, pl.BlockSpec((size, PROJ), lambda j, where: (0, 0))],
+        (inner, outer, kept, old, gate, po_t, token, *bring),
+        [INSIDE, INSIDE, INSIDE, INSIDE, OUTSIDE, ANYWHERE, ANYWHERE] + [OUTSIDE] * len(bring),
+        [INSIDE, INSIDE, pl.BlockSpec((size, PROJ), lambda j, where: (0, 0))] + [INSIDE] * len(bring),
         [
             pltpu.VMEM(kept.shape, kept.dtype),
             pltpu.VMEM(old.shape, old.dtype),
             jax.ShapeDtypeStruct((size, PROJ), jnp.float32),
+            *[pltpu.VMEM(a.shape, a.dtype) for a in bring],
         ],
         [
             pltpu.VMEM((tiles, size, TILE), gate.dtype),
             pltpu.VMEM(po_t.shape, po_t.dtype),
             pltpu.SemaphoreType.DMA((tiles,)),
             pltpu.SemaphoreType.DMA,
+            pltpu.SemaphoreType.DMA((max(len(bring), 1),)),
         ],
         LIMIT,
         aliases={3: 0, 4: 1},
@@ -295,8 +303,8 @@
         "scores",
         order,
         (1,),
-        (grads, *[pltpu.with_memory_space_constraint(a, pltpu.HBM) for a in parts]),
-        [fixed(grads.shape)] + [fixed(a.shape) for a in parts],
+        (grads, *parts),
+        [fixed(grads.shape)] + [INSIDE] * len(parts),
         [pl.BlockSpec(shape, lambda j, order: (0, 0))],
         [jax.ShapeDtypeStruct(shape, jnp.float32)],
         [],
@@ -313,26 +321,18 @@
     return high, middle, low
 
 
-def update_body(scale, row, grads, mine, hessian, out, old, new, in_sems, out_sems):
-    count, columns = grads.shape
-    width = old.shape[2]
-    parts = columns // width
-    reads = [
-        pltpu.make_async_copy(hessian.at[:, pl.ds(t * width, width)], old.at[t], in_sems.at[t]) for t in range(parts)
-    ]
-    writes = [
-        pltpu.make_async_copy(new.at[t], out.at[:, pl.ds(t * width, width)], out_sems.at[t]) for t in range(parts)
-    ]
-    for read in reads:
-        read.start()
+def update_body(scale, row, grads, mine, hessian, out, new, out_sems):
+    columns = grads.shape[1]
+    parts, _, width = new.shape
     high, middle, low = pieces(mine[...])
     left = jnp.concatenate([high, high, middle, middle, high, low], axis=0).T
+    writes = []
     for t in range(parts):
-        high, middle, low = pieces(grads[:, t * width : (t + 1) * width])
+        span = pl.ds(t * width, width)
+        high, middle, low = pieces(grads[:, span])
         right = jnp.concatenate([high, middle, high, middle, low, high], axis=0)
-        total = dot(left, right) * scale
-        reads[t].wait()
-        new[t] = old[t] + total
+        new[t] = hessian[:, span] + dot(left, right) * scale
+        writes.append(pltpu.make_async_copy(new.at[t], out.at[:, span], out_sems.at[t]))
         writes[t].start()
     for write in writes:
         write.wait()
@@ -352,22 +352,17 @@
         [
             fixed(grads.shape),
             pl.BlockSpec((count, rows), lambda j, row: (0, row[0]), pipeline_mode=pl.Buffered(1)),
-            OUTSIDE,
+            INSIDE,
         ],
         [ANYWHERE],
         [jax.ShapeDtypeStruct((rows, columns), jnp.float32)],
-        [
-            pltpu.VMEM((parts, rows, width), jnp.float32),
-            pltpu.VMEM((parts, rows, width), jnp.float32),
-            pltpu.SemaphoreType.DMA((parts,)),
-            pltpu.SemaphoreType.DMA((parts,)),
-        ],
+        [pltpu.VMEM((parts, rows, width), jnp.float32), pltpu.SemaphoreType.DMA((parts,))],
         LIMIT,
     )
     return updated
 
 
-def line_of_four(inputs, gate_pre, grad_out, w_down, proj_in, proj_out, early):
+def line_of_four(inputs, gate_pre, grad_out, w_down, proj_in, proj_out, early, late):
     send = functools.partial(lax.ppermute, axis_name="tensor")
     pairs = [(0, 1), (1, 0), (2, 3), (3, 2)]
     inner = [(1, 2), (2, 1)]
@@ -406,23 +401,26 @@
         ahead = arrived[n + 1] if n < 4 else arrived[n]
         end_outer = send(after(end_inner[h][at : at + size], ahead, done[n]), perm=outward)
         arrived.append(end_outer)
-        kept, acc, right = last_block(
-            where, end_inner[h], at, end_outer, start, kept, acc, gate_pre, proj_out.T, second
+        bring = [*early, late] if n == len(sizes) - 2 else []
+        kept, acc, right, *brought = last_block(
+            where, end_inner[h], at, end_outer, start, kept, acc, gate_pre, proj_out.T, second, bring
         )
+        if bring:
+            *early, late = brought
         rights.append(right)
         done.append(right)
         start += size
-    return outer_products(where, total, sent, rights).reshape(-1, PROJ * PROJ)
-
-
-def any_line(inputs, gate_pre, grad_out, w_down, proj_in, proj_out, early):
+    return outer_products(where, total, sent, rights).reshape(-1, PROJ * PROJ), early, late
+
+
+def any_line(inputs, gate_pre, grad_out, w_down, proj_in, proj_out, early, late):
     in_part = jnp.dot(inputs, proj_in, preferred_element_type=jnp.float32)
     in_proj = lax.psum(in_part, "tensor").reshape(-1, LEN, PROJ)
     gathered = lax.all_gather(grad_out, "tensor", axis=1, tiled=True)
     up_grad = (dot_nt(gathered, w_down) * silu(gate_pre.astype(jnp.float32))).astype(jnp.bfloat16)
     out_part = jnp.dot(up_grad, proj_out, preferred_element_type=jnp.float32).reshape(-1, LEN, PROJ)
     grads = jnp.einsum("sti,stj->sij", in_proj, out_part, precision=HIGHEST)
-    return grads.reshape(-1, PROJ * PROJ)
+    return grads.reshape(-1, PROJ * PROJ), early, late
 
 
 def swap(a, axis, bit):
@@ -439,30 +437,25 @@
     return a
 
 
-def xor_order_sum(terms):
-    while len(terms) > 1:
-        terms = [terms[i] + terms[i + 1] for i in range(0, len(terms), 2)]
-    return terms[0]
-
-
-def xor_gather(a, axis):
-    for bit in bits(axis):
-        a = jnp.concatenate([a, swap(a, axis, bit)], axis=0)
-    return a
-
-
 def on_device(inputs, gate_pre, grad_out, w_down, proj_in, proj_out, hessian, queries):
     count = lax.axis_size("dp")
     parts = [queries] + [swap(queries, "dp", s) for s in range(1, count)]
     line = line_of_four if lax.axis_size("tensor") == 4 else any_line
-    grads = line(inputs, gate_pre, grad_out, w_down, proj_in, proj_out, parts)
+    grads, parts, hessian = line(inputs, gate_pre, grad_out, w_down, proj_in, proj_out, parts, hessian)
     grads = xor_sum(grads, "tensor")
 
     me = lax.axis_index("dp")
     order = lax.axis_index("tensor") * count + jnp.stack([me ^ s for s in range(count)])
     scores = score_parts(order.astype(jnp.int32), grads, parts)
-    others = [swap(scores, "tensor", bit) for bit in range(1, lax.axis_size("tensor"))]
-    all_grads = after(xor_gather(grads, "dp"), scores)
+    all_grads = after(grads, scores)
+    *first, last = bits("tensor")
+    for n, bit in enumerate(bits("dp")):
+        all_grads = jnp.concatenate([all_grads, swap(all_grads, "dp", bit)], axis=0)
+        if n == 0:
+            for score_bit in first:
+                scores = scores + swap(scores, "tensor", score_bit)
+            all_grads = after(all_grads, scores)
+    others = swap(scores, "tensor", last)
     row_count = hessian.shape[0]
     at = lax.axis_index(("tensor", "dp"))
     if row_count % 128:
@@ -470,8 +463,8 @@
         updated = hessian + jnp.dot(mine.T, all_grads, precision=HIGHEST) / all_grads.shape[0]
     else:
         updated = update(at.reshape(1).astype(jnp.int32), all_grads, hessian)
-    updated, *others = lax.optimization_barrier((updated, *others))
-    return (updated, xor_order_sum([scores, *others]))
+    updated, others = lax.optimization_barrier((updated, others))
+    return (updated, scores + others)
 
 
 def solution(mesh):

time: 171 us -> 170 us (level)
  waiting for transfers between devices: 56.4 us -> 53.7 us
  local copies, waits for them, and re-layouts: 7.58 us -> 9.78 us
    unnamed x10 -> x14, local copies, waits for them, and re-layouts: 2.51 us -> 4.7 us
    ppermute x10 -> x9, waiting for transfers between devices: 16.9 us -> 15.4 us  [swap(): lax.ppermute(a, axis, [(i, i ^ bit) for i in range(lax.axis_size(axis))])]
    ppermute x10 -> x9, starting transfers between devices: 10.5 us -> 11.2 us  [swap(): lax.ppermute(a, axis, [(i, i ^ bit) for i in range(lax.axis_size(axis))])]
  transfers between devices with their start and end apart: 25 -> 24, of which waited for: 14 -> 13; matrix products, arithmetic and copies ran while one was open for 3% -> 3% of each run, Pallas kernels for 41% -> 40%
where the time goes in v9:
time: 170 us; the launch traced here: 169 us
  Pallas kernels  69.8 us (41%)
  waiting for transfers between devices  53.7 us (32%)
  starting transfers between devices  34.1 us (20%)
  local copies, waits for them, and re-layouts  9.78 us (6%)
    pallas_call x14, Pallas kernels, call(): pl.pallas_call(body, grid_spec=pltpu.PrefetchScalarGridSpec(num_scalar_pr...  69.8 us
    ppermute x9, waiting for transfers between devices, swap(): lax.ppermute(a, axis, [(i, i ^ bit) for i in range(lax.axis_size(axis))])  15.4 us
    ppermute x1, waiting for transfers between devices, line_of_four(): pair = send(grad_out, perm=pairs)  15.3 us
    ppermute x2, waiting for transfers between devices, line_of_four(): mid_outer = [send(after(a, begun), perm=outward) for a in mid_inner]  14.3 us
    ppermute x9, starting transfers between devices, swap(): lax.ppermute(a, axis, [(i, i ^ bit) for i in range(lax.axis_size(axis))])  11.2 us
    ppermute x5, starting transfers between devices, line_of_four(): send(after(end_inner[h][at:at + size], ahead, done[n]), perm=outward)  6.63 us
    ppermute x5, waiting for transfers between devices, line_of_four(): send(after(end_inner[h][at:at + size], ahead, done[n]), perm=outward)  5.84 us
    ppermute x1, starting transfers between devices, line_of_four(): from_end = send(after(in_part, mid_inner[0]), perm=inward)  5.83 us
  transfers between devices with their start and end apart: 24, of which 13 were waited for; matrix products, arithmetic and copies ran while one was open for 3% of the time, Pallas kernels for 40%

profile of v9, /device:TPU:0, one launch (start us, length us, event | category | flops | bytes accessed | tf_op | source)
XLA Modules:
  0.0 169.2 jit_solution(12315091445587829694)
XLA Ops:
  0.6 3.1 %collective-permute-start.5 = (bf16[1024,1024]{1,0:T(8,128)(2,1)}, bf16[1024,1024]{1,0:T(8,128)(2,1)}, u32[]{:S(2)}, u32[]{:S(2)}) collective-permute-start(bf16[1024,1024]{1,0:T(8,128)(2,1)} %own), channel_id=1, source_target_pairs={{0,4},{4,0},{8,12},{12,8},{1,5},{5,1},{9,13},{13,9},{2,6},{6,2},{1... | collective-permute-start | bytes 6291464 | tf_op jit(solution)/shard_map/ppermute | solution.py:380
  3.7 3.1 %fusion.1 = (bf16[512,1024]{1,0:T(8,128)(2,1)}, bf16[512,1024]{1,0:T(8,128)(2,1)}) fusion(bf16[1024,1024]{1,0:T(8,128)(2,1)} %own), kind=kLoop, calls=%fused_computation.4 | loop fusion | bytes 4194304 | tf_op jit(solution)/shard_map/slice | solution.py:381
  7.6 1.6 collective-permute-start.3
  9.5 1.6 copy-done.4
  12.0 1.3 input_block.1.a
  14.1 3.0 %collective-permute-done.3.rest_2_ = f32[256,256]{1,0:T(8,128)} collective-permute-done((f32[256,256]{1,0:T(8,128)}, f32[256,256]{1,0:T(8,128)}, u32[]{:S(2)}, u32[]{:S(2)}) %collective-permute-start.3) | collective-permute-done | bytes 262176 | tf_op jit(solution)/shard_map/ppermute | solution.py:427
  17.1 4.7 %collective-permute-done.4.rest_3_ = f32[256,256]{1,0:T(8,128)} collective-permute-done((f32[256,256]{1,0:T(8,128)}, f32[256,256]{1,0:T(8,128)}, u32[]{:S(2)}, u32[]{:S(2)}) %collective-permute-start.4) | collective-permute-done | bytes 262176 | tf_op jit(solution)/shard_map/ppermute | solution.py:427
  21.8 12.0 %own_block.1 = (f32[1024,3584]{1,0:T(8,128)S(1)}, bf16[1024,3584]{1,0:T(8,128)(2,1)S(1)}, f32[8,128]{1,0:T(8,128)S(1)}) custom-call(s32[5]{0:T(128)S(1)} %stack.42.where, bf16[1024,1024]{1,0:T(8,128)(2,1)S(1)} %copy-done.1, bf16[3584,4096]{1,0:T(8,128)(2,1)} %refs_4_.1, bf16[3584,4096]{1,0:T(8,128)(2,1)} %refs_4_.1), custom_call_target="tpu_custom_call" | custom-call | flops 1000 | bytes 1000 | tf_op jit(solution)/shard_map/own_block/pallas_call | solution.py:40
  35.2 15.3 %collective-permute-done.5.refs_0_ = bf16[1024,1024]{1,0:T(8,128)(2,1)} collective-permute-done((bf16[1024,1024]{1,0:T(8,128)(2,1)}, bf16[1024,1024]{1,0:T(8,128)(2,1)}, u32[]{:S(2)}, u32[]{:S(2)}) %collective-permute-start.5) | collective-permute-done | bytes 2097184 | tf_op jit(solution)/shard_map/ppermute | solution.py:380
  50.5 1.7 %fusion = (bf16[512,1024]{1,0:T(8,128)(2,1)S(1)}, bf16[512,1024]{1,0:T(8,128)(2,1)S(1)}) fusion(bf16[1024,1024]{1,0:T(8,128)(2,1)} %collective-permute-done.5.refs_0_), kind=kLoop, calls=%fused_computation.3 | loop fusion | bytes 4194304 | tf_op jit(solution)/shard_map/slice | solution.py:387
  53.0 5.8 %collective-permute-start.1 = (f32[64,1024]{1,0:T(8,128)S(1)}, f32[64,1024]{1,0:T(8,128)S(1)}, u32[]{:S(2)}, u32[]{:S(2)}) collective-permute-start(f32[64,1024]{1,0:T(8,128)S(1)} %input_block.1.a), channel_id=1, source_target_pairs={{0,4},{12,8},{1,5},{13,9},{2,6},{14,10},{3,7},{15,11},{16,20},{28,... | collective-permute-start | bytes 786440 | tf_op jit(solution)/shard_map/ppermute | solution.py:384
  60.1 2.8 %collective-permute-done.1.b = f32[64,1024]{1,0:T(8,128)S(1)} collective-permute-done((f32[64,1024]{1,0:T(8,128)S(1)}, f32[64,1024]{1,0:T(8,128)S(1)}, u32[]{:S(2)}, u32[]{:S(2)}) %collective-permute-start.1) | collective-permute-done | bytes 262176 | tf_op jit(solution)/shard_map/ppermute | solution.py:384
  63.5 9.4 %collective-permute-done.9.refs_2_ = bf16[512,1024]{1,0:T(8,128)(2,1)S(1)} collective-permute-done((bf16[512,1024]{1,0:T(8,128)(2,1)S(1)}, bf16[512,1024]{1,0:T(8,128)(2,1)S(1)}, u32[]{:S(2)}, u32[]{:S(2)}) %collective-permute-start.9) | collective-permute-done | bytes 1048608 | tf_op jit(solution)/shard_map/ppermute | solution.py:386
  74.3 12.9 %add_block_1.1 = (f32[1024,3584]{1,0:T(8,128)S(1)}, f32[8,128]{1,0:T(8,128)S(1)}) custom-call(s32[5]{0:T(128)S(1)} %stack.42.where, bf16[1024,1024]{1,0:T(8,128)(2,1)} %collective-permute-done.5.refs_0_, bf16[3584,4096]{1,0:T(8,128)(2,1)} %refs_4_.1, f32[1024,3584]{1,0:T(8,128)S(1)} %get-tuple-element.48.refs_2_, ...), custom_call_target="tpu_custom_call", output_to_operand_aliasing={{0}: (3, {})} | custom-call | flops 7516192768 | bytes 1000 | tf_op jit(solution)/shard_map/add_block_1/pallas_call | solution.py:40
  90.4 4.9 %collective-permute-done.12.refs_3_ = bf16[512,1024]{1,0:T(8,128)(2,1)S(1)} collective-permute-done((bf16[512,1024]{1,0:T(8,128)(2,1)S(1)}, bf16[512,1024]{1,0:T(8,128)(2,1)S(1)}, u32[]{:S(2)}, u32[]{:S(2)}) %collective-permute-start.12) | collective-permute-done | bytes 1048608 | tf_op jit(solution)/shard_map/ppermute | solution.py:386
  95.3 12.3 %add_block_2.1 = (f32[1024,3584]{1,0:T(8,128)S(1)}, f32[8,128]{1,0:T(8,128)S(1)}) custom-call(s32[5]{0:T(128)S(1)} %stack.42.where, bf16[512,1024]{1,0:T(8,128)(2,1)S(1)} %collective-permute-done.refs_0_, bf16[512,1024]{1,0:T(8,128)(2,1)S(1)} %collective-permute-done.11.refs_1_, ...), custom_call_target="tpu_custom_call", output_to_operand_aliasing={{0}: (6, {})} | custom-call | flops 1000 | bytes 1000 | tf_op jit(solution)/shard_map/add_block_2/pallas_call | solution.py:40
  109.1 5.5 %last_block.5 = (bf16[1024,3584]{1,0:T(8,128)(2,1)S(1)}, f32[1024,3584]{1,0:T(8,128)S(1)}, f32[256,64]{1,0:T(8,128)S(1)}) custom-call(s32[5]{0:T(128)S(1)} %stack.42.where, bf16[512,1024]{1,0:T(8,128)(2,1)S(1)} %collective-permute-done.8.inner, bf16[256,1024]{1,0:T(8,128)(2,1)S(1)} %collective-permute-done.10.outer, ...), custom_call_target="tpu_custom_call", output_to_operand_aliasing={{0}: (3, {}), {1}: (4, {})} | custom-call | flops 1000 | bytes 1000 | tf_op jit(solution)/shard_map/last_block/pallas_call | solution.py:40
  114.6 3.8 %collective-permute-done.13.outer = bf16[256,1024]{1,0:T(8,128)(2,1)S(1)} collective-permute-done((bf16[256,1024]{1,0:T(8,128)(2,1)S(1)}, bf16[256,1024]{1,0:T(8,128)(2,1)S(1)}, u32[]{:S(2)}, u32[]{:S(2)}) %collective-permute-start.13) | collective-permute-done | bytes 524320 | tf_op jit(solution)/shard_map/ppermute | solution.py:402
  118.3 1.5 collective-permute-start.16
  119.8 5.5 %last_block.6 = (bf16[1024,3584]{1,0:T(8,128)(2,1)S(1)}, f32[1024,3584]{1,0:T(8,128)S(1)}, f32[256,64]{1,0:T(8,128)S(1)}) custom-call(s32[5]{0:T(128)S(1)} %stack.42.where, bf16[512,1024]{1,0:T(8,128)(2,1)S(1)} %collective-permute-done.8.inner, bf16[256,1024]{1,0:T(8,128)(2,1)S(1)} %collective-permute-done.13.outer, ...), custom_call_target="tpu_custom_call", output_to_operand_aliasing={{0}: (3, {}), {1}: (4, {})} | custom-call | flops 1000 | bytes 1000 | tf_op jit(solution)/shard_map/last_block/pallas_call | solution.py:40
  127.9 1.6 collective-permute-done.15.outer
  129.6 5.5 %last_block.7 = (bf16[1024,3584]{1,0:T(8,128)(2,1)S(1)}, f32[1024,3584]{1,0:T(8,128)S(1)}, f32[256,64]{1,0:T(8,128)S(1)}) custom-call(s32[5]{0:T(128)S(1)} %stack.42.where, bf16[512,1024]{1,0:T(8,128)(2,1)S(1)} %collective-permute-done.14.inner, bf16[256,1024]{1,0:T(8,128)(2,1)S(1)} %collective-permute-done.15.outer, ...), custom_call_target="tpu_custom_call", output_to_operand_aliasing={{0}: (3, {}), {1}: (4, {})} | custom-call | flops 1000 | bytes 1000 | tf_op jit(solution)/shard_map/last_block/pallas_call | solution.py:40
  135.2 5.3 %last_block.8 = (bf16[1024,3584]{1,0:T(8,128)(2,1)S(1)}, f32[1024,3584]{1,0:T(8,128)S(1)}, f32[128,64]{1,0:T(8,128)S(1)}, f32[256,256]{1,0:T(8,128)S(1)}, f32[25...) custom-call(s32[5]{0:T(128)S(1)} %stack.42.where, ...), custom_call_target="tpu_custom_call", output_to_operand_aliasing={{0}: (3, {}), {1}: (4, {})} | custom-call | flops 1000 | bytes 1000 | tf_op jit(solution)/shard_map/last_block/pallas_call | solution.py:40
  140.8 4.2 %last_block.9 = (bf16[1024,3584]{1,0:T(8,128)(2,1)S(1)}, f32[1024,3584]{1,0:T(8,128)S(1)}, f32[128,64]{1,0:T(8,128)S(1)}) custom-call(s32[5]{0:T(128)S(1)} %stack.42.where, bf16[512,1024]{1,0:T(8,128)(2,1)S(1)} %collective-permute-done.14.inner, bf16[128,1024]{1,0:T(8,128)(2,1)S(1)} %collective-permute-done.17.outer, ...), custom_call_target="tpu_custom_call", output_to_operand_aliasing={{0}: (3, {}), {1}: (4, {})} | custom-call | flops 1000 | bytes 1000 | tf_op jit(solution)/shard_map/last_block/pallas_call | solution.py:40
  146.9 3.3 %collective-permute-done.18 = f32[2,4096]{1,0:T(2,128)S(1)} collective-permute-done((f32[2,4096]{1,0:T(2,128)S(1)}, f32[2,4096]{1,0:T(2,128)S(1)}, u32[]{:S(2)}, u32[]{:S(2)}) %collective-permute-start.18) | collective-permute-done | bytes 32800 | tf_op jit(solution)/shard_map/ppermute | solution.py:427
  150.2 2.8 %collective-permute-start.19 = (f32[2,4096]{1,0:T(2,128)S(1)}, f32[2,4096]{1,0:T(2,128)S(1)}, u32[]{:S(2)}, u32[]{:S(2)}) collective-permute-start(f32[2,4096]{1,0:T(2,128)S(1)} %add.31), channel_id=1, source_target_pairs={{0,8},{4,12},{8,0},{12,4},{1,9},{5,13},{9,1},{13,5},{2,10},{6,14},... | collective-permute-start | bytes 98312 | tf_op jit(solution)/shard_map/ppermute | solution.py:427
  153.0 2.0 %collective-permute-done.19 = f32[2,4096]{1,0:T(2,128)S(1)} collective-permute-done((f32[2,4096]{1,0:T(2,128)S(1)}, f32[2,4096]{1,0:T(2,128)S(1)}, u32[]{:S(2)}, u32[]{:S(2)}) %collective-permute-start.19) | collective-permute-done | bytes 32800 | tf_op jit(solution)/shard_map/ppermute | solution.py:427
  157.1 2.4 %collective-permute-done.21 = f32[2,256]{1,0:T(2,128)S(1)} collective-permute-done((f32[2,256]{1,0:T(2,128)S(1)}, f32[2,256]{1,0:T(2,128)S(1)}, u32[]{:S(2)}, u32[]{:S(2)}) %collective-permute-start.21) | collective-permute-done | bytes 2080 | tf_op jit(solution)/shard_map/ppermute | solution.py:427
  159.6 1.5 collective-permute-start.22
  161.1 2.9 %collective-permute-start.23 = (f32[2,256]{1,0:T(2,128)S(1)}, f32[2,256]{1,0:T(2,128)S(1)}, u32[]{:S(2)}, u32[]{:S(2)}) collective-permute-start(f32[2,256]{1,0:T(2,128)S(1)} %add.35), channel_id=1, source_target_pairs={{0,8},{4,12},{8,0},{12,4},{1,9},{5,13},{9,1},{13,5},{2,10},{6,14},... | collective-permute-start | bytes 6152 | tf_op jit(solution)/shard_map/ppermute | solution.py:427
  164.0 2.2 %copy-done.3 = f32[256,4096]{1,0:T(8,128)S(1)} copy-done((f32[256,4096]{1,0:T(8,128)S(1)}, f32[256,4096]{1,0:T(8,128)}, u32[]{:S(2)}) %copy-start.3) | copy-done | bytes 4194328
  166.2 2.3 %hessian_update.1 = f32[256,4096]{1,0:T(8,128)} custom-call(s32[1]{0:T(128)} %bitcast.row, f32[8,4096]{1,0:T(8,128)S(1)} %pad_maximum_fusion.grads.mine, f32[8,4096]{1,0:T(8,128)S(1)} %pad_maximum_fusion.grads.mine, f32[256,4096]{1,0:T(8,128)S(1)} %copy-done.3), custom_call_target="tpu_custom_call" | custom-call | flops 1000 | bytes 1000 | tf_op jit(solution)/shard_map/hessian_update/pallas_call | solution.py:40
  (59 shorter events, 20.4 us)
Async XLA Ops:
  0.6 21.2 %copy-start.1 = (bf16[1024,1024]{1,0:T(8,128)(2,1)S(1)}, bf16[1024,1024]{1,0:T(8,128)(2,1)}, u32[]{:S(2)}) copy-start(bf16[1024,1024]{1,0:T(8,128)(2,1)} %own) | copy-start | bytes 6291460
  0.6 49.9 %collective-permute-start.5 = (bf16[1024,1024]{1,0:T(8,128)(2,1)}, bf16[1024,1024]{1,0:T(8,128)(2,1)}, u32[]{:S(2)}, u32[]{:S(2)}) collective-permute-start(bf16[1024,1024]{1,0:T(8,128)(2,1)} %own), channel_id=1, source_target_pairs={{0,4},{4,0},{8,12},{12,8},{1,5},{5,1},{9,13},{13,9},{2,6},{6,2},{1... | collective-permute-start | bytes 6291464 | tf_op jit(solution)/shard_map/ppermute | solution.py:380
  6.8 27.1 %collective-permute-start = (bf16[512,1024]{1,0:T(8,128)(2,1)}, bf16[512,1024]{1,0:T(8,128)(2,1)S(1)}, u32[]{:S(2)}, u32[]{:S(2)}) collective-permute-start(bf16[512,1024]{1,0:T(8,128)(2,1)} %get-tuple-element.85), channel_id=1, source_target_pairs={{4,8},{8,4},{5,9},{9,5},{6,10},{10,6},{7,11},{11,7},{20,24},{24,20... | collective-permute-start | bytes 3145736 | tf_op jit(solution)/shard_map/ppermute | solution.py:382
  7.5 5.8 %collective-permute-start.2 = (f32[256,256]{1,0:T(8,128)}, f32[256,256]{1,0:T(8,128)S(1)}, u32[]{:S(2)}, u32[]{:S(2)}) collective-permute-start(f32[256,256]{1,0:T(8,128)} %rest_0_.1), channel_id=1, source_target_pairs={{0,1},{1,0},{2,3},{3,2},{4,5},{5,4},{6,7},{7,6},{8,9},{9,8},{10,11... | collective-permute-start | bytes 786440 | tf_op jit(solution)/shard_map/ppermute | solution.py:427
  7.6 9.5 %collective-permute-start.3 = (f32[256,256]{1,0:T(8,128)}, f32[256,256]{1,0:T(8,128)}, u32[]{:S(2)}, u32[]{:S(2)}) collective-permute-start(f32[256,256]{1,0:T(8,128)} %rest_0_.1), channel_id=1, source_target_pairs={{0,2},{1,3},{2,0},{3,1},{4,6},{5,7},{6,4},{7,5},{8,10},{9,11},{10,... | collective-permute-start | bytes 786440 | tf_op jit(solution)/shard_map/ppermute | solution.py:427
  9.1 12.6 %collective-permute-start.4 = (f32[256,256]{1,0:T(8,128)}, f32[256,256]{1,0:T(8,128)}, u32[]{:S(2)}, u32[]{:S(2)}) collective-permute-start(f32[256,256]{1,0:T(8,128)} %rest_0_.1), channel_id=1, source_target_pairs={{0,3},{1,2},{2,1},{3,0},{4,7},{5,6},{6,5},{7,4},{8,11},{9,10},{10,... | collective-permute-start | bytes 786440 | tf_op jit(solution)/shard_map/ppermute | solution.py:427
  9.5 1.6 copy-start.4
  11.1 0.9 copy-start.5
  13.3 20.5 %copy-start.6 = (f32[256,256]{1,0:T(8,128)}, f32[256,256]{1,0:T(8,128)S(1)}, u32[]{:S(2)}) copy-start(f32[256,256]{1,0:T(8,128)S(1)} %collective-permute-done.2.rest_1_) | copy-start | bytes 786436
  13.3 45.5 %collective-permute-start.11 = (bf16[512,1024]{1,0:T(8,128)(2,1)}, bf16[512,1024]{1,0:T(8,128)(2,1)S(1)}, u32[]{:S(2)}, u32[]{:S(2)}) collective-permute-start(bf16[512,1024]{1,0:T(8,128)(2,1)} %get-tuple-element.84), channel_id=1, source_target_pairs={{4,8},{8,4},{5,9},{9,5},{6,10},{10,6},{7,11},{11,7},{20,24},{24,20... | collective-permute-start | bytes 3145736 | tf_op jit(solution)/shard_map/ppermute | solution.py:382
  33.9 39.0 %collective-permute-start.9 = (bf16[512,1024]{1,0:T(8,128)(2,1)S(1)}, bf16[512,1024]{1,0:T(8,128)(2,1)S(1)}, u32[]{:S(2)}, u32[]{:S(2)}) collective-permute-start(bf16[512,1024]{1,0:T(8,128)(2,1)S(1)} %collective-permute-done.refs_0_), channel_id=1, source_target_pairs={{4,0},{8,12},{5,1},{9,13},{6,2},{10,14},{7,3},{11,15},{20,16},{24,... | collective-permute-start | bytes 3145736 | tf_op jit(solution)/shard_map/ppermute | solution.py:386
  52.2 35.5 %collective-permute-start.8 = (bf16[512,1024]{1,0:T(8,128)(2,1)S(1)}, bf16[512,1024]{1,0:T(8,128)(2,1)S(1)}, u32[]{:S(2)}, u32[]{:S(2)}) collective-permute-start(bf16[512,1024]{1,0:T(8,128)(2,1)S(1)} %get-tuple-element.83), channel_id=1, source_target_pairs={{4,8},{8,4},{5,9},{9,5},{6,10},{10,6},{7,11},{11,7},{20,24},{24,20... | collective-permute-start | bytes 3145736 | tf_op jit(solution)/shard_map/ppermute | solution.py:387
  53.0 10.0 %collective-permute-start.1 = (f32[64,1024]{1,0:T(8,128)S(1)}, f32[64,1024]{1,0:T(8,128)S(1)}, u32[]{:S(2)}, u32[]{:S(2)}) collective-permute-start(f32[64,1024]{1,0:T(8,128)S(1)} %input_block.1.a), channel_id=1, source_target_pairs={{0,4},{12,8},{1,5},{13,9},{2,6},{14,10},{3,7},{15,11},{16,20},{28,... | collective-permute-start | bytes 786440 | tf_op jit(solution)/shard_map/ppermute | solution.py:384
  58.8 36.5 %collective-permute-start.12 = (bf16[512,1024]{1,0:T(8,128)(2,1)S(1)}, bf16[512,1024]{1,0:T(8,128)(2,1)S(1)}, u32[]{:S(2)}, u32[]{:S(2)}) collective-permute-start(bf16[512,1024]{1,0:T(8,128)(2,1)S(1)} %collective-permute-done.11.refs_1_), channel_id=1, source_target_pairs={{4,0},{8,12},{5,1},{9,13},{6,2},{10,14},{7,3},{11,15},{20,16},{24,... | collective-permute-start | bytes 3145736 | tf_op jit(solution)/shard_map/ppermute | solution.py:386
  72.9 14.3 %collective-permute-start.6 = (f32[64,1024]{1,0:T(8,128)S(1)}, f32[64,1024]{1,0:T(8,128)S(1)}, u32[]{:S(2)}, u32[]{:S(2)}) collective-permute-start(f32[64,1024]{1,0:T(8,128)S(1)} %side.1.a), channel_id=1, source_target_pairs={{4,8},{8,4},{5,9},{9,5},{6,10},{10,6},{7,11},{11,7},{20,24},{24,20... | collective-permute-start | bytes 786440 | tf_op jit(solution)/shard_map/ppermute | solution.py:389
  73.5 34.1 %collective-permute-start.14 = (bf16[512,1024]{1,0:T(8,128)(2,1)S(1)}, bf16[512,1024]{1,0:T(8,128)(2,1)S(1)}, u32[]{:S(2)}, u32[]{:S(2)}) collective-permute-start(bf16[512,1024]{1,0:T(8,128)(2,1)S(1)} %get-tuple-element.82), channel_id=1, source_target_pairs={{4,8},{8,4},{5,9},{9,5},{6,10},{10,6},{7,11},{11,7},{20,24},{24,20... | collective-permute-start | bytes 3145736 | tf_op jit(solution)/shard_map/ppermute | solution.py:387
  87.8 19.8 %collective-permute-start.10 = (bf16[256,1024]{1,0:T(8,128)(2,1)S(1)}, bf16[256,1024]{1,0:T(8,128)(2,1)S(1)}, u32[]{:S(2)}, u32[]{:S(2)}) collective-permute-start(bf16[256,1024]{1,0:T(8,128)(2,1)S(1)} %get-tuple-element.50), channel_id=1, source_target_pairs={{4,0},{8,12},{5,1},{9,13},{6,2},{10,14},{7,3},{11,15},{20,16},{24,... | collective-permute-start | bytes 1572872 | tf_op jit(solution)/shard_map/ppermute | solution.py:402
  89.1 29.2 %collective-permute-start.13 = (bf16[256,1024]{1,0:T(8,128)(2,1)S(1)}, bf16[256,1024]{1,0:T(8,128)(2,1)S(1)}, u32[]{:S(2)}, u32[]{:S(2)}) collective-permute-start(bf16[256,1024]{1,0:T(8,128)(2,1)S(1)} %get-tuple-element.57), channel_id=1, source_target_pairs={{4,0},{8,12},{5,1},{9,13},{6,2},{10,14},{7,3},{11,15},{20,16},{24,... | collective-permute-start | bytes 1572872 | tf_op jit(solution)/shard_map/ppermute | solution.py:402
  95.3 13.7 %copy-start = (bf16[3584,64]{0,1:T(8,128)(2,1)S(1)}, bf16[3584,64]{0,1:T(8,128)(2,1)}, u32[]{:S(2)}) copy-start(bf16[3584,64]{0,1:T(8,128)(2,1)} %param.13) | copy-start | bytes 1376260
  107.7 21.9 %collective-permute-start.15 = (bf16[256,1024]{1,0:T(8,128)(2,1)S(1)}, bf16[256,1024]{1,0:T(8,128)(2,1)S(1)}, u32[]{:S(2)}, u32[]{:S(2)}) collective-permute-start(bf16[256,1024]{1,0:T(8,128)(2,1)S(1)} %slice.40), channel_id=1, source_target_pairs={{4,0},{8,12},{5,1},{9,13},{6,2},{10,14},{7,3},{11,15},{20,16},{24,... | collective-permute-start | bytes 1572872 | tf_op jit(solution)/shard_map/ppermute | solution.py:402
  118.3 16.9 %collective-permute-start.16 = (bf16[128,1024]{1,0:T(8,128)(2,1)S(1)}, bf16[128,1024]{1,0:T(8,128)(2,1)S(1)}, u32[]{:S(2)}, u32[]{:S(2)}) collective-permute-start(bf16[128,1024]{1,0:T(8,128)(2,1)S(1)} %get-tuple-element.65), channel_id=1, source_target_pairs={{4,0},{8,12},{5,1},{9,13},{6,2},{10,14},{7,3},{11,15},{20,16},{24,... | collective-permute-start | bytes 786440 | tf_op jit(solution)/shard_map/ppermute | solution.py:402
  125.3 15.5 %collective-permute-start.17 = (bf16[128,1024]{1,0:T(8,128)(2,1)S(1)}, bf16[128,1024]{1,0:T(8,128)(2,1)S(1)}, u32[]{:S(2)}, u32[]{:S(2)}) collective-permute-start(bf16[128,1024]{1,0:T(8,128)(2,1)S(1)} %get-tuple-element.69), channel_id=1, source_target_pairs={{4,0},{8,12},{5,1},{9,13},{6,2},{10,14},{7,3},{11,15},{20,16},{24,... | collective-permute-start | bytes 786440 | tf_op jit(solution)/shard_map/ppermute | solution.py:402
  126.6 18.4 %collective-permute-start.7 = (bf16[64,1024]{1,0:T(8,128)(2,1)S(1)}, bf16[64,1024]{1,0:T(8,128)(2,1)S(1)}, u32[]{:S(2)}, u32[]{:S(2)}) collective-permute-start(bf16[64,1024]{1,0:T(8,128)(2,1)S(1)} %convert_element_type.4), channel_id=1, source_target_pairs={{4,0},{8,12},{5,1},{9,13},{6,2},{10,14},{7,3},{11,15},{20,16},{24,... | collective-permute-start | bytes 393224 | tf_op jit(solution)/shard_map/ppermute | solution.py:390
  140.5 4.6 %copy-start.2 = (f32[256,4096]{1,0:T(8,128)}, f32[256,4096]{1,0:T(8,128)S(1)}, u32[]{:S(2)}) copy-start(f32[256,4096]{1,0:T(8,128)S(1)} %get-tuple-element.79.hessian) | copy-start | bytes 12582916
  146.1 4.0 %collective-permute-start.18 = (f32[2,4096]{1,0:T(2,128)S(1)}, f32[2,4096]{1,0:T(2,128)S(1)}, u32[]{:S(2)}, u32[]{:S(2)}) collective-permute-start(f32[2,4096]{1,0:T(2,128)S(1)} %reshape.11), channel_id=1, source_target_pairs={{0,4},{4,0},{8,12},{12,8},{1,5},{5,1},{9,13},{13,9},{2,6},{6,2},{1... | collective-permute-start | bytes 98312 | tf_op jit(solution)/shard_map/ppermute | solution.py:427
  150.2 4.9 %collective-permute-start.19 = (f32[2,4096]{1,0:T(2,128)S(1)}, f32[2,4096]{1,0:T(2,128)S(1)}, u32[]{:S(2)}, u32[]{:S(2)}) collective-permute-start(f32[2,4096]{1,0:T(2,128)S(1)} %add.31), channel_id=1, source_target_pairs={{0,8},{4,12},{8,0},{12,4},{1,9},{5,13},{9,1},{13,5},{2,10},{6,14},... | collective-permute-start | bytes 98312 | tf_op jit(solution)/shard_map/ppermute | solution.py:427
  155.8 3.7 %collective-permute-start.20 = (f32[2,4096]{1,0:T(2,128)S(1)}, f32[2,4096]{1,0:T(2,128)S(1)}, u32[]{:S(2)}, u32[]{:S(2)}) collective-permute-start(f32[2,4096]{1,0:T(2,128)S(1)} %add.32.grads), channel_id=1, source_target_pairs={{0,1},{1,0},{2,3},{3,2},{4,5},{5,4},{6,7},{7,6},{8,9},{9,8},{10,11... | collective-permute-start | bytes 98312 | tf_op jit(solution)/shard_map/ppermute | solution.py:427
  155.9 3.7 %collective-permute-start.21 = (f32[2,256]{1,0:T(2,128)S(1)}, f32[2,256]{1,0:T(2,128)S(1)}, u32[]{:S(2)}, u32[]{:S(2)}) collective-permute-start(f32[2,256]{1,0:T(2,128)S(1)} %scores.1), channel_id=1, source_target_pairs={{0,4},{4,0},{8,12},{12,8},{1,5},{5,1},{9,13},{13,9},{2,6},{6,2},{1... | collective-permute-start | bytes 6152 | tf_op jit(solution)/shard_map/ppermute | solution.py:427
  159.6 4.4 %collective-permute-start.22 = (f32[4,4096]{1,0:T(4,128)S(1)}, f32[4,4096]{1,0:T(4,128)S(1)}, u32[]{:S(2)}, u32[]{:S(2)}) collective-permute-start(f32[4,4096]{1,0:T(4,128)S(1)} %pad_maximum_fusion.1), channel_id=1, source_target_pairs={{0,2},{1,3},{2,0},{3,1},{4,6},{5,7},{6,4},{7,5},{8,10},{9,11},{10,... | collective-permute-start | bytes 196616 | tf_op jit(solution)/shard_map/ppermute | solution.py:427
  161.1 7.5 %collective-permute-start.23 = (f32[2,256]{1,0:T(2,128)S(1)}, f32[2,256]{1,0:T(2,128)S(1)}, u32[]{:S(2)}, u32[]{:S(2)}) collective-permute-start(f32[2,256]{1,0:T(2,128)S(1)} %add.35), channel_id=1, source_target_pairs={{0,8},{4,12},{8,0},{12,4},{1,9},{5,13},{9,1},{13,5},{2,10},{6,14},... | collective-permute-start | bytes 6152 | tf_op jit(solution)/shard_map/ppermute | solution.py:427
  164.0 2.2 %copy-start.3 = (f32[256,4096]{1,0:T(8,128)S(1)}, f32[256,4096]{1,0:T(8,128)}, u32[]{:S(2)}) copy-start(f32[256,4096]{1,0:T(8,128)} %copy-done.2) | copy-start | bytes 12582916

commit v10 on v9

--- a/solution.py
+++ b/solution.py
@@ -13,6 +13,7 @@
 NT = (((1,), (1,)), ((), ()))
 TILE = 512
 LIMIT = 16
+FIRST_PART = 5
 ANYWHERE = pl.BlockSpec(memory_space=pl.ANY)
 INSIDE = pl.BlockSpec(memory_space=pltpu.VMEM)
 OUTSIDE = pl.BlockSpec(memory_space=pltpu.HBM)
@@ -224,8 +225,9 @@
 
 
 def outer_body(where, total, sent, *refs):
-    *rights, grads = refs
+    *rights, grads, wide = refs
     left_t = jnp.where(where[4] == 1, total[...], sent[...].astype(jnp.float32))
+    wide[...] = jnp.zeros_like(wide)
     start = 0
     terms = [None] * grads.shape[0]
     for right in rights:
@@ -237,11 +239,16 @@
         terms[s] = term if terms[s] is None else terms[s] + term
         start += size
     for s, term in enumerate(terms):
-        grads[s] = term
+        wide[:, :PROJ] = term
+        even = wide[pl.ds(0, PROJ // 2, stride=2), :]
+        odd = wide[pl.ds(1, PROJ // 2, stride=2), :]
+        rows = even + pltpu.roll(odd, PROJ, 1)
+        for i in range(PROJ // 2):
+            grads[s : s + 1, i * 2 * PROJ : (i + 1) * 2 * PROJ] = rows[i : i + 1, :]
 
 
 def outer_products(where, total, sent, rights):
-    shape = (total.shape[1] // LEN, PROJ, PROJ)
+    shape = (total.shape[1] // LEN, PROJ * PROJ)
     (grads,) = call(
         outer_body,
         "outer_products",
@@ -249,9 +256,9 @@
         (1,),
         (total, sent, *rights),
         [fixed(a.shape) for a in (total, sent, *rights)],
-        [pl.BlockSpec(shape, lambda j, where: (0, 0, 0))],
+        [pl.BlockSpec(shape, lambda j, where: (0, 0))],
         [jax.ShapeDtypeStruct(shape, jnp.float32)],
-        [],
+        [pltpu.VMEM((PROJ, 2 * PROJ), jnp.float32)],
         LIMIT,
     )
     return grads
@@ -277,7 +284,7 @@
     out[...] = a[...] + b[...]
 
 
-def score_body(order, grads, *rest):
+def score_body(where, grads, *rest):
     *parts, out = rest
     rows, width = parts[0].shape
     count = grads.shape[0]
@@ -286,26 +293,28 @@
     for s in range(count):
         products = None
         for p, part in enumerate(parts):
-            term = part[...] * grads[s : s + 1, columns(order, p, width)]
+            term = part[...] * grads[s : s + 1, columns(where, FIRST_PART + p, width)]
             products = term if products is None else products + term
         total = jnp.where(lane == s, jnp.sum(products, axis=1, keepdims=True), total)
     out[...] = total.T[:count, :]
 
 
-def score_parts(order, grads, parts):
+def score_parts(where, grads, parts):
     width = parts[0].shape[1]
     shape = (grads.shape[0], parts[0].shape[0])
     if width % 128:
-        slices = [lax.dynamic_slice_in_dim(grads, order[s] * width, width, 1) for s in range(len(parts))]
+        slices = [
+            lax.dynamic_slice_in_dim(grads, where[FIRST_PART + p] * width, width, 1) for p in range(len(parts))
+        ]
         return jnp.dot(jnp.concatenate(slices, axis=1), jnp.concatenate(parts, axis=1).T, precision=HIGHEST)
     (scores,) = call(
         score_body,
         "scores",
-        order,
+        where,
         (1,),
         (grads, *parts),
         [fixed(grads.shape)] + [INSIDE] * len(parts),
-        [pl.BlockSpec(shape, lambda j, order: (0, 0))],
+        [pl.BlockSpec(shape, lambda j, where: (0, 0))],
         [jax.ShapeDtypeStruct(shape, jnp.float32)],
         [],
         LIMIT,
@@ -321,7 +330,7 @@
     return high, middle, low
 
 
-def update_body(scale, row, grads, mine, hessian, out, new, out_sems):
+def update_body(scale, where, grads, mine, hessian, out, new, out_sems):
     columns = grads.shape[1]
     parts, _, width = new.shape
     high, middle, low = pieces(mine[...])
@@ -338,7 +347,7 @@
         write.wait()
 
 
-def update(row, grads, hessian):
+def update(where, grads, hessian):
     rows, columns = hessian.shape
     count = grads.shape[0]
     parts = 8
@@ -346,12 +355,12 @@
     (updated,) = call(
         functools.partial(update_body, 1.0 / count),
         "hessian_update",
-        row,
+        where,
         (1,),
         (grads, grads, hessian),
         [
             fixed(grads.shape),
-            pl.BlockSpec((count, rows), lambda j, row: (0, row[0]), pipeline_mode=pl.Buffered(1)),
+            pl.BlockSpec((count, rows), lambda j, where: (0, where[FIRST_PART]), pipeline_mode=pl.Buffered(1)),
             INSIDE,
         ],
         [ANYWHERE],
@@ -362,20 +371,13 @@
     return updated
 
 
-def line_of_four(inputs, gate_pre, grad_out, w_down, proj_in, proj_out, early, late):
+def line_of_four(where, inputs, gate_pre, grad_out, w_down, proj_in, proj_out, early, late):
     send = functools.partial(lax.ppermute, axis_name="tensor")
     pairs = [(0, 1), (1, 0), (2, 3), (3, 2)]
     inner = [(1, 2), (2, 1)]
     outward = [(1, 0), (2, 3)]
     inward = [(0, 1), (3, 2)]
     tokens = grad_out.shape[0]
-    z = lax.axis_index("tensor")
-    low = z < 2
-    middle = jnp.logical_and(z > 0, z < 3)
-    where = jnp.stack(
-        [z, z + 1 - 2 * (z % 2), jnp.where(low, 2, 1), jnp.where(low, 3, 0), middle.astype(z.dtype)]
-    ).astype(jnp.int32)
-
     halves = [slice(0, tokens // 2), slice(tokens // 2, tokens)]
     pair = send(grad_out, perm=pairs)
     own = [grad_out[half] for half in halves]
@@ -410,10 +412,10 @@
         rights.append(right)
         done.append(right)
         start += size
-    return outer_products(where, total, sent, rights).reshape(-1, PROJ * PROJ), early, late
-
-
-def any_line(inputs, gate_pre, grad_out, w_down, proj_in, proj_out, early, late):
+    return outer_products(where, total, sent, rights), early, late
+
+
+def any_line(where, inputs, gate_pre, grad_out, w_down, proj_in, proj_out, early, late):
     in_part = jnp.dot(inputs, proj_in, preferred_element_type=jnp.float32)
     in_proj = lax.psum(in_part, "tensor").reshape(-1, LEN, PROJ)
     gathered = lax.all_gather(grad_out, "tensor", axis=1, tiled=True)
@@ -437,16 +439,24 @@
     return a
 
 
+def positions():
+    z, me, count = lax.axis_index("tensor"), lax.axis_index("dp"), lax.axis_size("dp")
+    low = z < 2
+    middle = jnp.logical_and(z > 0, z < 3)
+    blocks = [z, z + 1 - 2 * (z % 2), jnp.where(low, 2, 1), jnp.where(low, 3, 0), middle]
+    parts = [z * count + (me ^ s) for s in range(count)]
+    return jnp.stack([a.astype(jnp.int32) for a in blocks + parts])
+
+
 def on_device(inputs, gate_pre, grad_out, w_down, proj_in, proj_out, hessian, queries):
+    where = positions()
     count = lax.axis_size("dp")
     parts = [queries] + [swap(queries, "dp", s) for s in range(1, count)]
     line = line_of_four if lax.axis_size("tensor") == 4 else any_line
-    grads, parts, hessian = line(inputs, gate_pre, grad_out, w_down, proj_in, proj_out, parts, hessian)
+    grads, parts, hessian = line(where, inputs, gate_pre, grad_out, w_down, proj_in, proj_out, parts, hessian)
     grads = xor_sum(grads, "tensor")
 
-    me = lax.axis_index("dp")
-    order = lax.axis_index("tensor") * count + jnp.stack([me ^ s for s in range(count)])
-    scores = score_parts(order.astype(jnp.int32), grads, parts)
+    scores = score_parts(where, grads, parts)
     all_grads = after(grads, scores)
     *first, last = bits("tensor")
     for n, bit in enumerate(bits("dp")):
@@ -457,12 +467,11 @@
             all_grads = after(all_grads, scores)
     others = swap(scores, "tensor", last)
     row_count = hessian.shape[0]
-    at = lax.axis_index(("tensor", "dp"))
     if row_count % 128:
-        mine = lax.dynamic_slice_in_dim(all_grads, at * row_count, row_count, 1)
+        mine = lax.dynamic_slice_in_dim(all_grads, where[FIRST_PART] * row_count, row_count, 1)
         updated = hessian + jnp.dot(mine.T, all_grads, precision=HIGHEST) / all_grads.shape[0]
     else:
-        updated = update(at.reshape(1).astype(jnp.int32), all_grads, hessian)
+        updated = update(where, all_grads, hessian)
     updated, others = lax.optimization_barrier((updated, others))
     return (updated, scores + others)
 

time: 170 us -> 168 us (0.988)
  local copies, waits for them, and re-layouts: 9.78 us -> 7.48 us
    unnamed x14 -> x10, local copies, waits for them, and re-layouts: 4.7 us -> 2.51 us
  transfers between devices with their start and end apart: 24 -> 24, of which waited for: 13 -> 13; matrix products, arithmetic and copies ran while one was open for 3% -> 3% of each run, Pallas kernels for 40% -> 41%
where the time goes in v10:
time: 168 us; the launch traced here: 167 us
  Pallas kernels  70.4 us (42%)
  waiting for transfers between devices  53.5 us (32%)
  starting transfers between devices  34.4 us (20%)
  local copies, waits for them, and re-layouts  7.48 us (4%)
    pallas_call x14, Pallas kernels, call(): pl.pallas_call(body, grid_spec=pltpu.PrefetchScalarGridSpec(num_scalar_pr...  70.4 us
    ppermute x1, waiting for transfers between devices, line_of_four(): pair = send(grad_out, perm=pairs)  15.4 us
    ppermute x9, waiting for transfers between devices, swap(): lax.ppermute(a, axis, [(i, i ^ bit) for i in range(lax.axis_size(axis))])  15.3 us
    ppermute x2, waiting for transfers between devices, line_of_four(): mid_outer = [send(after(a, begun), perm=outward) for a in mid_inner]  14.3 us
    ppermute x9, starting transfers between devices, swap(): lax.ppermute(a, axis, [(i, i ^ bit) for i in range(lax.axis_size(axis))])  11.4 us
    ppermute x5, starting transfers between devices, line_of_four(): send(after(end_inner[h][at:at + size], ahead, done[n]), perm=outward)  6.63 us
    ppermute x1, starting transfers between devices, line_of_four(): from_end = send(after(in_part, mid_inner[0]), perm=inward)  5.83 us
    ppermute x5, waiting for transfers between devices, line_of_four(): send(after(end_inner[h][at:at + size], ahead, done[n]), perm=outward)  5.72 us
  transfers between devices with their start and end apart: 24, of which 13 were waited for; matrix products, arithmetic and copies ran while one was open for 3% of the time, Pallas kernels for 41%

profile of v10, /device:TPU:0, one launch (start us, length us, event | category | flops | bytes accessed | tf_op | source)
XLA Modules:
  0.0 167.5 jit_solution(11603935277771400362)
XLA Ops:
  0.6 3.1 %collective-permute-start.5 = (bf16[1024,1024]{1,0:T(8,128)(2,1)}, bf16[1024,1024]{1,0:T(8,128)(2,1)}, u32[]{:S(2)}, u32[]{:S(2)}) collective-permute-start(bf16[1024,1024]{1,0:T(8,128)(2,1)} %own), channel_id=1, source_target_pairs={{0,4},{4,0},{8,12},{12,8},{1,5},{5,1},{9,13},{13,9},{2,6},{6,2},{1... | collective-permute-start | bytes 6291464 | tf_op jit(solution)/shard_map/ppermute | solution.py:382
  3.7 3.0 %fusion.1 = (bf16[512,1024]{1,0:T(8,128)(2,1)}, bf16[512,1024]{1,0:T(8,128)(2,1)}) fusion(bf16[1024,1024]{1,0:T(8,128)(2,1)} %own), kind=kLoop, calls=%fused_computation.3 | loop fusion | bytes 4194304 | tf_op jit(solution)/shard_map/slice | solution.py:383
  7.6 1.6 collective-permute-start.3
  9.5 1.6 copy-done.2
  12.0 1.3 input_block.1.a
  14.1 3.0 %collective-permute-done.3.rest_2_ = f32[256,256]{1,0:T(8,128)} collective-permute-done((f32[256,256]{1,0:T(8,128)}, f32[256,256]{1,0:T(8,128)}, u32[]{:S(2)}, u32[]{:S(2)}) %collective-permute-start.3) | collective-permute-done | bytes 262176 | tf_op jit(solution)/shard_map/ppermute | solution.py:429
  17.1 4.7 %collective-permute-done.4.rest_3_ = f32[256,256]{1,0:T(8,128)} collective-permute-done((f32[256,256]{1,0:T(8,128)}, f32[256,256]{1,0:T(8,128)}, u32[]{:S(2)}, u32[]{:S(2)}) %collective-permute-start.4) | collective-permute-done | bytes 262176 | tf_op jit(solution)/shard_map/ppermute | solution.py:429
  21.8 12.0 %own_block.1 = (f32[1024,3584]{1,0:T(8,128)S(1)}, bf16[1024,3584]{1,0:T(8,128)(2,1)S(1)}, f32[8,128]{1,0:T(8,128)S(1)}) custom-call(s32[9]{0:T(128)S(1)} %stack.43.where, bf16[1024,1024]{1,0:T(8,128)(2,1)S(1)} %copy-done.1, bf16[3584,4096]{1,0:T(8,128)(2,1)} %refs_4_.1, bf16[3584,4096]{1,0:T(8,128)(2,1)} %refs_4_.1), custom_call_target="tpu_custom_call" | custom-call | flops 1000 | bytes 1000 | tf_op jit(solution)/shard_map/own_block/pallas_call | solution.py:41
  33.8 1.3 collective-permute-start.9
  35.1 15.4 %collective-permute-done.5.refs_0_ = bf16[1024,1024]{1,0:T(8,128)(2,1)} collective-permute-done((bf16[1024,1024]{1,0:T(8,128)(2,1)}, bf16[1024,1024]{1,0:T(8,128)(2,1)}, u32[]{:S(2)}, u32[]{:S(2)}) %collective-permute-start.5) | collective-permute-done | bytes 2097184 | tf_op jit(solution)/shard_map/ppermute | solution.py:382
  50.5 1.7 %fusion = (bf16[512,1024]{1,0:T(8,128)(2,1)S(1)}, bf16[512,1024]{1,0:T(8,128)(2,1)S(1)}) fusion(bf16[1024,1024]{1,0:T(8,128)(2,1)} %collective-permute-done.5.refs_0_), kind=kLoop, calls=%fused_computation.2 | loop fusion | bytes 4194304 | tf_op jit(solution)/shard_map/slice | solution.py:389
  53.0 5.8 %collective-permute-start.1 = (f32[64,1024]{1,0:T(8,128)S(1)}, f32[64,1024]{1,0:T(8,128)S(1)}, u32[]{:S(2)}, u32[]{:S(2)}) collective-permute-start(f32[64,1024]{1,0:T(8,128)S(1)} %input_block.1.a), channel_id=1, source_target_pairs={{0,4},{12,8},{1,5},{13,9},{2,6},{14,10},{3,7},{15,11},{16,20},{28,... | collective-permute-start | bytes 786440 | tf_op jit(solution)/shard_map/ppermute | solution.py:386
  60.1 2.8 %collective-permute-done.1.b = f32[64,1024]{1,0:T(8,128)S(1)} collective-permute-done((f32[64,1024]{1,0:T(8,128)S(1)}, f32[64,1024]{1,0:T(8,128)S(1)}, u32[]{:S(2)}, u32[]{:S(2)}) %collective-permute-start.1) | collective-permute-done | bytes 262176 | tf_op jit(solution)/shard_map/ppermute | solution.py:386
  63.5 9.4 %collective-permute-done.9.refs_2_ = bf16[512,1024]{1,0:T(8,128)(2,1)S(1)} collective-permute-done((bf16[512,1024]{1,0:T(8,128)(2,1)S(1)}, bf16[512,1024]{1,0:T(8,128)(2,1)S(1)}, u32[]{:S(2)}, u32[]{:S(2)}) %collective-permute-start.9) | collective-permute-done | bytes 1048608 | tf_op jit(solution)/shard_map/ppermute | solution.py:388
  74.3 12.9 %add_block_1.1 = (f32[1024,3584]{1,0:T(8,128)S(1)}, f32[8,128]{1,0:T(8,128)S(1)}) custom-call(s32[9]{0:T(128)S(1)} %stack.43.where, bf16[1024,1024]{1,0:T(8,128)(2,1)} %collective-permute-done.5.refs_0_, bf16[3584,4096]{1,0:T(8,128)(2,1)} %refs_4_.1, f32[1024,3584]{1,0:T(8,128)S(1)} %get-tuple-element.48.refs_2_, ...), custom_call_target="tpu_custom_call", output_to_operand_aliasing={{0}: (3, {})} | custom-call | flops 7516192768 | bytes 1000 | tf_op jit(solution)/shard_map/add_block_1/pallas_call | solution.py:41
  90.4 4.9 %collective-permute-done.12.refs_3_ = bf16[512,1024]{1,0:T(8,128)(2,1)S(1)} collective-permute-done((bf16[512,1024]{1,0:T(8,128)(2,1)S(1)}, bf16[512,1024]{1,0:T(8,128)(2,1)S(1)}, u32[]{:S(2)}, u32[]{:S(2)}) %collective-permute-start.12) | collective-permute-done | bytes 1048608 | tf_op jit(solution)/shard_map/ppermute | solution.py:388
  95.3 12.3 %add_block_2.1 = (f32[1024,3584]{1,0:T(8,128)S(1)}, f32[8,128]{1,0:T(8,128)S(1)}) custom-call(s32[9]{0:T(128)S(1)} %stack.43.where, bf16[512,1024]{1,0:T(8,128)(2,1)S(1)} %collective-permute-done.refs_0_, bf16[512,1024]{1,0:T(8,128)(2,1)S(1)} %collective-permute-done.11.refs_1_, ...), custom_call_target="tpu_custom_call", output_to_operand_aliasing={{0}: (6, {})} | custom-call | flops 1000 | bytes 1000 | tf_op jit(solution)/shard_map/add_block_2/pallas_call | solution.py:41
  109.0 5.5 %last_block.5 = (bf16[1024,3584]{1,0:T(8,128)(2,1)S(1)}, f32[1024,3584]{1,0:T(8,128)S(1)}, f32[256,64]{1,0:T(8,128)S(1)}) custom-call(s32[9]{0:T(128)S(1)} %stack.43.where, bf16[512,1024]{1,0:T(8,128)(2,1)S(1)} %collective-permute-done.8.inner, bf16[256,1024]{1,0:T(8,128)(2,1)S(1)} %collective-permute-done.10.outer, ...), custom_call_target="tpu_custom_call", output_to_operand_aliasing={{0}: (3, {}), {1}: (4, {})} | custom-call | flops 1000 | bytes 1000 | tf_op jit(solution)/shard_map/last_block/pallas_call | solution.py:41
  114.6 3.8 %collective-permute-done.13.outer = bf16[256,1024]{1,0:T(8,128)(2,1)S(1)} collective-permute-done((bf16[256,1024]{1,0:T(8,128)(2,1)S(1)}, bf16[256,1024]{1,0:T(8,128)(2,1)S(1)}, u32[]{:S(2)}, u32[]{:S(2)}) %collective-permute-start.13) | collective-permute-done | bytes 524320 | tf_op jit(solution)/shard_map/ppermute | solution.py:404
  118.3 1.5 collective-permute-start.16
  119.8 5.5 %last_block.6 = (bf16[1024,3584]{1,0:T(8,128)(2,1)S(1)}, f32[1024,3584]{1,0:T(8,128)S(1)}, f32[256,64]{1,0:T(8,128)S(1)}) custom-call(s32[9]{0:T(128)S(1)} %stack.43.where, bf16[512,1024]{1,0:T(8,128)(2,1)S(1)} %collective-permute-done.8.inner, bf16[256,1024]{1,0:T(8,128)(2,1)S(1)} %collective-permute-done.13.outer, ...), custom_call_target="tpu_custom_call", output_to_operand_aliasing={{0}: (3, {}), {1}: (4, {})} | custom-call | flops 1000 | bytes 1000 | tf_op jit(solution)/shard_map/last_block/pallas_call | solution.py:41
  128.0 1.6 collective-permute-done.15.outer
  129.6 5.5 %last_block.7 = (bf16[1024,3584]{1,0:T(8,128)(2,1)S(1)}, f32[1024,3584]{1,0:T(8,128)S(1)}, f32[256,64]{1,0:T(8,128)S(1)}) custom-call(s32[9]{0:T(128)S(1)} %stack.43.where, bf16[512,1024]{1,0:T(8,128)(2,1)S(1)} %collective-permute-done.14.inner, bf16[256,1024]{1,0:T(8,128)(2,1)S(1)} %collective-permute-done.15.outer, ...), custom_call_target="tpu_custom_call", output_to_operand_aliasing={{0}: (3, {}), {1}: (4, {})} | custom-call | flops 1000 | bytes 1000 | tf_op jit(solution)/shard_map/last_block/pallas_call | solution.py:41
  135.2 5.3 %last_block.8 = (bf16[1024,3584]{1,0:T(8,128)(2,1)S(1)}, f32[1024,3584]{1,0:T(8,128)S(1)}, f32[128,64]{1,0:T(8,128)S(1)}, f32[256,256]{1,0:T(8,128)S(1)}, f32[25...) custom-call(s32[9]{0:T(128)S(1)} %stack.43.where, ...), custom_call_target="tpu_custom_call", output_to_operand_aliasing={{0}: (3, {}), {1}: (4, {})} | custom-call | flops 1000 | bytes 1000 | tf_op jit(solution)/shard_map/last_block/pallas_call | solution.py:41
  140.8 4.1 %last_block.9 = (bf16[1024,3584]{1,0:T(8,128)(2,1)S(1)}, f32[1024,3584]{1,0:T(8,128)S(1)}, f32[128,64]{1,0:T(8,128)S(1)}) custom-call(s32[9]{0:T(128)S(1)} %stack.43.where, bf16[512,1024]{1,0:T(8,128)(2,1)S(1)} %collective-permute-done.14.inner, bf16[128,1024]{1,0:T(8,128)(2,1)S(1)} %collective-permute-done.17.outer, ...), custom_call_target="tpu_custom_call", output_to_operand_aliasing={{0}: (3, {}), {1}: (4, {})} | custom-call | flops 1000 | bytes 1000 | tf_op jit(solution)/shard_map/last_block/pallas_call | solution.py:41
  146.8 3.2 %collective-permute-done.18 = f32[2,4096]{1,0:T(2,128)S(1)} collective-permute-done((f32[2,4096]{1,0:T(2,128)S(1)}, f32[2,4096]{1,0:T(2,128)S(1)}, u32[]{:S(2)}, u32[]{:S(2)}) %collective-permute-start.18) | collective-permute-done | bytes 32800 | tf_op jit(solution)/shard_map/ppermute | solution.py:429
  150.0 2.9 %collective-permute-start.19 = (f32[2,4096]{1,0:T(2,128)S(1)}, f32[2,4096]{1,0:T(2,128)S(1)}, u32[]{:S(2)}, u32[]{:S(2)}) collective-permute-start(f32[2,4096]{1,0:T(2,128)S(1)} %add.37), channel_id=1, source_target_pairs={{0,8},{4,12},{8,0},{12,4},{1,9},{5,13},{9,1},{13,5},{2,10},{6,14},... | collective-permute-start | bytes 98312 | tf_op jit(solution)/shard_map/ppermute | solution.py:429
  152.9 2.0 %collective-permute-done.19 = f32[2,4096]{1,0:T(2,128)S(1)} collective-permute-done((f32[2,4096]{1,0:T(2,128)S(1)}, f32[2,4096]{1,0:T(2,128)S(1)}, u32[]{:S(2)}, u32[]{:S(2)}) %collective-permute-start.19) | collective-permute-done | bytes 32800 | tf_op jit(solution)/shard_map/ppermute | solution.py:429
  157.0 2.4 %collective-permute-done.21 = f32[2,256]{1,0:T(2,128)S(1)} collective-permute-done((f32[2,256]{1,0:T(2,128)S(1)}, f32[2,256]{1,0:T(2,128)S(1)}, u32[]{:S(2)}, u32[]{:S(2)}) %collective-permute-start.21) | collective-permute-done | bytes 2080 | tf_op jit(solution)/shard_map/ppermute | solution.py:429
  159.5 1.6 collective-permute-start.22
  161.0 2.9 %collective-permute-start.23 = (f32[2,256]{1,0:T(2,128)S(1)}, f32[2,256]{1,0:T(2,128)S(1)}, u32[]{:S(2)}, u32[]{:S(2)}) collective-permute-start(f32[2,256]{1,0:T(2,128)S(1)} %add.39), channel_id=1, source_target_pairs={{0,8},{4,12},{8,0},{12,4},{1,9},{5,13},{9,1},{13,5},{2,10},{6,14},... | collective-permute-start | bytes 6152 | tf_op jit(solution)/shard_map/ppermute | solution.py:429
  164.0 2.9 %hessian_update.1 = f32[256,4096]{1,0:T(8,128)} custom-call(s32[9]{0:T(128)S(1)} %stack.43.where, f32[8,4096]{1,0:T(8,128)S(1)} %pad_maximum_fusion.grads.mine, f32[8,4096]{1,0:T(8,128)S(1)} %pad_maximum_fusion.grads.mine, f32[256,4096]{1,0:T(8,128)S(1)} %get-tuple-element.79.hessian), custom_call_target="tpu_custom_call" | custom-call | flops 1000 | bytes 1000 | tf_op jit(solution)/shard_map/hessian_update/pallas_call | solution.py:41
  (53 shorter events, 19.1 us)
Async XLA Ops:
  0.6 21.1 %copy-start.1 = (bf16[1024,1024]{1,0:T(8,128)(2,1)S(1)}, bf16[1024,1024]{1,0:T(8,128)(2,1)}, u32[]{:S(2)}) copy-start(bf16[1024,1024]{1,0:T(8,128)(2,1)} %own) | copy-start | bytes 6291460
  0.6 49.9 %collective-permute-start.5 = (bf16[1024,1024]{1,0:T(8,128)(2,1)}, bf16[1024,1024]{1,0:T(8,128)(2,1)}, u32[]{:S(2)}, u32[]{:S(2)}) collective-permute-start(bf16[1024,1024]{1,0:T(8,128)(2,1)} %own), channel_id=1, source_target_pairs={{0,4},{4,0},{8,12},{12,8},{1,5},{5,1},{9,13},{13,9},{2,6},{6,2},{1... | collective-permute-start | bytes 6291464 | tf_op jit(solution)/shard_map/ppermute | solution.py:382
  6.8 27.0 %collective-permute-start = (bf16[512,1024]{1,0:T(8,128)(2,1)}, bf16[512,1024]{1,0:T(8,128)(2,1)S(1)}, u32[]{:S(2)}, u32[]{:S(2)}) collective-permute-start(bf16[512,1024]{1,0:T(8,128)(2,1)} %get-tuple-element.85), channel_id=1, source_target_pairs={{4,8},{8,4},{5,9},{9,5},{6,10},{10,6},{7,11},{11,7},{20,24},{24,20... | collective-permute-start | bytes 3145736 | tf_op jit(solution)/shard_map/ppermute | solution.py:384
  7.5 5.8 %collective-permute-start.2 = (f32[256,256]{1,0:T(8,128)}, f32[256,256]{1,0:T(8,128)S(1)}, u32[]{:S(2)}, u32[]{:S(2)}) collective-permute-start(f32[256,256]{1,0:T(8,128)} %rest_0_.1), channel_id=1, source_target_pairs={{0,1},{1,0},{2,3},{3,2},{4,5},{5,4},{6,7},{7,6},{8,9},{9,8},{10,11... | collective-permute-start | bytes 786440 | tf_op jit(solution)/shard_map/ppermute | solution.py:429
  7.6 9.5 %collective-permute-start.3 = (f32[256,256]{1,0:T(8,128)}, f32[256,256]{1,0:T(8,128)}, u32[]{:S(2)}, u32[]{:S(2)}) collective-permute-start(f32[256,256]{1,0:T(8,128)} %rest_0_.1), channel_id=1, source_target_pairs={{0,2},{1,3},{2,0},{3,1},{4,6},{5,7},{6,4},{7,5},{8,10},{9,11},{10,... | collective-permute-start | bytes 786440 | tf_op jit(solution)/shard_map/ppermute | solution.py:429
  9.1 12.6 %collective-permute-start.4 = (f32[256,256]{1,0:T(8,128)}, f32[256,256]{1,0:T(8,128)}, u32[]{:S(2)}, u32[]{:S(2)}) collective-permute-start(f32[256,256]{1,0:T(8,128)} %rest_0_.1), channel_id=1, source_target_pairs={{0,3},{1,2},{2,1},{3,0},{4,7},{5,6},{6,5},{7,4},{8,11},{9,10},{10,... | collective-permute-start | bytes 786440 | tf_op jit(solution)/shard_map/ppermute | solution.py:429
  9.5 1.6 copy-start.2
  11.1 0.9 copy-start.3
  13.3 20.5 %copy-start.4 = (f32[256,256]{1,0:T(8,128)}, f32[256,256]{1,0:T(8,128)S(1)}, u32[]{:S(2)}) copy-start(f32[256,256]{1,0:T(8,128)S(1)} %collective-permute-done.2.rest_1_) | copy-start | bytes 786436
  13.3 45.5 %collective-permute-start.11 = (bf16[512,1024]{1,0:T(8,128)(2,1)}, bf16[512,1024]{1,0:T(8,128)(2,1)S(1)}, u32[]{:S(2)}, u32[]{:S(2)}) collective-permute-start(bf16[512,1024]{1,0:T(8,128)(2,1)} %get-tuple-element.84), channel_id=1, source_target_pairs={{4,8},{8,4},{5,9},{9,5},{6,10},{10,6},{7,11},{11,7},{20,24},{24,20... | collective-permute-start | bytes 3145736 | tf_op jit(solution)/shard_map/ppermute | solution.py:384
  33.8 39.1 %collective-permute-start.9 = (bf16[512,1024]{1,0:T(8,128)(2,1)S(1)}, bf16[512,1024]{1,0:T(8,128)(2,1)S(1)}, u32[]{:S(2)}, u32[]{:S(2)}) collective-permute-start(bf16[512,1024]{1,0:T(8,128)(2,1)S(1)} %collective-permute-done.refs_0_), channel_id=1, source_target_pairs={{4,0},{8,12},{5,1},{9,13},{6,2},{10,14},{7,3},{11,15},{20,16},{24,... | collective-permute-start | bytes 3145736 | tf_op jit(solution)/shard_map/ppermute | solution.py:388
  52.2 35.5 %collective-permute-start.8 = (bf16[512,1024]{1,0:T(8,128)(2,1)S(1)}, bf16[512,1024]{1,0:T(8,128)(2,1)S(1)}, u32[]{:S(2)}, u32[]{:S(2)}) collective-permute-start(bf16[512,1024]{1,0:T(8,128)(2,1)S(1)} %get-tuple-element.83), channel_id=1, source_target_pairs={{4,8},{8,4},{5,9},{9,5},{6,10},{10,6},{7,11},{11,7},{20,24},{24,20... | collective-permute-start | bytes 3145736 | tf_op jit(solution)/shard_map/ppermute | solution.py:389
  53.0 10.0 %collective-permute-start.1 = (f32[64,1024]{1,0:T(8,128)S(1)}, f32[64,1024]{1,0:T(8,128)S(1)}, u32[]{:S(2)}, u32[]{:S(2)}) collective-permute-start(f32[64,1024]{1,0:T(8,128)S(1)} %input_block.1.a), channel_id=1, source_target_pairs={{0,4},{12,8},{1,5},{13,9},{2,6},{14,10},{3,7},{15,11},{16,20},{28,... | collective-permute-start | bytes 786440 | tf_op jit(solution)/shard_map/ppermute | solution.py:386
  58.8 36.5 %collective-permute-start.12 = (bf16[512,1024]{1,0:T(8,128)(2,1)S(1)}, bf16[512,1024]{1,0:T(8,128)(2,1)S(1)}, u32[]{:S(2)}, u32[]{:S(2)}) collective-permute-start(bf16[512,1024]{1,0:T(8,128)(2,1)S(1)} %collective-permute-done.11.refs_1_), channel_id=1, source_target_pairs={{4,0},{8,12},{5,1},{9,13},{6,2},{10,14},{7,3},{11,15},{20,16},{24,... | collective-permute-start | bytes 3145736 | tf_op jit(solution)/shard_map/ppermute | solution.py:388
  72.9 14.3 %collective-permute-start.6 = (f32[64,1024]{1,0:T(8,128)S(1)}, f32[64,1024]{1,0:T(8,128)S(1)}, u32[]{:S(2)}, u32[]{:S(2)}) collective-permute-start(f32[64,1024]{1,0:T(8,128)S(1)} %side.1.a), channel_id=1, source_target_pairs={{4,8},{8,4},{5,9},{9,5},{6,10},{10,6},{7,11},{11,7},{20,24},{24,20... | collective-permute-start | bytes 786440 | tf_op jit(solution)/shard_map/ppermute | solution.py:391
  73.5 34.1 %collective-permute-start.14 = (bf16[512,1024]{1,0:T(8,128)(2,1)S(1)}, bf16[512,1024]{1,0:T(8,128)(2,1)S(1)}, u32[]{:S(2)}, u32[]{:S(2)}) collective-permute-start(bf16[512,1024]{1,0:T(8,128)(2,1)S(1)} %get-tuple-element.82), channel_id=1, source_target_pairs={{4,8},{8,4},{5,9},{9,5},{6,10},{10,6},{7,11},{11,7},{20,24},{24,20... | collective-permute-start | bytes 3145736 | tf_op jit(solution)/shard_map/ppermute | solution.py:389
  87.8 19.8 %collective-permute-start.10 = (bf16[256,1024]{1,0:T(8,128)(2,1)S(1)}, bf16[256,1024]{1,0:T(8,128)(2,1)S(1)}, u32[]{:S(2)}, u32[]{:S(2)}) collective-permute-start(bf16[256,1024]{1,0:T(8,128)(2,1)S(1)} %get-tuple-element.50), channel_id=1, source_target_pairs={{4,0},{8,12},{5,1},{9,13},{6,2},{10,14},{7,3},{11,15},{20,16},{24,... | collective-permute-start | bytes 1572872 | tf_op jit(solution)/shard_map/ppermute | solution.py:404
  89.1 29.2 %collective-permute-start.13 = (bf16[256,1024]{1,0:T(8,128)(2,1)S(1)}, bf16[256,1024]{1,0:T(8,128)(2,1)S(1)}, u32[]{:S(2)}, u32[]{:S(2)}) collective-permute-start(bf16[256,1024]{1,0:T(8,128)(2,1)S(1)} %get-tuple-element.57), channel_id=1, source_target_pairs={{4,0},{8,12},{5,1},{9,13},{6,2},{10,14},{7,3},{11,15},{20,16},{24,... | collective-permute-start | bytes 1572872 | tf_op jit(solution)/shard_map/ppermute | solution.py:404
  95.3 13.7 %copy-start = (bf16[3584,64]{0,1:T(8,128)(2,1)S(1)}, bf16[3584,64]{0,1:T(8,128)(2,1)}, u32[]{:S(2)}) copy-start(bf16[3584,64]{0,1:T(8,128)(2,1)} %param.13) | copy-start | bytes 1376260
  107.7 21.9 %collective-permute-start.15 = (bf16[256,1024]{1,0:T(8,128)(2,1)S(1)}, bf16[256,1024]{1,0:T(8,128)(2,1)S(1)}, u32[]{:S(2)}, u32[]{:S(2)}) collective-permute-start(bf16[256,1024]{1,0:T(8,128)(2,1)S(1)} %slice.40), channel_id=1, source_target_pairs={{4,0},{8,12},{5,1},{9,13},{6,2},{10,14},{7,3},{11,15},{20,16},{24,... | collective-permute-start | bytes 1572872 | tf_op jit(solution)/shard_map/ppermute | solution.py:404
  118.3 16.9 %collective-permute-start.16 = (bf16[128,1024]{1,0:T(8,128)(2,1)S(1)}, bf16[128,1024]{1,0:T(8,128)(2,1)S(1)}, u32[]{:S(2)}, u32[]{:S(2)}) collective-permute-start(bf16[128,1024]{1,0:T(8,128)(2,1)S(1)} %get-tuple-element.65), channel_id=1, source_target_pairs={{4,0},{8,12},{5,1},{9,13},{6,2},{10,14},{7,3},{11,15},{20,16},{24,... | collective-permute-start | bytes 786440 | tf_op jit(solution)/shard_map/ppermute | solution.py:404
  125.4 15.5 %collective-permute-start.17 = (bf16[128,1024]{1,0:T(8,128)(2,1)S(1)}, bf16[128,1024]{1,0:T(8,128)(2,1)S(1)}, u32[]{:S(2)}, u32[]{:S(2)}) collective-permute-start(bf16[128,1024]{1,0:T(8,128)(2,1)S(1)} %get-tuple-element.69), channel_id=1, source_target_pairs={{4,0},{8,12},{5,1},{9,13},{6,2},{10,14},{7,3},{11,15},{20,16},{24,... | collective-permute-start | bytes 786440 | tf_op jit(solution)/shard_map/ppermute | solution.py:404
  126.7 18.2 %collective-permute-start.7 = (bf16[64,1024]{1,0:T(8,128)(2,1)S(1)}, bf16[64,1024]{1,0:T(8,128)(2,1)S(1)}, u32[]{:S(2)}, u32[]{:S(2)}) collective-permute-start(bf16[64,1024]{1,0:T(8,128)(2,1)S(1)} %convert_element_type.4), channel_id=1, source_target_pairs={{4,0},{8,12},{5,1},{9,13},{6,2},{10,14},{7,3},{11,15},{20,16},{24,... | collective-permute-start | bytes 393224 | tf_op jit(solution)/shard_map/ppermute | solution.py:392
  146.0 4.0 %collective-permute-start.18 = (f32[2,4096]{1,0:T(2,128)S(1)}, f32[2,4096]{1,0:T(2,128)S(1)}, u32[]{:S(2)}, u32[]{:S(2)}) collective-permute-start(f32[2,4096]{1,0:T(2,128)S(1)} %outer_products.1), channel_id=1, source_target_pairs={{0,4},{4,0},{8,12},{12,8},{1,5},{5,1},{9,13},{13,9},{2,6},{6,2},{1... | collective-permute-start | bytes 98312 | tf_op jit(solution)/shard_map/ppermute | solution.py:429
  150.0 4.9 %collective-permute-start.19 = (f32[2,4096]{1,0:T(2,128)S(1)}, f32[2,4096]{1,0:T(2,128)S(1)}, u32[]{:S(2)}, u32[]{:S(2)}) collective-permute-start(f32[2,4096]{1,0:T(2,128)S(1)} %add.37), channel_id=1, source_target_pairs={{0,8},{4,12},{8,0},{12,4},{1,9},{5,13},{9,1},{13,5},{2,10},{6,14},... | collective-permute-start | bytes 98312 | tf_op jit(solution)/shard_map/ppermute | solution.py:429
  155.7 3.7 %collective-permute-start.20 = (f32[2,4096]{1,0:T(2,128)S(1)}, f32[2,4096]{1,0:T(2,128)S(1)}, u32[]{:S(2)}, u32[]{:S(2)}) collective-permute-start(f32[2,4096]{1,0:T(2,128)S(1)} %add.38.grads), channel_id=1, source_target_pairs={{0,1},{1,0},{2,3},{3,2},{4,5},{5,4},{6,7},{7,6},{8,9},{9,8},{10,11... | collective-permute-start | bytes 98312 | tf_op jit(solution)/shard_map/ppermute | solution.py:429
  155.8 3.7 %collective-permute-start.21 = (f32[2,256]{1,0:T(2,128)S(1)}, f32[2,256]{1,0:T(2,128)S(1)}, u32[]{:S(2)}, u32[]{:S(2)}) collective-permute-start(f32[2,256]{1,0:T(2,128)S(1)} %scores.1), channel_id=1, source_target_pairs={{0,4},{4,0},{8,12},{12,8},{1,5},{5,1},{9,13},{13,9},{2,6},{6,2},{1... | collective-permute-start | bytes 6152 | tf_op jit(solution)/shard_map/ppermute | solution.py:429
  159.5 4.5 %collective-permute-start.22 = (f32[4,4096]{1,0:T(4,128)S(1)}, f32[4,4096]{1,0:T(4,128)S(1)}, u32[]{:S(2)}, u32[]{:S(2)}) collective-permute-start(f32[4,4096]{1,0:T(4,128)S(1)} %pad_maximum_fusion.1), channel_id=1, source_target_pairs={{0,2},{1,3},{2,0},{3,1},{4,6},{5,7},{6,4},{7,5},{8,10},{9,11},{10,... | collective-permute-start | bytes 196616 | tf_op jit(solution)/shard_map/ppermute | solution.py:429
  161.0 5.8 %collective-permute-start.23 = (f32[2,256]{1,0:T(2,128)S(1)}, f32[2,256]{1,0:T(2,128)S(1)}, u32[]{:S(2)}, u32[]{:S(2)}) collective-permute-start(f32[2,256]{1,0:T(2,128)S(1)} %add.39), channel_id=1, source_target_pairs={{0,8},{4,12},{8,0},{12,4},{1,9},{5,13},{9,1},{13,5},{2,10},{6,14},... | collective-permute-start | bytes 6152 | tf_op jit(solution)/shard_map/ppermute | solution.py:429

commit v11 on v10

--- a/solution.py
+++ b/solution.py
@@ -454,7 +454,7 @@
     parts = [queries] + [swap(queries, "dp", s) for s in range(1, count)]
     line = line_of_four if lax.axis_size("tensor") == 4 else any_line
     grads, parts, hessian = line(where, inputs, gate_pre, grad_out, w_down, proj_in, proj_out, parts, hessian)
-    grads = xor_sum(grads, "tensor")
+    grads = lax.all_gather(grads, "tensor").sum(0)
 
     scores = score_parts(where, grads, parts)
     all_grads = after(grads, scores)

time: 168 us -> 176 us (1.048)
  blocking collectives: 0 us -> 14 us
  starting transfers between devices: 34.4 us -> 29.2 us
  waiting for transfers between devices: 53.5 us -> 49.6 us
  local copies, waits for them, and re-layouts: 7.48 us -> 9.68 us
    all_gather x0 -> x1, blocking collectives: none -> 14 us  [on_device(): grads = lax.all_gather(grads, 'tensor').sum(0)]
    ppermute x9 -> x7, starting transfers between devices: 11.4 us -> 6.23 us  [swap(): lax.ppermute(a, axis, [(i, i ^ bit) for i in range(lax.axis_size(axis))])]
    ppermute x9 -> x7, waiting for transfers between devices: 15.3 us -> 11.4 us  [swap(): lax.ppermute(a, axis, [(i, i ^ bit) for i in range(lax.axis_size(axis))])]
    unnamed x10 -> x14, local copies, waits for them, and re-layouts: 2.51 us -> 4.7 us
  transfers between devices with their start and end apart: 24 -> 22, of which waited for: 13 -> 12; matrix products, arithmetic and copies ran while one was open for 3% -> 3% of each run, Pallas kernels for 41% -> 39%
where the time goes in v11:
time: 176 us; the launch traced here: 175 us
  Pallas kernels  70.5 us (40%)
  waiting for transfers between devices  49.6 us (28%)
  starting transfers between devices  29.2 us (17%)
  blocking collectives  14 us (8%)
  local copies, waits for them, and re-layouts  9.68 us (6%)
    pallas_call x14, Pallas kernels, call(): pl.pallas_call(body, grid_spec=pltpu.PrefetchScalarGridSpec(num_scalar_pr...  70.5 us
    ppermute x1, waiting for transfers between devices, line_of_four(): pair = send(grad_out, perm=pairs)  15.4 us
    ppermute x2, waiting for transfers between devices, line_of_four(): mid_outer = [send(after(a, begun), perm=outward) for a in mid_inner]  14.3 us
    all_gather x1, blocking collectives, on_device(): grads = lax.all_gather(grads, 'tensor').sum(0)  14 us
    ppermute x7, waiting for transfers between devices, swap(): lax.ppermute(a, axis, [(i, i ^ bit) for i in range(lax.axis_size(axis))])  11.4 us
    ppermute x5, starting transfers between devices, line_of_four(): send(after(end_inner[h][at:at + size], ahead, done[n]), perm=outward)  6.63 us
    ppermute x7, starting transfers between devices, swap(): lax.ppermute(a, axis, [(i, i ^ bit) for i in range(lax.axis_size(axis))])  6.23 us
    ppermute x1, starting transfers between devices, line_of_four(): from_end = send(after(in_part, mid_inner[0]), perm=inward)  5.83 us
  transfers between devices with their start and end apart: 22, of which 12 were waited for; matrix products, arithmetic and copies ran while one was open for 3% of the time, Pallas kernels for 39%

profile of v11, /device:TPU:0, one launch (start us, length us, event | category | flops | bytes accessed | tf_op | source)
XLA Modules:
  0.0 174.8 jit_solution(8352045815012322492)
XLA Ops:
  0.6 3.1 %collective-permute-start.5 = (bf16[1024,1024]{1,0:T(8,128)(2,1)}, bf16[1024,1024]{1,0:T(8,128)(2,1)}, u32[]{:S(2)}, u32[]{:S(2)}) collective-permute-start(bf16[1024,1024]{1,0:T(8,128)(2,1)} %own), channel_id=1, source_target_pairs={{0,4},{4,0},{8,12},{12,8},{1,5},{5,1},{9,13},{13,9},{2,6},{6,2},{1... | collective-permute-start | bytes 6291464 | tf_op jit(solution)/shard_map/ppermute | solution.py:382
  3.7 3.0 %fusion.1 = (bf16[512,1024]{1,0:T(8,128)(2,1)}, bf16[512,1024]{1,0:T(8,128)(2,1)}) fusion(bf16[1024,1024]{1,0:T(8,128)(2,1)} %own), kind=kLoop, calls=%fused_computation.3 | loop fusion | bytes 4194304 | tf_op jit(solution)/shard_map/slice | solution.py:383
  7.6 1.6 collective-permute-start.3
  9.5 1.6 copy-done.4
  12.0 1.3 input_block.1.a
  14.1 3.0 %collective-permute-done.3.rest_2_ = f32[256,256]{1,0:T(8,128)} collective-permute-done((f32[256,256]{1,0:T(8,128)}, f32[256,256]{1,0:T(8,128)}, u32[]{:S(2)}, u32[]{:S(2)}) %collective-permute-start.3) | collective-permute-done | bytes 262176 | tf_op jit(solution)/shard_map/ppermute | solution.py:429
  17.1 4.7 %collective-permute-done.4.rest_3_ = f32[256,256]{1,0:T(8,128)} collective-permute-done((f32[256,256]{1,0:T(8,128)}, f32[256,256]{1,0:T(8,128)}, u32[]{:S(2)}, u32[]{:S(2)}) %collective-permute-start.4) | collective-permute-done | bytes 262176 | tf_op jit(solution)/shard_map/ppermute | solution.py:429
  21.8 12.0 %own_block.1 = (f32[1024,3584]{1,0:T(8,128)S(1)}, bf16[1024,3584]{1,0:T(8,128)(2,1)S(1)}, f32[8,128]{1,0:T(8,128)S(1)}) custom-call(s32[9]{0:T(128)S(1)} %stack.43.where, bf16[1024,1024]{1,0:T(8,128)(2,1)S(1)} %copy-done.1, bf16[3584,4096]{1,0:T(8,128)(2,1)} %refs_4_.1, bf16[3584,4096]{1,0:T(8,128)(2,1)} %refs_4_.1), custom_call_target="tpu_custom_call" | custom-call | flops 1000 | bytes 1000 | tf_op jit(solution)/shard_map/own_block/pallas_call | solution.py:41
  33.8 1.3 collective-permute-start.9
  35.1 15.4 %collective-permute-done.5.refs_0_ = bf16[1024,1024]{1,0:T(8,128)(2,1)} collective-permute-done((bf16[1024,1024]{1,0:T(8,128)(2,1)}, bf16[1024,1024]{1,0:T(8,128)(2,1)}, u32[]{:S(2)}, u32[]{:S(2)}) %collective-permute-start.5) | collective-permute-done | bytes 2097184 | tf_op jit(solution)/shard_map/ppermute | solution.py:382
  50.5 1.7 fusion
  53.0 5.8 %collective-permute-start.1 = (f32[64,1024]{1,0:T(8,128)S(1)}, f32[64,1024]{1,0:T(8,128)S(1)}, u32[]{:S(2)}, u32[]{:S(2)}) collective-permute-start(f32[64,1024]{1,0:T(8,128)S(1)} %input_block.1.a), channel_id=1, source_target_pairs={{0,4},{12,8},{1,5},{13,9},{2,6},{14,10},{3,7},{15,11},{16,20},{28,... | collective-permute-start | bytes 786440 | tf_op jit(solution)/shard_map/ppermute | solution.py:386
  60.1 2.8 %collective-permute-done.1.b = f32[64,1024]{1,0:T(8,128)S(1)} collective-permute-done((f32[64,1024]{1,0:T(8,128)S(1)}, f32[64,1024]{1,0:T(8,128)S(1)}, u32[]{:S(2)}, u32[]{:S(2)}) %collective-permute-start.1) | collective-permute-done | bytes 262176 | tf_op jit(solution)/shard_map/ppermute | solution.py:386
  63.5 9.4 %collective-permute-done.9.refs_2_ = bf16[512,1024]{1,0:T(8,128)(2,1)S(1)} collective-permute-done((bf16[512,1024]{1,0:T(8,128)(2,1)S(1)}, bf16[512,1024]{1,0:T(8,128)(2,1)S(1)}, u32[]{:S(2)}, u32[]{:S(2)}) %collective-permute-start.9) | collective-permute-done | bytes 1048608 | tf_op jit(solution)/shard_map/ppermute | solution.py:388
  74.3 12.9 %add_block_1.1 = (f32[1024,3584]{1,0:T(8,128)S(1)}, f32[8,128]{1,0:T(8,128)S(1)}) custom-call(s32[9]{0:T(128)S(1)} %stack.43.where, bf16[1024,1024]{1,0:T(8,128)(2,1)} %collective-permute-done.5.refs_0_, bf16[3584,4096]{1,0:T(8,128)(2,1)} %refs_4_.1, f32[1024,3584]{1,0:T(8,128)S(1)} %get-tuple-element.48.refs_2_, ...), custom_call_target="tpu_custom_call", output_to_operand_aliasing={{0}: (3, {})} | custom-call | flops 7516192768 | bytes 1000 | tf_op jit(solution)/shard_map/add_block_1/pallas_call | solution.py:41
  90.4 4.9 %collective-permute-done.12.refs_3_ = bf16[512,1024]{1,0:T(8,128)(2,1)S(1)} collective-permute-done((bf16[512,1024]{1,0:T(8,128)(2,1)S(1)}, bf16[512,1024]{1,0:T(8,128)(2,1)S(1)}, u32[]{:S(2)}, u32[]{:S(2)}) %collective-permute-start.12) | collective-permute-done | bytes 1048608 | tf_op jit(solution)/shard_map/ppermute | solution.py:388
  95.3 12.3 %add_block_2.1 = (f32[1024,3584]{1,0:T(8,128)S(1)}, f32[8,128]{1,0:T(8,128)S(1)}) custom-call(s32[9]{0:T(128)S(1)} %stack.43.where, bf16[512,1024]{1,0:T(8,128)(2,1)S(1)} %collective-permute-done.refs_0_, bf16[512,1024]{1,0:T(8,128)(2,1)S(1)} %collective-permute-done.11.refs_1_, ...), custom_call_target="tpu_custom_call", output_to_operand_aliasing={{0}: (6, {})} | custom-call | flops 1000 | bytes 1000 | tf_op jit(solution)/shard_map/add_block_2/pallas_call | solution.py:41
  109.0 5.5 %last_block.5 = (bf16[1024,3584]{1,0:T(8,128)(2,1)S(1)}, f32[1024,3584]{1,0:T(8,128)S(1)}, f32[256,64]{1,0:T(8,128)S(1)}) custom-call(s32[9]{0:T(128)S(1)} %stack.43.where, bf16[512,1024]{1,0:T(8,128)(2,1)S(1)} %collective-permute-done.8.inner, bf16[256,1024]{1,0:T(8,128)(2,1)S(1)} %collective-permute-done.10.outer, ...), custom_call_target="tpu_custom_call", output_to_operand_aliasing={{0}: (3, {}), {1}: (4, {})} | custom-call | flops 1000 | bytes 1000 | tf_op jit(solution)/shard_map/last_block/pallas_call | solution.py:41
  114.6 3.8 %collective-permute-done.13.outer = bf16[256,1024]{1,0:T(8,128)(2,1)S(1)} collective-permute-done((bf16[256,1024]{1,0:T(8,128)(2,1)S(1)}, bf16[256,1024]{1,0:T(8,128)(2,1)S(1)}, u32[]{:S(2)}, u32[]{:S(2)}) %collective-permute-start.13) | collective-permute-done | bytes 524320 | tf_op jit(solution)/shard_map/ppermute | solution.py:404
  118.3 1.5 collective-permute-start.16
  119.8 5.5 %last_block.6 = (bf16[1024,3584]{1,0:T(8,128)(2,1)S(1)}, f32[1024,3584]{1,0:T(8,128)S(1)}, f32[256,64]{1,0:T(8,128)S(1)}) custom-call(s32[9]{0:T(128)S(1)} %stack.43.where, bf16[512,1024]{1,0:T(8,128)(2,1)S(1)} %collective-permute-done.8.inner, bf16[256,1024]{1,0:T(8,128)(2,1)S(1)} %collective-permute-done.13.outer, ...), custom_call_target="tpu_custom_call", output_to_operand_aliasing={{0}: (3, {}), {1}: (4, {})} | custom-call | flops 1000 | bytes 1000 | tf_op jit(solution)/shard_map/last_block/pallas_call | solution.py:41
  126.7 1.3 collective-permute-start.7
  128.0 1.6 collective-permute-done.15.outer
  129.6 5.5 %last_block.7 = (bf16[1024,3584]{1,0:T(8,128)(2,1)S(1)}, f32[1024,3584]{1,0:T(8,128)S(1)}, f32[256,64]{1,0:T(8,128)S(1)}) custom-call(s32[9]{0:T(128)S(1)} %stack.43.where, bf16[512,1024]{1,0:T(8,128)(2,1)S(1)} %collective-permute-done.14.inner, bf16[256,1024]{1,0:T(8,128)(2,1)S(1)} %collective-permute-done.15.outer, ...), custom_call_target="tpu_custom_call", output_to_operand_aliasing={{0}: (3, {}), {1}: (4, {})} | custom-call | flops 1000 | bytes 1000 | tf_op jit(solution)/shard_map/last_block/pallas_call | solution.py:41
  135.2 5.3 %last_block.8 = (bf16[1024,3584]{1,0:T(8,128)(2,1)S(1)}, f32[1024,3584]{1,0:T(8,128)S(1)}, f32[128,64]{1,0:T(8,128)S(1)}, f32[256,256]{1,0:T(8,128)S(1)}, f32[25...) custom-call(s32[9]{0:T(128)S(1)} %stack.43.where, ...), custom_call_target="tpu_custom_call", output_to_operand_aliasing={{0}: (3, {}), {1}: (4, {})} | custom-call | flops 1000 | bytes 1000 | tf_op jit(solution)/shard_map/last_block/pallas_call | solution.py:41
  140.8 4.2 %last_block.9 = (bf16[1024,3584]{1,0:T(8,128)(2,1)S(1)}, f32[1024,3584]{1,0:T(8,128)S(1)}, f32[128,64]{1,0:T(8,128)S(1)}) custom-call(s32[9]{0:T(128)S(1)} %stack.43.where, bf16[512,1024]{1,0:T(8,128)(2,1)S(1)} %collective-permute-done.14.inner, bf16[128,1024]{1,0:T(8,128)(2,1)S(1)} %collective-permute-done.17.outer, ...), custom_call_target="tpu_custom_call", output_to_operand_aliasing={{0}: (3, {}), {1}: (4, {})} | custom-call | flops 1000 | bytes 1000 | tf_op jit(solution)/shard_map/last_block/pallas_call | solution.py:41
  146.2 14.0 %all-gather.1 = f32[4,2,4096]{2,1,0:T(2,128)S(1)} all-gather(f32[1,2,4096]{2,1,0:T(2,128)S(1)} %bitcast.17), channel_id=2, replica_groups=mesh['groups'=2,'tensor'=4,'dp'=4] {'tensor'}, dimensions={0}, use_global_device_ids=true | all-gather | bytes 163840 | tf_op jit(solution)/shard_map/all_gather | solution.py:457
  162.2 2.5 %collective-permute-done.19 = f32[2,256]{1,0:T(2,128)S(1)} collective-permute-done((f32[2,256]{1,0:T(2,128)S(1)}, f32[2,256]{1,0:T(2,128)S(1)}, u32[]{:S(2)}, u32[]{:S(2)}) %collective-permute-start.19) | collective-permute-done | bytes 2080 | tf_op jit(solution)/shard_map/ppermute | solution.py:429
  164.7 1.6 collective-permute-start.20
  166.3 1.5 collective-permute-start.21
  169.1 2.2 %copy-done.3 = f32[256,4096]{1,0:T(8,128)S(1)} copy-done((f32[256,4096]{1,0:T(8,128)S(1)}, f32[256,4096]{1,0:T(8,128)}, u32[]{:S(2)}) %copy-start.3) | copy-done | bytes 4194328
  171.3 2.9 %hessian_update.1 = f32[256,4096]{1,0:T(8,128)} custom-call(s32[9]{0:T(128)S(1)} %stack.43.where, f32[8,4096]{1,0:T(8,128)S(1)} %pad_maximum_fusion.grads.mine, f32[8,4096]{1,0:T(8,128)S(1)} %pad_maximum_fusion.grads.mine, f32[256,4096]{1,0:T(8,128)S(1)} %copy-done.3), custom_call_target="tpu_custom_call" | custom-call | flops 1000 | bytes 1000 | tf_op jit(solution)/shard_map/hessian_update/pallas_call | solution.py:41
  (53 shorter events, 18.2 us)
Async XLA Ops:
  0.6 21.1 %copy-start.1 = (bf16[1024,1024]{1,0:T(8,128)(2,1)S(1)}, bf16[1024,1024]{1,0:T(8,128)(2,1)}, u32[]{:S(2)}) copy-start(bf16[1024,1024]{1,0:T(8,128)(2,1)} %own) | copy-start | bytes 6291460
  0.6 49.9 %collective-permute-start.5 = (bf16[1024,1024]{1,0:T(8,128)(2,1)}, bf16[1024,1024]{1,0:T(8,128)(2,1)}, u32[]{:S(2)}, u32[]{:S(2)}) collective-permute-start(bf16[1024,1024]{1,0:T(8,128)(2,1)} %own), channel_id=1, source_target_pairs={{0,4},{4,0},{8,12},{12,8},{1,5},{5,1},{9,13},{13,9},{2,6},{6,2},{1... | collective-permute-start | bytes 6291464 | tf_op jit(solution)/shard_map/ppermute | solution.py:382
  6.8 27.0 %collective-permute-start = (bf16[512,1024]{1,0:T(8,128)(2,1)}, bf16[512,1024]{1,0:T(8,128)(2,1)S(1)}, u32[]{:S(2)}, u32[]{:S(2)}) collective-permute-start(bf16[512,1024]{1,0:T(8,128)(2,1)} %get-tuple-element.85), channel_id=1, source_target_pairs={{4,8},{8,4},{5,9},{9,5},{6,10},{10,6},{7,11},{11,7},{20,24},{24,20... | collective-permute-start | bytes 3145736 | tf_op jit(solution)/shard_map/ppermute | solution.py:384
  7.5 5.8 %collective-permute-start.2 = (f32[256,256]{1,0:T(8,128)}, f32[256,256]{1,0:T(8,128)S(1)}, u32[]{:S(2)}, u32[]{:S(2)}) collective-permute-start(f32[256,256]{1,0:T(8,128)} %rest_0_.1), channel_id=1, source_target_pairs={{0,1},{1,0},{2,3},{3,2},{4,5},{5,4},{6,7},{7,6},{8,9},{9,8},{10,11... | collective-permute-start | bytes 786440 | tf_op jit(solution)/shard_map/ppermute | solution.py:429
  7.6 9.5 %collective-permute-start.3 = (f32[256,256]{1,0:T(8,128)}, f32[256,256]{1,0:T(8,128)}, u32[]{:S(2)}, u32[]{:S(2)}) collective-permute-start(f32[256,256]{1,0:T(8,128)} %rest_0_.1), channel_id=1, source_target_pairs={{0,2},{1,3},{2,0},{3,1},{4,6},{5,7},{6,4},{7,5},{8,10},{9,11},{10,... | collective-permute-start | bytes 786440 | tf_op jit(solution)/shard_map/ppermute | solution.py:429
  9.1 12.6 %collective-permute-start.4 = (f32[256,256]{1,0:T(8,128)}, f32[256,256]{1,0:T(8,128)}, u32[]{:S(2)}, u32[]{:S(2)}) collective-permute-start(f32[256,256]{1,0:T(8,128)} %rest_0_.1), channel_id=1, source_target_pairs={{0,3},{1,2},{2,1},{3,0},{4,7},{5,6},{6,5},{7,4},{8,11},{9,10},{10,... | collective-permute-start | bytes 786440 | tf_op jit(solution)/shard_map/ppermute | solution.py:429
  9.5 1.6 copy-start.4
  11.1 0.9 copy-start.5
  13.3 20.5 %copy-start.6 = (f32[256,256]{1,0:T(8,128)}, f32[256,256]{1,0:T(8,128)S(1)}, u32[]{:S(2)}) copy-start(f32[256,256]{1,0:T(8,128)S(1)} %collective-permute-done.2.rest_1_) | copy-start | bytes 786436
  13.3 45.5 %collective-permute-start.11 = (bf16[512,1024]{1,0:T(8,128)(2,1)}, bf16[512,1024]{1,0:T(8,128)(2,1)S(1)}, u32[]{:S(2)}, u32[]{:S(2)}) collective-permute-start(bf16[512,1024]{1,0:T(8,128)(2,1)} %get-tuple-element.84), channel_id=1, source_target_pairs={{4,8},{8,4},{5,9},{9,5},{6,10},{10,6},{7,11},{11,7},{20,24},{24,20... | collective-permute-start | bytes 3145736 | tf_op jit(solution)/shard_map/ppermute | solution.py:384
  33.8 39.1 %collective-permute-start.9 = (bf16[512,1024]{1,0:T(8,128)(2,1)S(1)}, bf16[512,1024]{1,0:T(8,128)(2,1)S(1)}, u32[]{:S(2)}, u32[]{:S(2)}) collective-permute-start(bf16[512,1024]{1,0:T(8,128)(2,1)S(1)} %collective-permute-done.refs_0_), channel_id=1, source_target_pairs={{4,0},{8,12},{5,1},{9,13},{6,2},{10,14},{7,3},{11,15},{20,16},{24,... | collective-permute-start | bytes 3145736 | tf_op jit(solution)/shard_map/ppermute | solution.py:388
  52.2 35.5 %collective-permute-start.8 = (bf16[512,1024]{1,0:T(8,128)(2,1)S(1)}, bf16[512,1024]{1,0:T(8,128)(2,1)S(1)}, u32[]{:S(2)}, u32[]{:S(2)}) collective-permute-start(bf16[512,1024]{1,0:T(8,128)(2,1)S(1)} %get-tuple-element.83), channel_id=1, source_target_pairs={{4,8},{8,4},{5,9},{9,5},{6,10},{10,6},{7,11},{11,7},{20,24},{24,20... | collective-permute-start | bytes 3145736 | tf_op jit(solution)/shard_map/ppermute | solution.py:389
  53.0 10.0 %collective-permute-start.1 = (f32[64,1024]{1,0:T(8,128)S(1)}, f32[64,1024]{1,0:T(8,128)S(1)}, u32[]{:S(2)}, u32[]{:S(2)}) collective-permute-start(f32[64,1024]{1,0:T(8,128)S(1)} %input_block.1.a), channel_id=1, source_target_pairs={{0,4},{12,8},{1,5},{13,9},{2,6},{14,10},{3,7},{15,11},{16,20},{28,... | collective-permute-start | bytes 786440 | tf_op jit(solution)/shard_map/ppermute | solution.py:386
  58.8 36.5 %collective-permute-start.12 = (bf16[512,1024]{1,0:T(8,128)(2,1)S(1)}, bf16[512,1024]{1,0:T(8,128)(2,1)S(1)}, u32[]{:S(2)}, u32[]{:S(2)}) collective-permute-start(bf16[512,1024]{1,0:T(8,128)(2,1)S(1)} %collective-permute-done.11.refs_1_), channel_id=1, source_target_pairs={{4,0},{8,12},{5,1},{9,13},{6,2},{10,14},{7,3},{11,15},{20,16},{24,... | collective-permute-start | bytes 3145736 | tf_op jit(solution)/shard_map/ppermute | solution.py:388
  72.9 14.3 %collective-permute-start.6 = (f32[64,1024]{1,0:T(8,128)S(1)}, f32[64,1024]{1,0:T(8,128)S(1)}, u32[]{:S(2)}, u32[]{:S(2)}) collective-permute-start(f32[64,1024]{1,0:T(8,128)S(1)} %side.1.a), channel_id=1, source_target_pairs={{4,8},{8,4},{5,9},{9,5},{6,10},{10,6},{7,11},{11,7},{20,24},{24,20... | collective-permute-start | bytes 786440 | tf_op jit(solution)/shard_map/ppermute | solution.py:391
  73.5 34.1 %collective-permute-start.14 = (bf16[512,1024]{1,0:T(8,128)(2,1)S(1)}, bf16[512,1024]{1,0:T(8,128)(2,1)S(1)}, u32[]{:S(2)}, u32[]{:S(2)}) collective-permute-start(bf16[512,1024]{1,0:T(8,128)(2,1)S(1)} %get-tuple-element.82), channel_id=1, source_target_pairs={{4,8},{8,4},{5,9},{9,5},{6,10},{10,6},{7,11},{11,7},{20,24},{24,20... | collective-permute-start | bytes 3145736 | tf_op jit(solution)/shard_map/ppermute | solution.py:389
  87.8 19.8 %collective-permute-start.10 = (bf16[256,1024]{1,0:T(8,128)(2,1)S(1)}, bf16[256,1024]{1,0:T(8,128)(2,1)S(1)}, u32[]{:S(2)}, u32[]{:S(2)}) collective-permute-start(bf16[256,1024]{1,0:T(8,128)(2,1)S(1)} %get-tuple-element.50), channel_id=1, source_target_pairs={{4,0},{8,12},{5,1},{9,13},{6,2},{10,14},{7,3},{11,15},{20,16},{24,... | collective-permute-start | bytes 1572872 | tf_op jit(solution)/shard_map/ppermute | solution.py:404
  89.1 29.2 %collective-permute-start.13 = (bf16[256,1024]{1,0:T(8,128)(2,1)S(1)}, bf16[256,1024]{1,0:T(8,128)(2,1)S(1)}, u32[]{:S(2)}, u32[]{:S(2)}) collective-permute-start(bf16[256,1024]{1,0:T(8,128)(2,1)S(1)} %get-tuple-element.57), channel_id=1, source_target_pairs={{4,0},{8,12},{5,1},{9,13},{6,2},{10,14},{7,3},{11,15},{20,16},{24,... | collective-permute-start | bytes 1572872 | tf_op jit(solution)/shard_map/ppermute | solution.py:404
  95.3 13.7 %copy-start = (bf16[3584,64]{0,1:T(8,128)(2,1)S(1)}, bf16[3584,64]{0,1:T(8,128)(2,1)}, u32[]{:S(2)}) copy-start(bf16[3584,64]{0,1:T(8,128)(2,1)} %param.13) | copy-start | bytes 1376260
  107.7 21.9 %collective-permute-start.15 = (bf16[256,1024]{1,0:T(8,128)(2,1)S(1)}, bf16[256,1024]{1,0:T(8,128)(2,1)S(1)}, u32[]{:S(2)}, u32[]{:S(2)}) collective-permute-start(bf16[256,1024]{1,0:T(8,128)(2,1)S(1)} %slice.40), channel_id=1, source_target_pairs={{4,0},{8,12},{5,1},{9,13},{6,2},{10,14},{7,3},{11,15},{20,16},{24,... | collective-permute-start | bytes 1572872 | tf_op jit(solution)/shard_map/ppermute | solution.py:404
  118.3 16.9 %collective-permute-start.16 = (bf16[128,1024]{1,0:T(8,128)(2,1)S(1)}, bf16[128,1024]{1,0:T(8,128)(2,1)S(1)}, u32[]{:S(2)}, u32[]{:S(2)}) collective-permute-start(bf16[128,1024]{1,0:T(8,128)(2,1)S(1)} %get-tuple-element.65), channel_id=1, source_target_pairs={{4,0},{8,12},{5,1},{9,13},{6,2},{10,14},{7,3},{11,15},{20,16},{24,... | collective-permute-start | bytes 786440 | tf_op jit(solution)/shard_map/ppermute | solution.py:404
  125.4 15.5 %collective-permute-start.17 = (bf16[128,1024]{1,0:T(8,128)(2,1)S(1)}, bf16[128,1024]{1,0:T(8,128)(2,1)S(1)}, u32[]{:S(2)}, u32[]{:S(2)}) collective-permute-start(bf16[128,1024]{1,0:T(8,128)(2,1)S(1)} %get-tuple-element.69), channel_id=1, source_target_pairs={{4,0},{8,12},{5,1},{9,13},{6,2},{10,14},{7,3},{11,15},{20,16},{24,... | collective-permute-start | bytes 786440 | tf_op jit(solution)/shard_map/ppermute | solution.py:404
  126.7 18.4 %collective-permute-start.7 = (bf16[64,1024]{1,0:T(8,128)(2,1)S(1)}, bf16[64,1024]{1,0:T(8,128)(2,1)S(1)}, u32[]{:S(2)}, u32[]{:S(2)}) collective-permute-start(bf16[64,1024]{1,0:T(8,128)(2,1)S(1)} %convert_element_type.4), channel_id=1, source_target_pairs={{4,0},{8,12},{5,1},{9,13},{6,2},{10,14},{7,3},{11,15},{20,16},{24,... | collective-permute-start | bytes 393224 | tf_op jit(solution)/shard_map/ppermute | solution.py:392
  140.5 4.6 %copy-start.2 = (f32[256,4096]{1,0:T(8,128)}, f32[256,4096]{1,0:T(8,128)S(1)}, u32[]{:S(2)}) copy-start(f32[256,4096]{1,0:T(8,128)S(1)} %get-tuple-element.79.hessian) | copy-start | bytes 12582916
  161.0 3.7 %collective-permute-start.18 = (f32[2,4096]{1,0:T(2,128)S(1)}, f32[2,4096]{1,0:T(2,128)S(1)}, u32[]{:S(2)}, u32[]{:S(2)}) collective-permute-start(f32[2,4096]{1,0:T(2,128)S(1)} %reduce_sum.9.grads), channel_id=1, source_target_pairs={{0,1},{1,0},{2,3},{3,2},{4,5},{5,4},{6,7},{7,6},{8,9},{9,8},{10,11... | collective-permute-start | bytes 98312 | tf_op jit(solution)/shard_map/ppermute | solution.py:429
  161.0 3.7 %collective-permute-start.19 = (f32[2,256]{1,0:T(2,128)S(1)}, f32[2,256]{1,0:T(2,128)S(1)}, u32[]{:S(2)}, u32[]{:S(2)}) collective-permute-start(f32[2,256]{1,0:T(2,128)S(1)} %scores.1), channel_id=1, source_target_pairs={{0,4},{4,0},{8,12},{12,8},{1,5},{5,1},{9,13},{13,9},{2,6},{6,2},{1... | collective-permute-start | bytes 6152 | tf_op jit(solution)/shard_map/ppermute | solution.py:429
  164.7 4.3 %collective-permute-start.20 = (f32[4,4096]{1,0:T(4,128)S(1)}, f32[4,4096]{1,0:T(4,128)S(1)}, u32[]{:S(2)}, u32[]{:S(2)}) collective-permute-start(f32[4,4096]{1,0:T(4,128)S(1)} %pad_maximum_fusion.1), channel_id=1, source_target_pairs={{0,2},{1,3},{2,0},{3,1},{4,6},{5,7},{6,4},{7,5},{8,10},{9,11},{10,... | collective-permute-start | bytes 196616 | tf_op jit(solution)/shard_map/ppermute | solution.py:429
  166.3 7.9 %collective-permute-start.21 = (f32[2,256]{1,0:T(2,128)S(1)}, f32[2,256]{1,0:T(2,128)S(1)}, u32[]{:S(2)}, u32[]{:S(2)}) collective-permute-start(f32[2,256]{1,0:T(2,128)S(1)} %add.31), channel_id=1, source_target_pairs={{0,8},{4,12},{8,0},{12,4},{1,9},{5,13},{9,1},{13,5},{2,10},{6,14},... | collective-permute-start | bytes 6152 | tf_op jit(solution)/shard_map/ppermute | solution.py:429
  169.1 2.2 %copy-start.3 = (f32[256,4096]{1,0:T(8,128)S(1)}, f32[256,4096]{1,0:T(8,128)}, u32[]{:S(2)}) copy-start(f32[256,4096]{1,0:T(8,128)} %copy-done.2) | copy-start | bytes 12582916

commit v12 on v10

--- a/solution.py
+++ b/solution.py
@@ -162,11 +162,50 @@
     )
 
 
-def last_body(start, inner_at, bring, where, inner, outer, kept, old, gate, po_t, _, *rest):
+def part_body(start, inner_at, low, bring, where, inner, outer, kept, old, *rest):
     far, rest = rest[:bring], rest[bring:]
-    _, _, right, *near = rest[: 3 + bring]
-    gates, po, gate_sems, po_sem, near_sems = rest[3 + bring :]
-    size = outer.shape[0]
+    _, acc, token, *near = rest[: 3 + bring]
+    near_sems = rest[3 + bring]
+    size, width = outer.shape
+    feats = pl.ds(low, width)
+    tokens = pl.ds(start, size)
+    brought = [pltpu.make_async_copy(a, b, near_sems.at[i]) for i, (a, b) in enumerate(zip(far, near))]
+    for copy in brought:
+        copy.start()
+    token[...] = jnp.zeros_like(token)
+    block = select(where, inner.at[pl.ds(inner_at, size), feats], outer)
+    for t in range(kept.shape[1] // TILE):
+        span = pl.ds(t * TILE, TILE)
+        acc[tokens, span] = old[tokens, span] + dot(block, kept[feats, span])
+    for copy in brought:
+        copy.wait()
+
+
+def part_block(where, inner, inner_at, low, outer, start, kept, old, bring):
+    return call(
+        functools.partial(part_body, start, inner_at, low, len(bring)),
+        "part_block",
+        where,
+        (1,),
+        (inner, outer, kept, old, *bring),
+        [INSIDE] * 4 + [OUTSIDE] * len(bring),
+        [INSIDE, INSIDE, pl.BlockSpec((8, 128), lambda j, where: (0, 0))] + [INSIDE] * len(bring),
+        [
+            pltpu.VMEM(kept.shape, kept.dtype),
+            pltpu.VMEM(old.shape, old.dtype),
+            jax.ShapeDtypeStruct((8, 128), jnp.float32),
+            *[pltpu.VMEM(a.shape, a.dtype) for a in bring],
+        ],
+        [pltpu.SemaphoreType.DMA((len(bring),))],
+        LIMIT,
+        aliases={3: 0, 4: 1},
+    )
+
+
+def last_body(start, inner_at, low, where, inner, outer, kept, old, gate, po_t, _, *rest):
+    _, _, right, gates, po, gate_sems, po_sem = rest
+    size, width = outer.shape
+    feats = pl.ds(low, width)
     hidden = kept.shape[1]
     tokens = pl.ds(start, size)
     spans = [pl.ds(t * TILE, TILE) for t in range(hidden // TILE)]
@@ -178,46 +217,39 @@
     po_read.start()
     for read in reads[1:]:
         read.start()
-    brought = [pltpu.make_async_copy(a, b, near_sems.at[i]) for i, (a, b) in enumerate(zip(far, near))]
-    for copy in brought:
-        copy.start()
-    block = select(where, inner.at[pl.ds(inner_at, size)], outer)
+    block = select(where, inner.at[pl.ds(inner_at, size), feats], outer)
     total = jnp.zeros((size, PROJ), jnp.float32)
     for t, span in enumerate(spans):
-        hidden_grad = old[tokens, span] + dot(block, kept[:, span])
+        hidden_grad = old[tokens, span] + dot(block, kept[feats, span])
         reads[t].wait()
         up_grad = (hidden_grad * silu(gates[t].astype(jnp.float32))).astype(jnp.bfloat16)
         if t == 0:
             po_read.wait()
         total = total + dot_nt(up_grad, po[:, span])
     right[...] = total
-    for copy in brought:
-        copy.wait()
-
-
-def last_block(where, inner, inner_at, outer, start, kept, old, gate, po_t, token, bring):
+
+
+def last_block(where, inner, inner_at, low, outer, start, kept, old, gate, po_t, token):
     size = outer.shape[0]
     tiles = kept.shape[1] // TILE
     return call(
-        functools.partial(last_body, start, inner_at, len(bring)),
+        functools.partial(last_body, start, inner_at, low),
         "last_block",
         where,
         (1,),
-        (inner, outer, kept, old, gate, po_t, token, *bring),
-        [INSIDE, INSIDE, INSIDE, INSIDE, OUTSIDE, ANYWHERE, ANYWHERE] + [OUTSIDE] * len(bring),
-        [INSIDE, INSIDE, pl.BlockSpec((size, PROJ), lambda j, where: (0, 0))] + [INSIDE] * len(bring),
+        (inner, outer, kept, old, gate, po_t, token),
+        [INSIDE, INSIDE, INSIDE, INSIDE, OUTSIDE, ANYWHERE, ANYWHERE],
+        [INSIDE, INSIDE, pl.BlockSpec((size, PROJ), lambda j, where: (0, 0))],
         [
             pltpu.VMEM(kept.shape, kept.dtype),
             pltpu.VMEM(old.shape, old.dtype),
             jax.ShapeDtypeStruct((size, PROJ), jnp.float32),
-            *[pltpu.VMEM(a.shape, a.dtype) for a in bring],
         ],
         [
             pltpu.VMEM((tiles, size, TILE), gate.dtype),
             pltpu.VMEM(po_t.shape, po_t.dtype),
             pltpu.SemaphoreType.DMA((tiles,)),
             pltpu.SemaphoreType.DMA,
-            pltpu.SemaphoreType.DMA((max(len(bring), 1),)),
         ],
         LIMIT,
         aliases={3: 0, 4: 1},
@@ -280,6 +312,14 @@
     return out
 
 
+def score_sum(where, a, b):
+    out = pltpu.VMEM(a.shape, a.dtype)
+    (total,) = call(
+        sum_body, "score_sum", where, (1,), (a, b), [INSIDE, INSIDE], [INSIDE], [out], [], LIMIT, flops=3 * 10**9
+    )
+    return total
+
+
 def sum_body(where, a, b, out):
     out[...] = a[...] + b[...]
 
@@ -367,6 +407,7 @@
         [jax.ShapeDtypeStruct((rows, columns), jnp.float32)],
         [pltpu.VMEM((parts, rows, width), jnp.float32), pltpu.SemaphoreType.DMA((parts,))],
         LIMIT,
+        flops=1000,
     )
     return updated
 
@@ -394,24 +435,28 @@
     acc, first = add_block(where, 1, [pair], w_down, after(acc, mid_outer[0]), begun, 2 * grad_out.size * w_down.shape[0])
     acc, second = add_block(where, 2, mid_inner + mid_outer, w_down, acc, first, 1000)
 
-    sizes = [256] * (tokens // 256 - 1) + [128, 128]
+    size, feats = 256, grad_out.shape[1]
+    pieces_at = [(start, 0, feats) for start in range(0, tokens - size, size)]
+    pieces_at += [(tokens - size, 0, feats // 2), (tokens - size, feats // 2, feats)]
     arrived, done = [total, total, total], [first, first, second]
     rights = []
-    start = 0
-    for n, size in enumerate(sizes):
+    for n, (start, low, high) in enumerate(pieces_at):
         h, at = divmod(start, tokens // 2)
         ahead = arrived[n + 1] if n < 4 else arrived[n]
-        end_outer = send(after(end_inner[h][at : at + size], ahead, done[n]), perm=outward)
+        end_outer = send(after(end_inner[h][at : at + size, low:high], ahead, done[n]), perm=outward)
         arrived.append(end_outer)
-        bring = [*early, late] if n == len(sizes) - 2 else []
-        kept, acc, right, *brought = last_block(
-            where, end_inner[h], at, end_outer, start, kept, acc, gate_pre, proj_out.T, second, bring
+        if high < feats:
+            kept, acc, token, *brought = part_block(
+                where, end_inner[h], at, low, end_outer, start, kept, acc, [*early, late]
+            )
+            *early, late = brought
+            done.append(token)
+            continue
+        kept, acc, right = last_block(
+            where, end_inner[h], at, low, end_outer, start, kept, acc, gate_pre, proj_out.T, second
         )
-        if bring:
-            *early, late = brought
         rights.append(right)
         done.append(right)
-        start += size
     return outer_products(where, total, sent, rights), early, late
 
 
@@ -459,13 +504,12 @@
     scores = score_parts(where, grads, parts)
     all_grads = after(grads, scores)
     *first, last = bits("tensor")
-    for n, bit in enumerate(bits("dp")):
+    for bit in bits("dp"):
         all_grads = jnp.concatenate([all_grads, swap(all_grads, "dp", bit)], axis=0)
-        if n == 0:
-            for score_bit in first:
-                scores = scores + swap(scores, "tensor", score_bit)
-            all_grads = after(all_grads, scores)
+    for bit in first:
+        scores = score_sum(where, scores, swap(scores, "tensor", bit))
     others = swap(scores, "tensor", last)
+    all_grads = after(all_grads, scores)
     row_count = hessian.shape[0]
     if row_count % 128:
         mine = lax.dynamic_slice_in_dim(all_grads, where[FIRST_PART] * row_count, row_count, 1)

time: 168 us -> 182 us (1.083)
  waiting for transfers between devices: 53.5 us -> 70.5 us
  starting transfers between devices: 34.4 us -> 30.6 us
    ppermute x5, waiting for transfers between devices: 5.72 us -> 22.4 us  [line_of_four(): send(after(end_inner[h][at:at + size, low:high], ahead, done[n]), perm=ou...]
    ppermute x9, starting transfers between devices: 11.4 us -> 7.63 us  [swap(): lax.ppermute(a, axis, [(i, i ^ bit) for i in range(lax.axis_size(axis))])]
    pallas_call x14 -> x15, Pallas kernels: 70.4 us -> 70.4 us  [call(): pl.pallas_call(body, grid_spec=pltpu.PrefetchScalarGridSpec(num_scalar_pr...]
  transfers between devices with their start and end apart: 24 -> 24, of which waited for: 13 -> 16; matrix products, arithmetic and copies ran while one was open for 3% -> 3% of each run, Pallas kernels for 41% -> 38%
where the time goes in v12:
time: 182 us; the launch traced here: 181 us
  waiting for transfers between devices  70.5 us (39%)
  Pallas kernels  70.4 us (39%)
  starting transfers between devices  30.6 us (17%)
  local copies, waits for them, and re-layouts  7.48 us (4%)
    pallas_call x15, Pallas kernels, call(): pl.pallas_call(body, grid_spec=pltpu.PrefetchScalarGridSpec(num_scalar_pr...  70.4 us
    ppermute x5, waiting for transfers between devices, line_of_four(): send(after(end_inner[h][at:at + size, low:high], ahead, done[n]), perm=ou...  22.4 us
    ppermute x9, waiting for transfers between devices, swap(): lax.ppermute(a, axis, [(i, i ^ bit) for i in range(lax.axis_size(axis))])  16.8 us
    ppermute x1, waiting for transfers between devices, line_of_four(): pair = send(grad_out, perm=pairs)  15.1 us
    ppermute x2, waiting for transfers between devices, line_of_four(): mid_outer = [send(after(a, begun), perm=outward) for a in mid_inner]  14.2 us
    ppermute x9, starting transfers between devices, swap(): lax.ppermute(a, axis, [(i, i ^ bit) for i in range(lax.axis_size(axis))])  7.63 us
    ppermute x5, starting transfers between devices, line_of_four(): send(after(end_inner[h][at:at + size, low:high], ahead, done[n]), perm=ou...  6.62 us
    ppermute x1, starting transfers between devices, line_of_four(): from_end = send(after(in_part, mid_inner[0]), perm=inward)  5.83 us
  transfers between devices with their start and end apart: 24, of which 16 were waited for; matrix products, arithmetic and copies ran while one was open for 3% of the time, Pallas kernels for 38%

profile of v12, /device:TPU:0, one launch (start us, length us, event | category | flops | bytes accessed | tf_op | source)
XLA Modules:
  0.0 180.8 jit_solution(17226756705726663561)
XLA Ops:
  0.6 3.1 %collective-permute-start.5 = (bf16[1024,1024]{1,0:T(8,128)(2,1)}, bf16[1024,1024]{1,0:T(8,128)(2,1)}, u32[]{:S(2)}, u32[]{:S(2)}) collective-permute-start(bf16[1024,1024]{1,0:T(8,128)(2,1)} %own), channel_id=1, source_target_pairs={{0,4},{4,0},{8,12},{12,8},{1,5},{5,1},{9,13},{13,9},{2,6},{6,2},{1... | collective-permute-start | bytes 6291464 | tf_op jit(solution)/shard_map/ppermute | solution.py:423
  3.7 3.0 %fusion.1 = (bf16[512,1024]{1,0:T(8,128)(2,1)}, bf16[512,1024]{1,0:T(8,128)(2,1)}) fusion(bf16[1024,1024]{1,0:T(8,128)(2,1)} %own), kind=kLoop, calls=%fused_computation.3 | loop fusion | bytes 4194304 | tf_op jit(solution)/shard_map/slice | solution.py:424
  9.5 1.6 copy-done.2
  12.0 1.3 input_block.1.a
  13.3 3.0 %collective-permute-done.4.rest_3_ = f32[256,256]{1,0:T(8,128)S(1)} collective-permute-done((f32[256,256]{1,0:T(8,128)}, f32[256,256]{1,0:T(8,128)S(1)}, u32[]{:S(2)}, u32[]{:S(2)}) %collective-permute-start.4) | collective-permute-done | bytes 262176 | tf_op jit(solution)/shard_map/ppermute | solution.py:474
  17.0 5.0 %collective-permute-done.3.rest_2_ = f32[256,256]{1,0:T(8,128)} collective-permute-done((f32[256,256]{1,0:T(8,128)}, f32[256,256]{1,0:T(8,128)}, u32[]{:S(2)}, u32[]{:S(2)}) %collective-permute-start.3) | collective-permute-done | bytes 262176 | tf_op jit(solution)/shard_map/ppermute | solution.py:474
  22.1 12.0 %own_block.1 = (f32[1024,3584]{1,0:T(8,128)S(1)}, bf16[1024,3584]{1,0:T(8,128)(2,1)S(1)}, f32[8,128]{1,0:T(8,128)S(1)}) custom-call(s32[9]{0:T(128)S(1)} %stack.43.where, bf16[1024,1024]{1,0:T(8,128)(2,1)S(1)} %copy-done, bf16[3584,4096]{1,0:T(8,128)(2,1)} %refs_4_.1, bf16[3584,4096]{1,0:T(8,128)(2,1)} %refs_4_.1), custom_call_target="tpu_custom_call" | custom-call | flops 1000 | bytes 1000 | tf_op jit(solution)/shard_map/own_block/pallas_call | solution.py:41
  34.1 1.3 collective-permute-start.9
  35.4 15.1 %collective-permute-done.5.refs_0_ = bf16[1024,1024]{1,0:T(8,128)(2,1)} collective-permute-done((bf16[1024,1024]{1,0:T(8,128)(2,1)}, bf16[1024,1024]{1,0:T(8,128)(2,1)}, u32[]{:S(2)}, u32[]{:S(2)}) %collective-permute-start.5) | collective-permute-done | bytes 2097184 | tf_op jit(solution)/shard_map/ppermute | solution.py:423
  50.5 1.7 fusion
  53.0 5.8 %collective-permute-start.1 = (f32[64,1024]{1,0:T(8,128)S(1)}, f32[64,1024]{1,0:T(8,128)S(1)}, u32[]{:S(2)}, u32[]{:S(2)}) collective-permute-start(f32[64,1024]{1,0:T(8,128)S(1)} %input_block.1.a), channel_id=1, source_target_pairs={{0,4},{12,8},{1,5},{13,9},{2,6},{14,10},{3,7},{15,11},{16,20},{28,... | collective-permute-start | bytes 786440 | tf_op jit(solution)/shard_map/ppermute | solution.py:427
  58.8 1.3 collective-permute-start.12
  60.8 2.1 %collective-permute-done.1.b = f32[64,1024]{1,0:T(8,128)S(1)} collective-permute-done((f32[64,1024]{1,0:T(8,128)S(1)}, f32[64,1024]{1,0:T(8,128)S(1)}, u32[]{:S(2)}, u32[]{:S(2)}) %collective-permute-start.1) | collective-permute-done | bytes 262176 | tf_op jit(solution)/shard_map/ppermute | solution.py:427
  64.2 8.7 %collective-permute-done.9.refs_2_ = bf16[512,1024]{1,0:T(8,128)(2,1)S(1)} collective-permute-done((bf16[512,1024]{1,0:T(8,128)(2,1)S(1)}, bf16[512,1024]{1,0:T(8,128)(2,1)S(1)}, u32[]{:S(2)}, u32[]{:S(2)}) %collective-permute-start.9) | collective-permute-done | bytes 1048608 | tf_op jit(solution)/shard_map/ppermute | solution.py:429
  72.9 12.9 %add_block_1.1 = (f32[1024,3584]{1,0:T(8,128)S(1)}, f32[8,128]{1,0:T(8,128)S(1)}) custom-call(s32[9]{0:T(128)S(1)} %stack.43.where, bf16[1024,1024]{1,0:T(8,128)(2,1)} %collective-permute-done.5.refs_0_, bf16[3584,4096]{1,0:T(8,128)(2,1)} %refs_4_.1, f32[1024,3584]{1,0:T(8,128)S(1)} %get-tuple-element.47.refs_2_, ...), custom_call_target="tpu_custom_call", output_to_operand_aliasing={{0}: (3, {})} | custom-call | flops 7516192768 | bytes 1000 | tf_op jit(solution)/shard_map/add_block_1/pallas_call | solution.py:41
  89.0 5.5 %collective-permute-done.12.refs_3_ = bf16[512,1024]{1,0:T(8,128)(2,1)S(1)} collective-permute-done((bf16[512,1024]{1,0:T(8,128)(2,1)S(1)}, bf16[512,1024]{1,0:T(8,128)(2,1)S(1)}, u32[]{:S(2)}, u32[]{:S(2)}) %collective-permute-start.12) | collective-permute-done | bytes 1048608 | tf_op jit(solution)/shard_map/ppermute | solution.py:429
  94.5 12.3 %add_block_2.1 = (f32[1024,3584]{1,0:T(8,128)S(1)}, f32[8,128]{1,0:T(8,128)S(1)}) custom-call(s32[9]{0:T(128)S(1)} %stack.43.where, bf16[512,1024]{1,0:T(8,128)(2,1)S(1)} %collective-permute-done.refs_0_, bf16[512,1024]{1,0:T(8,128)(2,1)S(1)} %collective-permute-done.11.refs_1_, ...), custom_call_target="tpu_custom_call", output_to_operand_aliasing={{0}: (6, {})} | custom-call | flops 1000 | bytes 1000 | tf_op jit(solution)/shard_map/add_block_2/pallas_call | solution.py:41
  106.9 15.8 %collective-permute-done.10.outer = bf16[256,1024]{1,0:T(8,128)(2,1)S(1)} collective-permute-done((bf16[256,1024]{1,0:T(8,128)(2,1)S(1)}, bf16[256,1024]{1,0:T(8,128)(2,1)S(1)}, u32[]{:S(2)}, u32[]{:S(2)}) %collective-permute-start.10) | collective-permute-done | bytes 524320 | tf_op jit(solution)/shard_map/ppermute | solution.py:446
  124.0 5.5 %last_block.4 = (bf16[1024,3584]{1,0:T(8,128)(2,1)S(1)}, f32[1024,3584]{1,0:T(8,128)S(1)}, f32[256,64]{1,0:T(8,128)S(1)}) custom-call(s32[9]{0:T(128)S(1)} %stack.43.where, bf16[512,1024]{1,0:T(8,128)(2,1)S(1)} %collective-permute-done.8.inner, bf16[256,1024]{1,0:T(8,128)(2,1)S(1)} %collective-permute-done.10.outer, ...), custom_call_target="tpu_custom_call", output_to_operand_aliasing={{0}: (3, {}), {1}: (4, {})} | custom-call | flops 1000 | bytes 1000 | tf_op jit(solution)/shard_map/last_block/pallas_call | solution.py:41
  129.6 4.4 %collective-permute-done.13.outer = bf16[256,1024]{1,0:T(8,128)(2,1)S(1)} collective-permute-done((bf16[256,1024]{1,0:T(8,128)(2,1)S(1)}, bf16[256,1024]{1,0:T(8,128)(2,1)S(1)}, u32[]{:S(2)}, u32[]{:S(2)}) %collective-permute-start.13) | collective-permute-done | bytes 524320 | tf_op jit(solution)/shard_map/ppermute | solution.py:446
  133.9 1.5 collective-permute-start.17
  135.4 5.5 %last_block.5 = (bf16[1024,3584]{1,0:T(8,128)(2,1)S(1)}, f32[1024,3584]{1,0:T(8,128)S(1)}, f32[256,64]{1,0:T(8,128)S(1)}) custom-call(s32[9]{0:T(128)S(1)} %stack.43.where, bf16[512,1024]{1,0:T(8,128)(2,1)S(1)} %collective-permute-done.8.inner, bf16[256,1024]{1,0:T(8,128)(2,1)S(1)} %collective-permute-done.13.outer, ...), custom_call_target="tpu_custom_call", output_to_operand_aliasing={{0}: (3, {}), {1}: (4, {})} | custom-call | flops 1000 | bytes 1000 | tf_op jit(solution)/shard_map/last_block/pallas_call | solution.py:41
  143.6 1.6 collective-permute-done.15.outer
  145.2 5.5 %last_block.6 = (bf16[1024,3584]{1,0:T(8,128)(2,1)S(1)}, f32[1024,3584]{1,0:T(8,128)S(1)}, f32[256,64]{1,0:T(8,128)S(1)}) custom-call(s32[9]{0:T(128)S(1)} %stack.43.where, bf16[512,1024]{1,0:T(8,128)(2,1)S(1)} %collective-permute-done.14.inner, bf16[256,1024]{1,0:T(8,128)(2,1)S(1)} %collective-permute-done.15.outer, ...), custom_call_target="tpu_custom_call", output_to_operand_aliasing={{0}: (3, {}), {1}: (4, {})} | custom-call | flops 1000 | bytes 1000 | tf_op jit(solution)/shard_map/last_block/pallas_call | solution.py:41
  150.8 4.6 %part_block.1 = (bf16[1024,3584]{1,0:T(8,128)(2,1)S(1)}, f32[1024,3584]{1,0:T(8,128)S(1)}, f32[8,128]{1,0:T(8,128)}, f32[256,256]{1,0:T(8,128)S(1)}, f32[256,256...) custom-call(s32[9]{0:T(128)S(1)} %stack.43.where, ...), custom_call_target="tpu_custom_call", output_to_operand_aliasing={{0}: (3, {}), {1}: (4, {})} | custom-call | flops 1000 | bytes 1000 | tf_op jit(solution)/shard_map/part_block/pallas_call | solution.py:41
  155.9 4.4 %last_block.7 = (bf16[1024,3584]{1,0:T(8,128)(2,1)S(1)}, f32[1024,3584]{1,0:T(8,128)S(1)}, f32[256,64]{1,0:T(8,128)S(1)}) custom-call(s32[9]{0:T(128)S(1)} %stack.43.where, bf16[512,1024]{1,0:T(8,128)(2,1)S(1)} %collective-permute-done.14.inner, bf16[256,512]{1,0:T(8,128)(2,1)S(1)} %collective-permute-done.16.outer, ...), custom_call_target="tpu_custom_call", output_to_operand_aliasing={{0}: (3, {}), {1}: (4, {})} | custom-call | flops 1000 | bytes 1000 | tf_op jit(solution)/shard_map/last_block/pallas_call | solution.py:41
  161.9 3.5 %collective-permute-done.18 = f32[2,4096]{1,0:T(2,128)S(1)} collective-permute-done((f32[2,4096]{1,0:T(2,128)S(1)}, f32[2,4096]{1,0:T(2,128)S(1)}, u32[]{:S(2)}, u32[]{:S(2)}) %collective-permute-start.18) | collective-permute-done | bytes 32800 | tf_op jit(solution)/shard_map/ppermute | solution.py:474
  165.5 1.7 collective-permute-start.19
  167.1 3.4 %collective-permute-done.19 = f32[2,4096]{1,0:T(2,128)S(1)} collective-permute-done((f32[2,4096]{1,0:T(2,128)S(1)}, f32[2,4096]{1,0:T(2,128)S(1)}, u32[]{:S(2)}, u32[]{:S(2)}) %collective-permute-start.19) | collective-permute-done | bytes 32800 | tf_op jit(solution)/shard_map/ppermute | solution.py:474
  172.7 1.6 collective-permute-start.21
  175.6 1.6 collective-permute-start.23
  177.2 2.9 %hessian_update.1 = f32[256,4096]{1,0:T(8,128)} custom-call(s32[9]{0:T(128)S(1)} %stack.43.where, f32[8,4096]{1,0:T(8,128)S(1)} %pad_maximum_fusion.grads.mine, f32[8,4096]{1,0:T(8,128)S(1)} %pad_maximum_fusion.grads.mine, f32[256,4096]{1,0:T(8,128)S(1)} %get-tuple-element.77.hessian), custom_call_target="tpu_custom_call" | custom-call | flops 1000 | bytes 1000 | tf_op jit(solution)/shard_map/hessian_update/pallas_call | solution.py:41
  (53 shorter events, 20.7 us)
Async XLA Ops:
  0.6 21.5 %copy-start = (bf16[1024,1024]{1,0:T(8,128)(2,1)S(1)}, bf16[1024,1024]{1,0:T(8,128)(2,1)}, u32[]{:S(2)}) copy-start(bf16[1024,1024]{1,0:T(8,128)(2,1)} %own) | copy-start | bytes 6291460
  0.6 49.9 %collective-permute-start.5 = (bf16[1024,1024]{1,0:T(8,128)(2,1)}, bf16[1024,1024]{1,0:T(8,128)(2,1)}, u32[]{:S(2)}, u32[]{:S(2)}) collective-permute-start(bf16[1024,1024]{1,0:T(8,128)(2,1)} %own), channel_id=1, source_target_pairs={{0,4},{4,0},{8,12},{12,8},{1,5},{5,1},{9,13},{13,9},{2,6},{6,2},{1... | collective-permute-start | bytes 6291464 | tf_op jit(solution)/shard_map/ppermute | solution.py:423
  6.8 27.4 %collective-permute-start = (bf16[512,1024]{1,0:T(8,128)(2,1)}, bf16[512,1024]{1,0:T(8,128)(2,1)S(1)}, u32[]{:S(2)}, u32[]{:S(2)}) collective-permute-start(bf16[512,1024]{1,0:T(8,128)(2,1)} %get-tuple-element.83), channel_id=1, source_target_pairs={{4,8},{8,4},{5,9},{9,5},{6,10},{10,6},{7,11},{11,7},{20,24},{24,20... | collective-permute-start | bytes 3145736 | tf_op jit(solution)/shard_map/ppermute | solution.py:425
  7.5 8.8 %collective-permute-start.4 = (f32[256,256]{1,0:T(8,128)}, f32[256,256]{1,0:T(8,128)S(1)}, u32[]{:S(2)}, u32[]{:S(2)}) collective-permute-start(f32[256,256]{1,0:T(8,128)} %rest_0_.1), channel_id=1, source_target_pairs={{0,3},{1,2},{2,1},{3,0},{4,7},{5,6},{6,5},{7,4},{8,11},{9,10},{10,... | collective-permute-start | bytes 786440 | tf_op jit(solution)/shard_map/ppermute | solution.py:474
  8.2 13.9 %collective-permute-start.3 = (f32[256,256]{1,0:T(8,128)}, f32[256,256]{1,0:T(8,128)}, u32[]{:S(2)}, u32[]{:S(2)}) collective-permute-start(f32[256,256]{1,0:T(8,128)} %rest_0_.1), channel_id=1, source_target_pairs={{0,2},{1,3},{2,0},{3,1},{4,6},{5,7},{6,4},{7,5},{8,10},{9,11},{10,... | collective-permute-start | bytes 786440 | tf_op jit(solution)/shard_map/ppermute | solution.py:474
  9.1 13.0 %collective-permute-start.2 = (f32[256,256]{1,0:T(8,128)}, f32[256,256]{1,0:T(8,128)}, u32[]{:S(2)}, u32[]{:S(2)}) collective-permute-start(f32[256,256]{1,0:T(8,128)} %rest_0_.1), channel_id=1, source_target_pairs={{0,1},{1,0},{2,3},{3,2},{4,5},{5,4},{6,7},{7,6},{8,9},{9,8},{10,11... | collective-permute-start | bytes 786440 | tf_op jit(solution)/shard_map/ppermute | solution.py:474
  9.5 1.6 copy-start.2
  11.1 0.9 copy-start.3
  16.3 17.8 %copy-start.4 = (f32[256,256]{1,0:T(8,128)}, f32[256,256]{1,0:T(8,128)S(1)}, u32[]{:S(2)}) copy-start(f32[256,256]{1,0:T(8,128)S(1)} %collective-permute-done.4.rest_3_) | copy-start | bytes 786436
  16.3 42.5 %collective-permute-start.11 = (bf16[512,1024]{1,0:T(8,128)(2,1)}, bf16[512,1024]{1,0:T(8,128)(2,1)S(1)}, u32[]{:S(2)}, u32[]{:S(2)}) collective-permute-start(bf16[512,1024]{1,0:T(8,128)(2,1)} %get-tuple-element.82), channel_id=1, source_target_pairs={{4,8},{8,4},{5,9},{9,5},{6,10},{10,6},{7,11},{11,7},{20,24},{24,20... | collective-permute-start | bytes 3145736 | tf_op jit(solution)/shard_map/ppermute | solution.py:425
  34.1 38.7 %collective-permute-start.9 = (bf16[512,1024]{1,0:T(8,128)(2,1)S(1)}, bf16[512,1024]{1,0:T(8,128)(2,1)S(1)}, u32[]{:S(2)}, u32[]{:S(2)}) collective-permute-start(bf16[512,1024]{1,0:T(8,128)(2,1)S(1)} %collective-permute-done.refs_0_), channel_id=1, source_target_pairs={{4,0},{8,12},{5,1},{9,13},{6,2},{10,14},{7,3},{11,15},{20,16},{24,... | collective-permute-start | bytes 3145736 | tf_op jit(solution)/shard_map/ppermute | solution.py:429
  52.2 34.1 %collective-permute-start.8 = (bf16[512,1024]{1,0:T(8,128)(2,1)S(1)}, bf16[512,1024]{1,0:T(8,128)(2,1)S(1)}, u32[]{:S(2)}, u32[]{:S(2)}) collective-permute-start(bf16[512,1024]{1,0:T(8,128)(2,1)S(1)} %get-tuple-element.81), channel_id=1, source_target_pairs={{4,8},{8,4},{5,9},{9,5},{6,10},{10,6},{7,11},{11,7},{20,24},{24,20... | collective-permute-start | bytes 3145736 | tf_op jit(solution)/shard_map/ppermute | solution.py:430
  53.0 10.0 %collective-permute-start.1 = (f32[64,1024]{1,0:T(8,128)S(1)}, f32[64,1024]{1,0:T(8,128)S(1)}, u32[]{:S(2)}, u32[]{:S(2)}) collective-permute-start(f32[64,1024]{1,0:T(8,128)S(1)} %input_block.1.a), channel_id=1, source_target_pairs={{0,4},{12,8},{1,5},{13,9},{2,6},{14,10},{3,7},{15,11},{16,20},{28,... | collective-permute-start | bytes 786440 | tf_op jit(solution)/shard_map/ppermute | solution.py:427
  58.8 35.7 %collective-permute-start.12 = (bf16[512,1024]{1,0:T(8,128)(2,1)S(1)}, bf16[512,1024]{1,0:T(8,128)(2,1)S(1)}, u32[]{:S(2)}, u32[]{:S(2)}) collective-permute-start(bf16[512,1024]{1,0:T(8,128)(2,1)S(1)} %collective-permute-done.11.refs_1_), channel_id=1, source_target_pairs={{4,0},{8,12},{5,1},{9,13},{6,2},{10,14},{7,3},{11,15},{20,16},{24,... | collective-permute-start | bytes 3145736 | tf_op jit(solution)/shard_map/ppermute | solution.py:429
  60.1 46.7 %collective-permute-start.14 = (bf16[512,1024]{1,0:T(8,128)(2,1)S(1)}, bf16[512,1024]{1,0:T(8,128)(2,1)S(1)}, u32[]{:S(2)}, u32[]{:S(2)}) collective-permute-start(bf16[512,1024]{1,0:T(8,128)(2,1)S(1)} %get-tuple-element.80), channel_id=1, source_target_pairs={{4,8},{8,4},{5,9},{9,5},{6,10},{10,6},{7,11},{11,7},{20,24},{24,20... | collective-permute-start | bytes 3145736 | tf_op jit(solution)/shard_map/ppermute | solution.py:430
  63.5 22.3 %collective-permute-start.6 = (f32[64,1024]{1,0:T(8,128)S(1)}, f32[64,1024]{1,0:T(8,128)S(1)}, u32[]{:S(2)}, u32[]{:S(2)}) collective-permute-start(f32[64,1024]{1,0:T(8,128)S(1)} %side.1.a), channel_id=1, source_target_pairs={{4,8},{8,4},{5,9},{9,5},{6,10},{10,6},{7,11},{11,7},{20,24},{24,20... | collective-permute-start | bytes 786440 | tf_op jit(solution)/shard_map/ppermute | solution.py:432
  86.4 36.3 %collective-permute-start.10 = (bf16[256,1024]{1,0:T(8,128)(2,1)S(1)}, bf16[256,1024]{1,0:T(8,128)(2,1)S(1)}, u32[]{:S(2)}, u32[]{:S(2)}) collective-permute-start(bf16[256,1024]{1,0:T(8,128)(2,1)S(1)} %get-tuple-element.49), channel_id=1, source_target_pairs={{4,0},{8,12},{5,1},{9,13},{6,2},{10,14},{7,3},{11,15},{20,16},{24,... | collective-permute-start | bytes 1572872 | tf_op jit(solution)/shard_map/ppermute | solution.py:446
  87.7 46.2 %collective-permute-start.13 = (bf16[256,1024]{1,0:T(8,128)(2,1)S(1)}, bf16[256,1024]{1,0:T(8,128)(2,1)S(1)}, u32[]{:S(2)}, u32[]{:S(2)}) collective-permute-start(bf16[256,1024]{1,0:T(8,128)(2,1)S(1)} %get-tuple-element.56), channel_id=1, source_target_pairs={{4,0},{8,12},{5,1},{9,13},{6,2},{10,14},{7,3},{11,15},{20,16},{24,... | collective-permute-start | bytes 1572872 | tf_op jit(solution)/shard_map/ppermute | solution.py:446
  94.5 29.5 %copy-start.1 = (bf16[3584,64]{0,1:T(8,128)(2,1)S(1)}, bf16[3584,64]{0,1:T(8,128)(2,1)}, u32[]{:S(2)}) copy-start(bf16[3584,64]{0,1:T(8,128)(2,1)} %param.13) | copy-start | bytes 1376260
  122.7 22.5 %collective-permute-start.15 = (bf16[256,1024]{1,0:T(8,128)(2,1)S(1)}, bf16[256,1024]{1,0:T(8,128)(2,1)S(1)}, u32[]{:S(2)}, u32[]{:S(2)}) collective-permute-start(bf16[256,1024]{1,0:T(8,128)(2,1)S(1)} %slice.40), channel_id=1, source_target_pairs={{4,0},{8,12},{5,1},{9,13},{6,2},{10,14},{7,3},{11,15},{20,16},{24,... | collective-permute-start | bytes 1572872 | tf_op jit(solution)/shard_map/ppermute | solution.py:446
  133.9 16.9 %collective-permute-start.17 = (bf16[256,512]{1,0:T(8,128)(2,1)S(1)}, bf16[256,512]{1,0:T(8,128)(2,1)S(1)}, u32[]{:S(2)}, u32[]{:S(2)}) collective-permute-start(bf16[256,512]{1,0:T(8,128)(2,1)S(1)} %get-tuple-element.65), channel_id=1, source_target_pairs={{4,0},{8,12},{5,1},{9,13},{6,2},{10,14},{7,3},{11,15},{20,16},{24,... | collective-permute-start | bytes 786440 | tf_op jit(solution)/shard_map/ppermute | solution.py:446
  140.9 14.9 %collective-permute-start.16 = (bf16[256,512]{1,0:T(8,128)(2,1)S(1)}, bf16[256,512]{1,0:T(8,128)(2,1)S(1)}, u32[]{:S(2)}, u32[]{:S(2)}) collective-permute-start(bf16[256,512]{1,0:T(8,128)(2,1)S(1)} %get-tuple-element.64), channel_id=1, source_target_pairs={{4,0},{8,12},{5,1},{9,13},{6,2},{10,14},{7,3},{11,15},{20,16},{24,... | collective-permute-start | bytes 786440 | tf_op jit(solution)/shard_map/ppermute | solution.py:446
  142.3 18.1 %collective-permute-start.7 = (bf16[64,1024]{1,0:T(8,128)(2,1)S(1)}, bf16[64,1024]{1,0:T(8,128)(2,1)S(1)}, u32[]{:S(2)}, u32[]{:S(2)}) collective-permute-start(bf16[64,1024]{1,0:T(8,128)(2,1)S(1)} %convert_element_type.4), channel_id=1, source_target_pairs={{4,0},{8,12},{5,1},{9,13},{6,2},{10,14},{7,3},{11,15},{20,16},{24,... | collective-permute-start | bytes 393224 | tf_op jit(solution)/shard_map/ppermute | solution.py:433
  161.4 4.1 %collective-permute-start.18 = (f32[2,4096]{1,0:T(2,128)S(1)}, f32[2,4096]{1,0:T(2,128)S(1)}, u32[]{:S(2)}, u32[]{:S(2)}) collective-permute-start(f32[2,4096]{1,0:T(2,128)S(1)} %outer_products.1), channel_id=1, source_target_pairs={{0,4},{4,0},{8,12},{12,8},{1,5},{5,1},{9,13},{13,9},{2,6},{6,2},{1... | collective-permute-start | bytes 98312 | tf_op jit(solution)/shard_map/ppermute | solution.py:474
  165.5 5.1 %collective-permute-start.19 = (f32[2,4096]{1,0:T(2,128)S(1)}, f32[2,4096]{1,0:T(2,128)S(1)}, u32[]{:S(2)}, u32[]{:S(2)}) collective-permute-start(f32[2,4096]{1,0:T(2,128)S(1)} %add.34), channel_id=1, source_target_pairs={{0,8},{4,12},{8,0},{12,4},{1,9},{5,13},{9,1},{13,5},{2,10},{6,14},... | collective-permute-start | bytes 98312 | tf_op jit(solution)/shard_map/ppermute | solution.py:474
  171.4 1.2 collective-permute-start.20
  171.4 3.7 %collective-permute-start.22 = (f32[2,256]{1,0:T(2,128)S(1)}, f32[2,256]{1,0:T(2,128)S(1)}, u32[]{:S(2)}, u32[]{:S(2)}) collective-permute-start(f32[2,256]{1,0:T(2,128)S(1)} %scores.1.a), channel_id=1, source_target_pairs={{0,4},{4,0},{8,12},{12,8},{1,5},{5,1},{9,13},{13,9},{2,6},{6,2},{1... | collective-permute-start | bytes 6152 | tf_op jit(solution)/shard_map/ppermute | solution.py:474
  172.7 4.5 %collective-permute-start.21 = (f32[4,4096]{1,0:T(4,128)S(1)}, f32[4,4096]{1,0:T(4,128)S(1)}, u32[]{:S(2)}, u32[]{:S(2)}) collective-permute-start(f32[4,4096]{1,0:T(4,128)S(1)} %pad_maximum_fusion.1), channel_id=1, source_target_pairs={{0,2},{1,3},{2,0},{3,1},{4,6},{5,7},{6,4},{7,5},{8,10},{9,11},{10,... | collective-permute-start | bytes 196616 | tf_op jit(solution)/shard_map/ppermute | solution.py:474
  175.6 4.5 %collective-permute-start.23 = (f32[2,256]{1,0:T(2,128)S(1)}, f32[2,256]{1,0:T(2,128)S(1)}, u32[]{:S(2)}, u32[]{:S(2)}) collective-permute-start(f32[2,256]{1,0:T(2,128)S(1)} %score_sum.1), channel_id=1, source_target_pairs={{0,8},{4,12},{8,0},{12,4},{1,9},{5,13},{9,1},{13,5},{2,10},{6,14},... | collective-permute-start | bytes 6152 | tf_op jit(solution)/shard_map/ppermute | solution.py:474

commit v13 on v10

--- a/solution.py
+++ b/solution.py
@@ -280,6 +280,14 @@
     return out
 
 
+def score_sum(where, a, b):
+    out = pltpu.VMEM(a.shape, a.dtype)
+    (total,) = call(
+        sum_body, "score_sum", where, (1,), (a, b), [INSIDE, INSIDE], [INSIDE], [out], [], LIMIT, flops=3 * 10**9
+    )
+    return total
+
+
 def sum_body(where, a, b, out):
     out[...] = a[...] + b[...]
 
@@ -367,6 +375,7 @@
         [jax.ShapeDtypeStruct((rows, columns), jnp.float32)],
         [pltpu.VMEM((parts, rows, width), jnp.float32), pltpu.SemaphoreType.DMA((parts,))],
         LIMIT,
+        flops=1000,
     )
     return updated
 
@@ -386,8 +395,9 @@
     from_end = send(after(in_part, mid_inner[0]), perm=inward)
     acc, kept, begun = own_block(where, after(grad_out, in_part, *early), w_down)
     mid_outer = [send(after(a, begun), perm=outward) for a in mid_inner]
-    end_inner = [send(pair[half], perm=inner) for half in halves]
     side = small_kernel(sum_body, "side", where, in_part, after(from_end, begun, pair))
+    end_inner = [send(pair[halves[0]], perm=inner)]
+    end_inner.append(send(after(pair[halves[1]], mid_outer[0], side), perm=inner))
     total = small_kernel(sum_body, "total", where, side, send(side, perm=inner))
     sent = send(total.astype(jnp.bfloat16), perm=outward)
 
@@ -459,13 +469,12 @@
     scores = score_parts(where, grads, parts)
     all_grads = after(grads, scores)
     *first, last = bits("tensor")
-    for n, bit in enumerate(bits("dp")):
+    for bit in bits("dp"):
         all_grads = jnp.concatenate([all_grads, swap(all_grads, "dp", bit)], axis=0)
-        if n == 0:
-            for score_bit in first:
-                scores = scores + swap(scores, "tensor", score_bit)
-            all_grads = after(all_grads, scores)
+    for bit in first:
+        scores = score_sum(where, scores, swap(scores, "tensor", bit))
     others = swap(scores, "tensor", last)
+    all_grads = after(all_grads, scores)
     row_count = hessian.shape[0]
     if row_count % 128:
         mine = lax.dynamic_slice_in_dim(all_grads, where[FIRST_PART] * row_count, row_count, 1)

time: 168 us -> 167 us (level)
    pallas_call x14 -> x15, Pallas kernels: 70.4 us -> 70.9 us  [call(): pl.pallas_call(body, grid_spec=pltpu.PrefetchScalarGridSpec(num_scalar_pr...]
where the time goes in v13:
time: 167 us; the launch traced here: 166 us
  Pallas kernels  70.9 us (42%)
  waiting for transfers between devices  51.9 us (31%)
  starting transfers between devices  34.5 us (21%)
  local copies, waits for them, and re-layouts  7.48 us (4%)
    pallas_call x15, Pallas kernels, call(): pl.pallas_call(body, grid_spec=pltpu.PrefetchScalarGridSpec(num_scalar_pr...  70.9 us
    ppermute x1, waiting for transfers between devices, line_of_four(): pair = send(grad_out, perm=pairs)  15.4 us
    ppermute x2, waiting for transfers between devices, line_of_four(): mid_outer = [send(after(a, begun), perm=outward) for a in mid_inner]  14.3 us
    ppermute x9, waiting for transfers between devices, swap(): lax.ppermute(a, axis, [(i, i ^ bit) for i in range(lax.axis_size(axis))])  13.7 us
    ppermute x9, starting transfers between devices, swap(): lax.ppermute(a, axis, [(i, i ^ bit) for i in range(lax.axis_size(axis))])  11.5 us
    ppermute x5, starting transfers between devices, line_of_four(): send(after(end_inner[h][at:at + size], ahead, done[n]), perm=outward)  6.63 us
    ppermute x1, starting transfers between devices, line_of_four(): from_end = send(after(in_part, mid_inner[0]), perm=inward)  5.83 us
    ppermute x5, waiting for transfers between devices, line_of_four(): send(after(end_inner[h][at:at + size], ahead, done[n]), perm=outward)  5.72 us
  transfers between devices with their start and end apart: 24, of which 13 were waited for; matrix products, arithmetic and copies ran while one was open for 3% of the time, Pallas kernels for 41%

profile of v13, /device:TPU:0, one launch (start us, length us, event | category | flops | bytes accessed | tf_op | source)
XLA Modules:
  0.0 166.5 jit_solution(1419322024551937973)
XLA Ops:
  0.6 3.1 %collective-permute-start.5 = (bf16[1024,1024]{1,0:T(8,128)(2,1)}, bf16[1024,1024]{1,0:T(8,128)(2,1)}, u32[]{:S(2)}, u32[]{:S(2)}) collective-permute-start(bf16[1024,1024]{1,0:T(8,128)(2,1)} %own), channel_id=1, source_target_pairs={{0,4},{4,0},{8,12},{12,8},{1,5},{5,1},{9,13},{13,9},{2,6},{6,2},{1... | collective-permute-start | bytes 6291464 | tf_op jit(solution)/shard_map/ppermute | solution.py:391
  3.7 3.0 %fusion.1 = (bf16[512,1024]{1,0:T(8,128)(2,1)}, bf16[512,1024]{1,0:T(8,128)(2,1)}) fusion(bf16[1024,1024]{1,0:T(8,128)(2,1)} %own), kind=kLoop, calls=%fused_computation.3 | loop fusion | bytes 4194304 | tf_op jit(solution)/shard_map/slice | solution.py:392
  7.6 1.6 collective-permute-start.3
  9.5 1.6 copy-done.2
  12.0 1.3 input_block.1.a
  14.1 3.0 %collective-permute-done.3.rest_2_ = f32[256,256]{1,0:T(8,128)} collective-permute-done((f32[256,256]{1,0:T(8,128)}, f32[256,256]{1,0:T(8,128)}, u32[]{:S(2)}, u32[]{:S(2)}) %collective-permute-start.3) | collective-permute-done | bytes 262176 | tf_op jit(solution)/shard_map/ppermute | solution.py:439
  17.1 4.7 %collective-permute-done.4.rest_3_ = f32[256,256]{1,0:T(8,128)} collective-permute-done((f32[256,256]{1,0:T(8,128)}, f32[256,256]{1,0:T(8,128)}, u32[]{:S(2)}, u32[]{:S(2)}) %collective-permute-start.4) | collective-permute-done | bytes 262176 | tf_op jit(solution)/shard_map/ppermute | solution.py:439
  21.8 12.0 %own_block.1 = (f32[1024,3584]{1,0:T(8,128)S(1)}, bf16[1024,3584]{1,0:T(8,128)(2,1)S(1)}, f32[8,128]{1,0:T(8,128)S(1)}) custom-call(s32[9]{0:T(128)S(1)} %stack.43.where, bf16[1024,1024]{1,0:T(8,128)(2,1)S(1)} %copy-done.1, bf16[3584,4096]{1,0:T(8,128)(2,1)} %refs_4_.1, bf16[3584,4096]{1,0:T(8,128)(2,1)} %refs_4_.1), custom_call_target="tpu_custom_call" | custom-call | flops 1000 | bytes 1000 | tf_op jit(solution)/shard_map/own_block/pallas_call | solution.py:41
  35.1 15.4 %collective-permute-done.5.refs_0_ = bf16[1024,1024]{1,0:T(8,128)(2,1)} collective-permute-done((bf16[1024,1024]{1,0:T(8,128)(2,1)}, bf16[1024,1024]{1,0:T(8,128)(2,1)}, u32[]{:S(2)}, u32[]{:S(2)}) %collective-permute-start.5) | collective-permute-done | bytes 2097184 | tf_op jit(solution)/shard_map/ppermute | solution.py:391
  50.5 1.7 %fusion = (bf16[512,1024]{1,0:T(8,128)(2,1)S(1)}, bf16[512,1024]{1,0:T(8,128)(2,1)S(1)}) fusion(bf16[1024,1024]{1,0:T(8,128)(2,1)} %collective-permute-done.5.refs_0_), kind=kLoop, calls=%fused_computation.2 | loop fusion | bytes 4194304 | tf_op jit(solution)/shard_map/slice | solution.py:400
  53.0 5.8 %collective-permute-start.1 = (f32[64,1024]{1,0:T(8,128)S(1)}, f32[64,1024]{1,0:T(8,128)S(1)}, u32[]{:S(2)}, u32[]{:S(2)}) collective-permute-start(f32[64,1024]{1,0:T(8,128)S(1)} %input_block.1.a), channel_id=1, source_target_pairs={{0,4},{12,8},{1,5},{13,9},{2,6},{14,10},{3,7},{15,11},{16,20},{28,... | collective-permute-start | bytes 786440 | tf_op jit(solution)/shard_map/ppermute | solution.py:395
  60.1 2.8 %collective-permute-done.1.b = f32[64,1024]{1,0:T(8,128)S(1)} collective-permute-done((f32[64,1024]{1,0:T(8,128)S(1)}, f32[64,1024]{1,0:T(8,128)S(1)}, u32[]{:S(2)}, u32[]{:S(2)}) %collective-permute-start.1) | collective-permute-done | bytes 262176 | tf_op jit(solution)/shard_map/ppermute | solution.py:395
  63.5 9.4 %collective-permute-done.9.refs_2_ = bf16[512,1024]{1,0:T(8,128)(2,1)S(1)} collective-permute-done((bf16[512,1024]{1,0:T(8,128)(2,1)S(1)}, bf16[512,1024]{1,0:T(8,128)(2,1)S(1)}, u32[]{:S(2)}, u32[]{:S(2)}) %collective-permute-start.9) | collective-permute-done | bytes 1048608 | tf_op jit(solution)/shard_map/ppermute | solution.py:397
  74.3 12.9 %add_block_1.1 = (f32[1024,3584]{1,0:T(8,128)S(1)}, f32[8,128]{1,0:T(8,128)S(1)}) custom-call(s32[9]{0:T(128)S(1)} %stack.43.where, bf16[1024,1024]{1,0:T(8,128)(2,1)} %collective-permute-done.5.refs_0_, bf16[3584,4096]{1,0:T(8,128)(2,1)} %refs_4_.1, f32[1024,3584]{1,0:T(8,128)S(1)} %get-tuple-element.49.refs_2_, ...), custom_call_target="tpu_custom_call", output_to_operand_aliasing={{0}: (3, {})} | custom-call | flops 7516192768 | bytes 1000 | tf_op jit(solution)/shard_map/add_block_1/pallas_call | solution.py:41
  87.8 1.3 collective-permute-start.10
  89.1 1.3 collective-permute-start.13
  90.4 4.9 %collective-permute-done.12.refs_3_ = bf16[512,1024]{1,0:T(8,128)(2,1)S(1)} collective-permute-done((bf16[512,1024]{1,0:T(8,128)(2,1)S(1)}, bf16[512,1024]{1,0:T(8,128)(2,1)S(1)}, u32[]{:S(2)}, u32[]{:S(2)}) %collective-permute-start.12) | collective-permute-done | bytes 1048608 | tf_op jit(solution)/shard_map/ppermute | solution.py:397
  95.3 12.3 %add_block_2.1 = (f32[1024,3584]{1,0:T(8,128)S(1)}, f32[8,128]{1,0:T(8,128)S(1)}) custom-call(s32[9]{0:T(128)S(1)} %stack.43.where, bf16[512,1024]{1,0:T(8,128)(2,1)S(1)} %collective-permute-done.refs_0_, bf16[512,1024]{1,0:T(8,128)(2,1)S(1)} %collective-permute-done.11.refs_1_, ...), custom_call_target="tpu_custom_call", output_to_operand_aliasing={{0}: (6, {})} | custom-call | flops 1000 | bytes 1000 | tf_op jit(solution)/shard_map/add_block_2/pallas_call | solution.py:41
  109.0 5.5 %last_block.5 = (bf16[1024,3584]{1,0:T(8,128)(2,1)S(1)}, f32[1024,3584]{1,0:T(8,128)S(1)}, f32[256,64]{1,0:T(8,128)S(1)}) custom-call(s32[9]{0:T(128)S(1)} %stack.43.where, bf16[512,1024]{1,0:T(8,128)(2,1)S(1)} %collective-permute-done.8.inner, bf16[256,1024]{1,0:T(8,128)(2,1)S(1)} %collective-permute-done.10.outer, ...), custom_call_target="tpu_custom_call", output_to_operand_aliasing={{0}: (3, {}), {1}: (4, {})} | custom-call | flops 1000 | bytes 1000 | tf_op jit(solution)/shard_map/last_block/pallas_call | solution.py:41
  114.6 3.8 %collective-permute-done.13.outer = bf16[256,1024]{1,0:T(8,128)(2,1)S(1)} collective-permute-done((bf16[256,1024]{1,0:T(8,128)(2,1)S(1)}, bf16[256,1024]{1,0:T(8,128)(2,1)S(1)}, u32[]{:S(2)}, u32[]{:S(2)}) %collective-permute-start.13) | collective-permute-done | bytes 524320 | tf_op jit(solution)/shard_map/ppermute | solution.py:414
  118.3 1.5 collective-permute-start.16
  119.8 5.5 %last_block.6 = (bf16[1024,3584]{1,0:T(8,128)(2,1)S(1)}, f32[1024,3584]{1,0:T(8,128)S(1)}, f32[256,64]{1,0:T(8,128)S(1)}) custom-call(s32[9]{0:T(128)S(1)} %stack.43.where, bf16[512,1024]{1,0:T(8,128)(2,1)S(1)} %collective-permute-done.8.inner, bf16[256,1024]{1,0:T(8,128)(2,1)S(1)} %collective-permute-done.13.outer, ...), custom_call_target="tpu_custom_call", output_to_operand_aliasing={{0}: (3, {}), {1}: (4, {})} | custom-call | flops 1000 | bytes 1000 | tf_op jit(solution)/shard_map/last_block/pallas_call | solution.py:41
  128.0 1.6 collective-permute-done.15.outer
  129.6 5.5 %last_block.7 = (bf16[1024,3584]{1,0:T(8,128)(2,1)S(1)}, f32[1024,3584]{1,0:T(8,128)S(1)}, f32[256,64]{1,0:T(8,128)S(1)}) custom-call(s32[9]{0:T(128)S(1)} %stack.43.where, bf16[512,1024]{1,0:T(8,128)(2,1)S(1)} %collective-permute-done.14.inner, bf16[256,1024]{1,0:T(8,128)(2,1)S(1)} %collective-permute-done.15.outer, ...), custom_call_target="tpu_custom_call", output_to_operand_aliasing={{0}: (3, {}), {1}: (4, {})} | custom-call | flops 1000 | bytes 1000 | tf_op jit(solution)/shard_map/last_block/pallas_call | solution.py:41
  135.2 5.3 %last_block.8 = (bf16[1024,3584]{1,0:T(8,128)(2,1)S(1)}, f32[1024,3584]{1,0:T(8,128)S(1)}, f32[128,64]{1,0:T(8,128)S(1)}, f32[256,256]{1,0:T(8,128)S(1)}, f32[25...) custom-call(s32[9]{0:T(128)S(1)} %stack.43.where, ...), custom_call_target="tpu_custom_call", output_to_operand_aliasing={{0}: (3, {}), {1}: (4, {})} | custom-call | flops 1000 | bytes 1000 | tf_op jit(solution)/shard_map/last_block/pallas_call | solution.py:41
  140.8 4.1 %last_block.9 = (bf16[1024,3584]{1,0:T(8,128)(2,1)S(1)}, f32[1024,3584]{1,0:T(8,128)S(1)}, f32[128,64]{1,0:T(8,128)S(1)}) custom-call(s32[9]{0:T(128)S(1)} %stack.43.where, bf16[512,1024]{1,0:T(8,128)(2,1)S(1)} %collective-permute-done.14.inner, bf16[128,1024]{1,0:T(8,128)(2,1)S(1)} %collective-permute-done.17.outer, ...), custom_call_target="tpu_custom_call", output_to_operand_aliasing={{0}: (3, {}), {1}: (4, {})} | custom-call | flops 1000 | bytes 1000 | tf_op jit(solution)/shard_map/last_block/pallas_call | solution.py:41
  146.8 3.2 %collective-permute-done.18 = f32[2,4096]{1,0:T(2,128)S(1)} collective-permute-done((f32[2,4096]{1,0:T(2,128)S(1)}, f32[2,4096]{1,0:T(2,128)S(1)}, u32[]{:S(2)}, u32[]{:S(2)}) %collective-permute-start.18) | collective-permute-done | bytes 32800 | tf_op jit(solution)/shard_map/ppermute | solution.py:439
  150.0 2.9 %collective-permute-start.19 = (f32[2,4096]{1,0:T(2,128)S(1)}, f32[2,4096]{1,0:T(2,128)S(1)}, u32[]{:S(2)}, u32[]{:S(2)}) collective-permute-start(f32[2,4096]{1,0:T(2,128)S(1)} %add.34), channel_id=1, source_target_pairs={{0,8},{4,12},{8,0},{12,4},{1,9},{5,13},{9,1},{13,5},{2,10},{6,14},... | collective-permute-start | bytes 98312 | tf_op jit(solution)/shard_map/ppermute | solution.py:439
  152.9 2.0 %collective-permute-done.19 = f32[2,4096]{1,0:T(2,128)S(1)} collective-permute-done((f32[2,4096]{1,0:T(2,128)S(1)}, f32[2,4096]{1,0:T(2,128)S(1)}, u32[]{:S(2)}, u32[]{:S(2)}) %collective-permute-start.19) | collective-permute-done | bytes 32800 | tf_op jit(solution)/shard_map/ppermute | solution.py:439
  157.1 1.6 collective-permute-start.21
  160.0 3.0 %collective-permute-start.23 = (f32[2,256]{1,0:T(2,128)S(1)}, f32[2,256]{1,0:T(2,128)S(1)}, u32[]{:S(2)}, u32[]{:S(2)}) collective-permute-start(f32[2,256]{1,0:T(2,128)S(1)} %score_sum.1), channel_id=1, source_target_pairs={{0,8},{4,12},{8,0},{12,4},{1,9},{5,13},{9,1},{13,5},{2,10},{6,14},... | collective-permute-start | bytes 6152 | tf_op jit(solution)/shard_map/ppermute | solution.py:439
  163.0 2.9 %hessian_update.1 = f32[256,4096]{1,0:T(8,128)} custom-call(s32[9]{0:T(128)S(1)} %stack.43.where, f32[8,4096]{1,0:T(8,128)S(1)} %pad_maximum_fusion.grads.mine, f32[8,4096]{1,0:T(8,128)S(1)} %pad_maximum_fusion.grads.mine, f32[256,4096]{1,0:T(8,128)S(1)} %get-tuple-element.81.hessian), custom_call_target="tpu_custom_call" | custom-call | flops 1000 | bytes 1000 | tf_op jit(solution)/shard_map/hessian_update/pallas_call | solution.py:41
  (53 shorter events, 19.1 us)
Async XLA Ops:
  0.6 21.1 %copy-start.1 = (bf16[1024,1024]{1,0:T(8,128)(2,1)S(1)}, bf16[1024,1024]{1,0:T(8,128)(2,1)}, u32[]{:S(2)}) copy-start(bf16[1024,1024]{1,0:T(8,128)(2,1)} %own) | copy-start | bytes 6291460
  0.6 49.9 %collective-permute-start.5 = (bf16[1024,1024]{1,0:T(8,128)(2,1)}, bf16[1024,1024]{1,0:T(8,128)(2,1)}, u32[]{:S(2)}, u32[]{:S(2)}) collective-permute-start(bf16[1024,1024]{1,0:T(8,128)(2,1)} %own), channel_id=1, source_target_pairs={{0,4},{4,0},{8,12},{12,8},{1,5},{5,1},{9,13},{13,9},{2,6},{6,2},{1... | collective-permute-start | bytes 6291464 | tf_op jit(solution)/shard_map/ppermute | solution.py:391
  6.8 27.0 %collective-permute-start = (bf16[512,1024]{1,0:T(8,128)(2,1)}, bf16[512,1024]{1,0:T(8,128)(2,1)S(1)}, u32[]{:S(2)}, u32[]{:S(2)}) collective-permute-start(bf16[512,1024]{1,0:T(8,128)(2,1)} %get-tuple-element.87), channel_id=1, source_target_pairs={{4,8},{8,4},{5,9},{9,5},{6,10},{10,6},{7,11},{11,7},{20,24},{24,20... | collective-permute-start | bytes 3145736 | tf_op jit(solution)/shard_map/ppermute | solution.py:393
  7.5 5.8 %collective-permute-start.2 = (f32[256,256]{1,0:T(8,128)}, f32[256,256]{1,0:T(8,128)S(1)}, u32[]{:S(2)}, u32[]{:S(2)}) collective-permute-start(f32[256,256]{1,0:T(8,128)} %rest_0_.1), channel_id=1, source_target_pairs={{0,1},{1,0},{2,3},{3,2},{4,5},{5,4},{6,7},{7,6},{8,9},{9,8},{10,11... | collective-permute-start | bytes 786440 | tf_op jit(solution)/shard_map/ppermute | solution.py:439
  7.6 9.5 %collective-permute-start.3 = (f32[256,256]{1,0:T(8,128)}, f32[256,256]{1,0:T(8,128)}, u32[]{:S(2)}, u32[]{:S(2)}) collective-permute-start(f32[256,256]{1,0:T(8,128)} %rest_0_.1), channel_id=1, source_target_pairs={{0,2},{1,3},{2,0},{3,1},{4,6},{5,7},{6,4},{7,5},{8,10},{9,11},{10,... | collective-permute-start | bytes 786440 | tf_op jit(solution)/shard_map/ppermute | solution.py:439
  9.1 12.6 %collective-permute-start.4 = (f32[256,256]{1,0:T(8,128)}, f32[256,256]{1,0:T(8,128)}, u32[]{:S(2)}, u32[]{:S(2)}) collective-permute-start(f32[256,256]{1,0:T(8,128)} %rest_0_.1), channel_id=1, source_target_pairs={{0,3},{1,2},{2,1},{3,0},{4,7},{5,6},{6,5},{7,4},{8,11},{9,10},{10,... | collective-permute-start | bytes 786440 | tf_op jit(solution)/shard_map/ppermute | solution.py:439
  9.5 1.6 copy-start.2
  11.1 0.9 copy-start.3
  13.3 20.5 %copy-start.4 = (f32[256,256]{1,0:T(8,128)}, f32[256,256]{1,0:T(8,128)S(1)}, u32[]{:S(2)}) copy-start(f32[256,256]{1,0:T(8,128)S(1)} %collective-permute-done.2.rest_1_) | copy-start | bytes 786436
  13.3 45.5 %collective-permute-start.11 = (bf16[512,1024]{1,0:T(8,128)(2,1)}, bf16[512,1024]{1,0:T(8,128)(2,1)S(1)}, u32[]{:S(2)}, u32[]{:S(2)}) collective-permute-start(bf16[512,1024]{1,0:T(8,128)(2,1)} %get-tuple-element.86), channel_id=1, source_target_pairs={{4,8},{8,4},{5,9},{9,5},{6,10},{10,6},{7,11},{11,7},{20,24},{24,20... | collective-permute-start | bytes 3145736 | tf_op jit(solution)/shard_map/ppermute | solution.py:393
  33.8 39.1 %collective-permute-start.9 = (bf16[512,1024]{1,0:T(8,128)(2,1)S(1)}, bf16[512,1024]{1,0:T(8,128)(2,1)S(1)}, u32[]{:S(2)}, u32[]{:S(2)}) collective-permute-start(bf16[512,1024]{1,0:T(8,128)(2,1)S(1)} %collective-permute-done.refs_0_), channel_id=1, source_target_pairs={{4,0},{8,12},{5,1},{9,13},{6,2},{10,14},{7,3},{11,15},{20,16},{24,... | collective-permute-start | bytes 3145736 | tf_op jit(solution)/shard_map/ppermute | solution.py:397
  52.2 35.5 %collective-permute-start.8 = (bf16[512,1024]{1,0:T(8,128)(2,1)S(1)}, bf16[512,1024]{1,0:T(8,128)(2,1)S(1)}, u32[]{:S(2)}, u32[]{:S(2)}) collective-permute-start(bf16[512,1024]{1,0:T(8,128)(2,1)S(1)} %get-tuple-element.85), channel_id=1, source_target_pairs={{4,8},{8,4},{5,9},{9,5},{6,10},{10,6},{7,11},{11,7},{20,24},{24,20... | collective-permute-start | bytes 3145736 | tf_op jit(solution)/shard_map/ppermute | solution.py:399
  53.0 10.0 %collective-permute-start.1 = (f32[64,1024]{1,0:T(8,128)S(1)}, f32[64,1024]{1,0:T(8,128)S(1)}, u32[]{:S(2)}, u32[]{:S(2)}) collective-permute-start(f32[64,1024]{1,0:T(8,128)S(1)} %input_block.1.a), channel_id=1, source_target_pairs={{0,4},{12,8},{1,5},{13,9},{2,6},{14,10},{3,7},{15,11},{16,20},{28,... | collective-permute-start | bytes 786440 | tf_op jit(solution)/shard_map/ppermute | solution.py:395
  58.8 36.5 %collective-permute-start.12 = (bf16[512,1024]{1,0:T(8,128)(2,1)S(1)}, bf16[512,1024]{1,0:T(8,128)(2,1)S(1)}, u32[]{:S(2)}, u32[]{:S(2)}) collective-permute-start(bf16[512,1024]{1,0:T(8,128)(2,1)S(1)} %collective-permute-done.11.refs_1_), channel_id=1, source_target_pairs={{4,0},{8,12},{5,1},{9,13},{6,2},{10,14},{7,3},{11,15},{20,16},{24,... | collective-permute-start | bytes 3145736 | tf_op jit(solution)/shard_map/ppermute | solution.py:397
  72.9 14.3 %collective-permute-start.6 = (f32[64,1024]{1,0:T(8,128)S(1)}, f32[64,1024]{1,0:T(8,128)S(1)}, u32[]{:S(2)}, u32[]{:S(2)}) collective-permute-start(f32[64,1024]{1,0:T(8,128)S(1)} %side.1.a), channel_id=1, source_target_pairs={{4,8},{8,4},{5,9},{9,5},{6,10},{10,6},{7,11},{11,7},{20,24},{24,20... | collective-permute-start | bytes 786440 | tf_op jit(solution)/shard_map/ppermute | solution.py:401
  73.5 34.1 %collective-permute-start.14 = (bf16[512,1024]{1,0:T(8,128)(2,1)S(1)}, bf16[512,1024]{1,0:T(8,128)(2,1)S(1)}, u32[]{:S(2)}, u32[]{:S(2)}) collective-permute-start(bf16[512,1024]{1,0:T(8,128)(2,1)S(1)} %get-tuple-element.62), channel_id=1, source_target_pairs={{4,8},{8,4},{5,9},{9,5},{6,10},{10,6},{7,11},{11,7},{20,24},{24,20... | collective-permute-start | bytes 3145736 | tf_op jit(solution)/shard_map/ppermute | solution.py:400
  87.8 19.8 %collective-permute-start.10 = (bf16[256,1024]{1,0:T(8,128)(2,1)S(1)}, bf16[256,1024]{1,0:T(8,128)(2,1)S(1)}, u32[]{:S(2)}, u32[]{:S(2)}) collective-permute-start(bf16[256,1024]{1,0:T(8,128)(2,1)S(1)} %get-tuple-element.51), channel_id=1, source_target_pairs={{4,0},{8,12},{5,1},{9,13},{6,2},{10,14},{7,3},{11,15},{20,16},{24,... | collective-permute-start | bytes 1572872 | tf_op jit(solution)/shard_map/ppermute | solution.py:414
  89.1 29.2 %collective-permute-start.13 = (bf16[256,1024]{1,0:T(8,128)(2,1)S(1)}, bf16[256,1024]{1,0:T(8,128)(2,1)S(1)}, u32[]{:S(2)}, u32[]{:S(2)}) collective-permute-start(bf16[256,1024]{1,0:T(8,128)(2,1)S(1)} %get-tuple-element.58), channel_id=1, source_target_pairs={{4,0},{8,12},{5,1},{9,13},{6,2},{10,14},{7,3},{11,15},{20,16},{24,... | collective-permute-start | bytes 1572872 | tf_op jit(solution)/shard_map/ppermute | solution.py:414
  95.3 13.7 %copy-start = (bf16[3584,64]{0,1:T(8,128)(2,1)S(1)}, bf16[3584,64]{0,1:T(8,128)(2,1)}, u32[]{:S(2)}) copy-start(bf16[3584,64]{0,1:T(8,128)(2,1)} %param.13) | copy-start | bytes 1376260
  107.7 21.9 %collective-permute-start.15 = (bf16[256,1024]{1,0:T(8,128)(2,1)S(1)}, bf16[256,1024]{1,0:T(8,128)(2,1)S(1)}, u32[]{:S(2)}, u32[]{:S(2)}) collective-permute-start(bf16[256,1024]{1,0:T(8,128)(2,1)S(1)} %slice.40), channel_id=1, source_target_pairs={{4,0},{8,12},{5,1},{9,13},{6,2},{10,14},{7,3},{11,15},{20,16},{24,... | collective-permute-start | bytes 1572872 | tf_op jit(solution)/shard_map/ppermute | solution.py:414
  118.3 16.9 %collective-permute-start.16 = (bf16[128,1024]{1,0:T(8,128)(2,1)S(1)}, bf16[128,1024]{1,0:T(8,128)(2,1)S(1)}, u32[]{:S(2)}, u32[]{:S(2)}) collective-permute-start(bf16[128,1024]{1,0:T(8,128)(2,1)S(1)} %get-tuple-element.67), channel_id=1, source_target_pairs={{4,0},{8,12},{5,1},{9,13},{6,2},{10,14},{7,3},{11,15},{20,16},{24,... | collective-permute-start | bytes 786440 | tf_op jit(solution)/shard_map/ppermute | solution.py:414
  125.4 15.5 %collective-permute-start.17 = (bf16[128,1024]{1,0:T(8,128)(2,1)S(1)}, bf16[128,1024]{1,0:T(8,128)(2,1)S(1)}, u32[]{:S(2)}, u32[]{:S(2)}) collective-permute-start(bf16[128,1024]{1,0:T(8,128)(2,1)S(1)} %get-tuple-element.71), channel_id=1, source_target_pairs={{4,0},{8,12},{5,1},{9,13},{6,2},{10,14},{7,3},{11,15},{20,16},{24,... | collective-permute-start | bytes 786440 | tf_op jit(solution)/shard_map/ppermute | solution.py:414
  126.7 18.2 %collective-permute-start.7 = (bf16[64,1024]{1,0:T(8,128)(2,1)S(1)}, bf16[64,1024]{1,0:T(8,128)(2,1)S(1)}, u32[]{:S(2)}, u32[]{:S(2)}) collective-permute-start(bf16[64,1024]{1,0:T(8,128)(2,1)S(1)} %convert_element_type.4), channel_id=1, source_target_pairs={{4,0},{8,12},{5,1},{9,13},{6,2},{10,14},{7,3},{11,15},{20,16},{24,... | collective-permute-start | bytes 393224 | tf_op jit(solution)/shard_map/ppermute | solution.py:402
  146.0 4.0 %collective-permute-start.18 = (f32[2,4096]{1,0:T(2,128)S(1)}, f32[2,4096]{1,0:T(2,128)S(1)}, u32[]{:S(2)}, u32[]{:S(2)}) collective-permute-start(f32[2,4096]{1,0:T(2,128)S(1)} %outer_products.1), channel_id=1, source_target_pairs={{0,4},{4,0},{8,12},{12,8},{1,5},{5,1},{9,13},{13,9},{2,6},{6,2},{1... | collective-permute-start | bytes 98312 | tf_op jit(solution)/shard_map/ppermute | solution.py:439
  150.0 4.9 %collective-permute-start.19 = (f32[2,4096]{1,0:T(2,128)S(1)}, f32[2,4096]{1,0:T(2,128)S(1)}, u32[]{:S(2)}, u32[]{:S(2)}) collective-permute-start(f32[2,4096]{1,0:T(2,128)S(1)} %add.34), channel_id=1, source_target_pairs={{0,8},{4,12},{8,0},{12,4},{1,9},{5,13},{9,1},{13,5},{2,10},{6,14},... | collective-permute-start | bytes 98312 | tf_op jit(solution)/shard_map/ppermute | solution.py:439
  155.7 1.3 collective-permute-start.20
  155.8 3.7 %collective-permute-start.22 = (f32[2,256]{1,0:T(2,128)S(1)}, f32[2,256]{1,0:T(2,128)S(1)}, u32[]{:S(2)}, u32[]{:S(2)}) collective-permute-start(f32[2,256]{1,0:T(2,128)S(1)} %scores.1.a), channel_id=1, source_target_pairs={{0,4},{4,0},{8,12},{12,8},{1,5},{5,1},{9,13},{13,9},{2,6},{6,2},{1... | collective-permute-start | bytes 6152 | tf_op jit(solution)/shard_map/ppermute | solution.py:439
  157.1 5.9 %collective-permute-start.21 = (f32[4,4096]{1,0:T(4,128)S(1)}, f32[4,4096]{1,0:T(4,128)S(1)}, u32[]{:S(2)}, u32[]{:S(2)}) collective-permute-start(f32[4,4096]{1,0:T(4,128)S(1)} %pad_maximum_fusion.1), channel_id=1, source_target_pairs={{0,2},{1,3},{2,0},{3,1},{4,6},{5,7},{6,4},{7,5},{8,10},{9,11},{10,... | collective-permute-start | bytes 196616 | tf_op jit(solution)/shard_map/ppermute | solution.py:439
  160.0 5.9 %collective-permute-start.23 = (f32[2,256]{1,0:T(2,128)S(1)}, f32[2,256]{1,0:T(2,128)S(1)}, u32[]{:S(2)}, u32[]{:S(2)}) collective-permute-start(f32[2,256]{1,0:T(2,128)S(1)} %score_sum.1), channel_id=1, source_target_pairs={{0,8},{4,12},{8,0},{12,4},{1,9},{5,13},{9,1},{13,5},{2,10},{6,14},... | collective-permute-start | bytes 6152 | tf_op jit(solution)/shard_map/ppermute | solution.py:439

commit v14 on v13

--- a/solution.py
+++ b/solution.py
@@ -163,9 +163,10 @@
 
 
 def last_body(start, inner_at, bring, where, inner, outer, kept, old, gate, po_t, _, *rest):
-    far, rest = rest[:bring], rest[bring:]
-    _, _, right, *near = rest[: 3 + bring]
-    gates, po, gate_sems, po_sem, near_sems = rest[3 + bring :]
+    count = len(bring)
+    far, rest = rest[:count], rest[count:]
+    _, _, right, *near = rest[: 3 + count]
+    gates, po, gate_sems, po_sem, near_sems = rest[3 + count :]
     size = outer.shape[0]
     hidden = kept.shape[1]
     tokens = pl.ds(start, size)
@@ -178,7 +179,10 @@
     po_read.start()
     for read in reads[1:]:
         read.start()
-    brought = [pltpu.make_async_copy(a, b, near_sems.at[i]) for i, (a, b) in enumerate(zip(far, near))]
+    brought = [
+        pltpu.make_async_copy(a.at[pl.ds(first, b.shape[0])], b, near_sems.at[i])
+        for i, (a, b, first) in enumerate(zip(far, near, bring))
+    ]
     for copy in brought:
         copy.start()
     block = select(where, inner.at[pl.ds(inner_at, size)], outer)
@@ -199,18 +203,18 @@
     size = outer.shape[0]
     tiles = kept.shape[1] // TILE
     return call(
-        functools.partial(last_body, start, inner_at, len(bring)),
+        functools.partial(last_body, start, inner_at, [first for _, first, _ in bring]),
         "last_block",
         where,
         (1,),
-        (inner, outer, kept, old, gate, po_t, token, *bring),
+        (inner, outer, kept, old, gate, po_t, token, *[a for a, _, _ in bring]),
         [INSIDE, INSIDE, INSIDE, INSIDE, OUTSIDE, ANYWHERE, ANYWHERE] + [OUTSIDE] * len(bring),
-        [INSIDE, INSIDE, pl.BlockSpec((size, PROJ), lambda j, where: (0, 0))] + [INSIDE] * len(bring),
+        [INSIDE] * (3 + len(bring)),
         [
             pltpu.VMEM(kept.shape, kept.dtype),
             pltpu.VMEM(old.shape, old.dtype),
-            jax.ShapeDtypeStruct((size, PROJ), jnp.float32),
-            *[pltpu.VMEM(a.shape, a.dtype) for a in bring],
+            pltpu.VMEM((size, PROJ), jnp.float32),
+            *[pltpu.VMEM((rows, a.shape[1]), a.dtype) for a, _, rows in bring],
         ],
         [
             pltpu.VMEM((tiles, size, TILE), gate.dtype),
@@ -222,6 +226,34 @@
         LIMIT,
         aliases={3: 0, 4: 1},
     )
+
+
+def final_body(start, inner_at, where, inner, outer, kept, old, gate, po, right):
+    size = outer.shape[0]
+    block = select(where, inner.at[pl.ds(inner_at, size)], outer)
+    total = jnp.zeros((size, PROJ), jnp.float32)
+    for t in range(kept.shape[1] // TILE):
+        span = pl.ds(t * TILE, TILE)
+        hidden_grad = old[pl.ds(start, size), span] + dot(block, kept[:, span])
+        up_grad = (hidden_grad * silu(gate[:, span].astype(jnp.float32))).astype(jnp.bfloat16)
+        total = total + dot_nt(up_grad, po[:, span])
+    right[...] = total
+
+
+def final_block(where, inner, inner_at, outer, start, kept, old, gate, po):
+    (right,) = call(
+        functools.partial(final_body, start, inner_at),
+        "final_block",
+        where,
+        (1,),
+        (inner, outer, kept, old, gate, po),
+        [INSIDE] * 6,
+        [INSIDE],
+        [pltpu.VMEM((outer.shape[0], PROJ), jnp.float32)],
+        [],
+        LIMIT,
+    )
+    return right
 
 
 def outer_body(where, total, sent, *refs):
@@ -255,9 +287,9 @@
         where,
         (1,),
         (total, sent, *rights),
-        [fixed(a.shape) for a in (total, sent, *rights)],
-        [pl.BlockSpec(shape, lambda j, where: (0, 0))],
-        [jax.ShapeDtypeStruct(shape, jnp.float32)],
+        [INSIDE] * (2 + len(rights)),
+        [INSIDE],
+        [pltpu.VMEM(shape, jnp.float32)],
         [pltpu.VMEM((PROJ, 2 * PROJ), jnp.float32)],
         LIMIT,
     )
@@ -321,7 +353,7 @@
         where,
         (1,),
         (grads, *parts),
-        [fixed(grads.shape)] + [INSIDE] * len(parts),
+        [INSIDE] * (1 + len(parts)),
         [pl.BlockSpec(shape, lambda j, where: (0, 0))],
         [jax.ShapeDtypeStruct(shape, jnp.float32)],
         [],
@@ -338,10 +370,9 @@
     return high, middle, low
 
 
-def update_body(scale, where, grads, mine, hessian, out, new, out_sems):
-    columns = grads.shape[1]
+def update_body(scale, where, grads, hessian, out, new, out_sems):
     parts, _, width = new.shape
-    high, middle, low = pieces(mine[...])
+    high, middle, low = pieces(grads[:, columns(where, FIRST_PART, new.shape[1])])
     left = jnp.concatenate([high, high, middle, middle, high, low], axis=0).T
     writes = []
     for t in range(parts):
@@ -356,23 +387,19 @@
 
 
 def update(where, grads, hessian):
-    rows, columns = hessian.shape
+    rows, length = hessian.shape
     count = grads.shape[0]
     parts = 8
-    width = columns // parts
+    width = length // parts
     (updated,) = call(
         functools.partial(update_body, 1.0 / count),
         "hessian_update",
         where,
         (1,),
-        (grads, grads, hessian),
-        [
-            fixed(grads.shape),
-            pl.BlockSpec((count, rows), lambda j, where: (0, where[FIRST_PART]), pipeline_mode=pl.Buffered(1)),
-            INSIDE,
-        ],
+        (grads, hessian),
+        [INSIDE, INSIDE],
         [ANYWHERE],
-        [jax.ShapeDtypeStruct((rows, columns), jnp.float32)],
+        [jax.ShapeDtypeStruct((rows, length), jnp.float32)],
         [pltpu.VMEM((parts, rows, width), jnp.float32), pltpu.SemaphoreType.DMA((parts,))],
         LIMIT,
         flops=1000,
@@ -413,12 +440,18 @@
         ahead = arrived[n + 1] if n < 4 else arrived[n]
         end_outer = send(after(end_inner[h][at : at + size], ahead, done[n]), perm=outward)
         arrived.append(end_outer)
-        bring = [*early, late] if n == len(sizes) - 2 else []
+        if n == len(sizes) - 1:
+            rights.append(final_block(where, end_inner[h], at, end_outer, start, kept, acc, gate_near, po_near))
+            break
+        bring = []
+        if n == len(sizes) - 2:
+            bring = [(a, 0, a.shape[0]) for a in (*early, late, proj_out.T)]
+            bring.append((gate_pre, start + size, tokens - start - size))
         kept, acc, right, *brought = last_block(
             where, end_inner[h], at, end_outer, start, kept, acc, gate_pre, proj_out.T, second, bring
         )
         if bring:
-            *early, late = brought
+            *early, late, po_near, gate_near = brought
         rights.append(right)
         done.append(right)
         start += size

time: 167 us -> 167 us (level)
  no operation moved by 1% of the time
where the time goes in v14:
time: 167 us; the launch traced here: 166 us
  Pallas kernels  70.4 us (42%)
  waiting for transfers between devices  51.4 us (31%)
  starting transfers between devices  34.9 us (21%)
  local copies, waits for them, and re-layouts  7.49 us (4%)
    pallas_call x15, Pallas kernels, call(): pl.pallas_call(body, grid_spec=pltpu.PrefetchScalarGridSpec(num_scalar_pr...  70.4 us
    ppermute x1, waiting for transfers between devices, line_of_four(): pair = send(grad_out, perm=pairs)  15.4 us
    ppermute x2, waiting for transfers between devices, line_of_four(): mid_outer = [send(after(a, begun), perm=outward) for a in mid_inner]  14.3 us
    ppermute x9, waiting for transfers between devices, swap(): lax.ppermute(a, axis, [(i, i ^ bit) for i in range(lax.axis_size(axis))])  13.5 us
    ppermute x9, starting transfers between devices, swap(): lax.ppermute(a, axis, [(i, i ^ bit) for i in range(lax.axis_size(axis))])  11.9 us
    ppermute x5, starting transfers between devices, line_of_four(): send(after(end_inner[h][at:at + size], ahead, done[n]), perm=outward)  6.63 us
    ppermute x1, starting transfers between devices, line_of_four(): from_end = send(after(in_part, mid_inner[0]), perm=inward)  5.83 us
    ppermute x5, waiting for transfers between devices, line_of_four(): send(after(end_inner[h][at:at + size], ahead, done[n]), perm=outward)  5.42 us
  transfers between devices with their start and end apart: 24, of which 13 were waited for; matrix products, arithmetic and copies ran while one was open for 3% of the time, Pallas kernels for 41%

profile of v14, /device:TPU:0, one launch (start us, length us, event | category | flops | bytes accessed | tf_op | source)
XLA Modules:
  0.0 165.9 jit_solution(5884677168923849444)
XLA Ops:
  0.6 3.1 %collective-permute-start.5 = (bf16[1024,1024]{1,0:T(8,128)(2,1)}, bf16[1024,1024]{1,0:T(8,128)(2,1)}, u32[]{:S(2)}, u32[]{:S(2)}) collective-permute-start(bf16[1024,1024]{1,0:T(8,128)(2,1)} %own), channel_id=1, source_target_pairs={{0,4},{4,0},{8,12},{12,8},{1,5},{5,1},{9,13},{13,9},{2,6},{6,2},{1... | collective-permute-start | bytes 6291464 | tf_op jit(solution)/shard_map/ppermute | solution.py:418
  3.7 3.0 %fusion.1 = (bf16[512,1024]{1,0:T(8,128)(2,1)}, bf16[512,1024]{1,0:T(8,128)(2,1)}) fusion(bf16[1024,1024]{1,0:T(8,128)(2,1)} %own), kind=kLoop, calls=%fused_computation.3 | loop fusion | bytes 4194304 | tf_op jit(solution)/shard_map/slice | solution.py:419
  7.6 1.6 collective-permute-start.3
  9.5 1.6 copy-done.2
  12.0 1.3 input_block.1.a
  14.1 3.0 %collective-permute-done.3.rest_2_ = f32[256,256]{1,0:T(8,128)} collective-permute-done((f32[256,256]{1,0:T(8,128)}, f32[256,256]{1,0:T(8,128)}, u32[]{:S(2)}, u32[]{:S(2)}) %collective-permute-start.3) | collective-permute-done | bytes 262176 | tf_op jit(solution)/shard_map/ppermute | solution.py:472
  17.1 4.7 %collective-permute-done.4.rest_3_ = f32[256,256]{1,0:T(8,128)} collective-permute-done((f32[256,256]{1,0:T(8,128)}, f32[256,256]{1,0:T(8,128)}, u32[]{:S(2)}, u32[]{:S(2)}) %collective-permute-start.4) | collective-permute-done | bytes 262176 | tf_op jit(solution)/shard_map/ppermute | solution.py:472
  21.8 12.0 %own_block.1 = (f32[1024,3584]{1,0:T(8,128)S(1)}, bf16[1024,3584]{1,0:T(8,128)(2,1)S(1)}, f32[8,128]{1,0:T(8,128)S(1)}) custom-call(s32[9]{0:T(128)S(1)} %stack.43.where, bf16[1024,1024]{1,0:T(8,128)(2,1)S(1)} %copy-done.1, bf16[3584,4096]{1,0:T(8,128)(2,1)} %refs_4_.1, bf16[3584,4096]{1,0:T(8,128)(2,1)} %refs_4_.1), custom_call_target="tpu_custom_call" | custom-call | flops 1000 | bytes 1000 | tf_op jit(solution)/shard_map/own_block/pallas_call | solution.py:41
  33.8 1.3 collective-permute-start.9
  35.1 15.4 %collective-permute-done.5.refs_0_ = bf16[1024,1024]{1,0:T(8,128)(2,1)} collective-permute-done((bf16[1024,1024]{1,0:T(8,128)(2,1)}, bf16[1024,1024]{1,0:T(8,128)(2,1)}, u32[]{:S(2)}, u32[]{:S(2)}) %collective-permute-start.5) | collective-permute-done | bytes 2097184 | tf_op jit(solution)/shard_map/ppermute | solution.py:418
  50.5 1.7 %fusion = (bf16[512,1024]{1,0:T(8,128)(2,1)S(1)}, bf16[512,1024]{1,0:T(8,128)(2,1)S(1)}) fusion(bf16[1024,1024]{1,0:T(8,128)(2,1)} %collective-permute-done.5.refs_0_), kind=kLoop, calls=%fused_computation.2 | loop fusion | bytes 4194304 | tf_op jit(solution)/shard_map/slice | solution.py:427
  53.0 5.8 %collective-permute-start.1 = (f32[64,1024]{1,0:T(8,128)S(1)}, f32[64,1024]{1,0:T(8,128)S(1)}, u32[]{:S(2)}, u32[]{:S(2)}) collective-permute-start(f32[64,1024]{1,0:T(8,128)S(1)} %input_block.1.a), channel_id=1, source_target_pairs={{0,4},{12,8},{1,5},{13,9},{2,6},{14,10},{3,7},{15,11},{16,20},{28,... | collective-permute-start | bytes 786440 | tf_op jit(solution)/shard_map/ppermute | solution.py:422
  60.1 2.8 %collective-permute-done.1.b = f32[64,1024]{1,0:T(8,128)S(1)} collective-permute-done((f32[64,1024]{1,0:T(8,128)S(1)}, f32[64,1024]{1,0:T(8,128)S(1)}, u32[]{:S(2)}, u32[]{:S(2)}) %collective-permute-start.1) | collective-permute-done | bytes 262176 | tf_op jit(solution)/shard_map/ppermute | solution.py:422
  63.5 9.4 %collective-permute-done.9.refs_2_ = bf16[512,1024]{1,0:T(8,128)(2,1)S(1)} collective-permute-done((bf16[512,1024]{1,0:T(8,128)(2,1)S(1)}, bf16[512,1024]{1,0:T(8,128)(2,1)S(1)}, u32[]{:S(2)}, u32[]{:S(2)}) %collective-permute-start.9) | collective-permute-done | bytes 1048608 | tf_op jit(solution)/shard_map/ppermute | solution.py:424
  74.3 12.9 %add_block_1.1 = (f32[1024,3584]{1,0:T(8,128)S(1)}, f32[8,128]{1,0:T(8,128)S(1)}) custom-call(s32[9]{0:T(128)S(1)} %stack.43.where, bf16[1024,1024]{1,0:T(8,128)(2,1)} %collective-permute-done.5.refs_0_, bf16[3584,4096]{1,0:T(8,128)(2,1)} %refs_4_.1, f32[1024,3584]{1,0:T(8,128)S(1)} %get-tuple-element.50.refs_2_, ...), custom_call_target="tpu_custom_call", output_to_operand_aliasing={{0}: (3, {})} | custom-call | flops 7516192768 | bytes 1000 | tf_op jit(solution)/shard_map/add_block_1/pallas_call | solution.py:41
  87.8 1.3 collective-permute-start.10
  90.4 4.9 %collective-permute-done.12.refs_3_ = bf16[512,1024]{1,0:T(8,128)(2,1)S(1)} collective-permute-done((bf16[512,1024]{1,0:T(8,128)(2,1)S(1)}, bf16[512,1024]{1,0:T(8,128)(2,1)S(1)}, u32[]{:S(2)}, u32[]{:S(2)}) %collective-permute-start.12) | collective-permute-done | bytes 1048608 | tf_op jit(solution)/shard_map/ppermute | solution.py:424
  95.3 12.3 %add_block_2.1 = (f32[1024,3584]{1,0:T(8,128)S(1)}, f32[8,128]{1,0:T(8,128)S(1)}) custom-call(s32[9]{0:T(128)S(1)} %stack.43.where, bf16[512,1024]{1,0:T(8,128)(2,1)S(1)} %collective-permute-done.refs_0_, bf16[512,1024]{1,0:T(8,128)(2,1)S(1)} %collective-permute-done.11.refs_1_, ...), custom_call_target="tpu_custom_call", output_to_operand_aliasing={{0}: (6, {})} | custom-call | flops 1000 | bytes 1000 | tf_op jit(solution)/shard_map/add_block_2/pallas_call | solution.py:41
  109.0 5.5 %last_block.4 = (bf16[1024,3584]{1,0:T(8,128)(2,1)S(1)}, f32[1024,3584]{1,0:T(8,128)S(1)}, f32[256,64]{1,0:T(8,128)S(1)}) custom-call(s32[9]{0:T(128)S(1)} %stack.43.where, bf16[512,1024]{1,0:T(8,128)(2,1)S(1)} %collective-permute-done.8.inner, bf16[256,1024]{1,0:T(8,128)(2,1)S(1)} %collective-permute-done.10.outer, ...), custom_call_target="tpu_custom_call", output_to_operand_aliasing={{0}: (3, {}), {1}: (4, {})} | custom-call | flops 1000 | bytes 1000 | tf_op jit(solution)/shard_map/last_block/pallas_call | solution.py:41
  114.6 3.8 %collective-permute-done.13.outer = bf16[256,1024]{1,0:T(8,128)(2,1)S(1)} collective-permute-done((bf16[256,1024]{1,0:T(8,128)(2,1)S(1)}, bf16[256,1024]{1,0:T(8,128)(2,1)S(1)}, u32[]{:S(2)}, u32[]{:S(2)}) %collective-permute-start.13) | collective-permute-done | bytes 524320 | tf_op jit(solution)/shard_map/ppermute | solution.py:441
  118.3 1.5 collective-permute-start.16
  119.8 5.5 %last_block.5 = (bf16[1024,3584]{1,0:T(8,128)(2,1)S(1)}, f32[1024,3584]{1,0:T(8,128)S(1)}, f32[256,64]{1,0:T(8,128)S(1)}) custom-call(s32[9]{0:T(128)S(1)} %stack.43.where, bf16[512,1024]{1,0:T(8,128)(2,1)S(1)} %collective-permute-done.8.inner, bf16[256,1024]{1,0:T(8,128)(2,1)S(1)} %collective-permute-done.13.outer, ...), custom_call_target="tpu_custom_call", output_to_operand_aliasing={{0}: (3, {}), {1}: (4, {})} | custom-call | flops 1000 | bytes 1000 | tf_op jit(solution)/shard_map/last_block/pallas_call | solution.py:41
  128.0 1.6 collective-permute-done.15.outer
  129.6 5.5 %last_block.6 = (bf16[1024,3584]{1,0:T(8,128)(2,1)S(1)}, f32[1024,3584]{1,0:T(8,128)S(1)}, f32[256,64]{1,0:T(8,128)S(1)}) custom-call(s32[9]{0:T(128)S(1)} %stack.43.where, bf16[512,1024]{1,0:T(8,128)(2,1)S(1)} %collective-permute-done.14.inner, bf16[256,1024]{1,0:T(8,128)(2,1)S(1)} %collective-permute-done.15.outer, ...), custom_call_target="tpu_custom_call", output_to_operand_aliasing={{0}: (3, {}), {1}: (4, {})} | custom-call | flops 1000 | bytes 1000 | tf_op jit(solution)/shard_map/last_block/pallas_call | solution.py:41
  135.2 6.4 %last_block.7 = (bf16[1024,3584]{1,0:T(8,128)(2,1)S(1)}, f32[1024,3584]{1,0:T(8,128)S(1)}, f32[128,64]{1,0:T(8,128)S(1)}, f32[256,256]{1,0:T(8,128)S(1)}, f32[25...) custom-call(s32[9]{0:T(128)S(1)} %stack.43.where, ...), custom_call_target="tpu_custom_call", output_to_operand_aliasing={{0}: (3, {}), {1}: (4, {})} | custom-call | flops 1000 | bytes 1000 | tf_op jit(solution)/shard_map/last_block/pallas_call | solution.py:41
  141.6 2.5 %final_block.1.refs_4_ = f32[128,64]{1,0:T(8,128)S(1)} custom-call(s32[9]{0:T(128)S(1)} %stack.43.where, bf16[512,1024]{1,0:T(8,128)(2,1)S(1)} %collective-permute-done.14.inner, bf16[128,1024]{1,0:T(8,128)(2,1)S(1)} %collective-permute-done.17.outer, bf16[1024,3584]{1,0:T(8,128)(2,1)S(1)} %get-tuple-element.73.kept, ...), custom_call_target="tpu_custom_call" | custom-call | flops 1000 | bytes 1000 | tf_op jit(solution)/shard_map/final_block/pallas_call | solution.py:41
  146.3 2.9 %collective-permute-done.18 = f32[2,4096]{1,0:T(2,128)S(1)} collective-permute-done((f32[2,4096]{1,0:T(2,128)S(1)}, f32[2,4096]{1,0:T(2,128)S(1)}, u32[]{:S(2)}, u32[]{:S(2)}) %collective-permute-start.18) | collective-permute-done | bytes 32800 | tf_op jit(solution)/shard_map/ppermute | solution.py:472
  149.2 3.2 %collective-permute-start.19 = (f32[2,4096]{1,0:T(2,128)S(1)}, f32[2,4096]{1,0:T(2,128)S(1)}, u32[]{:S(2)}, u32[]{:S(2)}) collective-permute-start(f32[2,4096]{1,0:T(2,128)S(1)} %add.34), channel_id=1, source_target_pairs={{0,8},{4,12},{8,0},{12,4},{1,9},{5,13},{9,1},{13,5},{2,10},{6,14},... | collective-permute-start | bytes 98312 | tf_op jit(solution)/shard_map/ppermute | solution.py:472
  152.4 1.9 %collective-permute-done.19 = f32[2,4096]{1,0:T(2,128)S(1)} collective-permute-done((f32[2,4096]{1,0:T(2,128)S(1)}, f32[2,4096]{1,0:T(2,128)S(1)}, u32[]{:S(2)}, u32[]{:S(2)}) %collective-permute-start.19) | collective-permute-done | bytes 32800 | tf_op jit(solution)/shard_map/ppermute | solution.py:472
  156.4 1.6 collective-permute-start.21
  159.4 3.0 %collective-permute-start.23 = (f32[2,256]{1,0:T(2,128)S(1)}, f32[2,256]{1,0:T(2,128)S(1)}, u32[]{:S(2)}, u32[]{:S(2)}) collective-permute-start(f32[2,256]{1,0:T(2,128)S(1)} %score_sum.1), channel_id=1, source_target_pairs={{0,8},{4,12},{8,0},{12,4},{1,9},{5,13},{9,1},{13,5},{2,10},{6,14},... | collective-permute-start | bytes 6152 | tf_op jit(solution)/shard_map/ppermute | solution.py:472
  162.4 2.9 %hessian_update.1 = f32[256,4096]{1,0:T(8,128)} custom-call(s32[9]{0:T(128)S(1)} %stack.43.where, f32[8,4096]{1,0:T(8,128)S(1)} %pad_maximum_fusion.grads, f32[256,4096]{1,0:T(8,128)S(1)} %get-tuple-element.83.hessian), custom_call_target="tpu_custom_call" | custom-call | flops 1000 | bytes 1000 | tf_op jit(solution)/shard_map/hessian_update/pallas_call | solution.py:41
  (53 shorter events, 19.1 us)
Async XLA Ops:
  0.6 21.1 %copy-start.1 = (bf16[1024,1024]{1,0:T(8,128)(2,1)S(1)}, bf16[1024,1024]{1,0:T(8,128)(2,1)}, u32[]{:S(2)}) copy-start(bf16[1024,1024]{1,0:T(8,128)(2,1)} %own) | copy-start | bytes 6291460
  0.6 49.9 %collective-permute-start.5 = (bf16[1024,1024]{1,0:T(8,128)(2,1)}, bf16[1024,1024]{1,0:T(8,128)(2,1)}, u32[]{:S(2)}, u32[]{:S(2)}) collective-permute-start(bf16[1024,1024]{1,0:T(8,128)(2,1)} %own), channel_id=1, source_target_pairs={{0,4},{4,0},{8,12},{12,8},{1,5},{5,1},{9,13},{13,9},{2,6},{6,2},{1... | collective-permute-start | bytes 6291464 | tf_op jit(solution)/shard_map/ppermute | solution.py:418
  6.8 27.0 %collective-permute-start = (bf16[512,1024]{1,0:T(8,128)(2,1)}, bf16[512,1024]{1,0:T(8,128)(2,1)S(1)}, u32[]{:S(2)}, u32[]{:S(2)}) collective-permute-start(bf16[512,1024]{1,0:T(8,128)(2,1)} %get-tuple-element.89), channel_id=1, source_target_pairs={{4,8},{8,4},{5,9},{9,5},{6,10},{10,6},{7,11},{11,7},{20,24},{24,20... | collective-permute-start | bytes 3145736 | tf_op jit(solution)/shard_map/ppermute | solution.py:420
  7.5 5.8 %collective-permute-start.2 = (f32[256,256]{1,0:T(8,128)}, f32[256,256]{1,0:T(8,128)S(1)}, u32[]{:S(2)}, u32[]{:S(2)}) collective-permute-start(f32[256,256]{1,0:T(8,128)} %rest_0_.1), channel_id=1, source_target_pairs={{0,1},{1,0},{2,3},{3,2},{4,5},{5,4},{6,7},{7,6},{8,9},{9,8},{10,11... | collective-permute-start | bytes 786440 | tf_op jit(solution)/shard_map/ppermute | solution.py:472
  7.6 9.5 %collective-permute-start.3 = (f32[256,256]{1,0:T(8,128)}, f32[256,256]{1,0:T(8,128)}, u32[]{:S(2)}, u32[]{:S(2)}) collective-permute-start(f32[256,256]{1,0:T(8,128)} %rest_0_.1), channel_id=1, source_target_pairs={{0,2},{1,3},{2,0},{3,1},{4,6},{5,7},{6,4},{7,5},{8,10},{9,11},{10,... | collective-permute-start | bytes 786440 | tf_op jit(solution)/shard_map/ppermute | solution.py:472
  9.1 12.6 %collective-permute-start.4 = (f32[256,256]{1,0:T(8,128)}, f32[256,256]{1,0:T(8,128)}, u32[]{:S(2)}, u32[]{:S(2)}) collective-permute-start(f32[256,256]{1,0:T(8,128)} %rest_0_.1), channel_id=1, source_target_pairs={{0,3},{1,2},{2,1},{3,0},{4,7},{5,6},{6,5},{7,4},{8,11},{9,10},{10,... | collective-permute-start | bytes 786440 | tf_op jit(solution)/shard_map/ppermute | solution.py:472
  9.5 1.6 copy-start.2
  11.1 0.9 copy-start.3
  13.3 20.5 %copy-start.4 = (f32[256,256]{1,0:T(8,128)}, f32[256,256]{1,0:T(8,128)S(1)}, u32[]{:S(2)}) copy-start(f32[256,256]{1,0:T(8,128)S(1)} %collective-permute-done.2.rest_1_) | copy-start | bytes 786436
  13.3 45.5 %collective-permute-start.11 = (bf16[512,1024]{1,0:T(8,128)(2,1)}, bf16[512,1024]{1,0:T(8,128)(2,1)S(1)}, u32[]{:S(2)}, u32[]{:S(2)}) collective-permute-start(bf16[512,1024]{1,0:T(8,128)(2,1)} %get-tuple-element.88), channel_id=1, source_target_pairs={{4,8},{8,4},{5,9},{9,5},{6,10},{10,6},{7,11},{11,7},{20,24},{24,20... | collective-permute-start | bytes 3145736 | tf_op jit(solution)/shard_map/ppermute | solution.py:420
  33.8 39.1 %collective-permute-start.9 = (bf16[512,1024]{1,0:T(8,128)(2,1)S(1)}, bf16[512,1024]{1,0:T(8,128)(2,1)S(1)}, u32[]{:S(2)}, u32[]{:S(2)}) collective-permute-start(bf16[512,1024]{1,0:T(8,128)(2,1)S(1)} %collective-permute-done.refs_0_), channel_id=1, source_target_pairs={{4,0},{8,12},{5,1},{9,13},{6,2},{10,14},{7,3},{11,15},{20,16},{24,... | collective-permute-start | bytes 3145736 | tf_op jit(solution)/shard_map/ppermute | solution.py:424
  52.2 35.5 %collective-permute-start.8 = (bf16[512,1024]{1,0:T(8,128)(2,1)S(1)}, bf16[512,1024]{1,0:T(8,128)(2,1)S(1)}, u32[]{:S(2)}, u32[]{:S(2)}) collective-permute-start(bf16[512,1024]{1,0:T(8,128)(2,1)S(1)} %get-tuple-element.87), channel_id=1, source_target_pairs={{4,8},{8,4},{5,9},{9,5},{6,10},{10,6},{7,11},{11,7},{20,24},{24,20... | collective-permute-start | bytes 3145736 | tf_op jit(solution)/shard_map/ppermute | solution.py:426
  53.0 10.0 %collective-permute-start.1 = (f32[64,1024]{1,0:T(8,128)S(1)}, f32[64,1024]{1,0:T(8,128)S(1)}, u32[]{:S(2)}, u32[]{:S(2)}) collective-permute-start(f32[64,1024]{1,0:T(8,128)S(1)} %input_block.1.a), channel_id=1, source_target_pairs={{0,4},{12,8},{1,5},{13,9},{2,6},{14,10},{3,7},{15,11},{16,20},{28,... | collective-permute-start | bytes 786440 | tf_op jit(solution)/shard_map/ppermute | solution.py:422
  58.8 36.5 %collective-permute-start.12 = (bf16[512,1024]{1,0:T(8,128)(2,1)S(1)}, bf16[512,1024]{1,0:T(8,128)(2,1)S(1)}, u32[]{:S(2)}, u32[]{:S(2)}) collective-permute-start(bf16[512,1024]{1,0:T(8,128)(2,1)S(1)} %collective-permute-done.11.refs_1_), channel_id=1, source_target_pairs={{4,0},{8,12},{5,1},{9,13},{6,2},{10,14},{7,3},{11,15},{20,16},{24,... | collective-permute-start | bytes 3145736 | tf_op jit(solution)/shard_map/ppermute | solution.py:424
  72.9 14.3 %collective-permute-start.6 = (f32[64,1024]{1,0:T(8,128)S(1)}, f32[64,1024]{1,0:T(8,128)S(1)}, u32[]{:S(2)}, u32[]{:S(2)}) collective-permute-start(f32[64,1024]{1,0:T(8,128)S(1)} %side.1.a), channel_id=1, source_target_pairs={{4,8},{8,4},{5,9},{9,5},{6,10},{10,6},{7,11},{11,7},{20,24},{24,20... | collective-permute-start | bytes 786440 | tf_op jit(solution)/shard_map/ppermute | solution.py:428
  73.5 34.1 %collective-permute-start.14 = (bf16[512,1024]{1,0:T(8,128)(2,1)S(1)}, bf16[512,1024]{1,0:T(8,128)(2,1)S(1)}, u32[]{:S(2)}, u32[]{:S(2)}) collective-permute-start(bf16[512,1024]{1,0:T(8,128)(2,1)S(1)} %get-tuple-element.63), channel_id=1, source_target_pairs={{4,8},{8,4},{5,9},{9,5},{6,10},{10,6},{7,11},{11,7},{20,24},{24,20... | collective-permute-start | bytes 3145736 | tf_op jit(solution)/shard_map/ppermute | solution.py:427
  87.8 19.8 %collective-permute-start.10 = (bf16[256,1024]{1,0:T(8,128)(2,1)S(1)}, bf16[256,1024]{1,0:T(8,128)(2,1)S(1)}, u32[]{:S(2)}, u32[]{:S(2)}) collective-permute-start(bf16[256,1024]{1,0:T(8,128)(2,1)S(1)} %get-tuple-element.52), channel_id=1, source_target_pairs={{4,0},{8,12},{5,1},{9,13},{6,2},{10,14},{7,3},{11,15},{20,16},{24,... | collective-permute-start | bytes 1572872 | tf_op jit(solution)/shard_map/ppermute | solution.py:441
  89.1 29.2 %collective-permute-start.13 = (bf16[256,1024]{1,0:T(8,128)(2,1)S(1)}, bf16[256,1024]{1,0:T(8,128)(2,1)S(1)}, u32[]{:S(2)}, u32[]{:S(2)}) collective-permute-start(bf16[256,1024]{1,0:T(8,128)(2,1)S(1)} %get-tuple-element.59), channel_id=1, source_target_pairs={{4,0},{8,12},{5,1},{9,13},{6,2},{10,14},{7,3},{11,15},{20,16},{24,... | collective-permute-start | bytes 1572872 | tf_op jit(solution)/shard_map/ppermute | solution.py:441
  95.3 13.7 %copy-start = (bf16[3584,64]{0,1:T(8,128)(2,1)S(1)}, bf16[3584,64]{0,1:T(8,128)(2,1)}, u32[]{:S(2)}) copy-start(bf16[3584,64]{0,1:T(8,128)(2,1)} %param.13) | copy-start | bytes 1376260
  107.7 21.9 %collective-permute-start.15 = (bf16[256,1024]{1,0:T(8,128)(2,1)S(1)}, bf16[256,1024]{1,0:T(8,128)(2,1)S(1)}, u32[]{:S(2)}, u32[]{:S(2)}) collective-permute-start(bf16[256,1024]{1,0:T(8,128)(2,1)S(1)} %slice.40), channel_id=1, source_target_pairs={{4,0},{8,12},{5,1},{9,13},{6,2},{10,14},{7,3},{11,15},{20,16},{24,... | collective-permute-start | bytes 1572872 | tf_op jit(solution)/shard_map/ppermute | solution.py:441
  118.3 16.9 %collective-permute-start.16 = (bf16[128,1024]{1,0:T(8,128)(2,1)S(1)}, bf16[128,1024]{1,0:T(8,128)(2,1)S(1)}, u32[]{:S(2)}, u32[]{:S(2)}) collective-permute-start(bf16[128,1024]{1,0:T(8,128)(2,1)S(1)} %get-tuple-element.68), channel_id=1, source_target_pairs={{4,0},{8,12},{5,1},{9,13},{6,2},{10,14},{7,3},{11,15},{20,16},{24,... | collective-permute-start | bytes 786440 | tf_op jit(solution)/shard_map/ppermute | solution.py:441
  125.4 16.3 %collective-permute-start.17 = (bf16[128,1024]{1,0:T(8,128)(2,1)S(1)}, bf16[128,1024]{1,0:T(8,128)(2,1)S(1)}, u32[]{:S(2)}, u32[]{:S(2)}) collective-permute-start(bf16[128,1024]{1,0:T(8,128)(2,1)S(1)} %get-tuple-element.72), channel_id=1, source_target_pairs={{4,0},{8,12},{5,1},{9,13},{6,2},{10,14},{7,3},{11,15},{20,16},{24,... | collective-permute-start | bytes 786440 | tf_op jit(solution)/shard_map/ppermute | solution.py:441
  126.7 17.4 %collective-permute-start.7 = (bf16[64,1024]{1,0:T(8,128)(2,1)S(1)}, bf16[64,1024]{1,0:T(8,128)(2,1)S(1)}, u32[]{:S(2)}, u32[]{:S(2)}) collective-permute-start(bf16[64,1024]{1,0:T(8,128)(2,1)S(1)} %convert_element_type.4), channel_id=1, source_target_pairs={{4,0},{8,12},{5,1},{9,13},{6,2},{10,14},{7,3},{11,15},{20,16},{24,... | collective-permute-start | bytes 393224 | tf_op jit(solution)/shard_map/ppermute | solution.py:429
  145.2 4.0 %collective-permute-start.18 = (f32[2,4096]{1,0:T(2,128)S(1)}, f32[2,4096]{1,0:T(2,128)S(1)}, u32[]{:S(2)}, u32[]{:S(2)}) collective-permute-start(f32[2,4096]{1,0:T(2,128)S(1)} %outer_products.1), channel_id=1, source_target_pairs={{0,4},{4,0},{8,12},{12,8},{1,5},{5,1},{9,13},{13,9},{2,6},{6,2},{1... | collective-permute-start | bytes 98312 | tf_op jit(solution)/shard_map/ppermute | solution.py:472
  149.2 5.1 %collective-permute-start.19 = (f32[2,4096]{1,0:T(2,128)S(1)}, f32[2,4096]{1,0:T(2,128)S(1)}, u32[]{:S(2)}, u32[]{:S(2)}) collective-permute-start(f32[2,4096]{1,0:T(2,128)S(1)} %add.34), channel_id=1, source_target_pairs={{0,8},{4,12},{8,0},{12,4},{1,9},{5,13},{9,1},{13,5},{2,10},{6,14},... | collective-permute-start | bytes 98312 | tf_op jit(solution)/shard_map/ppermute | solution.py:472
  155.1 1.2 collective-permute-start.20
  155.2 3.7 %collective-permute-start.22 = (f32[2,256]{1,0:T(2,128)S(1)}, f32[2,256]{1,0:T(2,128)S(1)}, u32[]{:S(2)}, u32[]{:S(2)}) collective-permute-start(f32[2,256]{1,0:T(2,128)S(1)} %scores.1.a), channel_id=1, source_target_pairs={{0,4},{4,0},{8,12},{12,8},{1,5},{5,1},{9,13},{13,9},{2,6},{6,2},{1... | collective-permute-start | bytes 6152 | tf_op jit(solution)/shard_map/ppermute | solution.py:472
  156.4 6.0 %collective-permute-start.21 = (f32[4,4096]{1,0:T(4,128)S(1)}, f32[4,4096]{1,0:T(4,128)S(1)}, u32[]{:S(2)}, u32[]{:S(2)}) collective-permute-start(f32[4,4096]{1,0:T(4,128)S(1)} %pad_maximum_fusion.1), channel_id=1, source_target_pairs={{0,2},{1,3},{2,0},{3,1},{4,6},{5,7},{6,4},{7,5},{8,10},{9,11},{10,... | collective-permute-start | bytes 196616 | tf_op jit(solution)/shard_map/ppermute | solution.py:472
  159.4 5.9 %collective-permute-start.23 = (f32[2,256]{1,0:T(2,128)S(1)}, f32[2,256]{1,0:T(2,128)S(1)}, u32[]{:S(2)}, u32[]{:S(2)}) collective-permute-start(f32[2,256]{1,0:T(2,128)S(1)} %score_sum.1), channel_id=1, source_target_pairs={{0,8},{4,12},{8,0},{12,4},{1,9},{5,13},{9,1},{13,5},{2,10},{6,14},... | collective-permute-start | bytes 6152 | tf_op jit(solution)/shard_map/ppermute | solution.py:472

commit v15 on v14

--- a/solution.py
+++ b/solution.py
@@ -228,8 +228,17 @@
     )
 
 
-def final_body(start, inner_at, where, inner, outer, kept, old, gate, po, right):
+def near_body(start, inner_at, bring, where, inner, outer, kept, old, gate, po, *rest):
+    far, rest = rest[: len(bring)], rest[len(bring) :]
+    _, _, right, *near = rest[: 3 + len(bring)]
+    near_sems = rest[-1]
     size = outer.shape[0]
+    brought = [
+        pltpu.make_async_copy(a.at[pl.ds(first, b.shape[0])], b, near_sems.at[i])
+        for i, (a, b, first) in enumerate(zip(far, near, bring))
+    ]
+    for copy in brought:
+        copy.start()
     block = select(where, inner.at[pl.ds(inner_at, size)], outer)
     total = jnp.zeros((size, PROJ), jnp.float32)
     for t in range(kept.shape[1] // TILE):
@@ -238,22 +247,29 @@
         up_grad = (hidden_grad * silu(gate[:, span].astype(jnp.float32))).astype(jnp.bfloat16)
         total = total + dot_nt(up_grad, po[:, span])
     right[...] = total
-
-
-def final_block(where, inner, inner_at, outer, start, kept, old, gate, po):
-    (right,) = call(
-        functools.partial(final_body, start, inner_at),
-        "final_block",
-        where,
-        (1,),
-        (inner, outer, kept, old, gate, po),
-        [INSIDE] * 6,
-        [INSIDE],
-        [pltpu.VMEM((outer.shape[0], PROJ), jnp.float32)],
-        [],
-        LIMIT,
-    )
-    return right
+    for copy in brought:
+        copy.wait()
+
+
+def near_block(where, inner, inner_at, outer, start, kept, old, gate, po, bring):
+    return call(
+        functools.partial(near_body, start, inner_at, [first for _, first, _ in bring]),
+        "near_block",
+        where,
+        (1,),
+        (inner, outer, kept, old, gate, po, *[a for a, _, _ in bring]),
+        [INSIDE] * 6 + [OUTSIDE] * len(bring),
+        [INSIDE] * (3 + len(bring)),
+        [
+            pltpu.VMEM(kept.shape, kept.dtype),
+            pltpu.VMEM(old.shape, old.dtype),
+            pltpu.VMEM((outer.shape[0], PROJ), jnp.float32),
+            *[pltpu.VMEM((rows, a.shape[1]), a.dtype) for a, _, rows in bring],
+        ],
+        [pltpu.SemaphoreType.DMA((max(len(bring), 1),))],
+        LIMIT,
+        aliases={3: 0, 4: 1},
+    )
 
 
 def outer_body(where, total, sent, *refs):
@@ -440,18 +456,23 @@
         ahead = arrived[n + 1] if n < 4 else arrived[n]
         end_outer = send(after(end_inner[h][at : at + size], ahead, done[n]), perm=outward)
         arrived.append(end_outer)
-        if n == len(sizes) - 1:
-            rights.append(final_block(where, end_inner[h], at, end_outer, start, kept, acc, gate_near, po_near))
-            break
         bring = []
-        if n == len(sizes) - 2:
-            bring = [(a, 0, a.shape[0]) for a in (*early, late, proj_out.T)]
-            bring.append((gate_pre, start + size, tokens - start - size))
-        kept, acc, right, *brought = last_block(
-            where, end_inner[h], at, end_outer, start, kept, acc, gate_pre, proj_out.T, second, bring
-        )
+        if n + 1 < len(sizes):
+            bring.append((gate_pre, start + size, sizes[n + 1]))
+        if n == 0:
+            bring.append((proj_out.T, 0, PROJ))
+        if n == len(sizes) - 3:
+            bring += [(a, 0, a.shape[0]) for a in (*early, late)]
+        place = where, end_inner[h], at, end_outer, start, kept, acc
+        if n == 0:
+            kept, acc, right, *brought = last_block(*place, gate_pre, proj_out.T, second, bring)
+            po_near = brought[1]
+        else:
+            kept, acc, right, *brought = near_block(*place, gate_near, po_near, bring)
+        if n == len(sizes) - 3:
+            *early, late = brought[1:]
         if bring:
-            *early, late, po_near, gate_near = brought
+            gate_near = brought[0]
         rights.append(right)
         done.append(right)
         start += size

time: 167 us -> 165 us (0.988)
  waiting for transfers between devices: 51.4 us -> 56.5 us
  Pallas kernels: 70.4 us -> 66.1 us
  starting transfers between devices: 34.9 us -> 32.3 us
    pallas_call x15, Pallas kernels: 70.4 us -> 66.1 us  [call(): pl.pallas_call(body, grid_spec=pltpu.PrefetchScalarGridSpec(num_scalar_pr...]
    ppermute x5, waiting for transfers between devices: 5.42 us -> 8.9 us  [line_of_four(): send(after(end_inner[h][at:at + size], ahead, done[n]), perm=outward)]
    ppermute x9, starting transfers between devices: 11.9 us -> 9.29 us  [swap(): lax.ppermute(a, axis, [(i, i ^ bit) for i in range(lax.axis_size(axis))])]
  transfers between devices with their start and end apart: 24 -> 24, of which waited for: 13 -> 12; matrix products, arithmetic and copies ran while one was open for 3% -> 3% of each run, Pallas kernels for 41% -> 39%
where the time goes in v15:
time: 165 us; the launch traced here: 164 us
  Pallas kernels  66.1 us (40%)
  waiting for transfers between devices  56.5 us (34%)
  starting transfers between devices  32.3 us (20%)
  local copies, waits for them, and re-layouts  7.48 us (5%)
    pallas_call x15, Pallas kernels, call(): pl.pallas_call(body, grid_spec=pltpu.PrefetchScalarGridSpec(num_scalar_pr...  66.1 us
    ppermute x1, waiting for transfers between devices, line_of_four(): pair = send(grad_out, perm=pairs)  15.4 us
    ppermute x9, waiting for transfers between devices, swap(): lax.ppermute(a, axis, [(i, i ^ bit) for i in range(lax.axis_size(axis))])  15.1 us
    ppermute x2, waiting for transfers between devices, line_of_four(): mid_outer = [send(after(a, begun), perm=outward) for a in mid_inner]  14.3 us
    ppermute x9, starting transfers between devices, swap(): lax.ppermute(a, axis, [(i, i ^ bit) for i in range(lax.axis_size(axis))])  9.29 us
    ppermute x5, waiting for transfers between devices, line_of_four(): send(after(end_inner[h][at:at + size], ahead, done[n]), perm=outward)  8.9 us
    ppermute x5, starting transfers between devices, line_of_four(): send(after(end_inner[h][at:at + size], ahead, done[n]), perm=outward)  6.63 us
    ppermute x1, starting transfers between devices, line_of_four(): from_end = send(after(in_part, mid_inner[0]), perm=inward)  5.83 us
  transfers between devices with their start and end apart: 24, of which 12 were waited for; matrix products, arithmetic and copies ran while one was open for 3% of the time, Pallas kernels for 39%

profile of v15, /device:TPU:0, one launch (start us, length us, event | category | flops | bytes accessed | tf_op | source)
XLA Modules:
  0.0 164.1 jit_solution(14654673284713081858)
XLA Ops:
  0.6 3.1 %collective-permute-start.5 = (bf16[1024,1024]{1,0:T(8,128)(2,1)}, bf16[1024,1024]{1,0:T(8,128)(2,1)}, u32[]{:S(2)}, u32[]{:S(2)}) collective-permute-start(bf16[1024,1024]{1,0:T(8,128)(2,1)} %own), channel_id=1, source_target_pairs={{0,4},{4,0},{8,12},{12,8},{1,5},{5,1},{9,13},{13,9},{2,6},{6,2},{1... | collective-permute-start | bytes 6291464 | tf_op jit(solution)/shard_map/ppermute | solution.py:434
  3.7 3.0 %fusion.1 = (bf16[512,1024]{1,0:T(8,128)(2,1)}, bf16[512,1024]{1,0:T(8,128)(2,1)}) fusion(bf16[1024,1024]{1,0:T(8,128)(2,1)} %own), kind=kLoop, calls=%fused_computation.3 | loop fusion | bytes 4194304 | tf_op jit(solution)/shard_map/slice | solution.py:435
  7.6 1.6 collective-permute-start.3
  9.5 1.6 copy-done.1
  12.0 1.3 input_block.1.a
  14.1 3.0 %collective-permute-done.3.rest_3_ = f32[256,256]{1,0:T(8,128)} collective-permute-done((f32[256,256]{1,0:T(8,128)}, f32[256,256]{1,0:T(8,128)}, u32[]{:S(2)}, u32[]{:S(2)}) %collective-permute-start.3) | collective-permute-done | bytes 262176 | tf_op jit(solution)/shard_map/ppermute | solution.py:493
  17.1 4.7 %collective-permute-done.4.rest_4_ = f32[256,256]{1,0:T(8,128)} collective-permute-done((f32[256,256]{1,0:T(8,128)}, f32[256,256]{1,0:T(8,128)}, u32[]{:S(2)}, u32[]{:S(2)}) %collective-permute-start.4) | collective-permute-done | bytes 262176 | tf_op jit(solution)/shard_map/ppermute | solution.py:493
  21.8 12.0 %own_block.1 = (f32[1024,3584]{1,0:T(8,128)S(1)}, bf16[1024,3584]{1,0:T(8,128)(2,1)S(1)}, f32[8,128]{1,0:T(8,128)S(1)}) custom-call(s32[9]{0:T(128)S(1)} %stack.43.where, bf16[1024,1024]{1,0:T(8,128)(2,1)S(1)} %copy-done, bf16[3584,4096]{1,0:T(8,128)(2,1)} %refs_4_.1, bf16[3584,4096]{1,0:T(8,128)(2,1)} %refs_4_.1), custom_call_target="tpu_custom_call" | custom-call | flops 1000 | bytes 1000 | tf_op jit(solution)/shard_map/own_block/pallas_call | solution.py:41
  33.8 1.3 collective-permute-start.9
  35.1 15.4 %collective-permute-done.5.refs_0_ = bf16[1024,1024]{1,0:T(8,128)(2,1)} collective-permute-done((bf16[1024,1024]{1,0:T(8,128)(2,1)}, bf16[1024,1024]{1,0:T(8,128)(2,1)}, u32[]{:S(2)}, u32[]{:S(2)}) %collective-permute-start.5) | collective-permute-done | bytes 2097184 | tf_op jit(solution)/shard_map/ppermute | solution.py:434
  50.5 1.7 %fusion = (bf16[512,1024]{1,0:T(8,128)(2,1)S(1)}, bf16[512,1024]{1,0:T(8,128)(2,1)S(1)}) fusion(bf16[1024,1024]{1,0:T(8,128)(2,1)} %collective-permute-done.5.refs_0_), kind=kLoop, calls=%fused_computation.2 | loop fusion | bytes 4194304 | tf_op jit(solution)/shard_map/slice | solution.py:443
  53.0 5.8 %collective-permute-start.1 = (f32[64,1024]{1,0:T(8,128)S(1)}, f32[64,1024]{1,0:T(8,128)S(1)}, u32[]{:S(2)}, u32[]{:S(2)}) collective-permute-start(f32[64,1024]{1,0:T(8,128)S(1)} %input_block.1.a), channel_id=1, source_target_pairs={{0,4},{12,8},{1,5},{13,9},{2,6},{14,10},{3,7},{15,11},{16,20},{28,... | collective-permute-start | bytes 786440 | tf_op jit(solution)/shard_map/ppermute | solution.py:438
  60.1 2.8 %collective-permute-done.1.b = f32[64,1024]{1,0:T(8,128)S(1)} collective-permute-done((f32[64,1024]{1,0:T(8,128)S(1)}, f32[64,1024]{1,0:T(8,128)S(1)}, u32[]{:S(2)}, u32[]{:S(2)}) %collective-permute-start.1) | collective-permute-done | bytes 262176 | tf_op jit(solution)/shard_map/ppermute | solution.py:438
  63.5 9.4 %collective-permute-done.9.refs_2_ = bf16[512,1024]{1,0:T(8,128)(2,1)S(1)} collective-permute-done((bf16[512,1024]{1,0:T(8,128)(2,1)S(1)}, bf16[512,1024]{1,0:T(8,128)(2,1)S(1)}, u32[]{:S(2)}, u32[]{:S(2)}) %collective-permute-start.9) | collective-permute-done | bytes 1048608 | tf_op jit(solution)/shard_map/ppermute | solution.py:440
  74.3 12.9 %add_block_1.1 = (f32[1024,3584]{1,0:T(8,128)S(1)}, f32[8,128]{1,0:T(8,128)S(1)}) custom-call(s32[9]{0:T(128)S(1)} %stack.43.where, bf16[1024,1024]{1,0:T(8,128)(2,1)} %collective-permute-done.5.refs_0_, bf16[3584,4096]{1,0:T(8,128)(2,1)} %refs_4_.1, f32[1024,3584]{1,0:T(8,128)S(1)} %get-tuple-element.54.refs_2_, ...), custom_call_target="tpu_custom_call", output_to_operand_aliasing={{0}: (3, {})} | custom-call | flops 7516192768 | bytes 1000 | tf_op jit(solution)/shard_map/add_block_1/pallas_call | solution.py:41
  90.5 4.9 %collective-permute-done.12.refs_3_ = bf16[512,1024]{1,0:T(8,128)(2,1)S(1)} collective-permute-done((bf16[512,1024]{1,0:T(8,128)(2,1)S(1)}, bf16[512,1024]{1,0:T(8,128)(2,1)S(1)}, u32[]{:S(2)}, u32[]{:S(2)}) %collective-permute-start.12) | collective-permute-done | bytes 1048608 | tf_op jit(solution)/shard_map/ppermute | solution.py:440
  95.3 12.3 %add_block_2.1 = (f32[1024,3584]{1,0:T(8,128)S(1)}, f32[8,128]{1,0:T(8,128)S(1)}) custom-call(s32[9]{0:T(128)S(1)} %stack.43.where, bf16[512,1024]{1,0:T(8,128)(2,1)S(1)} %collective-permute-done.refs_0_, bf16[512,1024]{1,0:T(8,128)(2,1)S(1)} %collective-permute-done.11.refs_1_, ...), custom_call_target="tpu_custom_call", output_to_operand_aliasing={{0}: (6, {})} | custom-call | flops 1000 | bytes 1000 | tf_op jit(solution)/shard_map/add_block_2/pallas_call | solution.py:41
  109.0 6.7 %last_block.1 = (bf16[1024,3584]{1,0:T(8,128)(2,1)S(1)}, f32[1024,3584]{1,0:T(8,128)S(1)}, f32[256,64]{1,0:T(8,128)S(1)}, bf16[256,3584]{1,0:T(8,128)(2,1)S(1)}, bf16[64,3584]{1,0:T(8,128)(2,1)S(1)}) custom-call(s32[9]{0:T(128)S(1)} %stack.43.where, ...), custom_call_target="tpu_custom_call", output_to_operand_aliasing={{0}: (3, {}), {1}: (4, {})} | custom-call | flops 1000 | bytes 1000 | tf_op jit(solution)/shard_map/last_block/pallas_call | solution.py:41
  115.7 2.6 %collective-permute-done.13.outer = bf16[256,1024]{1,0:T(8,128)(2,1)S(1)} collective-permute-done((bf16[256,1024]{1,0:T(8,128)(2,1)S(1)}, bf16[256,1024]{1,0:T(8,128)(2,1)S(1)}, u32[]{:S(2)}, u32[]{:S(2)}) %collective-permute-start.13) | collective-permute-done | bytes 524320 | tf_op jit(solution)/shard_map/ppermute | solution.py:457
  118.4 1.5 collective-permute-start.16
  119.8 3.8 %near_block.4 = (bf16[1024,3584]{1,0:T(8,128)(2,1)S(1)}, f32[1024,3584]{1,0:T(8,128)S(1)}, f32[256,64]{1,0:T(8,128)S(1)}, bf16[256,3584]{1,0:T(8,128)(2,1)S(1)}) custom-call(s32[9]{0:T(128)S(1)} %stack.43.where, bf16[512,1024]{1,0:T(8,128)(2,1)S(1)} %collective-permute-done.8.inner, ...), custom_call_target="tpu_custom_call", output_to_operand_aliasing={{0}: (3, {}), {1}: (4, {})} | custom-call | flops 1000 | bytes 1000 | tf_op jit(solution)/shard_map/near_block/pallas_call | solution.py:41
  126.3 3.3 %collective-permute-done.15.outer = bf16[256,1024]{1,0:T(8,128)(2,1)S(1)} collective-permute-done((bf16[256,1024]{1,0:T(8,128)(2,1)S(1)}, bf16[256,1024]{1,0:T(8,128)(2,1)S(1)}, u32[]{:S(2)}, u32[]{:S(2)}) %collective-permute-start.15) | collective-permute-done | bytes 524320 | tf_op jit(solution)/shard_map/ppermute | solution.py:457
  129.6 5.8 %near_block.5 = (bf16[1024,3584]{1,0:T(8,128)(2,1)S(1)}, f32[1024,3584]{1,0:T(8,128)S(1)}, f32[256,64]{1,0:T(8,128)S(1)}, bf16[128,3584]{1,0:T(8,128)(2,1)S(1)},...) custom-call(s32[9]{0:T(128)S(1)} %stack.43.where, ...), custom_call_target="tpu_custom_call", output_to_operand_aliasing={{0}: (3, {}), {1}: (4, {})} | custom-call | flops 1000 | bytes 1000 | tf_op jit(solution)/shard_map/near_block/pallas_call | solution.py:41
  135.4 2.5 %near_block.6 = (bf16[1024,3584]{1,0:T(8,128)(2,1)S(1)}, f32[1024,3584]{1,0:T(8,128)S(1)}, f32[128,64]{1,0:T(8,128)S(1)}, bf16[128,3584]{1,0:T(8,128)(2,1)S(1)}) custom-call(s32[9]{0:T(128)S(1)} %stack.43.where, bf16[512,1024]{1,0:T(8,128)(2,1)S(1)} %collective-permute-done.14.inner, ...), custom_call_target="tpu_custom_call", output_to_operand_aliasing={{0}: (3, {}), {1}: (4, {})} | custom-call | flops 1000 | bytes 1000 | tf_op jit(solution)/shard_map/near_block/pallas_call | solution.py:41
  137.9 2.9 %collective-permute-done.17.outer = bf16[128,1024]{1,0:T(8,128)(2,1)S(1)} collective-permute-done((bf16[128,1024]{1,0:T(8,128)(2,1)S(1)}, bf16[128,1024]{1,0:T(8,128)(2,1)S(1)}, u32[]{:S(2)}, u32[]{:S(2)}) %collective-permute-start.17) | collective-permute-done | bytes 262176 | tf_op jit(solution)/shard_map/ppermute | solution.py:457
  140.8 2.5 %near_block.7 = (bf16[1024,3584]{1,0:T(8,128)(2,1)S(1)}, f32[1024,3584]{1,0:T(8,128)S(1)}, f32[128,64]{1,0:T(8,128)S(1)}) custom-call(s32[9]{0:T(128)S(1)} %stack.43.where, bf16[512,1024]{1,0:T(8,128)(2,1)S(1)} %collective-permute-done.14.inner, bf16[128,1024]{1,0:T(8,128)(2,1)S(1)} %collective-permute-done.17.outer, ...), custom_call_target="tpu_custom_call", output_to_operand_aliasing={{0}: (3, {}), {1}: (4, {})} | custom-call | flops 1000 | bytes 1000 | tf_op jit(solution)/shard_map/near_block/pallas_call | solution.py:41
  144.5 3.9 %collective-permute-done.18 = f32[2,4096]{1,0:T(2,128)S(1)} collective-permute-done((f32[2,4096]{1,0:T(2,128)S(1)}, f32[2,4096]{1,0:T(2,128)S(1)}, u32[]{:S(2)}, u32[]{:S(2)}) %collective-permute-start.18) | collective-permute-done | bytes 32800 | tf_op jit(solution)/shard_map/ppermute | solution.py:493
  148.4 2.2 %collective-permute-start.19 = (f32[2,4096]{1,0:T(2,128)S(1)}, f32[2,4096]{1,0:T(2,128)S(1)}, u32[]{:S(2)}, u32[]{:S(2)}) collective-permute-start(f32[2,4096]{1,0:T(2,128)S(1)} %add.34), channel_id=1, source_target_pairs={{0,8},{4,12},{8,0},{12,4},{1,9},{5,13},{9,1},{13,5},{2,10},{6,14},... | collective-permute-start | bytes 98312 | tf_op jit(solution)/shard_map/ppermute | solution.py:493
  150.6 2.7 %collective-permute-done.19 = f32[2,4096]{1,0:T(2,128)S(1)} collective-permute-done((f32[2,4096]{1,0:T(2,128)S(1)}, f32[2,4096]{1,0:T(2,128)S(1)}, u32[]{:S(2)}, u32[]{:S(2)}) %collective-permute-start.19) | collective-permute-done | bytes 32800 | tf_op jit(solution)/shard_map/ppermute | solution.py:493
  155.4 1.6 collective-permute-start.21
  158.4 2.2 %collective-permute-start.23 = (f32[2,256]{1,0:T(2,128)S(1)}, f32[2,256]{1,0:T(2,128)S(1)}, u32[]{:S(2)}, u32[]{:S(2)}) collective-permute-start(f32[2,256]{1,0:T(2,128)S(1)} %score_sum.1), channel_id=1, source_target_pairs={{0,8},{4,12},{8,0},{12,4},{1,9},{5,13},{9,1},{13,5},{2,10},{6,14},... | collective-permute-start | bytes 6152 | tf_op jit(solution)/shard_map/ppermute | solution.py:493
  160.6 2.9 %hessian_update.1 = f32[256,4096]{1,0:T(8,128)} custom-call(s32[9]{0:T(128)S(1)} %stack.43.where, f32[8,4096]{1,0:T(8,128)S(1)} %pad_maximum_fusion.grads, f32[256,4096]{1,0:T(8,128)S(1)} %get-tuple-element.91.hessian), custom_call_target="tpu_custom_call" | custom-call | flops 1000 | bytes 1000 | tf_op jit(solution)/shard_map/hessian_update/pallas_call | solution.py:41
  (51 shorter events, 19.3 us)
Async XLA Ops:
  0.6 21.1 %copy-start = (bf16[1024,1024]{1,0:T(8,128)(2,1)S(1)}, bf16[1024,1024]{1,0:T(8,128)(2,1)}, u32[]{:S(2)}) copy-start(bf16[1024,1024]{1,0:T(8,128)(2,1)} %own) | copy-start | bytes 6291460
  0.6 49.9 %collective-permute-start.5 = (bf16[1024,1024]{1,0:T(8,128)(2,1)}, bf16[1024,1024]{1,0:T(8,128)(2,1)}, u32[]{:S(2)}, u32[]{:S(2)}) collective-permute-start(bf16[1024,1024]{1,0:T(8,128)(2,1)} %own), channel_id=1, source_target_pairs={{0,4},{4,0},{8,12},{12,8},{1,5},{5,1},{9,13},{13,9},{2,6},{6,2},{1... | collective-permute-start | bytes 6291464 | tf_op jit(solution)/shard_map/ppermute | solution.py:434
  6.8 27.0 %collective-permute-start = (bf16[512,1024]{1,0:T(8,128)(2,1)}, bf16[512,1024]{1,0:T(8,128)(2,1)S(1)}, u32[]{:S(2)}, u32[]{:S(2)}) collective-permute-start(bf16[512,1024]{1,0:T(8,128)(2,1)} %get-tuple-element.97), channel_id=1, source_target_pairs={{4,8},{8,4},{5,9},{9,5},{6,10},{10,6},{7,11},{11,7},{20,24},{24,20... | collective-permute-start | bytes 3145736 | tf_op jit(solution)/shard_map/ppermute | solution.py:436
  7.5 5.8 %collective-permute-start.2 = (f32[256,256]{1,0:T(8,128)}, f32[256,256]{1,0:T(8,128)S(1)}, u32[]{:S(2)}, u32[]{:S(2)}) collective-permute-start(f32[256,256]{1,0:T(8,128)} %rest_1_.1), channel_id=1, source_target_pairs={{0,1},{1,0},{2,3},{3,2},{4,5},{5,4},{6,7},{7,6},{8,9},{9,8},{10,11... | collective-permute-start | bytes 786440 | tf_op jit(solution)/shard_map/ppermute | solution.py:493
  7.6 9.5 %collective-permute-start.3 = (f32[256,256]{1,0:T(8,128)}, f32[256,256]{1,0:T(8,128)}, u32[]{:S(2)}, u32[]{:S(2)}) collective-permute-start(f32[256,256]{1,0:T(8,128)} %rest_1_.1), channel_id=1, source_target_pairs={{0,2},{1,3},{2,0},{3,1},{4,6},{5,7},{6,4},{7,5},{8,10},{9,11},{10,... | collective-permute-start | bytes 786440 | tf_op jit(solution)/shard_map/ppermute | solution.py:493
  9.1 12.6 %collective-permute-start.4 = (f32[256,256]{1,0:T(8,128)}, f32[256,256]{1,0:T(8,128)}, u32[]{:S(2)}, u32[]{:S(2)}) collective-permute-start(f32[256,256]{1,0:T(8,128)} %rest_1_.1), channel_id=1, source_target_pairs={{0,3},{1,2},{2,1},{3,0},{4,7},{5,6},{6,5},{7,4},{8,11},{9,10},{10,... | collective-permute-start | bytes 786440 | tf_op jit(solution)/shard_map/ppermute | solution.py:493
  9.5 1.6 copy-start.1
  11.1 0.9 copy-start.2
  13.3 20.5 %copy-start.3 = (f32[256,256]{1,0:T(8,128)}, f32[256,256]{1,0:T(8,128)S(1)}, u32[]{:S(2)}) copy-start(f32[256,256]{1,0:T(8,128)S(1)} %collective-permute-done.2.rest_2_) | copy-start | bytes 786436
  13.3 45.5 %collective-permute-start.11 = (bf16[512,1024]{1,0:T(8,128)(2,1)}, bf16[512,1024]{1,0:T(8,128)(2,1)S(1)}, u32[]{:S(2)}, u32[]{:S(2)}) collective-permute-start(bf16[512,1024]{1,0:T(8,128)(2,1)} %get-tuple-element.96), channel_id=1, source_target_pairs={{4,8},{8,4},{5,9},{9,5},{6,10},{10,6},{7,11},{11,7},{20,24},{24,20... | collective-permute-start | bytes 3145736 | tf_op jit(solution)/shard_map/ppermute | solution.py:436
  33.8 39.1 %collective-permute-start.9 = (bf16[512,1024]{1,0:T(8,128)(2,1)S(1)}, bf16[512,1024]{1,0:T(8,128)(2,1)S(1)}, u32[]{:S(2)}, u32[]{:S(2)}) collective-permute-start(bf16[512,1024]{1,0:T(8,128)(2,1)S(1)} %collective-permute-done.refs_0_), channel_id=1, source_target_pairs={{4,0},{8,12},{5,1},{9,13},{6,2},{10,14},{7,3},{11,15},{20,16},{24,... | collective-permute-start | bytes 3145736 | tf_op jit(solution)/shard_map/ppermute | solution.py:440
  52.2 35.5 %collective-permute-start.8 = (bf16[512,1024]{1,0:T(8,128)(2,1)S(1)}, bf16[512,1024]{1,0:T(8,128)(2,1)S(1)}, u32[]{:S(2)}, u32[]{:S(2)}) collective-permute-start(bf16[512,1024]{1,0:T(8,128)(2,1)S(1)} %get-tuple-element.95), channel_id=1, source_target_pairs={{4,8},{8,4},{5,9},{9,5},{6,10},{10,6},{7,11},{11,7},{20,24},{24,20... | collective-permute-start | bytes 3145736 | tf_op jit(solution)/shard_map/ppermute | solution.py:442
  53.0 10.0 %collective-permute-start.1 = (f32[64,1024]{1,0:T(8,128)S(1)}, f32[64,1024]{1,0:T(8,128)S(1)}, u32[]{:S(2)}, u32[]{:S(2)}) collective-permute-start(f32[64,1024]{1,0:T(8,128)S(1)} %input_block.1.a), channel_id=1, source_target_pairs={{0,4},{12,8},{1,5},{13,9},{2,6},{14,10},{3,7},{15,11},{16,20},{28,... | collective-permute-start | bytes 786440 | tf_op jit(solution)/shard_map/ppermute | solution.py:438
  58.8 36.5 %collective-permute-start.12 = (bf16[512,1024]{1,0:T(8,128)(2,1)S(1)}, bf16[512,1024]{1,0:T(8,128)(2,1)S(1)}, u32[]{:S(2)}, u32[]{:S(2)}) collective-permute-start(bf16[512,1024]{1,0:T(8,128)(2,1)S(1)} %collective-permute-done.11.refs_1_), channel_id=1, source_target_pairs={{4,0},{8,12},{5,1},{9,13},{6,2},{10,14},{7,3},{11,15},{20,16},{24,... | collective-permute-start | bytes 3145736 | tf_op jit(solution)/shard_map/ppermute | solution.py:440
  72.9 14.3 %collective-permute-start.6 = (f32[64,1024]{1,0:T(8,128)S(1)}, f32[64,1024]{1,0:T(8,128)S(1)}, u32[]{:S(2)}, u32[]{:S(2)}) collective-permute-start(f32[64,1024]{1,0:T(8,128)S(1)} %side.1.a), channel_id=1, source_target_pairs={{4,8},{8,4},{5,9},{9,5},{6,10},{10,6},{7,11},{11,7},{20,24},{24,20... | collective-permute-start | bytes 786440 | tf_op jit(solution)/shard_map/ppermute | solution.py:444
  73.5 34.1 %collective-permute-start.14 = (bf16[512,1024]{1,0:T(8,128)(2,1)S(1)}, bf16[512,1024]{1,0:T(8,128)(2,1)S(1)}, u32[]{:S(2)}, u32[]{:S(2)}) collective-permute-start(bf16[512,1024]{1,0:T(8,128)(2,1)S(1)} %get-tuple-element.69), channel_id=1, source_target_pairs={{4,8},{8,4},{5,9},{9,5},{6,10},{10,6},{7,11},{11,7},{20,24},{24,20... | collective-permute-start | bytes 3145736 | tf_op jit(solution)/shard_map/ppermute | solution.py:443
  87.9 19.8 %collective-permute-start.10 = (bf16[256,1024]{1,0:T(8,128)(2,1)S(1)}, bf16[256,1024]{1,0:T(8,128)(2,1)S(1)}, u32[]{:S(2)}, u32[]{:S(2)}) collective-permute-start(bf16[256,1024]{1,0:T(8,128)(2,1)S(1)} %get-tuple-element.56), channel_id=1, source_target_pairs={{4,0},{8,12},{5,1},{9,13},{6,2},{10,14},{7,3},{11,15},{20,16},{24,... | collective-permute-start | bytes 1572872 | tf_op jit(solution)/shard_map/ppermute | solution.py:457
  89.2 29.2 %collective-permute-start.13 = (bf16[256,1024]{1,0:T(8,128)(2,1)S(1)}, bf16[256,1024]{1,0:T(8,128)(2,1)S(1)}, u32[]{:S(2)}, u32[]{:S(2)}) collective-permute-start(bf16[256,1024]{1,0:T(8,128)(2,1)S(1)} %get-tuple-element.63), channel_id=1, source_target_pairs={{4,0},{8,12},{5,1},{9,13},{6,2},{10,14},{7,3},{11,15},{20,16},{24,... | collective-permute-start | bytes 1572872 | tf_op jit(solution)/shard_map/ppermute | solution.py:457
  107.7 21.9 %collective-permute-start.15 = (bf16[256,1024]{1,0:T(8,128)(2,1)S(1)}, bf16[256,1024]{1,0:T(8,128)(2,1)S(1)}, u32[]{:S(2)}, u32[]{:S(2)}) collective-permute-start(bf16[256,1024]{1,0:T(8,128)(2,1)S(1)} %slice.40), channel_id=1, source_target_pairs={{4,0},{8,12},{5,1},{9,13},{6,2},{10,14},{7,3},{11,15},{20,16},{24,... | collective-permute-start | bytes 1572872 | tf_op jit(solution)/shard_map/ppermute | solution.py:457
  118.4 17.0 %collective-permute-start.16 = (bf16[128,1024]{1,0:T(8,128)(2,1)S(1)}, bf16[128,1024]{1,0:T(8,128)(2,1)S(1)}, u32[]{:S(2)}, u32[]{:S(2)}) collective-permute-start(bf16[128,1024]{1,0:T(8,128)(2,1)S(1)} %get-tuple-element.75), channel_id=1, source_target_pairs={{4,0},{8,12},{5,1},{9,13},{6,2},{10,14},{7,3},{11,15},{20,16},{24,... | collective-permute-start | bytes 786440 | tf_op jit(solution)/shard_map/ppermute | solution.py:457
  123.6 17.2 %collective-permute-start.17 = (bf16[128,1024]{1,0:T(8,128)(2,1)S(1)}, bf16[128,1024]{1,0:T(8,128)(2,1)S(1)}, u32[]{:S(2)}, u32[]{:S(2)}) collective-permute-start(bf16[128,1024]{1,0:T(8,128)(2,1)S(1)} %get-tuple-element.80), channel_id=1, source_target_pairs={{4,0},{8,12},{5,1},{9,13},{6,2},{10,14},{7,3},{11,15},{20,16},{24,... | collective-permute-start | bytes 786440 | tf_op jit(solution)/shard_map/ppermute | solution.py:457
  125.0 18.4 %collective-permute-start.7 = (bf16[64,1024]{1,0:T(8,128)(2,1)S(1)}, bf16[64,1024]{1,0:T(8,128)(2,1)S(1)}, u32[]{:S(2)}, u32[]{:S(2)}) collective-permute-start(bf16[64,1024]{1,0:T(8,128)(2,1)S(1)} %convert_element_type.4), channel_id=1, source_target_pairs={{4,0},{8,12},{5,1},{9,13},{6,2},{10,14},{7,3},{11,15},{20,16},{24,... | collective-permute-start | bytes 393224 | tf_op jit(solution)/shard_map/ppermute | solution.py:445
  144.4 4.0 %collective-permute-start.18 = (f32[2,4096]{1,0:T(2,128)S(1)}, f32[2,4096]{1,0:T(2,128)S(1)}, u32[]{:S(2)}, u32[]{:S(2)}) collective-permute-start(f32[2,4096]{1,0:T(2,128)S(1)} %outer_products.1), channel_id=1, source_target_pairs={{0,4},{4,0},{8,12},{12,8},{1,5},{5,1},{9,13},{13,9},{2,6},{6,2},{1... | collective-permute-start | bytes 98312 | tf_op jit(solution)/shard_map/ppermute | solution.py:493
  148.4 4.9 %collective-permute-start.19 = (f32[2,4096]{1,0:T(2,128)S(1)}, f32[2,4096]{1,0:T(2,128)S(1)}, u32[]{:S(2)}, u32[]{:S(2)}) collective-permute-start(f32[2,4096]{1,0:T(2,128)S(1)} %add.34), channel_id=1, source_target_pairs={{0,8},{4,12},{8,0},{12,4},{1,9},{5,13},{9,1},{13,5},{2,10},{6,14},... | collective-permute-start | bytes 98312 | tf_op jit(solution)/shard_map/ppermute | solution.py:493
  154.1 1.3 collective-permute-start.20
  154.2 3.7 %collective-permute-start.22 = (f32[2,256]{1,0:T(2,128)S(1)}, f32[2,256]{1,0:T(2,128)S(1)}, u32[]{:S(2)}, u32[]{:S(2)}) collective-permute-start(f32[2,256]{1,0:T(2,128)S(1)} %scores.1.a), channel_id=1, source_target_pairs={{0,4},{4,0},{8,12},{12,8},{1,5},{5,1},{9,13},{13,9},{2,6},{6,2},{1... | collective-permute-start | bytes 6152 | tf_op jit(solution)/shard_map/ppermute | solution.py:493
  155.4 5.1 %collective-permute-start.21 = (f32[4,4096]{1,0:T(4,128)S(1)}, f32[4,4096]{1,0:T(4,128)S(1)}, u32[]{:S(2)}, u32[]{:S(2)}) collective-permute-start(f32[4,4096]{1,0:T(4,128)S(1)} %pad_maximum_fusion.1), channel_id=1, source_target_pairs={{0,2},{1,3},{2,0},{3,1},{4,6},{5,7},{6,4},{7,5},{8,10},{9,11},{10,... | collective-permute-start | bytes 196616 | tf_op jit(solution)/shard_map/ppermute | solution.py:493
  158.4 5.2 %collective-permute-start.23 = (f32[2,256]{1,0:T(2,128)S(1)}, f32[2,256]{1,0:T(2,128)S(1)}, u32[]{:S(2)}, u32[]{:S(2)}) collective-permute-start(f32[2,256]{1,0:T(2,128)S(1)} %score_sum.1), channel_id=1, source_target_pairs={{0,8},{4,12},{8,0},{12,4},{1,9},{5,13},{9,1},{13,5},{2,10},{6,14},... | collective-permute-start | bytes 6152 | tf_op jit(solution)/shard_map/ppermute | solution.py:493

commit v16 on v15

--- a/solution.py
+++ b/solution.py
@@ -38,17 +38,18 @@
 
 
 def call(body, name, where, grid, operands, in_specs, out_specs, out_shapes, scratch, mib, aliases=None, flops=1000):
+    scalars = [] if where is None else [where]
     return pl.pallas_call(
         body,
         grid_spec=pltpu.PrefetchScalarGridSpec(
-            num_scalar_prefetch=1, grid=grid, in_specs=in_specs, out_specs=out_specs, scratch_shapes=scratch
+            num_scalar_prefetch=len(scalars), grid=grid, in_specs=in_specs, out_specs=out_specs, scratch_shapes=scratch
         ),
         out_shape=out_shapes,
         compiler_params=pltpu.CompilerParams(vmem_limit_bytes=mib * 2**20),
         cost_estimate=pl.CostEstimate(flops=flops, bytes_accessed=1000, transcendentals=0),
         name=name,
         input_output_aliases=aliases or {},
-    )(where, *[placed(a, spec) for a, spec in zip(operands, in_specs)])
+    )(*scalars, *[placed(a, spec) for a, spec in zip(operands, in_specs)])
 
 
 def after(a, *others):
@@ -162,7 +163,7 @@
     )
 
 
-def last_body(start, inner_at, bring, where, inner, outer, kept, old, gate, po_t, _, *rest):
+def last_body(start, inner_at, bring, inner, outer, kept, old, gate, po_t, _, *rest):
     count = len(bring)
     far, rest = rest[:count], rest[count:]
     _, _, right, *near = rest[: 3 + count]
@@ -185,7 +186,7 @@
     ]
     for copy in brought:
         copy.start()
-    block = select(where, inner.at[pl.ds(inner_at, size)], outer)
+    block = inner[pl.ds(inner_at, size), :] + outer[...]
     total = jnp.zeros((size, PROJ), jnp.float32)
     for t, span in enumerate(spans):
         hidden_grad = old[tokens, span] + dot(block, kept[:, span])
@@ -199,13 +200,13 @@
         copy.wait()
 
 
-def last_block(where, inner, inner_at, outer, start, kept, old, gate, po_t, token, bring):
+def last_block(inner, inner_at, outer, start, kept, old, gate, po_t, token, bring):
     size = outer.shape[0]
     tiles = kept.shape[1] // TILE
     return call(
         functools.partial(last_body, start, inner_at, [first for _, first, _ in bring]),
         "last_block",
-        where,
+        None,
         (1,),
         (inner, outer, kept, old, gate, po_t, token, *[a for a, _, _ in bring]),
         [INSIDE, INSIDE, INSIDE, INSIDE, OUTSIDE, ANYWHERE, ANYWHERE] + [OUTSIDE] * len(bring),
@@ -224,11 +225,11 @@
             pltpu.SemaphoreType.DMA((max(len(bring), 1),)),
         ],
         LIMIT,
-        aliases={3: 0, 4: 1},
-    )
-
-
-def near_body(start, inner_at, bring, where, inner, outer, kept, old, gate, po, *rest):
+        aliases={2: 0, 3: 1},
+    )
+
+
+def near_body(start, inner_at, bring, inner, outer, kept, old, gate, po, *rest):
     far, rest = rest[: len(bring)], rest[len(bring) :]
     _, _, right, *near = rest[: 3 + len(bring)]
     near_sems = rest[-1]
@@ -239,7 +240,7 @@
     ]
     for copy in brought:
         copy.start()
-    block = select(where, inner.at[pl.ds(inner_at, size)], outer)
+    block = inner[pl.ds(inner_at, size), :] + outer[...]
     total = jnp.zeros((size, PROJ), jnp.float32)
     for t in range(kept.shape[1] // TILE):
         span = pl.ds(t * TILE, TILE)
@@ -251,11 +252,11 @@
         copy.wait()
 
 
-def near_block(where, inner, inner_at, outer, start, kept, old, gate, po, bring):
+def near_block(inner, inner_at, outer, start, kept, old, gate, po, bring):
     return call(
         functools.partial(near_body, start, inner_at, [first for _, first, _ in bring]),
         "near_block",
-        where,
+        None,
         (1,),
         (inner, outer, kept, old, gate, po, *[a for a, _, _ in bring]),
         [INSIDE] * 6 + [OUTSIDE] * len(bring),
@@ -268,13 +269,13 @@
         ],
         [pltpu.SemaphoreType.DMA((max(len(bring), 1),))],
         LIMIT,
-        aliases={3: 0, 4: 1},
-    )
-
-
-def outer_body(where, total, sent, *refs):
+        aliases={2: 0, 3: 1},
+    )
+
+
+def outer_body(masked, sent, *refs):
     *rights, grads, wide = refs
-    left_t = jnp.where(where[4] == 1, total[...], sent[...].astype(jnp.float32))
+    left_t = masked[...] + sent[...].astype(jnp.float32)
     wide[...] = jnp.zeros_like(wide)
     start = 0
     terms = [None] * grads.shape[0]
@@ -295,14 +296,14 @@
             grads[s : s + 1, i * 2 * PROJ : (i + 1) * 2 * PROJ] = rows[i : i + 1, :]
 
 
-def outer_products(where, total, sent, rights):
-    shape = (total.shape[1] // LEN, PROJ * PROJ)
+def outer_products(masked, sent, rights):
+    shape = (masked.shape[1] // LEN, PROJ * PROJ)
     (grads,) = call(
         outer_body,
         "outer_products",
-        where,
-        (1,),
-        (total, sent, *rights),
+        None,
+        (1,),
+        (masked, sent, *rights),
         [INSIDE] * (2 + len(rights)),
         [INSIDE],
         [pltpu.VMEM(shape, jnp.float32)],
@@ -328,16 +329,21 @@
     return out
 
 
-def score_sum(where, a, b):
+def score_sum(a, b):
     out = pltpu.VMEM(a.shape, a.dtype)
     (total,) = call(
-        sum_body, "score_sum", where, (1,), (a, b), [INSIDE, INSIDE], [INSIDE], [out], [], LIMIT, flops=3 * 10**9
+        sum_body, "score_sum", None, (1,), (a, b), [INSIDE, INSIDE], [INSIDE], [out], [], LIMIT, flops=3 * 10**9
     )
     return total
 
 
-def sum_body(where, a, b, out):
+def sum_body(*refs):
+    a, b, out = refs[-3:]
     out[...] = a[...] + b[...]
+
+
+def mask_body(where, a, out):
+    out[...] = jnp.where(where[4] == 1, a[...], 0.0)
 
 
 def score_body(where, grads, *rest):
@@ -442,6 +448,7 @@
     end_inner = [send(pair[halves[0]], perm=inner)]
     end_inner.append(send(after(pair[halves[1]], mid_outer[0], side), perm=inner))
     total = small_kernel(sum_body, "total", where, side, send(side, perm=inner))
+    masked = small_kernel(mask_body, "masked", where, total)
     sent = send(total.astype(jnp.bfloat16), perm=outward)
 
     acc, first = add_block(where, 1, [pair], w_down, after(acc, mid_outer[0]), begun, 2 * grad_out.size * w_down.shape[0])
@@ -463,7 +470,7 @@
             bring.append((proj_out.T, 0, PROJ))
         if n == len(sizes) - 3:
             bring += [(a, 0, a.shape[0]) for a in (*early, late)]
-        place = where, end_inner[h], at, end_outer, start, kept, acc
+        place = end_inner[h], at, end_outer, start, kept, acc
         if n == 0:
             kept, acc, right, *brought = last_block(*place, gate_pre, proj_out.T, second, bring)
             po_near = brought[1]
@@ -476,7 +483,7 @@
         rights.append(right)
         done.append(right)
         start += size
-    return outer_products(where, total, sent, rights), early, late
+    return outer_products(masked, sent, rights), early, late
 
 
 def any_line(where, inputs, gate_pre, grad_out, w_down, proj_in, proj_out, early, late):
@@ -526,7 +533,7 @@
     for bit in bits("dp"):
         all_grads = jnp.concatenate([all_grads, swap(all_grads, "dp", bit)], axis=0)
     for bit in first:
-        scores = score_sum(where, scores, swap(scores, "tensor", bit))
+        scores = score_sum(scores, swap(scores, "tensor", bit))
     others = swap(scores, "tensor", last)
     all_grads = after(all_grads, scores)
     row_count = hessian.shape[0]

time: 165 us -> 163 us (0.988)
  Pallas kernels: 66.1 us -> 62.7 us
  waiting for transfers between devices: 56.5 us -> 58.3 us
    pallas_call x15 -> x16, Pallas kernels: 66.1 us -> 62.7 us  [call(): pl.pallas_call(body, grid_spec=pltpu.PrefetchScalarGridSpec(num_scalar_pr...]
    ppermute x5, waiting for transfers between devices: 8.9 us -> 10.7 us  [line_of_four(): send(after(end_inner[h][at:at + size], ahead, done[n]), perm=outward)]
  transfers between devices with their start and end apart: 24 -> 24, of which waited for: 12 -> 13; matrix products, arithmetic and copies ran while one was open for 3% -> 3% of each run, Pallas kernels for 39% -> 38%
where the time goes in v16:
time: 163 us; the launch traced here: 162 us
  Pallas kernels  62.7 us (38%)
  waiting for transfers between devices  58.3 us (36%)
  starting transfers between devices  32.1 us (20%)
  local copies, waits for them, and re-layouts  7.48 us (5%)
    pallas_call x16, Pallas kernels, call(): pl.pallas_call(body, grid_spec=pltpu.PrefetchScalarGridSpec(num_scalar_pr...  62.7 us
    ppermute x1, waiting for transfers between devices, line_of_four(): pair = send(grad_out, perm=pairs)  15.4 us
    ppermute x9, waiting for transfers between devices, swap(): lax.ppermute(a, axis, [(i, i ^ bit) for i in range(lax.axis_size(axis))])  15.1 us
    ppermute x2, waiting for transfers between devices, line_of_four(): mid_outer = [send(after(a, begun), perm=outward) for a in mid_inner]  14.3 us
    ppermute x5, waiting for transfers between devices, line_of_four(): send(after(end_inner[h][at:at + size], ahead, done[n]), perm=outward)  10.7 us
    ppermute x9, starting transfers between devices, swap(): lax.ppermute(a, axis, [(i, i ^ bit) for i in range(lax.axis_size(axis))])  9.14 us
    ppermute x5, starting transfers between devices, line_of_four(): send(after(end_inner[h][at:at + size], ahead, done[n]), perm=outward)  6.63 us
    ppermute x1, starting transfers between devices, line_of_four(): from_end = send(after(in_part, mid_inner[0]), perm=inward)  5.83 us
  transfers between devices with their start and end apart: 24, of which 13 were waited for; matrix products, arithmetic and copies ran while one was open for 3% of the time, Pallas kernels for 38%

profile of v16, /device:TPU:0, one launch (start us, length us, event | category | flops | bytes accessed | tf_op | source)
XLA Modules:
  0.0 162.3 jit_solution(16459826164790129173)
XLA Ops:
  0.6 3.1 %collective-permute-start.5 = (bf16[1024,1024]{1,0:T(8,128)(2,1)}, bf16[1024,1024]{1,0:T(8,128)(2,1)}, u32[]{:S(2)}, u32[]{:S(2)}) collective-permute-start(bf16[1024,1024]{1,0:T(8,128)(2,1)} %own), channel_id=1, source_target_pairs={{0,4},{4,0},{8,12},{12,8},{1,5},{5,1},{9,13},{13,9},{2,6},{6,2},{1... | collective-permute-start | bytes 6291464 | tf_op jit(solution)/shard_map/ppermute | solution.py:440
  3.7 3.0 %fusion.1 = (bf16[512,1024]{1,0:T(8,128)(2,1)}, bf16[512,1024]{1,0:T(8,128)(2,1)}) fusion(bf16[1024,1024]{1,0:T(8,128)(2,1)} %own), kind=kLoop, calls=%fused_computation.3 | loop fusion | bytes 4194304 | tf_op jit(solution)/shard_map/slice | solution.py:441
  7.6 1.6 collective-permute-start.3
  9.5 1.6 copy-done.1
  12.0 1.3 input_block.1.refs_1_
  14.1 3.0 %collective-permute-done.3.rest_3_ = f32[256,256]{1,0:T(8,128)} collective-permute-done((f32[256,256]{1,0:T(8,128)}, f32[256,256]{1,0:T(8,128)}, u32[]{:S(2)}, u32[]{:S(2)}) %collective-permute-start.3) | collective-permute-done | bytes 262176 | tf_op jit(solution)/shard_map/ppermute | solution.py:500
  17.1 4.7 %collective-permute-done.4.rest_4_ = f32[256,256]{1,0:T(8,128)} collective-permute-done((f32[256,256]{1,0:T(8,128)}, f32[256,256]{1,0:T(8,128)}, u32[]{:S(2)}, u32[]{:S(2)}) %collective-permute-start.4) | collective-permute-done | bytes 262176 | tf_op jit(solution)/shard_map/ppermute | solution.py:500
  21.8 12.0 %own_block.1 = (f32[1024,3584]{1,0:T(8,128)S(1)}, bf16[1024,3584]{1,0:T(8,128)(2,1)S(1)}, f32[8,128]{1,0:T(8,128)S(1)}) custom-call(s32[9]{0:T(128)S(1)} %stack.43.where.refs_0_, bf16[1024,1024]{1,0:T(8,128)(2,1)S(1)} %copy-done, bf16[3584,4096]{1,0:T(8,128)(2,1)} %refs_4_.1, bf16[3584,4096]{1,0:T(8,128)(2,1)} %refs_4_.1), custom_call_target="tpu_custom_call" | custom-call | flops 1000 | bytes 1000 | tf_op jit(solution)/shard_map/own_block/pallas_call | solution.py:42
  35.1 15.4 %collective-permute-done.5.refs_0_ = bf16[1024,1024]{1,0:T(8,128)(2,1)} collective-permute-done((bf16[1024,1024]{1,0:T(8,128)(2,1)}, bf16[1024,1024]{1,0:T(8,128)(2,1)}, u32[]{:S(2)}, u32[]{:S(2)}) %collective-permute-start.5) | collective-permute-done | bytes 2097184 | tf_op jit(solution)/shard_map/ppermute | solution.py:440
  50.5 1.7 %fusion = (bf16[512,1024]{1,0:T(8,128)(2,1)S(1)}, bf16[512,1024]{1,0:T(8,128)(2,1)S(1)}) fusion(bf16[1024,1024]{1,0:T(8,128)(2,1)} %collective-permute-done.5.refs_0_), kind=kLoop, calls=%fused_computation.2 | loop fusion | bytes 4194304 | tf_op jit(solution)/shard_map/slice | solution.py:449
  53.0 5.8 %collective-permute-start.1 = (f32[64,1024]{1,0:T(8,128)S(1)}, f32[64,1024]{1,0:T(8,128)S(1)}, u32[]{:S(2)}, u32[]{:S(2)}) collective-permute-start(f32[64,1024]{1,0:T(8,128)S(1)} %input_block.1.refs_1_), channel_id=1, source_target_pairs={{0,4},{12,8},{1,5},{13,9},{2,6},{14,10},{3,7},{15,11},{16,20},{28,... | collective-permute-start | bytes 786440 | tf_op jit(solution)/shard_map/ppermute | solution.py:444
  58.8 1.3 collective-permute-start.12
  60.1 2.8 %collective-permute-done.1.refs_2_ = f32[64,1024]{1,0:T(8,128)S(1)} collective-permute-done((f32[64,1024]{1,0:T(8,128)S(1)}, f32[64,1024]{1,0:T(8,128)S(1)}, u32[]{:S(2)}, u32[]{:S(2)}) %collective-permute-start.1) | collective-permute-done | bytes 262176 | tf_op jit(solution)/shard_map/ppermute | solution.py:444
  63.5 9.4 %collective-permute-done.9.refs_2_ = bf16[512,1024]{1,0:T(8,128)(2,1)S(1)} collective-permute-done((bf16[512,1024]{1,0:T(8,128)(2,1)S(1)}, bf16[512,1024]{1,0:T(8,128)(2,1)S(1)}, u32[]{:S(2)}, u32[]{:S(2)}) %collective-permute-start.9) | collective-permute-done | bytes 1048608 | tf_op jit(solution)/shard_map/ppermute | solution.py:446
  74.3 12.9 %add_block_1.1 = (f32[1024,3584]{1,0:T(8,128)S(1)}, f32[8,128]{1,0:T(8,128)S(1)}) custom-call(s32[9]{0:T(128)S(1)} %stack.43.where.refs_0_, bf16[1024,1024]{1,0:T(8,128)(2,1)} %collective-permute-done.5.refs_0_, bf16[3584,4096]{1,0:T(8,128)(2,1)} %refs_4_.1, f32[1024,3584]{1,0:T(8,128)S(1)} %get-tuple-element.54.refs_2_, ...), custom_call_target="tpu_custom_call", output_to_operand_aliasing={{0}: (3, {})} | custom-call | flops 7516192768 | bytes 1000 | tf_op jit(solution)/shard_map/add_block_1/pallas_call | solution.py:42
  90.4 4.9 %collective-permute-done.12.refs_3_ = bf16[512,1024]{1,0:T(8,128)(2,1)S(1)} collective-permute-done((bf16[512,1024]{1,0:T(8,128)(2,1)S(1)}, bf16[512,1024]{1,0:T(8,128)(2,1)S(1)}, u32[]{:S(2)}, u32[]{:S(2)}) %collective-permute-start.12) | collective-permute-done | bytes 1048608 | tf_op jit(solution)/shard_map/ppermute | solution.py:446
  95.3 12.3 %add_block_2.1 = (f32[1024,3584]{1,0:T(8,128)S(1)}, f32[8,128]{1,0:T(8,128)S(1)}) custom-call(s32[9]{0:T(128)S(1)} %stack.43.where.refs_0_, bf16[512,1024]{1,0:T(8,128)(2,1)S(1)} %collective-permute-done.refs_0_, bf16[512,1024]{1,0:T(8,128)(2,1)S(1)} %collective-permute-done.11.refs_1_, ...), custom_call_target="tpu_custom_call", output_to_operand_aliasing={{0}: (6, {})} | custom-call | flops 1000 | bytes 1000 | tf_op jit(solution)/shard_map/add_block_2/pallas_call | solution.py:42
  109.0 6.1 %last_block.1 = (bf16[1024,3584]{1,0:T(8,128)(2,1)S(1)}, f32[1024,3584]{1,0:T(8,128)S(1)}, f32[256,64]{1,0:T(8,128)S(1)}, bf16[256,3584]{1,0:T(8,128)(2,1)S(1)}, bf16[64,3584]{1,0:T(8,128)(2,1)S(1)}) custom-call(bf16[512,1024]{1,0:T(8,128)(2,1)S(1)} %collective-permute-done.8.inner, ...), custom_call_target="tpu_custom_call", output_to_operand_aliasing={{0}: (2, {}), {1}: (3, {})} | custom-call | flops 1000 | bytes 1000 | tf_op jit(solution)/shard_map/last_block/pallas_call | solution.py:42
  115.2 3.2 %collective-permute-done.13.outer = bf16[256,1024]{1,0:T(8,128)(2,1)S(1)} collective-permute-done((bf16[256,1024]{1,0:T(8,128)(2,1)S(1)}, bf16[256,1024]{1,0:T(8,128)(2,1)S(1)}, u32[]{:S(2)}, u32[]{:S(2)}) %collective-permute-start.13) | collective-permute-done | bytes 524320 | tf_op jit(solution)/shard_map/ppermute | solution.py:464
  118.3 1.5 collective-permute-start.16
  119.8 3.2 %near_block.4 = (bf16[1024,3584]{1,0:T(8,128)(2,1)S(1)}, f32[1024,3584]{1,0:T(8,128)S(1)}, f32[256,64]{1,0:T(8,128)S(1)}, bf16[256,3584]{1,0:T(8,128)(2,1)S(1)}) custom-call(bf16[512,1024]{1,0:T(8,128)(2,1)S(1)} %collective-permute-done.8.inner, bf16[256,1024]{1,0:T(8,128)(2,1)S(1)} %collective-permute-done.13.outer, ...), custom_call_target="tpu_custom_call", output_to_operand_aliasing={{0}: (2, {}), {1}: (3, {})} | custom-call | flops 1000 | bytes 1000 | tf_op jit(solution)/shard_map/near_block/pallas_call | solution.py:42
  126.2 3.4 %collective-permute-done.15.outer = bf16[256,1024]{1,0:T(8,128)(2,1)S(1)} collective-permute-done((bf16[256,1024]{1,0:T(8,128)(2,1)S(1)}, bf16[256,1024]{1,0:T(8,128)(2,1)S(1)}, u32[]{:S(2)}, u32[]{:S(2)}) %collective-permute-start.15) | collective-permute-done | bytes 524320 | tf_op jit(solution)/shard_map/ppermute | solution.py:464
  129.6 5.2 %near_block.5 = (bf16[1024,3584]{1,0:T(8,128)(2,1)S(1)}, f32[1024,3584]{1,0:T(8,128)S(1)}, f32[256,64]{1,0:T(8,128)S(1)}, bf16[128,3584]{1,0:T(8,128)(2,1)S(1)},...) custom-call(bf16[512,1024]{1,0:T(8,128)(2,1)S(1)} %collective-permut, ...), custom_call_target="tpu_custom_call", output_to_operand_aliasing={{0}: (2, {}), {1}: (3, {})} | custom-call | flops 1000 | bytes 1000 | tf_op jit(solution)/shard_map/near_block/pallas_call | solution.py:42
  135.2 1.9 %near_block.6 = (bf16[1024,3584]{1,0:T(8,128)(2,1)S(1)}, f32[1024,3584]{1,0:T(8,128)S(1)}, f32[128,64]{1,0:T(8,128)S(1)}, bf16[128,3584]{1,0:T(8,128)(2,1)S(1)}) custom-call(bf16[512,1024]{1,0:T(8,128)(2,1)S(1)} %collective-permute-done.14.inner, bf16[128,1024]{1,0:T(8,128)(2,1)S(1)} %collective-permute-done.16.outer, ...), custom_call_target="tpu_custom_call", output_to_operand_aliasing={{0}: (2, {}), {1}: (3, {})} | custom-call | flops 1000 | bytes 1000 | tf_op jit(solution)/shard_map/near_block/pallas_call | solution.py:42
  137.1 3.7 %collective-permute-done.17.outer = bf16[128,1024]{1,0:T(8,128)(2,1)S(1)} collective-permute-done((bf16[128,1024]{1,0:T(8,128)(2,1)S(1)}, bf16[128,1024]{1,0:T(8,128)(2,1)S(1)}, u32[]{:S(2)}, u32[]{:S(2)}) %collective-permute-start.17) | collective-permute-done | bytes 262176 | tf_op jit(solution)/shard_map/ppermute | solution.py:464
  140.8 1.9 %near_block.7 = (bf16[1024,3584]{1,0:T(8,128)(2,1)S(1)}, f32[1024,3584]{1,0:T(8,128)S(1)}, f32[128,64]{1,0:T(8,128)S(1)}) custom-call(bf16[512,1024]{1,0:T(8,128)(2,1)S(1)} %collective-permute-done.14.inner, bf16[128,1024]{1,0:T(8,128)(2,1)S(1)} %collective-permute-done.17.outer, ...), custom_call_target="tpu_custom_call", output_to_operand_aliasing={{0}: (2, {}), {1}: (3, {})} | custom-call | flops 1000 | bytes 1000 | tf_op jit(solution)/shard_map/near_block/pallas_call | solution.py:42
  143.3 3.9 %collective-permute-done.18 = f32[2,4096]{1,0:T(2,128)S(1)} collective-permute-done((f32[2,4096]{1,0:T(2,128)S(1)}, f32[2,4096]{1,0:T(2,128)S(1)}, u32[]{:S(2)}, u32[]{:S(2)}) %collective-permute-start.18) | collective-permute-done | bytes 32800 | tf_op jit(solution)/shard_map/ppermute | solution.py:500
  147.3 2.2 %collective-permute-start.19 = (f32[2,4096]{1,0:T(2,128)S(1)}, f32[2,4096]{1,0:T(2,128)S(1)}, u32[]{:S(2)}, u32[]{:S(2)}) collective-permute-start(f32[2,4096]{1,0:T(2,128)S(1)} %add.34), channel_id=1, source_target_pairs={{0,8},{4,12},{8,0},{12,4},{1,9},{5,13},{9,1},{13,5},{2,10},{6,14},... | collective-permute-start | bytes 98312 | tf_op jit(solution)/shard_map/ppermute | solution.py:500
  149.4 2.7 %collective-permute-done.19 = f32[2,4096]{1,0:T(2,128)S(1)} collective-permute-done((f32[2,4096]{1,0:T(2,128)S(1)}, f32[2,4096]{1,0:T(2,128)S(1)}, u32[]{:S(2)}, u32[]{:S(2)}) %collective-permute-start.19) | collective-permute-done | bytes 32800 | tf_op jit(solution)/shard_map/ppermute | solution.py:500
  154.3 1.6 collective-permute-start.21
  156.6 2.1 %collective-permute-start.23 = (f32[2,256]{1,0:T(2,128)S(1)}, f32[2,256]{1,0:T(2,128)S(1)}, u32[]{:S(2)}, u32[]{:S(2)}) collective-permute-start(f32[2,256]{1,0:T(2,128)S(1)} %score_sum.1), channel_id=1, source_target_pairs={{0,8},{4,12},{8,0},{12,4},{1,9},{5,13},{9,1},{13,5},{2,10},{6,14},... | collective-permute-start | bytes 6152 | tf_op jit(solution)/shard_map/ppermute | solution.py:500
  158.8 2.9 %hessian_update.1 = f32[256,4096]{1,0:T(8,128)} custom-call(s32[9]{0:T(128)S(1)} %stack.43.where.refs_0_, f32[8,4096]{1,0:T(8,128)S(1)} %pad_maximum_fusion.grads, f32[256,4096]{1,0:T(8,128)S(1)} %get-tuple-element.91.hessian), custom_call_target="tpu_custom_call" | custom-call | flops 1000 | bytes 1000 | tf_op jit(solution)/shard_map/hessian_update/pallas_call | solution.py:42
  (52 shorter events, 19.2 us)
Async XLA Ops:
  0.6 21.1 %copy-start = (bf16[1024,1024]{1,0:T(8,128)(2,1)S(1)}, bf16[1024,1024]{1,0:T(8,128)(2,1)}, u32[]{:S(2)}) copy-start(bf16[1024,1024]{1,0:T(8,128)(2,1)} %own) | copy-start | bytes 6291460
  0.6 49.9 %collective-permute-start.5 = (bf16[1024,1024]{1,0:T(8,128)(2,1)}, bf16[1024,1024]{1,0:T(8,128)(2,1)}, u32[]{:S(2)}, u32[]{:S(2)}) collective-permute-start(bf16[1024,1024]{1,0:T(8,128)(2,1)} %own), channel_id=1, source_target_pairs={{0,4},{4,0},{8,12},{12,8},{1,5},{5,1},{9,13},{13,9},{2,6},{6,2},{1... | collective-permute-start | bytes 6291464 | tf_op jit(solution)/shard_map/ppermute | solution.py:440
  6.8 27.1 %collective-permute-start = (bf16[512,1024]{1,0:T(8,128)(2,1)}, bf16[512,1024]{1,0:T(8,128)(2,1)S(1)}, u32[]{:S(2)}, u32[]{:S(2)}) collective-permute-start(bf16[512,1024]{1,0:T(8,128)(2,1)} %get-tuple-element.97), channel_id=1, source_target_pairs={{4,8},{8,4},{5,9},{9,5},{6,10},{10,6},{7,11},{11,7},{20,24},{24,20... | collective-permute-start | bytes 3145736 | tf_op jit(solution)/shard_map/ppermute | solution.py:442
  7.5 5.8 %collective-permute-start.2 = (f32[256,256]{1,0:T(8,128)}, f32[256,256]{1,0:T(8,128)S(1)}, u32[]{:S(2)}, u32[]{:S(2)}) collective-permute-start(f32[256,256]{1,0:T(8,128)} %rest_1_.1), channel_id=1, source_target_pairs={{0,1},{1,0},{2,3},{3,2},{4,5},{5,4},{6,7},{7,6},{8,9},{9,8},{10,11... | collective-permute-start | bytes 786440 | tf_op jit(solution)/shard_map/ppermute | solution.py:500
  7.6 9.5 %collective-permute-start.3 = (f32[256,256]{1,0:T(8,128)}, f32[256,256]{1,0:T(8,128)}, u32[]{:S(2)}, u32[]{:S(2)}) collective-permute-start(f32[256,256]{1,0:T(8,128)} %rest_1_.1), channel_id=1, source_target_pairs={{0,2},{1,3},{2,0},{3,1},{4,6},{5,7},{6,4},{7,5},{8,10},{9,11},{10,... | collective-permute-start | bytes 786440 | tf_op jit(solution)/shard_map/ppermute | solution.py:500
  9.1 12.6 %collective-permute-start.4 = (f32[256,256]{1,0:T(8,128)}, f32[256,256]{1,0:T(8,128)}, u32[]{:S(2)}, u32[]{:S(2)}) collective-permute-start(f32[256,256]{1,0:T(8,128)} %rest_1_.1), channel_id=1, source_target_pairs={{0,3},{1,2},{2,1},{3,0},{4,7},{5,6},{6,5},{7,4},{8,11},{9,10},{10,... | collective-permute-start | bytes 786440 | tf_op jit(solution)/shard_map/ppermute | solution.py:500
  9.5 1.6 copy-start.1
  11.1 0.9 copy-start.2
  13.3 20.5 %copy-start.3 = (f32[256,256]{1,0:T(8,128)}, f32[256,256]{1,0:T(8,128)S(1)}, u32[]{:S(2)}) copy-start(f32[256,256]{1,0:T(8,128)S(1)} %collective-permute-done.2.rest_2_) | copy-start | bytes 786436
  13.3 45.5 %collective-permute-start.11 = (bf16[512,1024]{1,0:T(8,128)(2,1)}, bf16[512,1024]{1,0:T(8,128)(2,1)S(1)}, u32[]{:S(2)}, u32[]{:S(2)}) collective-permute-start(bf16[512,1024]{1,0:T(8,128)(2,1)} %get-tuple-element.96), channel_id=1, source_target_pairs={{4,8},{8,4},{5,9},{9,5},{6,10},{10,6},{7,11},{11,7},{20,24},{24,20... | collective-permute-start | bytes 3145736 | tf_op jit(solution)/shard_map/ppermute | solution.py:442
  33.8 39.0 %collective-permute-start.9 = (bf16[512,1024]{1,0:T(8,128)(2,1)S(1)}, bf16[512,1024]{1,0:T(8,128)(2,1)S(1)}, u32[]{:S(2)}, u32[]{:S(2)}) collective-permute-start(bf16[512,1024]{1,0:T(8,128)(2,1)S(1)} %collective-permute-done.refs_0_), channel_id=1, source_target_pairs={{4,0},{8,12},{5,1},{9,13},{6,2},{10,14},{7,3},{11,15},{20,16},{24,... | collective-permute-start | bytes 3145736 | tf_op jit(solution)/shard_map/ppermute | solution.py:446
  52.2 35.5 %collective-permute-start.8 = (bf16[512,1024]{1,0:T(8,128)(2,1)S(1)}, bf16[512,1024]{1,0:T(8,128)(2,1)S(1)}, u32[]{:S(2)}, u32[]{:S(2)}) collective-permute-start(bf16[512,1024]{1,0:T(8,128)(2,1)S(1)} %get-tuple-element.95), channel_id=1, source_target_pairs={{4,8},{8,4},{5,9},{9,5},{6,10},{10,6},{7,11},{11,7},{20,24},{24,20... | collective-permute-start | bytes 3145736 | tf_op jit(solution)/shard_map/ppermute | solution.py:448
  53.0 10.0 %collective-permute-start.1 = (f32[64,1024]{1,0:T(8,128)S(1)}, f32[64,1024]{1,0:T(8,128)S(1)}, u32[]{:S(2)}, u32[]{:S(2)}) collective-permute-start(f32[64,1024]{1,0:T(8,128)S(1)} %input_block.1.refs_1_), channel_id=1, source_target_pairs={{0,4},{12,8},{1,5},{13,9},{2,6},{14,10},{3,7},{15,11},{16,20},{28,... | collective-permute-start | bytes 786440 | tf_op jit(solution)/shard_map/ppermute | solution.py:444
  58.8 36.5 %collective-permute-start.12 = (bf16[512,1024]{1,0:T(8,128)(2,1)S(1)}, bf16[512,1024]{1,0:T(8,128)(2,1)S(1)}, u32[]{:S(2)}, u32[]{:S(2)}) collective-permute-start(bf16[512,1024]{1,0:T(8,128)(2,1)S(1)} %collective-permute-done.11.refs_1_), channel_id=1, source_target_pairs={{4,0},{8,12},{5,1},{9,13},{6,2},{10,14},{7,3},{11,15},{20,16},{24,... | collective-permute-start | bytes 3145736 | tf_op jit(solution)/shard_map/ppermute | solution.py:446
  72.9 14.3 %collective-permute-start.6 = (f32[64,1024]{1,0:T(8,128)S(1)}, f32[64,1024]{1,0:T(8,128)S(1)}, u32[]{:S(2)}, u32[]{:S(2)}) collective-permute-start(f32[64,1024]{1,0:T(8,128)S(1)} %side.1.refs_1_), channel_id=1, source_target_pairs={{4,8},{8,4},{5,9},{9,5},{6,10},{10,6},{7,11},{11,7},{20,24},{24,20... | collective-permute-start | bytes 786440 | tf_op jit(solution)/shard_map/ppermute | solution.py:450
  73.5 34.1 %collective-permute-start.14 = (bf16[512,1024]{1,0:T(8,128)(2,1)S(1)}, bf16[512,1024]{1,0:T(8,128)(2,1)S(1)}, u32[]{:S(2)}, u32[]{:S(2)}) collective-permute-start(bf16[512,1024]{1,0:T(8,128)(2,1)S(1)} %get-tuple-element.69), channel_id=1, source_target_pairs={{4,8},{8,4},{5,9},{9,5},{6,10},{10,6},{7,11},{11,7},{20,24},{24,20... | collective-permute-start | bytes 3145736 | tf_op jit(solution)/shard_map/ppermute | solution.py:449
  87.8 19.8 %collective-permute-start.10 = (bf16[256,1024]{1,0:T(8,128)(2,1)S(1)}, bf16[256,1024]{1,0:T(8,128)(2,1)S(1)}, u32[]{:S(2)}, u32[]{:S(2)}) collective-permute-start(bf16[256,1024]{1,0:T(8,128)(2,1)S(1)} %get-tuple-element.56), channel_id=1, source_target_pairs={{4,0},{8,12},{5,1},{9,13},{6,2},{10,14},{7,3},{11,15},{20,16},{24,... | collective-permute-start | bytes 1572872 | tf_op jit(solution)/shard_map/ppermute | solution.py:464
  89.1 29.2 %collective-permute-start.13 = (bf16[256,1024]{1,0:T(8,128)(2,1)S(1)}, bf16[256,1024]{1,0:T(8,128)(2,1)S(1)}, u32[]{:S(2)}, u32[]{:S(2)}) collective-permute-start(bf16[256,1024]{1,0:T(8,128)(2,1)S(1)} %get-tuple-element.63), channel_id=1, source_target_pairs={{4,0},{8,12},{5,1},{9,13},{6,2},{10,14},{7,3},{11,15},{20,16},{24,... | collective-permute-start | bytes 1572872 | tf_op jit(solution)/shard_map/ppermute | solution.py:464
  107.7 21.9 %collective-permute-start.15 = (bf16[256,1024]{1,0:T(8,128)(2,1)S(1)}, bf16[256,1024]{1,0:T(8,128)(2,1)S(1)}, u32[]{:S(2)}, u32[]{:S(2)}) collective-permute-start(bf16[256,1024]{1,0:T(8,128)(2,1)S(1)} %slice.40), channel_id=1, source_target_pairs={{4,0},{8,12},{5,1},{9,13},{6,2},{10,14},{7,3},{11,15},{20,16},{24,... | collective-permute-start | bytes 1572872 | tf_op jit(solution)/shard_map/ppermute | solution.py:464
  118.3 16.9 %collective-permute-start.16 = (bf16[128,1024]{1,0:T(8,128)(2,1)S(1)}, bf16[128,1024]{1,0:T(8,128)(2,1)S(1)}, u32[]{:S(2)}, u32[]{:S(2)}) collective-permute-start(bf16[128,1024]{1,0:T(8,128)(2,1)S(1)} %get-tuple-element.75), channel_id=1, source_target_pairs={{4,0},{8,12},{5,1},{9,13},{6,2},{10,14},{7,3},{11,15},{20,16},{24,... | collective-permute-start | bytes 786440 | tf_op jit(solution)/shard_map/ppermute | solution.py:464
  123.0 17.8 %collective-permute-start.17 = (bf16[128,1024]{1,0:T(8,128)(2,1)S(1)}, bf16[128,1024]{1,0:T(8,128)(2,1)S(1)}, u32[]{:S(2)}, u32[]{:S(2)}) collective-permute-start(bf16[128,1024]{1,0:T(8,128)(2,1)S(1)} %get-tuple-element.80), channel_id=1, source_target_pairs={{4,0},{8,12},{5,1},{9,13},{6,2},{10,14},{7,3},{11,15},{20,16},{24,... | collective-permute-start | bytes 786440 | tf_op jit(solution)/shard_map/ppermute | solution.py:464
  124.3 18.4 %collective-permute-start.7 = (bf16[64,1024]{1,0:T(8,128)(2,1)S(1)}, bf16[64,1024]{1,0:T(8,128)(2,1)S(1)}, u32[]{:S(2)}, u32[]{:S(2)}) collective-permute-start(bf16[64,1024]{1,0:T(8,128)(2,1)S(1)} %convert_element_type.4), channel_id=1, source_target_pairs={{4,0},{8,12},{5,1},{9,13},{6,2},{10,14},{7,3},{11,15},{20,16},{24,... | collective-permute-start | bytes 393224 | tf_op jit(solution)/shard_map/ppermute | solution.py:452
  143.3 4.0 %collective-permute-start.18 = (f32[2,4096]{1,0:T(2,128)S(1)}, f32[2,4096]{1,0:T(2,128)S(1)}, u32[]{:S(2)}, u32[]{:S(2)}) collective-permute-start(f32[2,4096]{1,0:T(2,128)S(1)} %outer_products.1), channel_id=1, source_target_pairs={{0,4},{4,0},{8,12},{12,8},{1,5},{5,1},{9,13},{13,9},{2,6},{6,2},{1... | collective-permute-start | bytes 98312 | tf_op jit(solution)/shard_map/ppermute | solution.py:500
  147.3 4.9 %collective-permute-start.19 = (f32[2,4096]{1,0:T(2,128)S(1)}, f32[2,4096]{1,0:T(2,128)S(1)}, u32[]{:S(2)}, u32[]{:S(2)}) collective-permute-start(f32[2,4096]{1,0:T(2,128)S(1)} %add.34), channel_id=1, source_target_pairs={{0,8},{4,12},{8,0},{12,4},{1,9},{5,13},{9,1},{13,5},{2,10},{6,14},... | collective-permute-start | bytes 98312 | tf_op jit(solution)/shard_map/ppermute | solution.py:500
  152.9 1.3 collective-permute-start.20
  153.0 3.7 %collective-permute-start.22 = (f32[2,256]{1,0:T(2,128)S(1)}, f32[2,256]{1,0:T(2,128)S(1)}, u32[]{:S(2)}, u32[]{:S(2)}) collective-permute-start(f32[2,256]{1,0:T(2,128)S(1)} %scores.1.refs_0_), channel_id=1, source_target_pairs={{0,4},{4,0},{8,12},{12,8},{1,5},{5,1},{9,13},{13,9},{2,6},{6,2},{1... | collective-permute-start | bytes 6152 | tf_op jit(solution)/shard_map/ppermute | solution.py:500
  154.3 4.5 %collective-permute-start.21 = (f32[4,4096]{1,0:T(4,128)S(1)}, f32[4,4096]{1,0:T(4,128)S(1)}, u32[]{:S(2)}, u32[]{:S(2)}) collective-permute-start(f32[4,4096]{1,0:T(4,128)S(1)} %pad_maximum_fusion.1), channel_id=1, source_target_pairs={{0,2},{1,3},{2,0},{3,1},{4,6},{5,7},{6,4},{7,5},{8,10},{9,11},{10,... | collective-permute-start | bytes 196616 | tf_op jit(solution)/shard_map/ppermute | solution.py:500
  156.6 5.1 %collective-permute-start.23 = (f32[2,256]{1,0:T(2,128)S(1)}, f32[2,256]{1,0:T(2,128)S(1)}, u32[]{:S(2)}, u32[]{:S(2)}) collective-permute-start(f32[2,256]{1,0:T(2,128)S(1)} %score_sum.1), channel_id=1, source_target_pairs={{0,8},{4,12},{8,0},{12,4},{1,9},{5,13},{9,1},{13,5},{2,10},{6,14},... | collective-permute-start | bytes 6152 | tf_op jit(solution)/shard_map/ppermute | solution.py:500

commit v17 on v16

--- a/solution.py
+++ b/solution.py
@@ -58,6 +58,11 @@
 
 def fixed(shape):
     return pl.BlockSpec(shape, lambda j, where: (0, 0), pipeline_mode=pl.Buffered(1))
+
+
+def my_part(p, width):
+    at = lax.axis_index("tensor") * lax.axis_size("dp") + (lax.axis_index("dp") ^ p)
+    return pl.ds(pl.multiple_of(at * width, width), width)
 
 
 def tile_rows(t, size=TILE):
@@ -346,7 +351,7 @@
     out[...] = jnp.where(where[4] == 1, a[...], 0.0)
 
 
-def score_body(where, grads, *rest):
+def score_body(grads, *rest):
     *parts, out = rest
     rows, width = parts[0].shape
     count = grads.shape[0]
@@ -355,7 +360,7 @@
     for s in range(count):
         products = None
         for p, part in enumerate(parts):
-            term = part[...] * grads[s : s + 1, columns(where, FIRST_PART + p, width)]
+            term = part[...] * grads[s : s + 1, my_part(p, width)]
             products = term if products is None else products + term
         total = jnp.where(lane == s, jnp.sum(products, axis=1, keepdims=True), total)
     out[...] = total.T[:count, :]
@@ -372,11 +377,11 @@
     (scores,) = call(
         score_body,
         "scores",
-        where,
+        None,
         (1,),
         (grads, *parts),
         [INSIDE] * (1 + len(parts)),
-        [pl.BlockSpec(shape, lambda j, where: (0, 0))],
+        [pl.BlockSpec(shape, lambda j: (0, 0))],
         [jax.ShapeDtypeStruct(shape, jnp.float32)],
         [],
         LIMIT,
@@ -392,9 +397,9 @@
     return high, middle, low
 
 
-def update_body(scale, where, grads, hessian, out, new, out_sems):
+def update_body(scale, grads, hessian, out, new, out_sems):
     parts, _, width = new.shape
-    high, middle, low = pieces(grads[:, columns(where, FIRST_PART, new.shape[1])])
+    high, middle, low = pieces(grads[:, my_part(0, new.shape[1])])
     left = jnp.concatenate([high, high, middle, middle, high, low], axis=0).T
     writes = []
     for t in range(parts):
@@ -408,7 +413,7 @@
         write.wait()
 
 
-def update(where, grads, hessian):
+def update(grads, hessian):
     rows, length = hessian.shape
     count = grads.shape[0]
     parts = 8
@@ -416,7 +421,7 @@
     (updated,) = call(
         functools.partial(update_body, 1.0 / count),
         "hessian_update",
-        where,
+        None,
         (1,),
         (grads, hessian),
         [INSIDE, INSIDE],
@@ -541,7 +546,7 @@
         mine = lax.dynamic_slice_in_dim(all_grads, where[FIRST_PART] * row_count, row_count, 1)
         updated = hessian + jnp.dot(mine.T, all_grads, precision=HIGHEST) / all_grads.shape[0]
     else:
-        updated = update(where, all_grads, hessian)
+        updated = update(all_grads, hessian)
     updated, others = lax.optimization_barrier((updated, others))
     return (updated, scores + others)
 

time: 163 us -> 162 us (level)
  no operation moved by 1% of the time
where the time goes in v17:
time: 162 us; the launch traced here: 161 us
  Pallas kernels  61.5 us (38%)
  waiting for transfers between devices  58.4 us (36%)
  starting transfers between devices  32.1 us (20%)
  local copies, waits for them, and re-layouts  7.48 us (5%)
    pallas_call x16, Pallas kernels, call(): pl.pallas_call(body, grid_spec=pltpu.PrefetchScalarGridSpec(num_scalar_pr...  61.5 us
    ppermute x1, waiting for transfers between devices, line_of_four(): pair = send(grad_out, perm=pairs)  15.4 us
    ppermute x9, waiting for transfers between devices, swap(): lax.ppermute(a, axis, [(i, i ^ bit) for i in range(lax.axis_size(axis))])  15.1 us
    ppermute x2, waiting for transfers between devices, line_of_four(): mid_outer = [send(after(a, begun), perm=outward) for a in mid_inner]  14.3 us
    ppermute x5, waiting for transfers between devices, line_of_four(): send(after(end_inner[h][at:at + size], ahead, done[n]), perm=outward)  10.7 us
    ppermute x9, starting transfers between devices, swap(): lax.ppermute(a, axis, [(i, i ^ bit) for i in range(lax.axis_size(axis))])  9.14 us
    ppermute x5, starting transfers between devices, line_of_four(): send(after(end_inner[h][at:at + size], ahead, done[n]), perm=outward)  6.63 us
    ppermute x1, starting transfers between devices, line_of_four(): from_end = send(after(in_part, mid_inner[0]), perm=inward)  5.83 us
  transfers between devices with their start and end apart: 24, of which 13 were waited for; matrix products, arithmetic and copies ran while one was open for 3% of the time, Pallas kernels for 38%

profile of v17, /device:TPU:0, one launch (start us, length us, event | category | flops | bytes accessed | tf_op | source)
XLA Modules:
  0.0 161.2 jit_solution(354054931818260022)
XLA Ops:
  0.6 3.1 %collective-permute-start.5 = (bf16[1024,1024]{1,0:T(8,128)(2,1)}, bf16[1024,1024]{1,0:T(8,128)(2,1)}, u32[]{:S(2)}, u32[]{:S(2)}) collective-permute-start(bf16[1024,1024]{1,0:T(8,128)(2,1)} %own), channel_id=1, source_target_pairs={{0,4},{4,0},{8,12},{12,8},{1,5},{5,1},{9,13},{13,9},{2,6},{6,2},{1... | collective-permute-start | bytes 6291464 | tf_op jit(solution)/shard_map/ppermute | solution.py:445
  3.7 3.0 %fusion.1 = (bf16[512,1024]{1,0:T(8,128)(2,1)}, bf16[512,1024]{1,0:T(8,128)(2,1)}) fusion(bf16[1024,1024]{1,0:T(8,128)(2,1)} %own), kind=kLoop, calls=%fused_computation.3 | loop fusion | bytes 4194304 | tf_op jit(solution)/shard_map/slice | solution.py:446
  7.6 1.6 collective-permute-start.3
  9.5 1.6 copy-done.1
  12.0 1.3 input_block.1.refs_1_
  14.1 3.0 %collective-permute-done.3.rest_3_ = f32[256,256]{1,0:T(8,128)} collective-permute-done((f32[256,256]{1,0:T(8,128)}, f32[256,256]{1,0:T(8,128)}, u32[]{:S(2)}, u32[]{:S(2)}) %collective-permute-start.3) | collective-permute-done | bytes 262176 | tf_op jit(solution)/shard_map/ppermute | solution.py:505
  17.1 4.7 %collective-permute-done.4.rest_4_ = f32[256,256]{1,0:T(8,128)} collective-permute-done((f32[256,256]{1,0:T(8,128)}, f32[256,256]{1,0:T(8,128)}, u32[]{:S(2)}, u32[]{:S(2)}) %collective-permute-start.4) | collective-permute-done | bytes 262176 | tf_op jit(solution)/shard_map/ppermute | solution.py:505
  21.8 12.0 %own_block.1 = (f32[1024,3584]{1,0:T(8,128)S(1)}, bf16[1024,3584]{1,0:T(8,128)(2,1)S(1)}, f32[8,128]{1,0:T(8,128)S(1)}) custom-call(s32[9]{0:T(128)S(1)} %stack.43.where.refs_0_, bf16[1024,1024]{1,0:T(8,128)(2,1)S(1)} %copy-done, bf16[3584,4096]{1,0:T(8,128)(2,1)} %refs_4_.1, bf16[3584,4096]{1,0:T(8,128)(2,1)} %refs_4_.1), custom_call_target="tpu_custom_call" | custom-call | flops 1000 | bytes 1000 | tf_op jit(solution)/shard_map/own_block/pallas_call | solution.py:42
  33.8 1.3 collective-permute-start.9
  35.1 15.4 %collective-permute-done.5.refs_0_ = bf16[1024,1024]{1,0:T(8,128)(2,1)} collective-permute-done((bf16[1024,1024]{1,0:T(8,128)(2,1)}, bf16[1024,1024]{1,0:T(8,128)(2,1)}, u32[]{:S(2)}, u32[]{:S(2)}) %collective-permute-start.5) | collective-permute-done | bytes 2097184 | tf_op jit(solution)/shard_map/ppermute | solution.py:445
  50.5 1.7 %fusion = (bf16[512,1024]{1,0:T(8,128)(2,1)S(1)}, bf16[512,1024]{1,0:T(8,128)(2,1)S(1)}) fusion(bf16[1024,1024]{1,0:T(8,128)(2,1)} %collective-permute-done.5.refs_0_), kind=kLoop, calls=%fused_computation.2 | loop fusion | bytes 4194304 | tf_op jit(solution)/shard_map/slice | solution.py:454
  53.0 5.8 %collective-permute-start.1 = (f32[64,1024]{1,0:T(8,128)S(1)}, f32[64,1024]{1,0:T(8,128)S(1)}, u32[]{:S(2)}, u32[]{:S(2)}) collective-permute-start(f32[64,1024]{1,0:T(8,128)S(1)} %input_block.1.refs_1_), channel_id=1, source_target_pairs={{0,4},{12,8},{1,5},{13,9},{2,6},{14,10},{3,7},{15,11},{16,20},{28,... | collective-permute-start | bytes 786440 | tf_op jit(solution)/shard_map/ppermute | solution.py:449
  60.1 2.8 %collective-permute-done.1.refs_2_ = f32[64,1024]{1,0:T(8,128)S(1)} collective-permute-done((f32[64,1024]{1,0:T(8,128)S(1)}, f32[64,1024]{1,0:T(8,128)S(1)}, u32[]{:S(2)}, u32[]{:S(2)}) %collective-permute-start.1) | collective-permute-done | bytes 262176 | tf_op jit(solution)/shard_map/ppermute | solution.py:449
  63.5 9.4 %collective-permute-done.9.refs_2_ = bf16[512,1024]{1,0:T(8,128)(2,1)S(1)} collective-permute-done((bf16[512,1024]{1,0:T(8,128)(2,1)S(1)}, bf16[512,1024]{1,0:T(8,128)(2,1)S(1)}, u32[]{:S(2)}, u32[]{:S(2)}) %collective-permute-start.9) | collective-permute-done | bytes 1048608 | tf_op jit(solution)/shard_map/ppermute | solution.py:451
  74.3 12.9 %add_block_1.1 = (f32[1024,3584]{1,0:T(8,128)S(1)}, f32[8,128]{1,0:T(8,128)S(1)}) custom-call(s32[9]{0:T(128)S(1)} %stack.43.where.refs_0_, bf16[1024,1024]{1,0:T(8,128)(2,1)} %collective-permute-done.5.refs_0_, bf16[3584,4096]{1,0:T(8,128)(2,1)} %refs_4_.1, f32[1024,3584]{1,0:T(8,128)S(1)} %get-tuple-element.54.refs_2_, ...), custom_call_target="tpu_custom_call", output_to_operand_aliasing={{0}: (3, {})} | custom-call | flops 7516192768 | bytes 1000 | tf_op jit(solution)/shard_map/add_block_1/pallas_call | solution.py:42
  90.4 4.9 %collective-permute-done.12.refs_3_ = bf16[512,1024]{1,0:T(8,128)(2,1)S(1)} collective-permute-done((bf16[512,1024]{1,0:T(8,128)(2,1)S(1)}, bf16[512,1024]{1,0:T(8,128)(2,1)S(1)}, u32[]{:S(2)}, u32[]{:S(2)}) %collective-permute-start.12) | collective-permute-done | bytes 1048608 | tf_op jit(solution)/shard_map/ppermute | solution.py:451
  95.3 12.3 %add_block_2.1 = (f32[1024,3584]{1,0:T(8,128)S(1)}, f32[8,128]{1,0:T(8,128)S(1)}) custom-call(s32[9]{0:T(128)S(1)} %stack.43.where.refs_0_, bf16[512,1024]{1,0:T(8,128)(2,1)S(1)} %collective-permute-done.refs_0_, bf16[512,1024]{1,0:T(8,128)(2,1)S(1)} %collective-permute-done.11.refs_1_, ...), custom_call_target="tpu_custom_call", output_to_operand_aliasing={{0}: (6, {})} | custom-call | flops 1000 | bytes 1000 | tf_op jit(solution)/shard_map/add_block_2/pallas_call | solution.py:42
  109.1 6.1 %last_block.1 = (bf16[1024,3584]{1,0:T(8,128)(2,1)S(1)}, f32[1024,3584]{1,0:T(8,128)S(1)}, f32[256,64]{1,0:T(8,128)S(1)}, bf16[256,3584]{1,0:T(8,128)(2,1)S(1)}, bf16[64,3584]{1,0:T(8,128)(2,1)S(1)}) custom-call(bf16[512,1024]{1,0:T(8,128)(2,1)S(1)} %collective-permute-done.8.inner, ...), custom_call_target="tpu_custom_call", output_to_operand_aliasing={{0}: (2, {}), {1}: (3, {})} | custom-call | flops 1000 | bytes 1000 | tf_op jit(solution)/shard_map/last_block/pallas_call | solution.py:42
  115.2 3.2 %collective-permute-done.13.outer = bf16[256,1024]{1,0:T(8,128)(2,1)S(1)} collective-permute-done((bf16[256,1024]{1,0:T(8,128)(2,1)S(1)}, bf16[256,1024]{1,0:T(8,128)(2,1)S(1)}, u32[]{:S(2)}, u32[]{:S(2)}) %collective-permute-start.13) | collective-permute-done | bytes 524320 | tf_op jit(solution)/shard_map/ppermute | solution.py:469
  118.3 1.5 collective-permute-start.16
  119.8 3.2 %near_block.4 = (bf16[1024,3584]{1,0:T(8,128)(2,1)S(1)}, f32[1024,3584]{1,0:T(8,128)S(1)}, f32[256,64]{1,0:T(8,128)S(1)}, bf16[256,3584]{1,0:T(8,128)(2,1)S(1)}) custom-call(bf16[512,1024]{1,0:T(8,128)(2,1)S(1)} %collective-permute-done.8.inner, bf16[256,1024]{1,0:T(8,128)(2,1)S(1)} %collective-permute-done.13.outer, ...), custom_call_target="tpu_custom_call", output_to_operand_aliasing={{0}: (2, {}), {1}: (3, {})} | custom-call | flops 1000 | bytes 1000 | tf_op jit(solution)/shard_map/near_block/pallas_call | solution.py:42
  126.2 3.4 %collective-permute-done.15.outer = bf16[256,1024]{1,0:T(8,128)(2,1)S(1)} collective-permute-done((bf16[256,1024]{1,0:T(8,128)(2,1)S(1)}, bf16[256,1024]{1,0:T(8,128)(2,1)S(1)}, u32[]{:S(2)}, u32[]{:S(2)}) %collective-permute-start.15) | collective-permute-done | bytes 524320 | tf_op jit(solution)/shard_map/ppermute | solution.py:469
  129.6 5.1 %near_block.5 = (bf16[1024,3584]{1,0:T(8,128)(2,1)S(1)}, f32[1024,3584]{1,0:T(8,128)S(1)}, f32[256,64]{1,0:T(8,128)S(1)}, bf16[128,3584]{1,0:T(8,128)(2,1)S(1)},...) custom-call(bf16[512,1024]{1,0:T(8,128)(2,1)S(1)} %collective-permut, ...), custom_call_target="tpu_custom_call", output_to_operand_aliasing={{0}: (2, {}), {1}: (3, {})} | custom-call | flops 1000 | bytes 1000 | tf_op jit(solution)/shard_map/near_block/pallas_call | solution.py:42
  135.2 1.9 %near_block.6 = (bf16[1024,3584]{1,0:T(8,128)(2,1)S(1)}, f32[1024,3584]{1,0:T(8,128)S(1)}, f32[128,64]{1,0:T(8,128)S(1)}, bf16[128,3584]{1,0:T(8,128)(2,1)S(1)}) custom-call(bf16[512,1024]{1,0:T(8,128)(2,1)S(1)} %collective-permute-done.14.inner, bf16[128,1024]{1,0:T(8,128)(2,1)S(1)} %collective-permute-done.16.outer, ...), custom_call_target="tpu_custom_call", output_to_operand_aliasing={{0}: (2, {}), {1}: (3, {})} | custom-call | flops 1000 | bytes 1000 | tf_op jit(solution)/shard_map/near_block/pallas_call | solution.py:42
  137.1 3.7 %collective-permute-done.17.outer = bf16[128,1024]{1,0:T(8,128)(2,1)S(1)} collective-permute-done((bf16[128,1024]{1,0:T(8,128)(2,1)S(1)}, bf16[128,1024]{1,0:T(8,128)(2,1)S(1)}, u32[]{:S(2)}, u32[]{:S(2)}) %collective-permute-start.17) | collective-permute-done | bytes 262176 | tf_op jit(solution)/shard_map/ppermute | solution.py:469
  140.8 1.9 %near_block.7 = (bf16[1024,3584]{1,0:T(8,128)(2,1)S(1)}, f32[1024,3584]{1,0:T(8,128)S(1)}, f32[128,64]{1,0:T(8,128)S(1)}) custom-call(bf16[512,1024]{1,0:T(8,128)(2,1)S(1)} %collective-permute-done.14.inner, bf16[128,1024]{1,0:T(8,128)(2,1)S(1)} %collective-permute-done.17.outer, ...), custom_call_target="tpu_custom_call", output_to_operand_aliasing={{0}: (2, {}), {1}: (3, {})} | custom-call | flops 1000 | bytes 1000 | tf_op jit(solution)/shard_map/near_block/pallas_call | solution.py:42
  143.3 3.9 %collective-permute-done.18 = f32[2,4096]{1,0:T(2,128)S(1)} collective-permute-done((f32[2,4096]{1,0:T(2,128)S(1)}, f32[2,4096]{1,0:T(2,128)S(1)}, u32[]{:S(2)}, u32[]{:S(2)}) %collective-permute-start.18) | collective-permute-done | bytes 32800 | tf_op jit(solution)/shard_map/ppermute | solution.py:505
  147.3 2.2 %collective-permute-start.19 = (f32[2,4096]{1,0:T(2,128)S(1)}, f32[2,4096]{1,0:T(2,128)S(1)}, u32[]{:S(2)}, u32[]{:S(2)}) collective-permute-start(f32[2,4096]{1,0:T(2,128)S(1)} %add.34), channel_id=1, source_target_pairs={{0,8},{4,12},{8,0},{12,4},{1,9},{5,13},{9,1},{13,5},{2,10},{6,14},... | collective-permute-start | bytes 98312 | tf_op jit(solution)/shard_map/ppermute | solution.py:505
  149.4 2.7 %collective-permute-done.19 = f32[2,4096]{1,0:T(2,128)S(1)} collective-permute-done((f32[2,4096]{1,0:T(2,128)S(1)}, f32[2,4096]{1,0:T(2,128)S(1)}, u32[]{:S(2)}, u32[]{:S(2)}) %collective-permute-start.19) | collective-permute-done | bytes 32800 | tf_op jit(solution)/shard_map/ppermute | solution.py:505
  153.8 1.6 collective-permute-start.21
  156.1 2.1 %collective-permute-start.23 = (f32[2,256]{1,0:T(2,128)S(1)}, f32[2,256]{1,0:T(2,128)S(1)}, u32[]{:S(2)}, u32[]{:S(2)}) collective-permute-start(f32[2,256]{1,0:T(2,128)S(1)} %score_sum.1), channel_id=1, source_target_pairs={{0,8},{4,12},{8,0},{12,4},{1,9},{5,13},{9,1},{13,5},{2,10},{6,14},... | collective-permute-start | bytes 6152 | tf_op jit(solution)/shard_map/ppermute | solution.py:505
  158.3 2.3 %hessian_update.1 = f32[256,4096]{1,0:T(8,128)} custom-call(f32[8,4096]{1,0:T(8,128)S(1)} %pad_maximum_fusion.grads, f32[256,4096]{1,0:T(8,128)S(1)} %get-tuple-element.91.hessian), custom_call_target="tpu_custom_call" | custom-call | flops 1000 | bytes 1000 | tf_op jit(solution)/shard_map/hessian_update/pallas_call | solution.py:42
  (52 shorter events, 18.7 us)
Async XLA Ops:
  0.6 21.1 %copy-start = (bf16[1024,1024]{1,0:T(8,128)(2,1)S(1)}, bf16[1024,1024]{1,0:T(8,128)(2,1)}, u32[]{:S(2)}) copy-start(bf16[1024,1024]{1,0:T(8,128)(2,1)} %own) | copy-start | bytes 6291460
  0.6 49.9 %collective-permute-start.5 = (bf16[1024,1024]{1,0:T(8,128)(2,1)}, bf16[1024,1024]{1,0:T(8,128)(2,1)}, u32[]{:S(2)}, u32[]{:S(2)}) collective-permute-start(bf16[1024,1024]{1,0:T(8,128)(2,1)} %own), channel_id=1, source_target_pairs={{0,4},{4,0},{8,12},{12,8},{1,5},{5,1},{9,13},{13,9},{2,6},{6,2},{1... | collective-permute-start | bytes 6291464 | tf_op jit(solution)/shard_map/ppermute | solution.py:445
  6.8 27.0 %collective-permute-start = (bf16[512,1024]{1,0:T(8,128)(2,1)}, bf16[512,1024]{1,0:T(8,128)(2,1)S(1)}, u32[]{:S(2)}, u32[]{:S(2)}) collective-permute-start(bf16[512,1024]{1,0:T(8,128)(2,1)} %get-tuple-element.97), channel_id=1, source_target_pairs={{4,8},{8,4},{5,9},{9,5},{6,10},{10,6},{7,11},{11,7},{20,24},{24,20... | collective-permute-start | bytes 3145736 | tf_op jit(solution)/shard_map/ppermute | solution.py:447
  7.5 5.8 %collective-permute-start.2 = (f32[256,256]{1,0:T(8,128)}, f32[256,256]{1,0:T(8,128)S(1)}, u32[]{:S(2)}, u32[]{:S(2)}) collective-permute-start(f32[256,256]{1,0:T(8,128)} %rest_1_.1), channel_id=1, source_target_pairs={{0,1},{1,0},{2,3},{3,2},{4,5},{5,4},{6,7},{7,6},{8,9},{9,8},{10,11... | collective-permute-start | bytes 786440 | tf_op jit(solution)/shard_map/ppermute | solution.py:505
  7.6 9.5 %collective-permute-start.3 = (f32[256,256]{1,0:T(8,128)}, f32[256,256]{1,0:T(8,128)}, u32[]{:S(2)}, u32[]{:S(2)}) collective-permute-start(f32[256,256]{1,0:T(8,128)} %rest_1_.1), channel_id=1, source_target_pairs={{0,2},{1,3},{2,0},{3,1},{4,6},{5,7},{6,4},{7,5},{8,10},{9,11},{10,... | collective-permute-start | bytes 786440 | tf_op jit(solution)/shard_map/ppermute | solution.py:505
  9.1 12.6 %collective-permute-start.4 = (f32[256,256]{1,0:T(8,128)}, f32[256,256]{1,0:T(8,128)}, u32[]{:S(2)}, u32[]{:S(2)}) collective-permute-start(f32[256,256]{1,0:T(8,128)} %rest_1_.1), channel_id=1, source_target_pairs={{0,3},{1,2},{2,1},{3,0},{4,7},{5,6},{6,5},{7,4},{8,11},{9,10},{10,... | collective-permute-start | bytes 786440 | tf_op jit(solution)/shard_map/ppermute | solution.py:505
  9.5 1.6 copy-start.1
  11.1 0.9 copy-start.2
  13.3 20.4 %copy-start.3 = (f32[256,256]{1,0:T(8,128)}, f32[256,256]{1,0:T(8,128)S(1)}, u32[]{:S(2)}) copy-start(f32[256,256]{1,0:T(8,128)S(1)} %collective-permute-done.2.rest_2_) | copy-start | bytes 786436
  13.3 45.5 %collective-permute-start.11 = (bf16[512,1024]{1,0:T(8,128)(2,1)}, bf16[512,1024]{1,0:T(8,128)(2,1)S(1)}, u32[]{:S(2)}, u32[]{:S(2)}) collective-permute-start(bf16[512,1024]{1,0:T(8,128)(2,1)} %get-tuple-element.96), channel_id=1, source_target_pairs={{4,8},{8,4},{5,9},{9,5},{6,10},{10,6},{7,11},{11,7},{20,24},{24,20... | collective-permute-start | bytes 3145736 | tf_op jit(solution)/shard_map/ppermute | solution.py:447
  33.8 39.1 %collective-permute-start.9 = (bf16[512,1024]{1,0:T(8,128)(2,1)S(1)}, bf16[512,1024]{1,0:T(8,128)(2,1)S(1)}, u32[]{:S(2)}, u32[]{:S(2)}) collective-permute-start(bf16[512,1024]{1,0:T(8,128)(2,1)S(1)} %collective-permute-done.refs_0_), channel_id=1, source_target_pairs={{4,0},{8,12},{5,1},{9,13},{6,2},{10,14},{7,3},{11,15},{20,16},{24,... | collective-permute-start | bytes 3145736 | tf_op jit(solution)/shard_map/ppermute | solution.py:451
  52.2 35.5 %collective-permute-start.8 = (bf16[512,1024]{1,0:T(8,128)(2,1)S(1)}, bf16[512,1024]{1,0:T(8,128)(2,1)S(1)}, u32[]{:S(2)}, u32[]{:S(2)}) collective-permute-start(bf16[512,1024]{1,0:T(8,128)(2,1)S(1)} %get-tuple-element.95), channel_id=1, source_target_pairs={{4,8},{8,4},{5,9},{9,5},{6,10},{10,6},{7,11},{11,7},{20,24},{24,20... | collective-permute-start | bytes 3145736 | tf_op jit(solution)/shard_map/ppermute | solution.py:453
  53.0 10.0 %collective-permute-start.1 = (f32[64,1024]{1,0:T(8,128)S(1)}, f32[64,1024]{1,0:T(8,128)S(1)}, u32[]{:S(2)}, u32[]{:S(2)}) collective-permute-start(f32[64,1024]{1,0:T(8,128)S(1)} %input_block.1.refs_1_), channel_id=1, source_target_pairs={{0,4},{12,8},{1,5},{13,9},{2,6},{14,10},{3,7},{15,11},{16,20},{28,... | collective-permute-start | bytes 786440 | tf_op jit(solution)/shard_map/ppermute | solution.py:449
  58.8 36.5 %collective-permute-start.12 = (bf16[512,1024]{1,0:T(8,128)(2,1)S(1)}, bf16[512,1024]{1,0:T(8,128)(2,1)S(1)}, u32[]{:S(2)}, u32[]{:S(2)}) collective-permute-start(bf16[512,1024]{1,0:T(8,128)(2,1)S(1)} %collective-permute-done.11.refs_1_), channel_id=1, source_target_pairs={{4,0},{8,12},{5,1},{9,13},{6,2},{10,14},{7,3},{11,15},{20,16},{24,... | collective-permute-start | bytes 3145736 | tf_op jit(solution)/shard_map/ppermute | solution.py:451
  72.9 14.3 %collective-permute-start.6 = (f32[64,1024]{1,0:T(8,128)S(1)}, f32[64,1024]{1,0:T(8,128)S(1)}, u32[]{:S(2)}, u32[]{:S(2)}) collective-permute-start(f32[64,1024]{1,0:T(8,128)S(1)} %side.1.refs_1_), channel_id=1, source_target_pairs={{4,8},{8,4},{5,9},{9,5},{6,10},{10,6},{7,11},{11,7},{20,24},{24,20... | collective-permute-start | bytes 786440 | tf_op jit(solution)/shard_map/ppermute | solution.py:455
  73.5 34.1 %collective-permute-start.14 = (bf16[512,1024]{1,0:T(8,128)(2,1)S(1)}, bf16[512,1024]{1,0:T(8,128)(2,1)S(1)}, u32[]{:S(2)}, u32[]{:S(2)}) collective-permute-start(bf16[512,1024]{1,0:T(8,128)(2,1)S(1)} %get-tuple-element.69), channel_id=1, source_target_pairs={{4,8},{8,4},{5,9},{9,5},{6,10},{10,6},{7,11},{11,7},{20,24},{24,20... | collective-permute-start | bytes 3145736 | tf_op jit(solution)/shard_map/ppermute | solution.py:454
  87.8 19.9 %collective-permute-start.10 = (bf16[256,1024]{1,0:T(8,128)(2,1)S(1)}, bf16[256,1024]{1,0:T(8,128)(2,1)S(1)}, u32[]{:S(2)}, u32[]{:S(2)}) collective-permute-start(bf16[256,1024]{1,0:T(8,128)(2,1)S(1)} %get-tuple-element.56), channel_id=1, source_target_pairs={{4,0},{8,12},{5,1},{9,13},{6,2},{10,14},{7,3},{11,15},{20,16},{24,... | collective-permute-start | bytes 1572872 | tf_op jit(solution)/shard_map/ppermute | solution.py:469
  89.1 29.2 %collective-permute-start.13 = (bf16[256,1024]{1,0:T(8,128)(2,1)S(1)}, bf16[256,1024]{1,0:T(8,128)(2,1)S(1)}, u32[]{:S(2)}, u32[]{:S(2)}) collective-permute-start(bf16[256,1024]{1,0:T(8,128)(2,1)S(1)} %get-tuple-element.63), channel_id=1, source_target_pairs={{4,0},{8,12},{5,1},{9,13},{6,2},{10,14},{7,3},{11,15},{20,16},{24,... | collective-permute-start | bytes 1572872 | tf_op jit(solution)/shard_map/ppermute | solution.py:469
  107.7 21.9 %collective-permute-start.15 = (bf16[256,1024]{1,0:T(8,128)(2,1)S(1)}, bf16[256,1024]{1,0:T(8,128)(2,1)S(1)}, u32[]{:S(2)}, u32[]{:S(2)}) collective-permute-start(bf16[256,1024]{1,0:T(8,128)(2,1)S(1)} %slice.40), channel_id=1, source_target_pairs={{4,0},{8,12},{5,1},{9,13},{6,2},{10,14},{7,3},{11,15},{20,16},{24,... | collective-permute-start | bytes 1572872 | tf_op jit(solution)/shard_map/ppermute | solution.py:469
  118.3 16.9 %collective-permute-start.16 = (bf16[128,1024]{1,0:T(8,128)(2,1)S(1)}, bf16[128,1024]{1,0:T(8,128)(2,1)S(1)}, u32[]{:S(2)}, u32[]{:S(2)}) collective-permute-start(bf16[128,1024]{1,0:T(8,128)(2,1)S(1)} %get-tuple-element.75), channel_id=1, source_target_pairs={{4,0},{8,12},{5,1},{9,13},{6,2},{10,14},{7,3},{11,15},{20,16},{24,... | collective-permute-start | bytes 786440 | tf_op jit(solution)/shard_map/ppermute | solution.py:469
  123.0 17.8 %collective-permute-start.17 = (bf16[128,1024]{1,0:T(8,128)(2,1)S(1)}, bf16[128,1024]{1,0:T(8,128)(2,1)S(1)}, u32[]{:S(2)}, u32[]{:S(2)}) collective-permute-start(bf16[128,1024]{1,0:T(8,128)(2,1)S(1)} %get-tuple-element.80), channel_id=1, source_target_pairs={{4,0},{8,12},{5,1},{9,13},{6,2},{10,14},{7,3},{11,15},{20,16},{24,... | collective-permute-start | bytes 786440 | tf_op jit(solution)/shard_map/ppermute | solution.py:469
  124.3 18.4 %collective-permute-start.7 = (bf16[64,1024]{1,0:T(8,128)(2,1)S(1)}, bf16[64,1024]{1,0:T(8,128)(2,1)S(1)}, u32[]{:S(2)}, u32[]{:S(2)}) collective-permute-start(bf16[64,1024]{1,0:T(8,128)(2,1)S(1)} %convert_element_type.4), channel_id=1, source_target_pairs={{4,0},{8,12},{5,1},{9,13},{6,2},{10,14},{7,3},{11,15},{20,16},{24,... | collective-permute-start | bytes 393224 | tf_op jit(solution)/shard_map/ppermute | solution.py:457
  143.3 4.0 %collective-permute-start.18 = (f32[2,4096]{1,0:T(2,128)S(1)}, f32[2,4096]{1,0:T(2,128)S(1)}, u32[]{:S(2)}, u32[]{:S(2)}) collective-permute-start(f32[2,4096]{1,0:T(2,128)S(1)} %outer_products.1), channel_id=1, source_target_pairs={{0,4},{4,0},{8,12},{12,8},{1,5},{5,1},{9,13},{13,9},{2,6},{6,2},{1... | collective-permute-start | bytes 98312 | tf_op jit(solution)/shard_map/ppermute | solution.py:505
  147.3 4.9 %collective-permute-start.19 = (f32[2,4096]{1,0:T(2,128)S(1)}, f32[2,4096]{1,0:T(2,128)S(1)}, u32[]{:S(2)}, u32[]{:S(2)}) collective-permute-start(f32[2,4096]{1,0:T(2,128)S(1)} %add.34), channel_id=1, source_target_pairs={{0,8},{4,12},{8,0},{12,4},{1,9},{5,13},{9,1},{13,5},{2,10},{6,14},... | collective-permute-start | bytes 98312 | tf_op jit(solution)/shard_map/ppermute | solution.py:505
  152.4 1.3 collective-permute-start.20
  152.5 3.7 %collective-permute-start.22 = (f32[2,256]{1,0:T(2,128)S(1)}, f32[2,256]{1,0:T(2,128)S(1)}, u32[]{:S(2)}, u32[]{:S(2)}) collective-permute-start(f32[2,256]{1,0:T(2,128)S(1)} %scores.1.refs_0_), channel_id=1, source_target_pairs={{0,4},{4,0},{8,12},{12,8},{1,5},{5,1},{9,13},{13,9},{2,6},{6,2},{1... | collective-permute-start | bytes 6152 | tf_op jit(solution)/shard_map/ppermute | solution.py:505
  153.8 4.5 %collective-permute-start.21 = (f32[4,4096]{1,0:T(4,128)S(1)}, f32[4,4096]{1,0:T(4,128)S(1)}, u32[]{:S(2)}, u32[]{:S(2)}) collective-permute-start(f32[4,4096]{1,0:T(4,128)S(1)} %pad_maximum_fusion.1), channel_id=1, source_target_pairs={{0,2},{1,3},{2,0},{3,1},{4,6},{5,7},{6,4},{7,5},{8,10},{9,11},{10,... | collective-permute-start | bytes 196616 | tf_op jit(solution)/shard_map/ppermute | solution.py:505
  156.1 4.5 %collective-permute-start.23 = (f32[2,256]{1,0:T(2,128)S(1)}, f32[2,256]{1,0:T(2,128)S(1)}, u32[]{:S(2)}, u32[]{:S(2)}) collective-permute-start(f32[2,256]{1,0:T(2,128)S(1)} %score_sum.1), channel_id=1, source_target_pairs={{0,8},{4,12},{8,0},{12,4},{1,9},{5,13},{9,1},{13,5},{2,10},{6,14},... | collective-permute-start | bytes 6152 | tf_op jit(solution)/shard_map/ppermute | solution.py:505

commit v18 on v17

--- a/solution.py
+++ b/solution.py
@@ -454,26 +454,25 @@
     end_inner.append(send(after(pair[halves[1]], mid_outer[0], side), perm=inner))
     total = small_kernel(sum_body, "total", where, side, send(side, perm=inner))
     masked = small_kernel(mask_body, "masked", where, total)
-    sent = send(total.astype(jnp.bfloat16), perm=outward)
 
     acc, first = add_block(where, 1, [pair], w_down, after(acc, mid_outer[0]), begun, 2 * grad_out.size * w_down.shape[0])
     acc, second = add_block(where, 2, mid_inner + mid_outer, w_down, acc, first, 1000)
 
-    sizes = [256] * (tokens // 256 - 1) + [128, 128]
+    sizes = [256] * (tokens // 256 - 1) + [128, 64, 64]
     arrived, done = [total, total, total], [first, first, second]
     rights = []
     start = 0
     for n, size in enumerate(sizes):
         h, at = divmod(start, tokens // 2)
-        ahead = arrived[n + 1] if n < 4 else arrived[n]
-        end_outer = send(after(end_inner[h][at : at + size], ahead, done[n]), perm=outward)
+        ahead = arrived[min(n + 1, 4)]
+        end_outer = send(after(end_inner[h][at : at + size], ahead, done[min(n, 4)]), perm=outward)
         arrived.append(end_outer)
         bring = []
         if n + 1 < len(sizes):
             bring.append((gate_pre, start + size, sizes[n + 1]))
         if n == 0:
             bring.append((proj_out.T, 0, PROJ))
-        if n == len(sizes) - 3:
+        if n == len(sizes) - 4:
             bring += [(a, 0, a.shape[0]) for a in (*early, late)]
         place = end_inner[h], at, end_outer, start, kept, acc
         if n == 0:
@@ -481,13 +480,14 @@
             po_near = brought[1]
         else:
             kept, acc, right, *brought = near_block(*place, gate_near, po_near, bring)
-        if n == len(sizes) - 3:
+        if n == len(sizes) - 4:
             *early, late = brought[1:]
         if bring:
             gate_near = brought[0]
         rights.append(right)
         done.append(right)
         start += size
+    sent = send(after(total.astype(jnp.bfloat16), arrived[5]), perm=outward)
     return outer_products(masked, sent, rights), early, late
 
 

time: 162 us -> 165 us (1.019)
  starting transfers between devices: 32.1 us -> 38.9 us
  waiting for transfers between devices: 58.4 us -> 51.9 us
  Pallas kernels: 61.5 us -> 64.1 us
    ppermute x9, starting transfers between devices: 9.14 us -> 14.6 us  [swap(): lax.ppermute(a, axis, [(i, i ^ bit) for i in range(lax.axis_size(axis))])]
    ppermute x6 -> x7, waiting for transfers between devices: 10.7 us -> 7.12 us  [the longest x6 7.11 us: line_of_four(): send(after(end_inner[h][at:at + size], ahead, done[min(n, 4)]), perm=outw...]
    ppermute x9, waiting for transfers between devices: 15.1 us -> 12.3 us  [swap(): lax.ppermute(a, axis, [(i, i ^ bit) for i in range(lax.axis_size(axis))])]
    pallas_call x16 -> x17, Pallas kernels: 61.5 us -> 64.1 us  [call(): pl.pallas_call(body, grid_spec=pltpu.PrefetchScalarGridSpec(num_scalar_pr...]
    ppermute x6 -> x7, starting transfers between devices: 7.92 us -> 9.2 us  [the longest x6 7.92 us: line_of_four(): send(after(end_inner[h][at:at + size], ahead, done[min(n, 4)]), perm=outw...]
  transfers between devices with their start and end apart: 24 -> 25, of which waited for: 13 -> 12; matrix products, arithmetic and copies ran while one was open for 3% -> 3% of each run, Pallas kernels for 38% -> 39%
where the time goes in v18:
time: 165 us; the launch traced here: 164 us
  Pallas kernels  64.1 us (39%)
  waiting for transfers between devices  51.9 us (31%)
  starting transfers between devices  38.9 us (24%)
  local copies, waits for them, and re-layouts  7.49 us (5%)
    pallas_call x17, Pallas kernels, call(): pl.pallas_call(body, grid_spec=pltpu.PrefetchScalarGridSpec(num_scalar_pr...  64.1 us
    ppermute x1, waiting for transfers between devices, line_of_four(): pair = send(grad_out, perm=pairs)  15.4 us
    ppermute x9, starting transfers between devices, swap(): lax.ppermute(a, axis, [(i, i ^ bit) for i in range(lax.axis_size(axis))])  14.6 us
    ppermute x2, waiting for transfers between devices, line_of_four(): mid_outer = [send(after(a, begun), perm=outward) for a in mid_inner]  14.3 us
    ppermute x9, waiting for transfers between devices, swap(): lax.ppermute(a, axis, [(i, i ^ bit) for i in range(lax.axis_size(axis))])  12.3 us
    ppermute x6, starting transfers between devices, line_of_four(): send(after(end_inner[h][at:at + size], ahead, done[min(n, 4)]), perm=outw...  7.92 us
    ppermute x6, waiting for transfers between devices, line_of_four(): send(after(end_inner[h][at:at + size], ahead, done[min(n, 4)]), perm=outw...  7.11 us
    ppermute x1, starting transfers between devices, line_of_four(): from_end = send(after(in_part, mid_inner[0]), perm=inward)  5.83 us
  transfers between devices with their start and end apart: 25, of which 12 were waited for; matrix products, arithmetic and copies ran while one was open for 3% of the time, Pallas kernels for 39%

profile of v18, /device:TPU:0, one launch (start us, length us, event | category | flops | bytes accessed | tf_op | source)
XLA Modules:
  0.0 164.2 jit_solution(7144066468109452352)
XLA Ops:
  0.6 3.1 %collective-permute-start.5 = (bf16[1024,1024]{1,0:T(8,128)(2,1)}, bf16[1024,1024]{1,0:T(8,128)(2,1)}, u32[]{:S(2)}, u32[]{:S(2)}) collective-permute-start(bf16[1024,1024]{1,0:T(8,128)(2,1)} %own), channel_id=1, source_target_pairs={{0,4},{4,0},{8,12},{12,8},{1,5},{5,1},{9,13},{13,9},{2,6},{6,2},{1... | collective-permute-start | bytes 6291464 | tf_op jit(solution)/shard_map/ppermute | solution.py:445
  3.7 3.0 %fusion = (bf16[512,1024]{1,0:T(8,128)(2,1)}, bf16[512,1024]{1,0:T(8,128)(2,1)}) fusion(bf16[1024,1024]{1,0:T(8,128)(2,1)} %own), kind=kLoop, calls=%fused_computation.2 | loop fusion | bytes 4194304 | tf_op jit(solution)/shard_map/slice | solution.py:446
  7.6 1.6 collective-permute-start.3
  9.5 1.6 copy-done.1
  14.1 3.0 %collective-permute-done.3.rest_3_ = f32[256,256]{1,0:T(8,128)} collective-permute-done((f32[256,256]{1,0:T(8,128)}, f32[256,256]{1,0:T(8,128)}, u32[]{:S(2)}, u32[]{:S(2)}) %collective-permute-start.3) | collective-permute-done | bytes 262176 | tf_op jit(solution)/shard_map/ppermute | solution.py:505
  17.1 4.7 %collective-permute-done.4.rest_4_ = f32[256,256]{1,0:T(8,128)} collective-permute-done((f32[256,256]{1,0:T(8,128)}, f32[256,256]{1,0:T(8,128)}, u32[]{:S(2)}, u32[]{:S(2)}) %collective-permute-start.4) | collective-permute-done | bytes 262176 | tf_op jit(solution)/shard_map/ppermute | solution.py:505
  21.8 12.0 %own_block.1 = (f32[1024,3584]{1,0:T(8,128)S(1)}, bf16[1024,3584]{1,0:T(8,128)(2,1)S(1)}, f32[8,128]{1,0:T(8,128)S(1)}) custom-call(s32[9]{0:T(128)S(1)} %stack.43.where.refs_0_, bf16[1024,1024]{1,0:T(8,128)(2,1)S(1)} %copy-done, bf16[3584,4096]{1,0:T(8,128)(2,1)} %refs_4_.1, bf16[3584,4096]{1,0:T(8,128)(2,1)} %refs_4_.1), custom_call_target="tpu_custom_call" | custom-call | flops 1000 | bytes 1000 | tf_op jit(solution)/shard_map/own_block/pallas_call | solution.py:42
  35.1 15.4 %collective-permute-done.5.refs_0_ = bf16[1024,1024]{1,0:T(8,128)(2,1)} collective-permute-done((bf16[1024,1024]{1,0:T(8,128)(2,1)}, bf16[1024,1024]{1,0:T(8,128)(2,1)}, u32[]{:S(2)}, u32[]{:S(2)}) %collective-permute-start.5) | collective-permute-done | bytes 2097184 | tf_op jit(solution)/shard_map/ppermute | solution.py:445
  50.5 1.7 %fusion.1 = (bf16[512,1024]{1,0:T(8,128)(2,1)S(1)}, bf16[512,1024]{1,0:T(8,128)(2,1)S(1)}) fusion(bf16[1024,1024]{1,0:T(8,128)(2,1)} %collective-permute-done.5.refs_0_), kind=kLoop, calls=%fused_computation.3 | loop fusion | bytes 4194304 | tf_op jit(solution)/shard_map/slice | solution.py:453
  53.0 5.8 %collective-permute-start.1 = (f32[64,1024]{1,0:T(8,128)S(1)}, f32[64,1024]{1,0:T(8,128)S(1)}, u32[]{:S(2)}, u32[]{:S(2)}) collective-permute-start(f32[64,1024]{1,0:T(8,128)S(1)} %input_block.1.refs_1_), channel_id=1, source_target_pairs={{0,4},{12,8},{1,5},{13,9},{2,6},{14,10},{3,7},{15,11},{16,20},{28,... | collective-permute-start | bytes 786440 | tf_op jit(solution)/shard_map/ppermute | solution.py:449
  60.1 2.8 %collective-permute-done.1.refs_2_ = f32[64,1024]{1,0:T(8,128)S(1)} collective-permute-done((f32[64,1024]{1,0:T(8,128)S(1)}, f32[64,1024]{1,0:T(8,128)S(1)}, u32[]{:S(2)}, u32[]{:S(2)}) %collective-permute-start.1) | collective-permute-done | bytes 262176 | tf_op jit(solution)/shard_map/ppermute | solution.py:449
  63.5 9.4 %collective-permute-done.7.refs_2_ = bf16[512,1024]{1,0:T(8,128)(2,1)S(1)} collective-permute-done((bf16[512,1024]{1,0:T(8,128)(2,1)S(1)}, bf16[512,1024]{1,0:T(8,128)(2,1)S(1)}, u32[]{:S(2)}, u32[]{:S(2)}) %collective-permute-start.7) | collective-permute-done | bytes 1048608 | tf_op jit(solution)/shard_map/ppermute | solution.py:451
  74.3 12.9 %add_block_1.1 = (f32[1024,3584]{1,0:T(8,128)S(1)}, f32[8,128]{1,0:T(8,128)S(1)}) custom-call(s32[9]{0:T(128)S(1)} %stack.43.where.refs_0_, bf16[1024,1024]{1,0:T(8,128)(2,1)} %collective-permute-done.5.refs_0_, bf16[3584,4096]{1,0:T(8,128)(2,1)} %refs_4_.1, f32[1024,3584]{1,0:T(8,128)S(1)} %get-tuple-element.61.refs_2_, ...), custom_call_target="tpu_custom_call", output_to_operand_aliasing={{0}: (3, {})} | custom-call | flops 7516192768 | bytes 1000 | tf_op jit(solution)/shard_map/add_block_1/pallas_call | solution.py:42
  87.8 1.3 collective-permute-start.10
  90.4 4.9 %collective-permute-done.12.refs_3_ = bf16[512,1024]{1,0:T(8,128)(2,1)S(1)} collective-permute-done((bf16[512,1024]{1,0:T(8,128)(2,1)S(1)}, bf16[512,1024]{1,0:T(8,128)(2,1)S(1)}, u32[]{:S(2)}, u32[]{:S(2)}) %collective-permute-start.12) | collective-permute-done | bytes 1048608 | tf_op jit(solution)/shard_map/ppermute | solution.py:451
  95.3 12.3 %add_block_2.1 = (f32[1024,3584]{1,0:T(8,128)S(1)}, f32[8,128]{1,0:T(8,128)S(1)}) custom-call(s32[9]{0:T(128)S(1)} %stack.43.where.refs_0_, bf16[512,1024]{1,0:T(8,128)(2,1)S(1)} %collective-permute-done.refs_0_, bf16[512,1024]{1,0:T(8,128)(2,1)S(1)} %collective-permute-done.11.refs_1_, ...), custom_call_target="tpu_custom_call", output_to_operand_aliasing={{0}: (6, {})} | custom-call | flops 1000 | bytes 1000 | tf_op jit(solution)/shard_map/add_block_2/pallas_call | solution.py:42
  109.1 6.1 %last_block.1 = (bf16[1024,3584]{1,0:T(8,128)(2,1)S(1)}, f32[1024,3584]{1,0:T(8,128)S(1)}, f32[256,64]{1,0:T(8,128)S(1)}, bf16[256,3584]{1,0:T(8,128)(2,1)S(1)}, bf16[64,3584]{1,0:T(8,128)(2,1)S(1)}) custom-call(bf16[512,1024]{1,0:T(8,128)(2,1)S(1)} %collective-permute-done.9.inner, ...), custom_call_target="tpu_custom_call", output_to_operand_aliasing={{0}: (2, {}), {1}: (3, {})} | custom-call | flops 1000 | bytes 1000 | tf_op jit(solution)/shard_map/last_block/pallas_call | solution.py:42
  115.2 3.2 %collective-permute-done.15.outer = bf16[256,1024]{1,0:T(8,128)(2,1)S(1)} collective-permute-done((bf16[256,1024]{1,0:T(8,128)(2,1)S(1)}, bf16[256,1024]{1,0:T(8,128)(2,1)S(1)}, u32[]{:S(2)}, u32[]{:S(2)}) %collective-permute-start.15) | collective-permute-done | bytes 524320 | tf_op jit(solution)/shard_map/ppermute | solution.py:468
  118.3 1.5 collective-permute-start.16
  119.8 3.2 %near_block.5 = (bf16[1024,3584]{1,0:T(8,128)(2,1)S(1)}, f32[1024,3584]{1,0:T(8,128)S(1)}, f32[256,64]{1,0:T(8,128)S(1)}, bf16[256,3584]{1,0:T(8,128)(2,1)S(1)}) custom-call(bf16[512,1024]{1,0:T(8,128)(2,1)S(1)} %collective-permute-done.9.inner, bf16[256,1024]{1,0:T(8,128)(2,1)S(1)} %collective-permute-done.15.outer, ...), custom_call_target="tpu_custom_call", output_to_operand_aliasing={{0}: (2, {}), {1}: (3, {})} | custom-call | flops 1000 | bytes 1000 | tf_op jit(solution)/shard_map/near_block/pallas_call | solution.py:42
  125.6 3.9 %collective-permute-done.13.outer = bf16[256,1024]{1,0:T(8,128)(2,1)S(1)} collective-permute-done((bf16[256,1024]{1,0:T(8,128)(2,1)S(1)}, bf16[256,1024]{1,0:T(8,128)(2,1)S(1)}, u32[]{:S(2)}, u32[]{:S(2)}) %collective-permute-start.13) | collective-permute-done | bytes 524320 | tf_op jit(solution)/shard_map/ppermute | solution.py:468
  131.5 5.2 %near_block.6 = (bf16[1024,3584]{1,0:T(8,128)(2,1)S(1)}, f32[1024,3584]{1,0:T(8,128)S(1)}, f32[256,64]{1,0:T(8,128)S(1)}, bf16[128,3584]{1,0:T(8,128)(2,1)S(1)},...) custom-call(bf16[512,1024]{1,0:T(8,128)(2,1)S(1)} %collective-permut, ...), custom_call_target="tpu_custom_call", output_to_operand_aliasing={{0}: (2, {}), {1}: (3, {})} | custom-call | flops 1000 | bytes 1000 | tf_op jit(solution)/shard_map/near_block/pallas_call | solution.py:42
  136.6 1.9 %near_block.7 = (bf16[1024,3584]{1,0:T(8,128)(2,1)S(1)}, f32[1024,3584]{1,0:T(8,128)S(1)}, f32[128,64]{1,0:T(8,128)S(1)}, bf16[64,3584]{1,0:T(8,128)(2,1)S(1)}) custom-call(bf16[512,1024]{1,0:T(8,128)(2,1)S(1)} %collective-permute-done.8.inner, bf16[128,1024]{1,0:T(8,128)(2,1)S(1)} %collective-permute-done.16.outer, ...), custom_call_target="tpu_custom_call", output_to_operand_aliasing={{0}: (2, {}), {1}: (3, {})} | custom-call | flops 1000 | bytes 1000 | tf_op jit(solution)/shard_map/near_block/pallas_call | solution.py:42
  138.6 2.6 %near_block.8 = (bf16[1024,3584]{1,0:T(8,128)(2,1)S(1)}, f32[1024,3584]{1,0:T(8,128)S(1)}, f32[64,64]{1,0:T(8,128)S(1)}, bf16[64,3584]{1,0:T(8,128)(2,1)S(1)}) custom-call(bf16[512,1024]{1,0:T(8,128)(2,1)S(1)} %collective-permute-done.8.inner, bf16[64,1024]{1,0:T(8,128)(2,1)S(1)} %collective-permute-done.17.outer, ...), custom_call_target="tpu_custom_call", output_to_operand_aliasing={{0}: (2, {}), {1}: (3, {})} | custom-call | flops 1000 | bytes 1000 | tf_op jit(solution)/shard_map/near_block/pallas_call | solution.py:42
  141.2 1.9 %near_block.9 = (bf16[1024,3584]{1,0:T(8,128)(2,1)S(1)}, f32[1024,3584]{1,0:T(8,128)S(1)}, f32[64,64]{1,0:T(8,128)S(1)}) custom-call(bf16[512,1024]{1,0:T(8,128)(2,1)S(1)} %collective-permute-done.8.inner, bf16[64,1024]{1,0:T(8,128)(2,1)S(1)} %collective-permute-done.18.outer, ...), custom_call_target="tpu_custom_call", output_to_operand_aliasing={{0}: (2, {}), {1}: (3, {})} | custom-call | flops 1000 | bytes 1000 | tf_op jit(solution)/shard_map/near_block/pallas_call | solution.py:42
  143.6 2.7 %collective-permute-start.19 = (f32[2,4096]{1,0:T(2,128)S(1)}, f32[2,4096]{1,0:T(2,128)S(1)}, u32[]{:S(2)}, u32[]{:S(2)}) collective-permute-start(f32[2,4096]{1,0:T(2,128)S(1)} %outer_products.1), channel_id=1, source_target_pairs={{0,4},{4,0},{8,12},{12,8},{1,5},{5,1},{9,13},{13,9},{2,6},{6,2},{1... | collective-permute-start | bytes 98312 | tf_op jit(solution)/shard_map/ppermute | solution.py:505
  146.3 1.9 %collective-permute-done.19 = f32[2,4096]{1,0:T(2,128)S(1)} collective-permute-done((f32[2,4096]{1,0:T(2,128)S(1)}, f32[2,4096]{1,0:T(2,128)S(1)}, u32[]{:S(2)}, u32[]{:S(2)}) %collective-permute-start.19) | collective-permute-done | bytes 32800 | tf_op jit(solution)/shard_map/ppermute | solution.py:505
  148.2 4.2 %collective-permute-start.20 = (f32[2,4096]{1,0:T(2,128)S(1)}, f32[2,4096]{1,0:T(2,128)S(1)}, u32[]{:S(2)}, u32[]{:S(2)}) collective-permute-start(f32[2,4096]{1,0:T(2,128)S(1)} %add.34), channel_id=1, source_target_pairs={{0,8},{4,12},{8,0},{12,4},{1,9},{5,13},{9,1},{13,5},{2,10},{6,14},... | collective-permute-start | bytes 98312 | tf_op jit(solution)/shard_map/ppermute | solution.py:505
  152.4 1.9 %collective-permute-done.20 = f32[2,4096]{1,0:T(2,128)S(1)} collective-permute-done((f32[2,4096]{1,0:T(2,128)S(1)}, f32[2,4096]{1,0:T(2,128)S(1)}, u32[]{:S(2)}, u32[]{:S(2)}) %collective-permute-start.20) | collective-permute-done | bytes 32800 | tf_op jit(solution)/shard_map/ppermute | solution.py:505
  155.9 1.9 %collective-permute-start.22 = (f32[4,4096]{1,0:T(4,128)S(1)}, f32[4,4096]{1,0:T(4,128)S(1)}, u32[]{:S(2)}, u32[]{:S(2)}) collective-permute-start(f32[4,4096]{1,0:T(4,128)S(1)} %pad_maximum_fusion.1), channel_id=1, source_target_pairs={{0,2},{1,3},{2,0},{3,1},{4,6},{5,7},{6,4},{7,5},{8,10},{9,11},{10,... | collective-permute-start | bytes 196616 | tf_op jit(solution)/shard_map/ppermute | solution.py:505
  158.3 2.9 %collective-permute-start.24 = (f32[2,256]{1,0:T(2,128)S(1)}, f32[2,256]{1,0:T(2,128)S(1)}, u32[]{:S(2)}, u32[]{:S(2)}) collective-permute-start(f32[2,256]{1,0:T(2,128)S(1)} %score_sum.1), channel_id=1, source_target_pairs={{0,8},{4,12},{8,0},{12,4},{1,9},{5,13},{9,1},{13,5},{2,10},{6,14},... | collective-permute-start | bytes 6152 | tf_op jit(solution)/shard_map/ppermute | solution.py:505
  161.2 2.3 %hessian_update.1 = f32[256,4096]{1,0:T(8,128)} custom-call(f32[8,4096]{1,0:T(8,128)S(1)} %pad_maximum_fusion.grads, f32[256,4096]{1,0:T(8,128)S(1)} %get-tuple-element.103.hessian), custom_call_target="tpu_custom_call" | custom-call | flops 1000 | bytes 1000 | tf_op jit(solution)/shard_map/hessian_update/pallas_call | solution.py:42
  (56 shorter events, 20.4 us)
Async XLA Ops:
  0.6 21.1 %copy-start = (bf16[1024,1024]{1,0:T(8,128)(2,1)S(1)}, bf16[1024,1024]{1,0:T(8,128)(2,1)}, u32[]{:S(2)}) copy-start(bf16[1024,1024]{1,0:T(8,128)(2,1)} %own) | copy-start | bytes 6291460
  0.6 49.9 %collective-permute-start.5 = (bf16[1024,1024]{1,0:T(8,128)(2,1)}, bf16[1024,1024]{1,0:T(8,128)(2,1)}, u32[]{:S(2)}, u32[]{:S(2)}) collective-permute-start(bf16[1024,1024]{1,0:T(8,128)(2,1)} %own), channel_id=1, source_target_pairs={{0,4},{4,0},{8,12},{12,8},{1,5},{5,1},{9,13},{13,9},{2,6},{6,2},{1... | collective-permute-start | bytes 6291464 | tf_op jit(solution)/shard_map/ppermute | solution.py:445
  6.8 27.0 %collective-permute-start = (bf16[512,1024]{1,0:T(8,128)(2,1)}, bf16[512,1024]{1,0:T(8,128)(2,1)S(1)}, u32[]{:S(2)}, u32[]{:S(2)}) collective-permute-start(bf16[512,1024]{1,0:T(8,128)(2,1)} %get-tuple-element.107), channel_id=1, source_target_pairs={{4,8},{8,4},{5,9},{9,5},{6,10},{10,6},{7,11},{11,7},{20,24},{24,20... | collective-permute-start | bytes 3145736 | tf_op jit(solution)/shard_map/ppermute | solution.py:447
  7.5 5.8 %collective-permute-start.2 = (f32[256,256]{1,0:T(8,128)}, f32[256,256]{1,0:T(8,128)S(1)}, u32[]{:S(2)}, u32[]{:S(2)}) collective-permute-start(f32[256,256]{1,0:T(8,128)} %rest_1_.1), channel_id=1, source_target_pairs={{0,1},{1,0},{2,3},{3,2},{4,5},{5,4},{6,7},{7,6},{8,9},{9,8},{10,11... | collective-permute-start | bytes 786440 | tf_op jit(solution)/shard_map/ppermute | solution.py:505
  7.6 9.5 %collective-permute-start.3 = (f32[256,256]{1,0:T(8,128)}, f32[256,256]{1,0:T(8,128)}, u32[]{:S(2)}, u32[]{:S(2)}) collective-permute-start(f32[256,256]{1,0:T(8,128)} %rest_1_.1), channel_id=1, source_target_pairs={{0,2},{1,3},{2,0},{3,1},{4,6},{5,7},{6,4},{7,5},{8,10},{9,11},{10,... | collective-permute-start | bytes 786440 | tf_op jit(solution)/shard_map/ppermute | solution.py:505
  9.1 12.6 %collective-permute-start.4 = (f32[256,256]{1,0:T(8,128)}, f32[256,256]{1,0:T(8,128)}, u32[]{:S(2)}, u32[]{:S(2)}) collective-permute-start(f32[256,256]{1,0:T(8,128)} %rest_1_.1), channel_id=1, source_target_pairs={{0,3},{1,2},{2,1},{3,0},{4,7},{5,6},{6,5},{7,4},{8,11},{9,10},{10,... | collective-permute-start | bytes 786440 | tf_op jit(solution)/shard_map/ppermute | solution.py:505
  9.5 1.6 copy-start.1
  11.1 0.9 copy-start.2
  13.3 20.4 %copy-start.3 = (f32[256,256]{1,0:T(8,128)}, f32[256,256]{1,0:T(8,128)S(1)}, u32[]{:S(2)}) copy-start(f32[256,256]{1,0:T(8,128)S(1)} %collective-permute-done.2.rest_2_) | copy-start | bytes 786436
  13.3 45.5 %collective-permute-start.11 = (bf16[512,1024]{1,0:T(8,128)(2,1)}, bf16[512,1024]{1,0:T(8,128)(2,1)S(1)}, u32[]{:S(2)}, u32[]{:S(2)}) collective-permute-start(bf16[512,1024]{1,0:T(8,128)(2,1)} %get-tuple-element.106), channel_id=1, source_target_pairs={{4,8},{8,4},{5,9},{9,5},{6,10},{10,6},{7,11},{11,7},{20,24},{24,20... | collective-permute-start | bytes 3145736 | tf_op jit(solution)/shard_map/ppermute | solution.py:447
  33.8 39.1 %collective-permute-start.7 = (bf16[512,1024]{1,0:T(8,128)(2,1)S(1)}, bf16[512,1024]{1,0:T(8,128)(2,1)S(1)}, u32[]{:S(2)}, u32[]{:S(2)}) collective-permute-start(bf16[512,1024]{1,0:T(8,128)(2,1)S(1)} %collective-permute-done.refs_0_), channel_id=1, source_target_pairs={{4,0},{8,12},{5,1},{9,13},{6,2},{10,14},{7,3},{11,15},{20,16},{24,... | collective-permute-start | bytes 3145736 | tf_op jit(solution)/shard_map/ppermute | solution.py:451
  52.2 35.5 %collective-permute-start.9 = (bf16[512,1024]{1,0:T(8,128)(2,1)S(1)}, bf16[512,1024]{1,0:T(8,128)(2,1)S(1)}, u32[]{:S(2)}, u32[]{:S(2)}) collective-permute-start(bf16[512,1024]{1,0:T(8,128)(2,1)S(1)} %get-tuple-element.108), channel_id=1, source_target_pairs={{4,8},{8,4},{5,9},{9,5},{6,10},{10,6},{7,11},{11,7},{20,24},{24,20... | collective-permute-start | bytes 3145736 | tf_op jit(solution)/shard_map/ppermute | solution.py:453
  53.0 10.0 %collective-permute-start.1 = (f32[64,1024]{1,0:T(8,128)S(1)}, f32[64,1024]{1,0:T(8,128)S(1)}, u32[]{:S(2)}, u32[]{:S(2)}) collective-permute-start(f32[64,1024]{1,0:T(8,128)S(1)} %input_block.1.refs_1_), channel_id=1, source_target_pairs={{0,4},{12,8},{1,5},{13,9},{2,6},{14,10},{3,7},{15,11},{16,20},{28,... | collective-permute-start | bytes 786440 | tf_op jit(solution)/shard_map/ppermute | solution.py:449
  58.8 36.5 %collective-permute-start.12 = (bf16[512,1024]{1,0:T(8,128)(2,1)S(1)}, bf16[512,1024]{1,0:T(8,128)(2,1)S(1)}, u32[]{:S(2)}, u32[]{:S(2)}) collective-permute-start(bf16[512,1024]{1,0:T(8,128)(2,1)S(1)} %collective-permute-done.11.refs_1_), channel_id=1, source_target_pairs={{4,0},{8,12},{5,1},{9,13},{6,2},{10,14},{7,3},{11,15},{20,16},{24,... | collective-permute-start | bytes 3145736 | tf_op jit(solution)/shard_map/ppermute | solution.py:451
  72.9 14.3 %collective-permute-start.6 = (f32[64,1024]{1,0:T(8,128)S(1)}, f32[64,1024]{1,0:T(8,128)S(1)}, u32[]{:S(2)}, u32[]{:S(2)}) collective-permute-start(f32[64,1024]{1,0:T(8,128)S(1)} %side.1.refs_1_), channel_id=1, source_target_pairs={{4,8},{8,4},{5,9},{9,5},{6,10},{10,6},{7,11},{11,7},{20,24},{24,20... | collective-permute-start | bytes 786440 | tf_op jit(solution)/shard_map/ppermute | solution.py:455
  73.5 34.1 %collective-permute-start.8 = (bf16[512,1024]{1,0:T(8,128)(2,1)S(1)}, bf16[512,1024]{1,0:T(8,128)(2,1)S(1)}, u32[]{:S(2)}, u32[]{:S(2)}) collective-permute-start(bf16[512,1024]{1,0:T(8,128)(2,1)S(1)} %get-tuple-element.59), channel_id=1, source_target_pairs={{4,8},{8,4},{5,9},{9,5},{6,10},{10,6},{7,11},{11,7},{20,24},{24,20... | collective-permute-start | bytes 3145736 | tf_op jit(solution)/shard_map/ppermute | solution.py:454
  87.8 19.9 %collective-permute-start.10 = (bf16[256,1024]{1,0:T(8,128)(2,1)S(1)}, bf16[256,1024]{1,0:T(8,128)(2,1)S(1)}, u32[]{:S(2)}, u32[]{:S(2)}) collective-permute-start(bf16[256,1024]{1,0:T(8,128)(2,1)S(1)} %get-tuple-element.63), channel_id=1, source_target_pairs={{4,0},{8,12},{5,1},{9,13},{6,2},{10,14},{7,3},{11,15},{20,16},{24,... | collective-permute-start | bytes 1572872 | tf_op jit(solution)/shard_map/ppermute | solution.py:468
  89.1 29.2 %collective-permute-start.15 = (bf16[256,1024]{1,0:T(8,128)(2,1)S(1)}, bf16[256,1024]{1,0:T(8,128)(2,1)S(1)}, u32[]{:S(2)}, u32[]{:S(2)}) collective-permute-start(bf16[256,1024]{1,0:T(8,128)(2,1)S(1)} %get-tuple-element.72), channel_id=1, source_target_pairs={{4,0},{8,12},{5,1},{9,13},{6,2},{10,14},{7,3},{11,15},{20,16},{24,... | collective-permute-start | bytes 1572872 | tf_op jit(solution)/shard_map/ppermute | solution.py:468
  107.7 21.9 %collective-permute-start.13 = (bf16[256,1024]{1,0:T(8,128)(2,1)S(1)}, bf16[256,1024]{1,0:T(8,128)(2,1)S(1)}, u32[]{:S(2)}, u32[]{:S(2)}) collective-permute-start(bf16[256,1024]{1,0:T(8,128)(2,1)S(1)} %slice.41), channel_id=1, source_target_pairs={{4,0},{8,12},{5,1},{9,13},{6,2},{10,14},{7,3},{11,15},{20,16},{24,... | collective-permute-start | bytes 1572872 | tf_op jit(solution)/shard_map/ppermute | solution.py:468
  118.3 18.3 %collective-permute-start.16 = (bf16[128,1024]{1,0:T(8,128)(2,1)S(1)}, bf16[128,1024]{1,0:T(8,128)(2,1)S(1)}, u32[]{:S(2)}, u32[]{:S(2)}) collective-permute-start(bf16[128,1024]{1,0:T(8,128)(2,1)S(1)} %slice.45), channel_id=1, source_target_pairs={{4,0},{8,12},{5,1},{9,13},{6,2},{10,14},{7,3},{11,15},{20,16},{24,... | collective-permute-start | bytes 786440 | tf_op jit(solution)/shard_map/ppermute | solution.py:468
  123.0 15.5 %collective-permute-start.17 = (bf16[64,1024]{1,0:T(8,128)(2,1)S(1)}, bf16[64,1024]{1,0:T(8,128)(2,1)S(1)}, u32[]{:S(2)}, u32[]{:S(2)}) collective-permute-start(bf16[64,1024]{1,0:T(8,128)(2,1)S(1)} %get-tuple-element.87), channel_id=1, source_target_pairs={{4,0},{8,12},{5,1},{9,13},{6,2},{10,14},{7,3},{11,15},{20,16},{24,... | collective-permute-start | bytes 393224 | tf_op jit(solution)/shard_map/ppermute | solution.py:468
  124.3 16.8 %collective-permute-start.18 = (bf16[64,1024]{1,0:T(8,128)(2,1)S(1)}, bf16[64,1024]{1,0:T(8,128)(2,1)S(1)}, u32[]{:S(2)}, u32[]{:S(2)}) collective-permute-start(bf16[64,1024]{1,0:T(8,128)(2,1)S(1)} %get-tuple-element.92), channel_id=1, source_target_pairs={{4,0},{8,12},{5,1},{9,13},{6,2},{10,14},{7,3},{11,15},{20,16},{24,... | collective-permute-start | bytes 393224 | tf_op jit(solution)/shard_map/ppermute | solution.py:468
  129.6 13.5 %collective-permute-start.14 = (bf16[64,1024]{1,0:T(8,128)(2,1)S(1)}, bf16[64,1024]{1,0:T(8,128)(2,1)S(1)}, u32[]{:S(2)}, u32[]{:S(2)}) collective-permute-start(bf16[64,1024]{1,0:T(8,128)(2,1)S(1)} %convert_element_type.4), channel_id=1, source_target_pairs={{4,0},{8,12},{5,1},{9,13},{6,2},{10,14},{7,3},{11,15},{20,16},{24,... | collective-permute-start | bytes 393224 | tf_op jit(solution)/shard_map/ppermute | solution.py:490
  143.6 4.6 %collective-permute-start.19 = (f32[2,4096]{1,0:T(2,128)S(1)}, f32[2,4096]{1,0:T(2,128)S(1)}, u32[]{:S(2)}, u32[]{:S(2)}) collective-permute-start(f32[2,4096]{1,0:T(2,128)S(1)} %outer_products.1), channel_id=1, source_target_pairs={{0,4},{4,0},{8,12},{12,8},{1,5},{5,1},{9,13},{13,9},{2,6},{6,2},{1... | collective-permute-start | bytes 98312 | tf_op jit(solution)/shard_map/ppermute | solution.py:505
  148.2 6.1 %collective-permute-start.20 = (f32[2,4096]{1,0:T(2,128)S(1)}, f32[2,4096]{1,0:T(2,128)S(1)}, u32[]{:S(2)}, u32[]{:S(2)}) collective-permute-start(f32[2,4096]{1,0:T(2,128)S(1)} %add.34), channel_id=1, source_target_pairs={{0,8},{4,12},{8,0},{12,4},{1,9},{5,13},{9,1},{13,5},{2,10},{6,14},... | collective-permute-start | bytes 98312 | tf_op jit(solution)/shard_map/ppermute | solution.py:505
  154.6 1.2 collective-permute-start.21
  154.6 3.7 %collective-permute-start.23 = (f32[2,256]{1,0:T(2,128)S(1)}, f32[2,256]{1,0:T(2,128)S(1)}, u32[]{:S(2)}, u32[]{:S(2)}) collective-permute-start(f32[2,256]{1,0:T(2,128)S(1)} %scores.1.refs_0_), channel_id=1, source_target_pairs={{0,4},{4,0},{8,12},{12,8},{1,5},{5,1},{9,13},{13,9},{2,6},{6,2},{1... | collective-permute-start | bytes 6152 | tf_op jit(solution)/shard_map/ppermute | solution.py:505
  155.9 5.3 %collective-permute-start.22 = (f32[4,4096]{1,0:T(4,128)S(1)}, f32[4,4096]{1,0:T(4,128)S(1)}, u32[]{:S(2)}, u32[]{:S(2)}) collective-permute-start(f32[4,4096]{1,0:T(4,128)S(1)} %pad_maximum_fusion.1), channel_id=1, source_target_pairs={{0,2},{1,3},{2,0},{3,1},{4,6},{5,7},{6,4},{7,5},{8,10},{9,11},{10,... | collective-permute-start | bytes 196616 | tf_op jit(solution)/shard_map/ppermute | solution.py:505
  158.3 5.3 %collective-permute-start.24 = (f32[2,256]{1,0:T(2,128)S(1)}, f32[2,256]{1,0:T(2,128)S(1)}, u32[]{:S(2)}, u32[]{:S(2)}) collective-permute-start(f32[2,256]{1,0:T(2,128)S(1)} %score_sum.1), channel_id=1, source_target_pairs={{0,8},{4,12},{8,0},{12,4},{1,9},{5,13},{9,1},{13,5},{2,10},{6,14},... | collective-permute-start | bytes 6152 | tf_op jit(solution)/shard_map/ppermute | solution.py:505

commit v19 on v17

--- a/solution.py
+++ b/solution.py
@@ -399,14 +399,14 @@
 
 def update_body(scale, grads, hessian, out, new, out_sems):
     parts, _, width = new.shape
-    high, middle, low = pieces(grads[:, my_part(0, new.shape[1])])
+    high, middle, low = pieces(grads[:, my_part(0, new.shape[1])] * scale)
     left = jnp.concatenate([high, high, middle, middle, high, low], axis=0).T
     writes = []
     for t in range(parts):
         span = pl.ds(t * width, width)
         high, middle, low = pieces(grads[:, span])
         right = jnp.concatenate([high, middle, high, middle, low, high], axis=0)
-        new[t] = hessian[:, span] + dot(left, right) * scale
+        new[t] = hessian[:, span] + dot(left, right)
         writes.append(pltpu.make_async_copy(new.at[t], out.at[:, span], out_sems.at[t]))
         writes[t].start()
     for write in writes:
@@ -510,7 +510,7 @@
 
 
 def xor_sum(a, axis):
-    for bit in bits(axis):
+    for bit in reversed(bits(axis)):
         a = a + swap(a, axis, bit)
     return a
 

time: 162 us -> 162 us (level)
  no operation moved by 1% of the time
where the time goes in v19:
time: 162 us; the launch traced here: 161 us
  Pallas kernels  61.5 us (38%)
  waiting for transfers between devices  57.7 us (36%)
  starting transfers between devices  32.9 us (20%)
  local copies, waits for them, and re-layouts  7.48 us (5%)
    pallas_call x16, Pallas kernels, call(): pl.pallas_call(body, grid_spec=pltpu.PrefetchScalarGridSpec(num_scalar_pr...  61.5 us
    ppermute x1, waiting for transfers between devices, line_of_four(): pair = send(grad_out, perm=pairs)  15.4 us
    ppermute x9, waiting for transfers between devices, swap(): lax.ppermute(a, axis, [(i, i ^ bit) for i in range(lax.axis_size(axis))])  14.4 us
    ppermute x2, waiting for transfers between devices, line_of_four(): mid_outer = [send(after(a, begun), perm=outward) for a in mid_inner]  14.3 us
    ppermute x5, waiting for transfers between devices, line_of_four(): send(after(end_inner[h][at:at + size], ahead, done[n]), perm=outward)  10.7 us
    ppermute x9, starting transfers between devices, swap(): lax.ppermute(a, axis, [(i, i ^ bit) for i in range(lax.axis_size(axis))])  9.87 us
    ppermute x5, starting transfers between devices, line_of_four(): send(after(end_inner[h][at:at + size], ahead, done[n]), perm=outward)  6.63 us
    ppermute x1, starting transfers between devices, line_of_four(): from_end = send(after(in_part, mid_inner[0]), perm=inward)  5.83 us
  transfers between devices with their start and end apart: 24, of which 13 were waited for; matrix products, arithmetic and copies ran while one was open for 3% of the time, Pallas kernels for 38%

profile of v19, /device:TPU:0, one launch (start us, length us, event | category | flops | bytes accessed | tf_op | source)
XLA Modules:
  0.0 161.2 jit_solution(18248414813641648598)
XLA Ops:
  0.6 3.1 %collective-permute-start.5 = (bf16[1024,1024]{1,0:T(8,128)(2,1)}, bf16[1024,1024]{1,0:T(8,128)(2,1)}, u32[]{:S(2)}, u32[]{:S(2)}) collective-permute-start(bf16[1024,1024]{1,0:T(8,128)(2,1)} %own), channel_id=1, source_target_pairs={{0,4},{4,0},{8,12},{12,8},{1,5},{5,1},{9,13},{13,9},{2,6},{6,2},{1... | collective-permute-start | bytes 6291464 | tf_op jit(solution)/shard_map/ppermute | solution.py:445
  3.7 3.0 %fusion.1 = (bf16[512,1024]{1,0:T(8,128)(2,1)}, bf16[512,1024]{1,0:T(8,128)(2,1)}) fusion(bf16[1024,1024]{1,0:T(8,128)(2,1)} %own), kind=kLoop, calls=%fused_computation.3 | loop fusion | bytes 4194304 | tf_op jit(solution)/shard_map/slice | solution.py:446
  7.6 1.6 collective-permute-start.3
  9.5 1.6 copy-done.1
  12.0 1.3 input_block.1.refs_1_
  14.1 3.0 %collective-permute-done.3.rest_3_ = f32[256,256]{1,0:T(8,128)} collective-permute-done((f32[256,256]{1,0:T(8,128)}, f32[256,256]{1,0:T(8,128)}, u32[]{:S(2)}, u32[]{:S(2)}) %collective-permute-start.3) | collective-permute-done | bytes 262176 | tf_op jit(solution)/shard_map/ppermute | solution.py:505
  17.1 4.7 %collective-permute-done.4.rest_4_ = f32[256,256]{1,0:T(8,128)} collective-permute-done((f32[256,256]{1,0:T(8,128)}, f32[256,256]{1,0:T(8,128)}, u32[]{:S(2)}, u32[]{:S(2)}) %collective-permute-start.4) | collective-permute-done | bytes 262176 | tf_op jit(solution)/shard_map/ppermute | solution.py:505
  21.8 12.0 %own_block.1 = (f32[1024,3584]{1,0:T(8,128)S(1)}, bf16[1024,3584]{1,0:T(8,128)(2,1)S(1)}, f32[8,128]{1,0:T(8,128)S(1)}) custom-call(s32[9]{0:T(128)S(1)} %stack.43.where.refs_0_, bf16[1024,1024]{1,0:T(8,128)(2,1)S(1)} %copy-done, bf16[3584,4096]{1,0:T(8,128)(2,1)} %refs_4_.1, bf16[3584,4096]{1,0:T(8,128)(2,1)} %refs_4_.1), custom_call_target="tpu_custom_call" | custom-call | flops 1000 | bytes 1000 | tf_op jit(solution)/shard_map/own_block/pallas_call | solution.py:42
  33.8 1.3 collective-permute-start.9
  35.1 15.4 %collective-permute-done.5.refs_0_ = bf16[1024,1024]{1,0:T(8,128)(2,1)} collective-permute-done((bf16[1024,1024]{1,0:T(8,128)(2,1)}, bf16[1024,1024]{1,0:T(8,128)(2,1)}, u32[]{:S(2)}, u32[]{:S(2)}) %collective-permute-start.5) | collective-permute-done | bytes 2097184 | tf_op jit(solution)/shard_map/ppermute | solution.py:445
  50.5 1.7 %fusion = (bf16[512,1024]{1,0:T(8,128)(2,1)S(1)}, bf16[512,1024]{1,0:T(8,128)(2,1)S(1)}) fusion(bf16[1024,1024]{1,0:T(8,128)(2,1)} %collective-permute-done.5.refs_0_), kind=kLoop, calls=%fused_computation.2 | loop fusion | bytes 4194304 | tf_op jit(solution)/shard_map/slice | solution.py:454
  53.0 5.8 %collective-permute-start.1 = (f32[64,1024]{1,0:T(8,128)S(1)}, f32[64,1024]{1,0:T(8,128)S(1)}, u32[]{:S(2)}, u32[]{:S(2)}) collective-permute-start(f32[64,1024]{1,0:T(8,128)S(1)} %input_block.1.refs_1_), channel_id=1, source_target_pairs={{0,4},{12,8},{1,5},{13,9},{2,6},{14,10},{3,7},{15,11},{16,20},{28,... | collective-permute-start | bytes 786440 | tf_op jit(solution)/shard_map/ppermute | solution.py:449
  60.1 2.8 %collective-permute-done.1.refs_2_ = f32[64,1024]{1,0:T(8,128)S(1)} collective-permute-done((f32[64,1024]{1,0:T(8,128)S(1)}, f32[64,1024]{1,0:T(8,128)S(1)}, u32[]{:S(2)}, u32[]{:S(2)}) %collective-permute-start.1) | collective-permute-done | bytes 262176 | tf_op jit(solution)/shard_map/ppermute | solution.py:449
  63.5 9.4 %collective-permute-done.9.refs_2_ = bf16[512,1024]{1,0:T(8,128)(2,1)S(1)} collective-permute-done((bf16[512,1024]{1,0:T(8,128)(2,1)S(1)}, bf16[512,1024]{1,0:T(8,128)(2,1)S(1)}, u32[]{:S(2)}, u32[]{:S(2)}) %collective-permute-start.9) | collective-permute-done | bytes 1048608 | tf_op jit(solution)/shard_map/ppermute | solution.py:451
  74.3 12.9 %add_block_1.1 = (f32[1024,3584]{1,0:T(8,128)S(1)}, f32[8,128]{1,0:T(8,128)S(1)}) custom-call(s32[9]{0:T(128)S(1)} %stack.43.where.refs_0_, bf16[1024,1024]{1,0:T(8,128)(2,1)} %collective-permute-done.5.refs_0_, bf16[3584,4096]{1,0:T(8,128)(2,1)} %refs_4_.1, f32[1024,3584]{1,0:T(8,128)S(1)} %get-tuple-element.54.refs_2_, ...), custom_call_target="tpu_custom_call", output_to_operand_aliasing={{0}: (3, {})} | custom-call | flops 7516192768 | bytes 1000 | tf_op jit(solution)/shard_map/add_block_1/pallas_call | solution.py:42
  90.4 4.9 %collective-permute-done.12.refs_3_ = bf16[512,1024]{1,0:T(8,128)(2,1)S(1)} collective-permute-done((bf16[512,1024]{1,0:T(8,128)(2,1)S(1)}, bf16[512,1024]{1,0:T(8,128)(2,1)S(1)}, u32[]{:S(2)}, u32[]{:S(2)}) %collective-permute-start.12) | collective-permute-done | bytes 1048608 | tf_op jit(solution)/shard_map/ppermute | solution.py:451
  95.3 12.3 %add_block_2.1 = (f32[1024,3584]{1,0:T(8,128)S(1)}, f32[8,128]{1,0:T(8,128)S(1)}) custom-call(s32[9]{0:T(128)S(1)} %stack.43.where.refs_0_, bf16[512,1024]{1,0:T(8,128)(2,1)S(1)} %collective-permute-done.refs_0_, bf16[512,1024]{1,0:T(8,128)(2,1)S(1)} %collective-permute-done.11.refs_1_, ...), custom_call_target="tpu_custom_call", output_to_operand_aliasing={{0}: (6, {})} | custom-call | flops 1000 | bytes 1000 | tf_op jit(solution)/shard_map/add_block_2/pallas_call | solution.py:42
  109.1 6.1 %last_block.1 = (bf16[1024,3584]{1,0:T(8,128)(2,1)S(1)}, f32[1024,3584]{1,0:T(8,128)S(1)}, f32[256,64]{1,0:T(8,128)S(1)}, bf16[256,3584]{1,0:T(8,128)(2,1)S(1)}, bf16[64,3584]{1,0:T(8,128)(2,1)S(1)}) custom-call(bf16[512,1024]{1,0:T(8,128)(2,1)S(1)} %collective-permute-done.8.inner, ...), custom_call_target="tpu_custom_call", output_to_operand_aliasing={{0}: (2, {}), {1}: (3, {})} | custom-call | flops 1000 | bytes 1000 | tf_op jit(solution)/shard_map/last_block/pallas_call | solution.py:42
  115.2 3.2 %collective-permute-done.13.outer = bf16[256,1024]{1,0:T(8,128)(2,1)S(1)} collective-permute-done((bf16[256,1024]{1,0:T(8,128)(2,1)S(1)}, bf16[256,1024]{1,0:T(8,128)(2,1)S(1)}, u32[]{:S(2)}, u32[]{:S(2)}) %collective-permute-start.13) | collective-permute-done | bytes 524320 | tf_op jit(solution)/shard_map/ppermute | solution.py:469
  118.3 1.5 collective-permute-start.16
  119.8 3.2 %near_block.4 = (bf16[1024,3584]{1,0:T(8,128)(2,1)S(1)}, f32[1024,3584]{1,0:T(8,128)S(1)}, f32[256,64]{1,0:T(8,128)S(1)}, bf16[256,3584]{1,0:T(8,128)(2,1)S(1)}) custom-call(bf16[512,1024]{1,0:T(8,128)(2,1)S(1)} %collective-permute-done.8.inner, bf16[256,1024]{1,0:T(8,128)(2,1)S(1)} %collective-permute-done.13.outer, ...), custom_call_target="tpu_custom_call", output_to_operand_aliasing={{0}: (2, {}), {1}: (3, {})} | custom-call | flops 1000 | bytes 1000 | tf_op jit(solution)/shard_map/near_block/pallas_call | solution.py:42
  126.2 3.4 %collective-permute-done.15.outer = bf16[256,1024]{1,0:T(8,128)(2,1)S(1)} collective-permute-done((bf16[256,1024]{1,0:T(8,128)(2,1)S(1)}, bf16[256,1024]{1,0:T(8,128)(2,1)S(1)}, u32[]{:S(2)}, u32[]{:S(2)}) %collective-permute-start.15) | collective-permute-done | bytes 524320 | tf_op jit(solution)/shard_map/ppermute | solution.py:469
  129.6 5.1 %near_block.5 = (bf16[1024,3584]{1,0:T(8,128)(2,1)S(1)}, f32[1024,3584]{1,0:T(8,128)S(1)}, f32[256,64]{1,0:T(8,128)S(1)}, bf16[128,3584]{1,0:T(8,128)(2,1)S(1)},...) custom-call(bf16[512,1024]{1,0:T(8,128)(2,1)S(1)} %collective-permut, ...), custom_call_target="tpu_custom_call", output_to_operand_aliasing={{0}: (2, {}), {1}: (3, {})} | custom-call | flops 1000 | bytes 1000 | tf_op jit(solution)/shard_map/near_block/pallas_call | solution.py:42
  135.2 1.9 %near_block.6 = (bf16[1024,3584]{1,0:T(8,128)(2,1)S(1)}, f32[1024,3584]{1,0:T(8,128)S(1)}, f32[128,64]{1,0:T(8,128)S(1)}, bf16[128,3584]{1,0:T(8,128)(2,1)S(1)}) custom-call(bf16[512,1024]{1,0:T(8,128)(2,1)S(1)} %collective-permute-done.14.inner, bf16[128,1024]{1,0:T(8,128)(2,1)S(1)} %collective-permute-done.16.outer, ...), custom_call_target="tpu_custom_call", output_to_operand_aliasing={{0}: (2, {}), {1}: (3, {})} | custom-call | flops 1000 | bytes 1000 | tf_op jit(solution)/shard_map/near_block/pallas_call | solution.py:42
  137.1 3.7 %collective-permute-done.17.outer = bf16[128,1024]{1,0:T(8,128)(2,1)S(1)} collective-permute-done((bf16[128,1024]{1,0:T(8,128)(2,1)S(1)}, bf16[128,1024]{1,0:T(8,128)(2,1)S(1)}, u32[]{:S(2)}, u32[]{:S(2)}) %collective-permute-start.17) | collective-permute-done | bytes 262176 | tf_op jit(solution)/shard_map/ppermute | solution.py:469
  140.8 1.9 %near_block.7 = (bf16[1024,3584]{1,0:T(8,128)(2,1)S(1)}, f32[1024,3584]{1,0:T(8,128)S(1)}, f32[128,64]{1,0:T(8,128)S(1)}) custom-call(bf16[512,1024]{1,0:T(8,128)(2,1)S(1)} %collective-permute-done.14.inner, bf16[128,1024]{1,0:T(8,128)(2,1)S(1)} %collective-permute-done.17.outer, ...), custom_call_target="tpu_custom_call", output_to_operand_aliasing={{0}: (2, {}), {1}: (3, {})} | custom-call | flops 1000 | bytes 1000 | tf_op jit(solution)/shard_map/near_block/pallas_call | solution.py:42
  143.3 1.7 %collective-permute-start.18 = (f32[2,4096]{1,0:T(2,128)S(1)}, f32[2,4096]{1,0:T(2,128)S(1)}, u32[]{:S(2)}, u32[]{:S(2)}) collective-permute-start(f32[2,4096]{1,0:T(2,128)S(1)} %outer_products.1), channel_id=1, source_target_pairs={{0,8},{4,12},{8,0},{12,4},{1,9},{5,13},{9,1},{13,5},{2,10},{6,14},... | collective-permute-start | bytes 98312 | tf_op jit(solution)/shard_map/ppermute | solution.py:505
  144.9 3.2 %collective-permute-done.18 = f32[2,4096]{1,0:T(2,128)S(1)} collective-permute-done((f32[2,4096]{1,0:T(2,128)S(1)}, f32[2,4096]{1,0:T(2,128)S(1)}, u32[]{:S(2)}, u32[]{:S(2)}) %collective-permute-start.18) | collective-permute-done | bytes 32800 | tf_op jit(solution)/shard_map/ppermute | solution.py:505
  149.4 2.7 %collective-permute-done.19 = f32[2,4096]{1,0:T(2,128)S(1)} collective-permute-done((f32[2,4096]{1,0:T(2,128)S(1)}, f32[2,4096]{1,0:T(2,128)S(1)}, u32[]{:S(2)}, u32[]{:S(2)}) %collective-permute-start.19) | collective-permute-done | bytes 32800 | tf_op jit(solution)/shard_map/ppermute | solution.py:505
  153.8 1.6 collective-permute-start.21
  156.1 2.1 %collective-permute-start.23 = (f32[2,256]{1,0:T(2,128)S(1)}, f32[2,256]{1,0:T(2,128)S(1)}, u32[]{:S(2)}, u32[]{:S(2)}) collective-permute-start(f32[2,256]{1,0:T(2,128)S(1)} %score_sum.1), channel_id=1, source_target_pairs={{0,8},{4,12},{8,0},{12,4},{1,9},{5,13},{9,1},{13,5},{2,10},{6,14},... | collective-permute-start | bytes 6152 | tf_op jit(solution)/shard_map/ppermute | solution.py:505
  158.3 2.3 %hessian_update.1 = f32[256,4096]{1,0:T(8,128)} custom-call(f32[8,4096]{1,0:T(8,128)S(1)} %pad_maximum_fusion.grads, f32[256,4096]{1,0:T(8,128)S(1)} %get-tuple-element.91.hessian), custom_call_target="tpu_custom_call" | custom-call | flops 1000 | bytes 1000 | tf_op jit(solution)/shard_map/hessian_update/pallas_call | solution.py:42
  (52 shorter events, 19.9 us)
Async XLA Ops:
  0.6 21.1 %copy-start = (bf16[1024,1024]{1,0:T(8,128)(2,1)S(1)}, bf16[1024,1024]{1,0:T(8,128)(2,1)}, u32[]{:S(2)}) copy-start(bf16[1024,1024]{1,0:T(8,128)(2,1)} %own) | copy-start | bytes 6291460
  0.6 49.9 %collective-permute-start.5 = (bf16[1024,1024]{1,0:T(8,128)(2,1)}, bf16[1024,1024]{1,0:T(8,128)(2,1)}, u32[]{:S(2)}, u32[]{:S(2)}) collective-permute-start(bf16[1024,1024]{1,0:T(8,128)(2,1)} %own), channel_id=1, source_target_pairs={{0,4},{4,0},{8,12},{12,8},{1,5},{5,1},{9,13},{13,9},{2,6},{6,2},{1... | collective-permute-start | bytes 6291464 | tf_op jit(solution)/shard_map/ppermute | solution.py:445
  6.8 27.0 %collective-permute-start = (bf16[512,1024]{1,0:T(8,128)(2,1)}, bf16[512,1024]{1,0:T(8,128)(2,1)S(1)}, u32[]{:S(2)}, u32[]{:S(2)}) collective-permute-start(bf16[512,1024]{1,0:T(8,128)(2,1)} %get-tuple-element.97), channel_id=1, source_target_pairs={{4,8},{8,4},{5,9},{9,5},{6,10},{10,6},{7,11},{11,7},{20,24},{24,20... | collective-permute-start | bytes 3145736 | tf_op jit(solution)/shard_map/ppermute | solution.py:447
  7.5 5.8 %collective-permute-start.2 = (f32[256,256]{1,0:T(8,128)}, f32[256,256]{1,0:T(8,128)S(1)}, u32[]{:S(2)}, u32[]{:S(2)}) collective-permute-start(f32[256,256]{1,0:T(8,128)} %rest_1_.1), channel_id=1, source_target_pairs={{0,1},{1,0},{2,3},{3,2},{4,5},{5,4},{6,7},{7,6},{8,9},{9,8},{10,11... | collective-permute-start | bytes 786440 | tf_op jit(solution)/shard_map/ppermute | solution.py:505
  7.6 9.5 %collective-permute-start.3 = (f32[256,256]{1,0:T(8,128)}, f32[256,256]{1,0:T(8,128)}, u32[]{:S(2)}, u32[]{:S(2)}) collective-permute-start(f32[256,256]{1,0:T(8,128)} %rest_1_.1), channel_id=1, source_target_pairs={{0,2},{1,3},{2,0},{3,1},{4,6},{5,7},{6,4},{7,5},{8,10},{9,11},{10,... | collective-permute-start | bytes 786440 | tf_op jit(solution)/shard_map/ppermute | solution.py:505
  9.1 12.6 %collective-permute-start.4 = (f32[256,256]{1,0:T(8,128)}, f32[256,256]{1,0:T(8,128)}, u32[]{:S(2)}, u32[]{:S(2)}) collective-permute-start(f32[256,256]{1,0:T(8,128)} %rest_1_.1), channel_id=1, source_target_pairs={{0,3},{1,2},{2,1},{3,0},{4,7},{5,6},{6,5},{7,4},{8,11},{9,10},{10,... | collective-permute-start | bytes 786440 | tf_op jit(solution)/shard_map/ppermute | solution.py:505
  9.5 1.6 copy-start.1
  11.1 0.9 copy-start.2
  13.3 20.4 %copy-start.3 = (f32[256,256]{1,0:T(8,128)}, f32[256,256]{1,0:T(8,128)S(1)}, u32[]{:S(2)}) copy-start(f32[256,256]{1,0:T(8,128)S(1)} %collective-permute-done.2.rest_2_) | copy-start | bytes 786436
  13.3 45.5 %collective-permute-start.11 = (bf16[512,1024]{1,0:T(8,128)(2,1)}, bf16[512,1024]{1,0:T(8,128)(2,1)S(1)}, u32[]{:S(2)}, u32[]{:S(2)}) collective-permute-start(bf16[512,1024]{1,0:T(8,128)(2,1)} %get-tuple-element.96), channel_id=1, source_target_pairs={{4,8},{8,4},{5,9},{9,5},{6,10},{10,6},{7,11},{11,7},{20,24},{24,20... | collective-permute-start | bytes 3145736 | tf_op jit(solution)/shard_map/ppermute | solution.py:447
  33.8 39.1 %collective-permute-start.9 = (bf16[512,1024]{1,0:T(8,128)(2,1)S(1)}, bf16[512,1024]{1,0:T(8,128)(2,1)S(1)}, u32[]{:S(2)}, u32[]{:S(2)}) collective-permute-start(bf16[512,1024]{1,0:T(8,128)(2,1)S(1)} %collective-permute-done.refs_0_), channel_id=1, source_target_pairs={{4,0},{8,12},{5,1},{9,13},{6,2},{10,14},{7,3},{11,15},{20,16},{24,... | collective-permute-start | bytes 3145736 | tf_op jit(solution)/shard_map/ppermute | solution.py:451
  52.2 35.5 %collective-permute-start.8 = (bf16[512,1024]{1,0:T(8,128)(2,1)S(1)}, bf16[512,1024]{1,0:T(8,128)(2,1)S(1)}, u32[]{:S(2)}, u32[]{:S(2)}) collective-permute-start(bf16[512,1024]{1,0:T(8,128)(2,1)S(1)} %get-tuple-element.95), channel_id=1, source_target_pairs={{4,8},{8,4},{5,9},{9,5},{6,10},{10,6},{7,11},{11,7},{20,24},{24,20... | collective-permute-start | bytes 3145736 | tf_op jit(solution)/shard_map/ppermute | solution.py:453
  53.0 10.0 %collective-permute-start.1 = (f32[64,1024]{1,0:T(8,128)S(1)}, f32[64,1024]{1,0:T(8,128)S(1)}, u32[]{:S(2)}, u32[]{:S(2)}) collective-permute-start(f32[64,1024]{1,0:T(8,128)S(1)} %input_block.1.refs_1_), channel_id=1, source_target_pairs={{0,4},{12,8},{1,5},{13,9},{2,6},{14,10},{3,7},{15,11},{16,20},{28,... | collective-permute-start | bytes 786440 | tf_op jit(solution)/shard_map/ppermute | solution.py:449
  58.8 36.5 %collective-permute-start.12 = (bf16[512,1024]{1,0:T(8,128)(2,1)S(1)}, bf16[512,1024]{1,0:T(8,128)(2,1)S(1)}, u32[]{:S(2)}, u32[]{:S(2)}) collective-permute-start(bf16[512,1024]{1,0:T(8,128)(2,1)S(1)} %collective-permute-done.11.refs_1_), channel_id=1, source_target_pairs={{4,0},{8,12},{5,1},{9,13},{6,2},{10,14},{7,3},{11,15},{20,16},{24,... | collective-permute-start | bytes 3145736 | tf_op jit(solution)/shard_map/ppermute | solution.py:451
  72.9 14.3 %collective-permute-start.6 = (f32[64,1024]{1,0:T(8,128)S(1)}, f32[64,1024]{1,0:T(8,128)S(1)}, u32[]{:S(2)}, u32[]{:S(2)}) collective-permute-start(f32[64,1024]{1,0:T(8,128)S(1)} %side.1.refs_1_), channel_id=1, source_target_pairs={{4,8},{8,4},{5,9},{9,5},{6,10},{10,6},{7,11},{11,7},{20,24},{24,20... | collective-permute-start | bytes 786440 | tf_op jit(solution)/shard_map/ppermute | solution.py:455
  73.5 34.1 %collective-permute-start.14 = (bf16[512,1024]{1,0:T(8,128)(2,1)S(1)}, bf16[512,1024]{1,0:T(8,128)(2,1)S(1)}, u32[]{:S(2)}, u32[]{:S(2)}) collective-permute-start(bf16[512,1024]{1,0:T(8,128)(2,1)S(1)} %get-tuple-element.69), channel_id=1, source_target_pairs={{4,8},{8,4},{5,9},{9,5},{6,10},{10,6},{7,11},{11,7},{20,24},{24,20... | collective-permute-start | bytes 3145736 | tf_op jit(solution)/shard_map/ppermute | solution.py:454
  87.8 19.9 %collective-permute-start.10 = (bf16[256,1024]{1,0:T(8,128)(2,1)S(1)}, bf16[256,1024]{1,0:T(8,128)(2,1)S(1)}, u32[]{:S(2)}, u32[]{:S(2)}) collective-permute-start(bf16[256,1024]{1,0:T(8,128)(2,1)S(1)} %get-tuple-element.56), channel_id=1, source_target_pairs={{4,0},{8,12},{5,1},{9,13},{6,2},{10,14},{7,3},{11,15},{20,16},{24,... | collective-permute-start | bytes 1572872 | tf_op jit(solution)/shard_map/ppermute | solution.py:469
  89.1 29.2 %collective-permute-start.13 = (bf16[256,1024]{1,0:T(8,128)(2,1)S(1)}, bf16[256,1024]{1,0:T(8,128)(2,1)S(1)}, u32[]{:S(2)}, u32[]{:S(2)}) collective-permute-start(bf16[256,1024]{1,0:T(8,128)(2,1)S(1)} %get-tuple-element.63), channel_id=1, source_target_pairs={{4,0},{8,12},{5,1},{9,13},{6,2},{10,14},{7,3},{11,15},{20,16},{24,... | collective-permute-start | bytes 1572872 | tf_op jit(solution)/shard_map/ppermute | solution.py:469
  107.7 21.9 %collective-permute-start.15 = (bf16[256,1024]{1,0:T(8,128)(2,1)S(1)}, bf16[256,1024]{1,0:T(8,128)(2,1)S(1)}, u32[]{:S(2)}, u32[]{:S(2)}) collective-permute-start(bf16[256,1024]{1,0:T(8,128)(2,1)S(1)} %slice.40), channel_id=1, source_target_pairs={{4,0},{8,12},{5,1},{9,13},{6,2},{10,14},{7,3},{11,15},{20,16},{24,... | collective-permute-start | bytes 1572872 | tf_op jit(solution)/shard_map/ppermute | solution.py:469
  118.3 16.9 %collective-permute-start.16 = (bf16[128,1024]{1,0:T(8,128)(2,1)S(1)}, bf16[128,1024]{1,0:T(8,128)(2,1)S(1)}, u32[]{:S(2)}, u32[]{:S(2)}) collective-permute-start(bf16[128,1024]{1,0:T(8,128)(2,1)S(1)} %get-tuple-element.75), channel_id=1, source_target_pairs={{4,0},{8,12},{5,1},{9,13},{6,2},{10,14},{7,3},{11,15},{20,16},{24,... | collective-permute-start | bytes 786440 | tf_op jit(solution)/shard_map/ppermute | solution.py:469
  123.0 17.8 %collective-permute-start.17 = (bf16[128,1024]{1,0:T(8,128)(2,1)S(1)}, bf16[128,1024]{1,0:T(8,128)(2,1)S(1)}, u32[]{:S(2)}, u32[]{:S(2)}) collective-permute-start(bf16[128,1024]{1,0:T(8,128)(2,1)S(1)} %get-tuple-element.80), channel_id=1, source_target_pairs={{4,0},{8,12},{5,1},{9,13},{6,2},{10,14},{7,3},{11,15},{20,16},{24,... | collective-permute-start | bytes 786440 | tf_op jit(solution)/shard_map/ppermute | solution.py:469
  124.3 18.4 %collective-permute-start.7 = (bf16[64,1024]{1,0:T(8,128)(2,1)S(1)}, bf16[64,1024]{1,0:T(8,128)(2,1)S(1)}, u32[]{:S(2)}, u32[]{:S(2)}) collective-permute-start(bf16[64,1024]{1,0:T(8,128)(2,1)S(1)} %convert_element_type.4), channel_id=1, source_target_pairs={{4,0},{8,12},{5,1},{9,13},{6,2},{10,14},{7,3},{11,15},{20,16},{24,... | collective-permute-start | bytes 393224 | tf_op jit(solution)/shard_map/ppermute | solution.py:457
  143.3 4.9 %collective-permute-start.18 = (f32[2,4096]{1,0:T(2,128)S(1)}, f32[2,4096]{1,0:T(2,128)S(1)}, u32[]{:S(2)}, u32[]{:S(2)}) collective-permute-start(f32[2,4096]{1,0:T(2,128)S(1)} %outer_products.1), channel_id=1, source_target_pairs={{0,8},{4,12},{8,0},{12,4},{1,9},{5,13},{9,1},{13,5},{2,10},{6,14},... | collective-permute-start | bytes 98312 | tf_op jit(solution)/shard_map/ppermute | solution.py:505
  148.2 4.0 %collective-permute-start.19 = (f32[2,4096]{1,0:T(2,128)S(1)}, f32[2,4096]{1,0:T(2,128)S(1)}, u32[]{:S(2)}, u32[]{:S(2)}) collective-permute-start(f32[2,4096]{1,0:T(2,128)S(1)} %add.34), channel_id=1, source_target_pairs={{0,4},{4,0},{8,12},{12,8},{1,5},{5,1},{9,13},{13,9},{2,6},{6,2},{1... | collective-permute-start | bytes 98312 | tf_op jit(solution)/shard_map/ppermute | solution.py:505
  152.4 1.3 collective-permute-start.20
  152.5 3.7 %collective-permute-start.22 = (f32[2,256]{1,0:T(2,128)S(1)}, f32[2,256]{1,0:T(2,128)S(1)}, u32[]{:S(2)}, u32[]{:S(2)}) collective-permute-start(f32[2,256]{1,0:T(2,128)S(1)} %scores.1.refs_0_), channel_id=1, source_target_pairs={{0,4},{4,0},{8,12},{12,8},{1,5},{5,1},{9,13},{13,9},{2,6},{6,2},{1... | collective-permute-start | bytes 6152 | tf_op jit(solution)/shard_map/ppermute | solution.py:505
  153.8 4.5 %collective-permute-start.21 = (f32[4,4096]{1,0:T(4,128)S(1)}, f32[4,4096]{1,0:T(4,128)S(1)}, u32[]{:S(2)}, u32[]{:S(2)}) collective-permute-start(f32[4,4096]{1,0:T(4,128)S(1)} %pad_maximum_fusion.1), channel_id=1, source_target_pairs={{0,2},{1,3},{2,0},{3,1},{4,6},{5,7},{6,4},{7,5},{8,10},{9,11},{10,... | collective-permute-start | bytes 196616 | tf_op jit(solution)/shard_map/ppermute | solution.py:505
  156.1 4.5 %collective-permute-start.23 = (f32[2,256]{1,0:T(2,128)S(1)}, f32[2,256]{1,0:T(2,128)S(1)}, u32[]{:S(2)}, u32[]{:S(2)}) collective-permute-start(f32[2,256]{1,0:T(2,128)S(1)} %score_sum.1), channel_id=1, source_target_pairs={{0,8},{4,12},{8,0},{12,4},{1,9},{5,13},{9,1},{13,5},{2,10},{6,14},... | collective-permute-start | bytes 6152 | tf_op jit(solution)/shard_map/ppermute | solution.py:505

commit v20 on v17

--- a/solution.py
+++ b/solution.py
@@ -534,7 +534,7 @@
 
     scores = score_parts(where, grads, parts)
     all_grads = after(grads, scores)
-    *first, last = bits("tensor")
+    *first, last = reversed(bits("tensor"))
     for bit in bits("dp"):
         all_grads = jnp.concatenate([all_grads, swap(all_grads, "dp", bit)], axis=0)
     for bit in first:

time: 162 us -> 163 us (level)
  transfers between devices with their start and end apart: 24 -> 24, of which waited for: 13 -> 14; matrix products, arithmetic and copies ran while one was open for 3% -> 3% of each run, Pallas kernels for 38% -> 38%
where the time goes in v20:
time: 163 us; the launch traced here: 162 us
  Pallas kernels  61.5 us (38%)
  waiting for transfers between devices  59.1 us (36%)
  starting transfers between devices  32.1 us (20%)
  local copies, waits for them, and re-layouts  7.48 us (5%)
    pallas_call x16, Pallas kernels, call(): pl.pallas_call(body, grid_spec=pltpu.PrefetchScalarGridSpec(num_scalar_pr...  61.5 us
    ppermute x9, waiting for transfers between devices, swap(): lax.ppermute(a, axis, [(i, i ^ bit) for i in range(lax.axis_size(axis))])  15.9 us
    ppermute x1, waiting for transfers between devices, line_of_four(): pair = send(grad_out, perm=pairs)  15.4 us
    ppermute x2, waiting for transfers between devices, line_of_four(): mid_outer = [send(after(a, begun), perm=outward) for a in mid_inner]  14.3 us
    ppermute x5, waiting for transfers between devices, line_of_four(): send(after(end_inner[h][at:at + size], ahead, done[n]), perm=outward)  10.7 us
    ppermute x9, starting transfers between devices, swap(): lax.ppermute(a, axis, [(i, i ^ bit) for i in range(lax.axis_size(axis))])  9.14 us
    ppermute x5, starting transfers between devices, line_of_four(): send(after(end_inner[h][at:at + size], ahead, done[n]), perm=outward)  6.63 us
    ppermute x1, starting transfers between devices, line_of_four(): from_end = send(after(in_part, mid_inner[0]), perm=inward)  5.83 us
  transfers between devices with their start and end apart: 24, of which 14 were waited for; matrix products, arithmetic and copies ran while one was open for 3% of the time, Pallas kernels for 38%

profile of v20, /device:TPU:0, one launch (start us, length us, event | category | flops | bytes accessed | tf_op | source)
XLA Modules:
  0.0 162.0 jit_solution(16235506194324120130)
XLA Ops:
  0.6 3.1 %collective-permute-start.5 = (bf16[1024,1024]{1,0:T(8,128)(2,1)}, bf16[1024,1024]{1,0:T(8,128)(2,1)}, u32[]{:S(2)}, u32[]{:S(2)}) collective-permute-start(bf16[1024,1024]{1,0:T(8,128)(2,1)} %own), channel_id=1, source_target_pairs={{0,4},{4,0},{8,12},{12,8},{1,5},{5,1},{9,13},{13,9},{2,6},{6,2},{1... | collective-permute-start | bytes 6291464 | tf_op jit(solution)/shard_map/ppermute | solution.py:445
  3.7 3.0 %fusion.1 = (bf16[512,1024]{1,0:T(8,128)(2,1)}, bf16[512,1024]{1,0:T(8,128)(2,1)}) fusion(bf16[1024,1024]{1,0:T(8,128)(2,1)} %own), kind=kLoop, calls=%fused_computation.3 | loop fusion | bytes 4194304 | tf_op jit(solution)/shard_map/slice | solution.py:446
  7.6 1.6 collective-permute-start.3
  9.5 1.6 copy-done.1
  12.0 1.3 input_block.1.refs_1_
  14.1 3.0 %collective-permute-done.3.rest_3_ = f32[256,256]{1,0:T(8,128)} collective-permute-done((f32[256,256]{1,0:T(8,128)}, f32[256,256]{1,0:T(8,128)}, u32[]{:S(2)}, u32[]{:S(2)}) %collective-permute-start.3) | collective-permute-done | bytes 262176 | tf_op jit(solution)/shard_map/ppermute | solution.py:505
  17.1 4.7 %collective-permute-done.4.rest_4_ = f32[256,256]{1,0:T(8,128)} collective-permute-done((f32[256,256]{1,0:T(8,128)}, f32[256,256]{1,0:T(8,128)}, u32[]{:S(2)}, u32[]{:S(2)}) %collective-permute-start.4) | collective-permute-done | bytes 262176 | tf_op jit(solution)/shard_map/ppermute | solution.py:505
  21.8 12.0 %own_block.1 = (f32[1024,3584]{1,0:T(8,128)S(1)}, bf16[1024,3584]{1,0:T(8,128)(2,1)S(1)}, f32[8,128]{1,0:T(8,128)S(1)}) custom-call(s32[9]{0:T(128)S(1)} %stack.43.where.refs_0_, bf16[1024,1024]{1,0:T(8,128)(2,1)S(1)} %copy-done, bf16[3584,4096]{1,0:T(8,128)(2,1)} %refs_4_.1, bf16[3584,4096]{1,0:T(8,128)(2,1)} %refs_4_.1), custom_call_target="tpu_custom_call" | custom-call | flops 1000 | bytes 1000 | tf_op jit(solution)/shard_map/own_block/pallas_call | solution.py:42
  33.8 1.3 collective-permute-start.9
  35.1 15.4 %collective-permute-done.5.refs_0_ = bf16[1024,1024]{1,0:T(8,128)(2,1)} collective-permute-done((bf16[1024,1024]{1,0:T(8,128)(2,1)}, bf16[1024,1024]{1,0:T(8,128)(2,1)}, u32[]{:S(2)}, u32[]{:S(2)}) %collective-permute-start.5) | collective-permute-done | bytes 2097184 | tf_op jit(solution)/shard_map/ppermute | solution.py:445
  50.5 1.7 %fusion = (bf16[512,1024]{1,0:T(8,128)(2,1)S(1)}, bf16[512,1024]{1,0:T(8,128)(2,1)S(1)}) fusion(bf16[1024,1024]{1,0:T(8,128)(2,1)} %collective-permute-done.5.refs_0_), kind=kLoop, calls=%fused_computation.2 | loop fusion | bytes 4194304 | tf_op jit(solution)/shard_map/slice | solution.py:454
  53.0 5.8 %collective-permute-start.1 = (f32[64,1024]{1,0:T(8,128)S(1)}, f32[64,1024]{1,0:T(8,128)S(1)}, u32[]{:S(2)}, u32[]{:S(2)}) collective-permute-start(f32[64,1024]{1,0:T(8,128)S(1)} %input_block.1.refs_1_), channel_id=1, source_target_pairs={{0,4},{12,8},{1,5},{13,9},{2,6},{14,10},{3,7},{15,11},{16,20},{28,... | collective-permute-start | bytes 786440 | tf_op jit(solution)/shard_map/ppermute | solution.py:449
  60.1 2.8 %collective-permute-done.1.refs_2_ = f32[64,1024]{1,0:T(8,128)S(1)} collective-permute-done((f32[64,1024]{1,0:T(8,128)S(1)}, f32[64,1024]{1,0:T(8,128)S(1)}, u32[]{:S(2)}, u32[]{:S(2)}) %collective-permute-start.1) | collective-permute-done | bytes 262176 | tf_op jit(solution)/shard_map/ppermute | solution.py:449
  63.5 9.4 %collective-permute-done.9.refs_2_ = bf16[512,1024]{1,0:T(8,128)(2,1)S(1)} collective-permute-done((bf16[512,1024]{1,0:T(8,128)(2,1)S(1)}, bf16[512,1024]{1,0:T(8,128)(2,1)S(1)}, u32[]{:S(2)}, u32[]{:S(2)}) %collective-permute-start.9) | collective-permute-done | bytes 1048608 | tf_op jit(solution)/shard_map/ppermute | solution.py:451
  74.3 12.9 %add_block_1.1 = (f32[1024,3584]{1,0:T(8,128)S(1)}, f32[8,128]{1,0:T(8,128)S(1)}) custom-call(s32[9]{0:T(128)S(1)} %stack.43.where.refs_0_, bf16[1024,1024]{1,0:T(8,128)(2,1)} %collective-permute-done.5.refs_0_, bf16[3584,4096]{1,0:T(8,128)(2,1)} %refs_4_.1, f32[1024,3584]{1,0:T(8,128)S(1)} %get-tuple-element.54.refs_2_, ...), custom_call_target="tpu_custom_call", output_to_operand_aliasing={{0}: (3, {})} | custom-call | flops 7516192768 | bytes 1000 | tf_op jit(solution)/shard_map/add_block_1/pallas_call | solution.py:42
  90.4 4.9 %collective-permute-done.12.refs_3_ = bf16[512,1024]{1,0:T(8,128)(2,1)S(1)} collective-permute-done((bf16[512,1024]{1,0:T(8,128)(2,1)S(1)}, bf16[512,1024]{1,0:T(8,128)(2,1)S(1)}, u32[]{:S(2)}, u32[]{:S(2)}) %collective-permute-start.12) | collective-permute-done | bytes 1048608 | tf_op jit(solution)/shard_map/ppermute | solution.py:451
  95.3 12.3 %add_block_2.1 = (f32[1024,3584]{1,0:T(8,128)S(1)}, f32[8,128]{1,0:T(8,128)S(1)}) custom-call(s32[9]{0:T(128)S(1)} %stack.43.where.refs_0_, bf16[512,1024]{1,0:T(8,128)(2,1)S(1)} %collective-permute-done.refs_0_, bf16[512,1024]{1,0:T(8,128)(2,1)S(1)} %collective-permute-done.11.refs_1_, ...), custom_call_target="tpu_custom_call", output_to_operand_aliasing={{0}: (6, {})} | custom-call | flops 1000 | bytes 1000 | tf_op jit(solution)/shard_map/add_block_2/pallas_call | solution.py:42
  109.1 6.1 %last_block.1 = (bf16[1024,3584]{1,0:T(8,128)(2,1)S(1)}, f32[1024,3584]{1,0:T(8,128)S(1)}, f32[256,64]{1,0:T(8,128)S(1)}, bf16[256,3584]{1,0:T(8,128)(2,1)S(1)}, bf16[64,3584]{1,0:T(8,128)(2,1)S(1)}) custom-call(bf16[512,1024]{1,0:T(8,128)(2,1)S(1)} %collective-permute-done.8.inner, ...), custom_call_target="tpu_custom_call", output_to_operand_aliasing={{0}: (2, {}), {1}: (3, {})} | custom-call | flops 1000 | bytes 1000 | tf_op jit(solution)/shard_map/last_block/pallas_call | solution.py:42
  115.2 3.2 %collective-permute-done.13.outer = bf16[256,1024]{1,0:T(8,128)(2,1)S(1)} collective-permute-done((bf16[256,1024]{1,0:T(8,128)(2,1)S(1)}, bf16[256,1024]{1,0:T(8,128)(2,1)S(1)}, u32[]{:S(2)}, u32[]{:S(2)}) %collective-permute-start.13) | collective-permute-done | bytes 524320 | tf_op jit(solution)/shard_map/ppermute | solution.py:469
  118.3 1.5 collective-permute-start.16
  119.8 3.2 %near_block.4 = (bf16[1024,3584]{1,0:T(8,128)(2,1)S(1)}, f32[1024,3584]{1,0:T(8,128)S(1)}, f32[256,64]{1,0:T(8,128)S(1)}, bf16[256,3584]{1,0:T(8,128)(2,1)S(1)}) custom-call(bf16[512,1024]{1,0:T(8,128)(2,1)S(1)} %collective-permute-done.8.inner, bf16[256,1024]{1,0:T(8,128)(2,1)S(1)} %collective-permute-done.13.outer, ...), custom_call_target="tpu_custom_call", output_to_operand_aliasing={{0}: (2, {}), {1}: (3, {})} | custom-call | flops 1000 | bytes 1000 | tf_op jit(solution)/shard_map/near_block/pallas_call | solution.py:42
  126.2 3.4 %collective-permute-done.15.outer = bf16[256,1024]{1,0:T(8,128)(2,1)S(1)} collective-permute-done((bf16[256,1024]{1,0:T(8,128)(2,1)S(1)}, bf16[256,1024]{1,0:T(8,128)(2,1)S(1)}, u32[]{:S(2)}, u32[]{:S(2)}) %collective-permute-start.15) | collective-permute-done | bytes 524320 | tf_op jit(solution)/shard_map/ppermute | solution.py:469
  129.6 5.1 %near_block.5 = (bf16[1024,3584]{1,0:T(8,128)(2,1)S(1)}, f32[1024,3584]{1,0:T(8,128)S(1)}, f32[256,64]{1,0:T(8,128)S(1)}, bf16[128,3584]{1,0:T(8,128)(2,1)S(1)},...) custom-call(bf16[512,1024]{1,0:T(8,128)(2,1)S(1)} %collective-permut, ...), custom_call_target="tpu_custom_call", output_to_operand_aliasing={{0}: (2, {}), {1}: (3, {})} | custom-call | flops 1000 | bytes 1000 | tf_op jit(solution)/shard_map/near_block/pallas_call | solution.py:42
  135.2 1.9 %near_block.6 = (bf16[1024,3584]{1,0:T(8,128)(2,1)S(1)}, f32[1024,3584]{1,0:T(8,128)S(1)}, f32[128,64]{1,0:T(8,128)S(1)}, bf16[128,3584]{1,0:T(8,128)(2,1)S(1)}) custom-call(bf16[512,1024]{1,0:T(8,128)(2,1)S(1)} %collective-permute-done.14.inner, bf16[128,1024]{1,0:T(8,128)(2,1)S(1)} %collective-permute-done.16.outer, ...), custom_call_target="tpu_custom_call", output_to_operand_aliasing={{0}: (2, {}), {1}: (3, {})} | custom-call | flops 1000 | bytes 1000 | tf_op jit(solution)/shard_map/near_block/pallas_call | solution.py:42
  137.1 3.7 %collective-permute-done.17.outer = bf16[128,1024]{1,0:T(8,128)(2,1)S(1)} collective-permute-done((bf16[128,1024]{1,0:T(8,128)(2,1)S(1)}, bf16[128,1024]{1,0:T(8,128)(2,1)S(1)}, u32[]{:S(2)}, u32[]{:S(2)}) %collective-permute-start.17) | collective-permute-done | bytes 262176 | tf_op jit(solution)/shard_map/ppermute | solution.py:469
  140.8 1.9 %near_block.7 = (bf16[1024,3584]{1,0:T(8,128)(2,1)S(1)}, f32[1024,3584]{1,0:T(8,128)S(1)}, f32[128,64]{1,0:T(8,128)S(1)}) custom-call(bf16[512,1024]{1,0:T(8,128)(2,1)S(1)} %collective-permute-done.14.inner, bf16[128,1024]{1,0:T(8,128)(2,1)S(1)} %collective-permute-done.17.outer, ...), custom_call_target="tpu_custom_call", output_to_operand_aliasing={{0}: (2, {}), {1}: (3, {})} | custom-call | flops 1000 | bytes 1000 | tf_op jit(solution)/shard_map/near_block/pallas_call | solution.py:42
  143.3 3.9 %collective-permute-done.18 = f32[2,4096]{1,0:T(2,128)S(1)} collective-permute-done((f32[2,4096]{1,0:T(2,128)S(1)}, f32[2,4096]{1,0:T(2,128)S(1)}, u32[]{:S(2)}, u32[]{:S(2)}) %collective-permute-start.18) | collective-permute-done | bytes 32800 | tf_op jit(solution)/shard_map/ppermute | solution.py:505
  147.3 2.2 %collective-permute-start.19 = (f32[2,4096]{1,0:T(2,128)S(1)}, f32[2,4096]{1,0:T(2,128)S(1)}, u32[]{:S(2)}, u32[]{:S(2)}) collective-permute-start(f32[2,4096]{1,0:T(2,128)S(1)} %add.34), channel_id=1, source_target_pairs={{0,8},{4,12},{8,0},{12,4},{1,9},{5,13},{9,1},{13,5},{2,10},{6,14},... | collective-permute-start | bytes 98312 | tf_op jit(solution)/shard_map/ppermute | solution.py:505
  149.4 2.7 %collective-permute-done.19 = f32[2,4096]{1,0:T(2,128)S(1)} collective-permute-done((f32[2,4096]{1,0:T(2,128)S(1)}, f32[2,4096]{1,0:T(2,128)S(1)}, u32[]{:S(2)}, u32[]{:S(2)}) %collective-permute-start.19) | collective-permute-done | bytes 32800 | tf_op jit(solution)/shard_map/ppermute | solution.py:505
  152.5 2.2 %collective-permute-start.22 = (f32[2,256]{1,0:T(2,128)S(1)}, f32[2,256]{1,0:T(2,128)S(1)}, u32[]{:S(2)}, u32[]{:S(2)}) collective-permute-start(f32[2,256]{1,0:T(2,128)S(1)} %scores.1.refs_0_), channel_id=1, source_target_pairs={{0,8},{4,12},{8,0},{12,4},{1,9},{5,13},{9,1},{13,5},{2,10},{6,14},... | collective-permute-start | bytes 6152 | tf_op jit(solution)/shard_map/ppermute | solution.py:505
  154.7 1.6 collective-permute-start.21
  159.0 2.3 %hessian_update.1 = f32[256,4096]{1,0:T(8,128)} custom-call(f32[8,4096]{1,0:T(8,128)S(1)} %pad_maximum_fusion.grads, f32[256,4096]{1,0:T(8,128)S(1)} %get-tuple-element.91.hessian), custom_call_target="tpu_custom_call" | custom-call | flops 1000 | bytes 1000 | tf_op jit(solution)/shard_map/hessian_update/pallas_call | solution.py:42
  (52 shorter events, 19.4 us)
Async XLA Ops:
  0.6 21.1 %copy-start = (bf16[1024,1024]{1,0:T(8,128)(2,1)S(1)}, bf16[1024,1024]{1,0:T(8,128)(2,1)}, u32[]{:S(2)}) copy-start(bf16[1024,1024]{1,0:T(8,128)(2,1)} %own) | copy-start | bytes 6291460
  0.6 49.9 %collective-permute-start.5 = (bf16[1024,1024]{1,0:T(8,128)(2,1)}, bf16[1024,1024]{1,0:T(8,128)(2,1)}, u32[]{:S(2)}, u32[]{:S(2)}) collective-permute-start(bf16[1024,1024]{1,0:T(8,128)(2,1)} %own), channel_id=1, source_target_pairs={{0,4},{4,0},{8,12},{12,8},{1,5},{5,1},{9,13},{13,9},{2,6},{6,2},{1... | collective-permute-start | bytes 6291464 | tf_op jit(solution)/shard_map/ppermute | solution.py:445
  6.8 27.0 %collective-permute-start = (bf16[512,1024]{1,0:T(8,128)(2,1)}, bf16[512,1024]{1,0:T(8,128)(2,1)S(1)}, u32[]{:S(2)}, u32[]{:S(2)}) collective-permute-start(bf16[512,1024]{1,0:T(8,128)(2,1)} %get-tuple-element.97), channel_id=1, source_target_pairs={{4,8},{8,4},{5,9},{9,5},{6,10},{10,6},{7,11},{11,7},{20,24},{24,20... | collective-permute-start | bytes 3145736 | tf_op jit(solution)/shard_map/ppermute | solution.py:447
  7.5 5.8 %collective-permute-start.2 = (f32[256,256]{1,0:T(8,128)}, f32[256,256]{1,0:T(8,128)S(1)}, u32[]{:S(2)}, u32[]{:S(2)}) collective-permute-start(f32[256,256]{1,0:T(8,128)} %rest_1_.1), channel_id=1, source_target_pairs={{0,1},{1,0},{2,3},{3,2},{4,5},{5,4},{6,7},{7,6},{8,9},{9,8},{10,11... | collective-permute-start | bytes 786440 | tf_op jit(solution)/shard_map/ppermute | solution.py:505
  7.6 9.5 %collective-permute-start.3 = (f32[256,256]{1,0:T(8,128)}, f32[256,256]{1,0:T(8,128)}, u32[]{:S(2)}, u32[]{:S(2)}) collective-permute-start(f32[256,256]{1,0:T(8,128)} %rest_1_.1), channel_id=1, source_target_pairs={{0,2},{1,3},{2,0},{3,1},{4,6},{5,7},{6,4},{7,5},{8,10},{9,11},{10,... | collective-permute-start | bytes 786440 | tf_op jit(solution)/shard_map/ppermute | solution.py:505
  9.1 12.6 %collective-permute-start.4 = (f32[256,256]{1,0:T(8,128)}, f32[256,256]{1,0:T(8,128)}, u32[]{:S(2)}, u32[]{:S(2)}) collective-permute-start(f32[256,256]{1,0:T(8,128)} %rest_1_.1), channel_id=1, source_target_pairs={{0,3},{1,2},{2,1},{3,0},{4,7},{5,6},{6,5},{7,4},{8,11},{9,10},{10,... | collective-permute-start | bytes 786440 | tf_op jit(solution)/shard_map/ppermute | solution.py:505
  9.5 1.6 copy-start.1
  11.1 0.9 copy-start.2
  13.3 20.4 %copy-start.3 = (f32[256,256]{1,0:T(8,128)}, f32[256,256]{1,0:T(8,128)S(1)}, u32[]{:S(2)}) copy-start(f32[256,256]{1,0:T(8,128)S(1)} %collective-permute-done.2.rest_2_) | copy-start | bytes 786436
  13.3 45.5 %collective-permute-start.11 = (bf16[512,1024]{1,0:T(8,128)(2,1)}, bf16[512,1024]{1,0:T(8,128)(2,1)S(1)}, u32[]{:S(2)}, u32[]{:S(2)}) collective-permute-start(bf16[512,1024]{1,0:T(8,128)(2,1)} %get-tuple-element.96), channel_id=1, source_target_pairs={{4,8},{8,4},{5,9},{9,5},{6,10},{10,6},{7,11},{11,7},{20,24},{24,20... | collective-permute-start | bytes 3145736 | tf_op jit(solution)/shard_map/ppermute | solution.py:447
  33.8 39.1 %collective-permute-start.9 = (bf16[512,1024]{1,0:T(8,128)(2,1)S(1)}, bf16[512,1024]{1,0:T(8,128)(2,1)S(1)}, u32[]{:S(2)}, u32[]{:S(2)}) collective-permute-start(bf16[512,1024]{1,0:T(8,128)(2,1)S(1)} %collective-permute-done.refs_0_), channel_id=1, source_target_pairs={{4,0},{8,12},{5,1},{9,13},{6,2},{10,14},{7,3},{11,15},{20,16},{24,... | collective-permute-start | bytes 3145736 | tf_op jit(solution)/shard_map/ppermute | solution.py:451
  52.2 35.5 %collective-permute-start.8 = (bf16[512,1024]{1,0:T(8,128)(2,1)S(1)}, bf16[512,1024]{1,0:T(8,128)(2,1)S(1)}, u32[]{:S(2)}, u32[]{:S(2)}) collective-permute-start(bf16[512,1024]{1,0:T(8,128)(2,1)S(1)} %get-tuple-element.95), channel_id=1, source_target_pairs={{4,8},{8,4},{5,9},{9,5},{6,10},{10,6},{7,11},{11,7},{20,24},{24,20... | collective-permute-start | bytes 3145736 | tf_op jit(solution)/shard_map/ppermute | solution.py:453
  53.0 10.0 %collective-permute-start.1 = (f32[64,1024]{1,0:T(8,128)S(1)}, f32[64,1024]{1,0:T(8,128)S(1)}, u32[]{:S(2)}, u32[]{:S(2)}) collective-permute-start(f32[64,1024]{1,0:T(8,128)S(1)} %input_block.1.refs_1_), channel_id=1, source_target_pairs={{0,4},{12,8},{1,5},{13,9},{2,6},{14,10},{3,7},{15,11},{16,20},{28,... | collective-permute-start | bytes 786440 | tf_op jit(solution)/shard_map/ppermute | solution.py:449
  58.8 36.5 %collective-permute-start.12 = (bf16[512,1024]{1,0:T(8,128)(2,1)S(1)}, bf16[512,1024]{1,0:T(8,128)(2,1)S(1)}, u32[]{:S(2)}, u32[]{:S(2)}) collective-permute-start(bf16[512,1024]{1,0:T(8,128)(2,1)S(1)} %collective-permute-done.11.refs_1_), channel_id=1, source_target_pairs={{4,0},{8,12},{5,1},{9,13},{6,2},{10,14},{7,3},{11,15},{20,16},{24,... | collective-permute-start | bytes 3145736 | tf_op jit(solution)/shard_map/ppermute | solution.py:451
  72.9 14.3 %collective-permute-start.6 = (f32[64,1024]{1,0:T(8,128)S(1)}, f32[64,1024]{1,0:T(8,128)S(1)}, u32[]{:S(2)}, u32[]{:S(2)}) collective-permute-start(f32[64,1024]{1,0:T(8,128)S(1)} %side.1.refs_1_), channel_id=1, source_target_pairs={{4,8},{8,4},{5,9},{9,5},{6,10},{10,6},{7,11},{11,7},{20,24},{24,20... | collective-permute-start | bytes 786440 | tf_op jit(solution)/shard_map/ppermute | solution.py:455
  73.5 34.1 %collective-permute-start.14 = (bf16[512,1024]{1,0:T(8,128)(2,1)S(1)}, bf16[512,1024]{1,0:T(8,128)(2,1)S(1)}, u32[]{:S(2)}, u32[]{:S(2)}) collective-permute-start(bf16[512,1024]{1,0:T(8,128)(2,1)S(1)} %get-tuple-element.69), channel_id=1, source_target_pairs={{4,8},{8,4},{5,9},{9,5},{6,10},{10,6},{7,11},{11,7},{20,24},{24,20... | collective-permute-start | bytes 3145736 | tf_op jit(solution)/shard_map/ppermute | solution.py:454
  87.8 19.9 %collective-permute-start.10 = (bf16[256,1024]{1,0:T(8,128)(2,1)S(1)}, bf16[256,1024]{1,0:T(8,128)(2,1)S(1)}, u32[]{:S(2)}, u32[]{:S(2)}) collective-permute-start(bf16[256,1024]{1,0:T(8,128)(2,1)S(1)} %get-tuple-element.56), channel_id=1, source_target_pairs={{4,0},{8,12},{5,1},{9,13},{6,2},{10,14},{7,3},{11,15},{20,16},{24,... | collective-permute-start | bytes 1572872 | tf_op jit(solution)/shard_map/ppermute | solution.py:469
  89.1 29.2 %collective-permute-start.13 = (bf16[256,1024]{1,0:T(8,128)(2,1)S(1)}, bf16[256,1024]{1,0:T(8,128)(2,1)S(1)}, u32[]{:S(2)}, u32[]{:S(2)}) collective-permute-start(bf16[256,1024]{1,0:T(8,128)(2,1)S(1)} %get-tuple-element.63), channel_id=1, source_target_pairs={{4,0},{8,12},{5,1},{9,13},{6,2},{10,14},{7,3},{11,15},{20,16},{24,... | collective-permute-start | bytes 1572872 | tf_op jit(solution)/shard_map/ppermute | solution.py:469
  107.7 21.9 %collective-permute-start.15 = (bf16[256,1024]{1,0:T(8,128)(2,1)S(1)}, bf16[256,1024]{1,0:T(8,128)(2,1)S(1)}, u32[]{:S(2)}, u32[]{:S(2)}) collective-permute-start(bf16[256,1024]{1,0:T(8,128)(2,1)S(1)} %slice.40), channel_id=1, source_target_pairs={{4,0},{8,12},{5,1},{9,13},{6,2},{10,14},{7,3},{11,15},{20,16},{24,... | collective-permute-start | bytes 1572872 | tf_op jit(solution)/shard_map/ppermute | solution.py:469
  118.3 16.9 %collective-permute-start.16 = (bf16[128,1024]{1,0:T(8,128)(2,1)S(1)}, bf16[128,1024]{1,0:T(8,128)(2,1)S(1)}, u32[]{:S(2)}, u32[]{:S(2)}) collective-permute-start(bf16[128,1024]{1,0:T(8,128)(2,1)S(1)} %get-tuple-element.75), channel_id=1, source_target_pairs={{4,0},{8,12},{5,1},{9,13},{6,2},{10,14},{7,3},{11,15},{20,16},{24,... | collective-permute-start | bytes 786440 | tf_op jit(solution)/shard_map/ppermute | solution.py:469
  123.0 17.8 %collective-permute-start.17 = (bf16[128,1024]{1,0:T(8,128)(2,1)S(1)}, bf16[128,1024]{1,0:T(8,128)(2,1)S(1)}, u32[]{:S(2)}, u32[]{:S(2)}) collective-permute-start(bf16[128,1024]{1,0:T(8,128)(2,1)S(1)} %get-tuple-element.80), channel_id=1, source_target_pairs={{4,0},{8,12},{5,1},{9,13},{6,2},{10,14},{7,3},{11,15},{20,16},{24,... | collective-permute-start | bytes 786440 | tf_op jit(solution)/shard_map/ppermute | solution.py:469
  124.3 18.4 %collective-permute-start.7 = (bf16[64,1024]{1,0:T(8,128)(2,1)S(1)}, bf16[64,1024]{1,0:T(8,128)(2,1)S(1)}, u32[]{:S(2)}, u32[]{:S(2)}) collective-permute-start(bf16[64,1024]{1,0:T(8,128)(2,1)S(1)} %convert_element_type.4), channel_id=1, source_target_pairs={{4,0},{8,12},{5,1},{9,13},{6,2},{10,14},{7,3},{11,15},{20,16},{24,... | collective-permute-start | bytes 393224 | tf_op jit(solution)/shard_map/ppermute | solution.py:457
  143.3 4.0 %collective-permute-start.18 = (f32[2,4096]{1,0:T(2,128)S(1)}, f32[2,4096]{1,0:T(2,128)S(1)}, u32[]{:S(2)}, u32[]{:S(2)}) collective-permute-start(f32[2,4096]{1,0:T(2,128)S(1)} %outer_products.1), channel_id=1, source_target_pairs={{0,4},{4,0},{8,12},{12,8},{1,5},{5,1},{9,13},{13,9},{2,6},{6,2},{1... | collective-permute-start | bytes 98312 | tf_op jit(solution)/shard_map/ppermute | solution.py:505
  147.3 4.9 %collective-permute-start.19 = (f32[2,4096]{1,0:T(2,128)S(1)}, f32[2,4096]{1,0:T(2,128)S(1)}, u32[]{:S(2)}, u32[]{:S(2)}) collective-permute-start(f32[2,4096]{1,0:T(2,128)S(1)} %add.34), channel_id=1, source_target_pairs={{0,8},{4,12},{8,0},{12,4},{1,9},{5,13},{9,1},{13,5},{2,10},{6,14},... | collective-permute-start | bytes 98312 | tf_op jit(solution)/shard_map/ppermute | solution.py:505
  152.4 2.2 %collective-permute-start.20 = (f32[2,4096]{1,0:T(2,128)S(1)}, f32[2,4096]{1,0:T(2,128)S(1)}, u32[]{:S(2)}, u32[]{:S(2)}) collective-permute-start(f32[2,4096]{1,0:T(2,128)S(1)} %add.35.grads), channel_id=1, source_target_pairs={{0,1},{1,0},{2,3},{3,2},{4,5},{5,4},{6,7},{7,6},{8,9},{9,8},{10,11... | collective-permute-start | bytes 98312 | tf_op jit(solution)/shard_map/ppermute | solution.py:505
  152.5 4.5 %collective-permute-start.22 = (f32[2,256]{1,0:T(2,128)S(1)}, f32[2,256]{1,0:T(2,128)S(1)}, u32[]{:S(2)}, u32[]{:S(2)}) collective-permute-start(f32[2,256]{1,0:T(2,128)S(1)} %scores.1.refs_0_), channel_id=1, source_target_pairs={{0,8},{4,12},{8,0},{12,4},{1,9},{5,13},{9,1},{13,5},{2,10},{6,14},... | collective-permute-start | bytes 6152 | tf_op jit(solution)/shard_map/ppermute | solution.py:505
  154.7 4.3 %collective-permute-start.21 = (f32[4,4096]{1,0:T(4,128)S(1)}, f32[4,4096]{1,0:T(4,128)S(1)}, u32[]{:S(2)}, u32[]{:S(2)}) collective-permute-start(f32[4,4096]{1,0:T(4,128)S(1)} %pad_maximum_fusion.1), channel_id=1, source_target_pairs={{0,2},{1,3},{2,0},{3,1},{4,6},{5,7},{6,4},{7,5},{8,10},{9,11},{10,... | collective-permute-start | bytes 196616 | tf_op jit(solution)/shard_map/ppermute | solution.py:505
  157.0 4.4 %collective-permute-start.23 = (f32[2,256]{1,0:T(2,128)S(1)}, f32[2,256]{1,0:T(2,128)S(1)}, u32[]{:S(2)}, u32[]{:S(2)}) collective-permute-start(f32[2,256]{1,0:T(2,128)S(1)} %score_sum.1), channel_id=1, source_target_pairs={{0,4},{4,0},{8,12},{12,8},{1,5},{5,1},{9,13},{13,9},{2,6},{6,2},{1... | collective-permute-start | bytes 6152 | tf_op jit(solution)/shard_map/ppermute | solution.py:505
